TPU v7x, 128 devices: a whole 4x4x4 slice. The times are simulated.
128 devices in a mesh: row: 8 (over z, core), col: 16 (over y, x).
Axes of the slice: x: 4, y: 4, z: 4, core: 2. Of those that a mesh axis runs over, the one named last changes fastest.
Arguments:
- ancestor_inverse: bfloat16 [16384, 16384], P('col', 'row'), may hold values from -6 to 6
- level_one_panels: bfloat16 [2048, 16384], P('col', 'row'), may hold values from -0.046875 to 0.046875
- level_one_pattern: int32 [16, 128], P('col', 'row'), may hold values 0 or 1
- level_one_diag: float32 [2048, 128], replicated, may hold values from -6 to 6
- level_two_panels: bfloat16 [2048, 16384], P('col', 'row'), may hold values from -0.046875 to 0.046875
- level_two_pattern: int32 [16, 128], P('col', 'row'), may hold values 0 or 1
- parent_lead: bfloat16 [2048, 128], P('col'), may hold values from -0.5 to 0.5
- level_two_diag: float32 [2048, 128], P('col'), may hold values from -6 to 6
- parents: int32 [16], P('col'), may hold values from 0 to 15
Outputs:
- level_one_rows: bfloat16 [2048, 16384], P('col', 'row')
- level_one_inv: float32 [2048, 128], P('col')
- level_two_rows: bfloat16 [2048, 16384], P('col', 'row')
- level_two_lead: float32 [2048, 128], P('col')
- level_two_inv: float32 [2048, 128], P('col')
Inputs may be any that keep to these rules, and one draw needn't show every extreme that they name: `parents`: each entry names a first-level supernode, 0 to 15.
All inputs are finite; a program needn't handle non-finite values. No bound on the sum of `level_one_pattern` or of `level_two_pattern` on one device may be relied on, other than what follows from the above.
Results may differ from a plain program's by a relative error of at most 0.008.
Values may be sent and summed in bfloat16 or wider, within the bound.
No kernel may reach another device: no remote copies, remote signals or barrier semaphores. Data moves between devices by JAX's collectives and lax.ppermute only.
A program may use at most 192 MiB of HBM per device.

v0:
```python
import jax
import jax.numpy as jnp
from jax import lax
from jax.experimental import pallas as pl
from jax.experimental.pallas import tpu as pltpu
from jax.sharding import PartitionSpec as P

SIDE = 4
CORES = 2
F32 = jnp.float32


def x_step(d):
    return [(y * SIDE + x, y * SIDE + (x + d) % SIDE) for y in range(SIDE) for x in range(SIDE)]


def y_step(d):
    return [(y * SIDE + x, (y + d) % SIDE * SIDE + x) for y in range(SIDE) for x in range(SIDE)]


def z_step(d):
    return [(z * CORES + e, (z + d) % SIDE * CORES + e) for z in range(SIDE) for e in range(CORES)]


CORE_SWAP = [(i, i ^ 1) for i in range(SIDE * CORES)]


def turn(k):
    cols, rows = SIDE * SIDE, SIDE * CORES
    return [
        (r * cols + c, c // 2 * cols + 2 * r + (c + k) % 2) for r in range(rows) for c in range(cols)
    ]


def apply_pattern(panels, pattern, block):
    count, blocks = pattern.shape
    shaped = panels.reshape(count, block, blocks, block)
    return (shaped * pattern.astype(panels.dtype)[:, None, :, None]).reshape(panels.shape)


def own_panels(masked):
    col = lax.axis_index("col")
    half = masked.shape[1] // 2
    pieces = []
    for k in range(2):
        part = lax.dynamic_slice_in_dim(masked, (col + k) % 2 * half, half, 1)
        pieces.append(lax.ppermute(part, ("row", "col"), turn(k)))
    even = col % 2 == 0
    return jnp.stack(
        [jnp.where(even, pieces[0], pieces[1]), jnp.where(even, pieces[1], pieces[0])]
    )


def all_panels(own):
    below = lax.ppermute(own, "row", z_step(1))
    above = lax.ppermute(own, "row", z_step(-1))
    far = jnp.stack(
        [lax.ppermute(below[0], "row", z_step(1)), lax.ppermute(above[1], "row", z_step(-1))]
    )
    found = []
    for held in (own, below, above, far):
        found += [held, lax.ppermute(held, "row", CORE_SWAP)]
    return found


def arrival(supernode):
    row = lax.axis_index("row")
    z, core = row // CORES, row % CORES
    source = supernode // 2
    slot = jnp.array([0, 2, 3, 1], jnp.int32)[(source // CORES - z) % SIDE]
    return slot * 4 + (source + core) % CORES * 2 + supernode % 2


def ring_kernel(order, dots, operands, adds, last, shape):
    rows, columns = shape
    half = rows // 2
    kind = jnp.bfloat16
    split = not adds
    if last:
        outs = [((half, columns), kind)] * 2 + [((SIDE - 1, rows, columns), F32)]
    elif split:
        outs = [((SIDE, half, columns), kind)] * 2
    else:
        outs = [((SIDE, rows, columns), kind)]

    def kernel(order_ref, *refs):
        given = refs[: len(operands)]
        sums = refs[len(operands) : len(operands) + len(adds)]
        out = refs[len(operands) + len(adds) :]
        for j, start, term in dots(order_ref, *given):
            size = term.shape[0]
            for lo in range(start, start + size, min(size, half)):
                n = min(size, half)
                value = term[lo - start : lo - start + n]
                for ref, (_, first) in zip(sums, adds, strict=True):
                    if first <= lo < first + ref.shape[1]:
                        value = value + ref[j, lo - first : lo - first + n].astype(F32)
                side, at = lo // half, lo % half
                if last and j == 2:
                    out[side][at : at + n] = value.astype(kind)
                elif last:
                    out[2][min(j, 2), lo : lo + n] = value
                elif split:
                    out[side][j, at : at + n] = value.astype(kind)
                else:
                    out[0][j, lo : lo + n] = value.astype(kind)

    depth = operands[0].shape[-1]
    return pl.pallas_call(
        kernel,
        out_shape=[jax.ShapeDtypeStruct(*o) for o in outs],
        in_specs=[whole(pltpu.SMEM)] + [whole()] * (len(operands) + len(adds)),
        out_specs=[whole()] * len(outs),
        compiler_params=pltpu.CompilerParams(vmem_limit_bytes=32 * 2**20),
        cost_estimate=pl.CostEstimate(
            flops=2 * SIDE * rows * columns * depth,
            bytes_accessed=2 * SIDE * rows * columns,
            transcendentals=0,
        ),
    )(order, *operands, *[v for v, _ in adds])


def by_column(pieces, matrix, block):
    rows, depth = pieces[0].shape[0] * pieces[0].shape[1], pieces[0].shape[2]
    width = matrix.shape[1]
    steps = len(pieces)

    def kernel(*refs):
        matrix_ref, out_ref, held = refs[steps:]
        for i in range(steps):

            @pl.when(pl.program_id(0) == i)
            def _():
                held[...] = refs[i][...].reshape(rows, depth)

        total = jnp.dot(held[...], matrix_ref[...], preferred_element_type=F32)
        for d in range(width // block):
            out_ref[d] = total[:, d * block : (d + 1) * block].astype(out_ref.dtype)

    return pl.pallas_call(
        kernel,
        out_shape=jax.ShapeDtypeStruct((width // block, steps * rows, block), matrix.dtype),
        grid=(steps,),
        in_specs=[pl.BlockSpec(v.shape, lambda i: (0, 0, 0)) for v in pieces]
        + [pl.BlockSpec((depth, width), lambda i: (0, 0))],
        out_specs=pl.BlockSpec((width // block, rows, block), lambda i: (0, i, 0)),
        scratch_shapes=[pltpu.VMEM((rows, depth), matrix.dtype)],
        compiler_params=pltpu.CompilerParams(vmem_limit_bytes=52 * 2**20),
        cost_estimate=pl.CostEstimate(
            flops=2 * steps * rows * depth * width,
            bytes_accessed=2 * (steps * rows * (depth + width) + depth * width),
            transcendentals=0,
        ),
    )(*pieces, matrix)


def by_supernode(rows, matrix, part):
    block = rows.shape[1]
    width = matrix.shape[1] // 2

    def dots(order_ref, rows_ref, matrix_ref):
        left = jnp.concatenate([rows_ref[order_ref[j]] for j in range(SIDE)], 0)
        total = jnp.dot(
            left, matrix_ref[:, part * width : (part + 1) * width], preferred_element_type=F32
        )
        for j in range(SIDE):
            yield j, 0, total[j * block : (j + 1) * block]

    return lambda order, adds, last: ring_kernel(
        order, dots, [rows, matrix], adds, last, (block, width)
    )


def scatter_sum(step_of, orders, first, second):
    def send(value, step):
        return lax.ppermute(value.astype(jnp.bfloat16), "col", step)

    low, high = step_of(orders[2], [], False)
    half = low.shape[1]
    from_behind, from_ahead = send(low, first(1)), send(high, first(-1))
    (to_ahead,) = step_of(orders[1], [(from_behind, 0)], False)
    (to_behind,) = step_of(orders[3], [(from_ahead, half)], False)
    one, two = send(to_ahead, first(1)), send(to_behind, first(-1))
    low, high, rest = step_of(orders[0], [(one, 0), (two, 0)], True)

    far = jnp.concatenate([low, high], 0)
    terms = [send(rest[1], second(1)), send(rest[2], second(-1)), send(far, second(2))]
    return rest[0] + sum(v.astype(F32) for v in terms)


def row_parts(values):
    values = values + lax.ppermute(values, "row", CORE_SWAP)
    values = values.astype(jnp.bfloat16)
    return [values] + [lax.ppermute(values, "row", z_step(-d)) for d in range(1, SIDE)]


def whole(space=None):
    return pl.BlockSpec(memory_space=space or pltpu.VMEM)


def small_call(kernel, shapes, scalars, arrays, scratch=()):
    return pl.pallas_call(
        kernel,
        out_shape=[jax.ShapeDtypeStruct(shape, kind) for shape, kind in shapes],
        in_specs=[whole(pltpu.SMEM)] * len(scalars) + [whole()] * len(arrays),
        out_specs=[whole()] * len(shapes),
        scratch_shapes=list(scratch),
        compiler_params=pltpu.CompilerParams(vmem_limit_bytes=24 * 2**20),
    )(*scalars, *arrays)


def outgoing(place, readers, pattern, total):
    count, block = total.shape[:2]

    def kernel(place_ref, readers_ref, pattern_ref, total_ref, out_ref):
        for d in range(count):
            for j, k in enumerate((d, readers_ref[d])):
                value = total_ref[place_ref[k]].astype(F32) * pattern_ref[k].astype(F32)
                out_ref[d, j] = (-value).astype(out_ref.dtype)

    return small_call(
        kernel,
        [((count, 2, block, block), jnp.bfloat16)],
        [place, readers, pattern],
        [total],
    )[0]


def finish_rows(pattern, back, parent_panels, masked_one, masked_two, second, lead):
    count, _, block, _ = back.shape
    width = count * block
    kind = back.dtype

    def over(a, b):
        return lax.dot_general(a, b, (((1,), (1,)), ((), ())), preferred_element_type=F32)

    def kernel(
        pattern_ref, back_ref, panels_ref, one_ref, two_ref, second_ref, lead_ref,
        rows_one_ref, rows_two_ref, sums_ref, chosen, panels,
    ):
        for i in range(count):
            part = pl.ds(i * block, block)
            rows_one_ref[:, part] = back_ref[i, 0]
            chosen[:, part] = back_ref[i, 1]
            panels[:, part] = panels_ref[i]
        for i in range(count):
            part = pl.ds(i * block, block)
            total = second_ref[:, part].astype(F32) + jnp.dot(
                lead_ref[...], chosen[:, part], preferred_element_type=F32
            )
            rows_two_ref[:, part] = (-(total * pattern_ref[0, i].astype(F32))).astype(kind)
        sums_ref[0] = over(one_ref[...], rows_one_ref[...])
        sums_ref[1] = over(two_ref[...], chosen[...])
        sums_ref[2] = over(panels[...], chosen[...])
        sums_ref[3] = over(two_ref[...], rows_two_ref[...])

    return small_call(
        kernel,
        [((block, width), kind), ((block, width), kind), ((4, block, block), F32)],
        [pattern],
        [back, parent_panels, masked_one, masked_two, second, lead],
        [pltpu.VMEM((block, width), kind), pltpu.VMEM((block, width), kind)],
    )


def finish_blocks(z, parts, own_diag, parent_diag, two_diag, lead):
    block = lead.shape[0]

    def kernel(z_ref, a, b, c, d, own_ref, parent_ref, two_ref, lead_ref, one_out, lead_out, two_out, sums):
        held = (a, b, c, d)
        for k in range(SIDE):

            @pl.when(z_ref[0] == k)
            def _():
                w = [held[(i - k) % SIDE][...].astype(F32) for i in range(SIDE)]
                sums[...] = (w[0] + w[1]) + (w[2] + w[3])

        one_out[...] = own_ref[...] - sums[0]
        lead_wide = lead_ref[...].astype(F32)
        found = -(
            sums[1]
            + jnp.dot(
                lead_wide,
                parent_ref[...] - sums[2],
                precision=lax.Precision.HIGHEST,
                preferred_element_type=F32,
            )
        )
        lead_out[...] = found
        two_out[...] = (
            two_ref[...]
            - sums[3]
            - lax.dot_general(
                lead_wide,
                found,
                (((1,), (1,)), ((), ())),
                precision=lax.Precision.HIGHEST,
                preferred_element_type=F32,
            )
        )

    return small_call(
        kernel,
        [((block, block), F32)] * 3,
        [z],
        [*parts, own_diag, parent_diag, two_diag, lead],
        [pltpu.VMEM((4, block, block), F32)],
    )


def per_device(
    ancestor_inverse,
    level_one_panels,
    level_one_pattern,
    level_one_diag,
    level_two_panels,
    level_two_pattern,
    parent_lead,
    level_two_diag,
    parents,
):
    block = level_one_diag.shape[1]
    bf16 = jnp.bfloat16
    col = lax.axis_index("col")
    x, y = col % SIDE, col // SIDE
    count = SIDE * SIDE
    span, width = ancestor_inverse.shape
    masked_one = apply_pattern(level_one_panels, level_one_pattern, block)
    masked_two = apply_pattern(level_two_panels, level_two_pattern, block)

    own_one = own_panels(masked_one)
    later_two, _ = lax.optimization_barrier((masked_two, own_one))
    own_two = own_panels(later_two)
    found_one = all_panels(own_one)
    own_two, found_one = lax.optimization_barrier((own_two, found_one))
    found_two = all_panels(own_two)
    product_one = by_column(found_one, ancestor_inverse, block)
    later_one, product_one = lax.optimization_barrier((masked_one, product_one))
    first_sum = lax.psum_scatter(
        product_one.reshape(count * count * block, block), "col", scatter_dimension=0, tiled=True
    ).reshape(count, block, block)

    facts = jnp.concatenate(
        [
            jnp.broadcast_to(level_one_pattern.reshape(count, 1, 1), (count, 8, block)),
            jnp.broadcast_to(parents.reshape(1, 1, 1), (count, 8, block)),
        ],
        1,
    ).astype(bf16)
    cut = jnp.swapaxes(later_one.reshape(block, count, block), 0, 1)
    cut = lax.all_to_all(jnp.concatenate([cut, facts], 1), "col", 0, 0, tiled=True)
    cut_pattern = cut[:, block, 0].astype(jnp.int32)
    readers = cut[:, block + 8, 0].astype(jnp.int32)
    parent_panels = lax.all_to_all(
        jnp.take(cut[:, :block], readers, axis=0), "col", 0, 0, tiled=True
    )

    steps = jnp.arange(count, dtype=jnp.int32)
    place = arrival(steps)
    outer, inner = steps // SIDE, steps % SIDE
    x_major = (y + inner) % SIDE * SIDE + (x + outer) % SIDE
    y_major = (y + outer) % SIDE * SIDE + (x + inner) % SIDE

    rows_two = jnp.concatenate(found_two, 0)

    def two_part(part, order, first, second):
        return scatter_sum(
            by_supernode(rows_two, ancestor_inverse, part),
            place[order].reshape(SIDE, SIDE),
            first,
            second,
        )

    second_sum = jnp.concatenate(
        [two_part(0, x_major, x_step, y_step), two_part(1, y_major, y_step, x_step)], 1
    )
    back = lax.all_to_all(
        outgoing(place, readers, cut_pattern, first_sum), "col", 0, 0, tiled=True
    )
    level_one_rows, level_two_rows, sums = finish_rows(
        level_two_pattern, back, parent_panels, masked_one, masked_two, second_sum, parent_lead
    )

    diag_blocks = level_one_diag.reshape(count, block, block)
    level_one_inv, level_two_lead, level_two_inv = finish_blocks(
        (lax.axis_index("row") // CORES).reshape(1),
        row_parts(sums),
        lax.dynamic_index_in_dim(diag_blocks, col, 0, keepdims=False),
        lax.dynamic_index_in_dim(diag_blocks, parents[0], 0, keepdims=False),
        level_two_diag,
        parent_lead,
    )
    return level_one_rows, level_one_inv, level_two_rows, level_two_lead, level_two_inv


def solution(mesh):
    in_specs = (
        P("col", "row"),
        P("col", "row"),
        P("col", "row"),
        P(),
        P("col", "row"),
        P("col", "row"),
        P("col", None),
        P("col", None),
        P("col"),
    )
    out_specs = (P("col", "row"), P("col", None), P("col", "row"), P("col", None), P("col", None))
    return jax.shard_map(
        per_device, mesh=mesh, in_specs=in_specs, out_specs=out_specs, check_vma=False
    )
```

profile of v0, /device:TPU:1, one launch (start us, length us, event | category | flops | bytes accessed | tf_op | source)
XLA Modules:
  0.0 287.5 jit_solution(586644754116337638)
XLA Ops:
  10.0 6.0 %collective-permute-start = (bf16[128,1024]{1,0:T(8,128)(2,1)S(1)}, bf16[128,1024]{1,0:T(8,128)(2,1)S(1)}, u32[]{:S(2)}, u32[]{:S(2)}) collective-permute-start(bf16[128,1024]{1,0:T(8,128)(2,1)S(1)} %get-tuple-element.75), channel_id=1, source_target_pairs={{0,0},{1,1},{2,16},{3,17},{4,32},{5,33},{6,48},{7,49},{8,64},{9,65... | collective-permute-start | bytes 786440 | tf_op jit(solution)/shard_map/ppermute | solution.py:47
  16.7 5.2 %collective-permute-done = bf16[128,1024]{1,0:T(8,128)(2,1)S(1)} collective-permute-done((bf16[128,1024]{1,0:T(8,128)(2,1)S(1)}, bf16[128,1024]{1,0:T(8,128)(2,1)S(1)}, u32[]{:S(2)}, u32[]{:S(2)}) %collective-permute-start) | collective-permute-done | bytes 262176 | tf_op jit(solution)/shard_map/ppermute | solution.py:47
  24.6 15.4 %collective-permute-start.7 = (bf16[2,128,1024]{2,1,0:T(8,128)(2,1)S(1)}, bf16[2,128,1024]{2,1,0:T(8,128)(2,1)S(1)}, u32[]{:S(2)}, u32[]{:S(2)}) collective-permute-start(bf16[2,128,1024]{2,1,0:T(8,128)(2,1)S(1)} %pad_maximum_fusion.1.refs_0_), channel_id=1, source_target_pairs={{0,96},{16,112},{32,0},{48,16},{64,32},{80,48},{96,64},{112,80},{1... | collective-permute-start | bytes 1572872 | tf_op jit(solution)/shard_map/ppermute | solution.py:56
  40.0 8.9 %collective-permute-done.7.refs_4_ = bf16[2,128,1024]{2,1,0:T(8,128)(2,1)S(1)} collective-permute-done((bf16[2,128,1024]{2,1,0:T(8,128)(2,1)S(1)}, bf16[2,128,1024]{2,1,0:T(8,128)(2,1)S(1)}, u32[]{:S(2)}, u32[]{:S(2)}) %collective-permute-start.7) | collective-permute-done | bytes 524320 | tf_op jit(solution)/shard_map/ppermute | solution.py:56
  48.9 3.5 %collective-permute-start.10 = (bf16[128,1024]{1,0:T(8,128)(2,1)S(1)}, bf16[128,1024]{1,0:T(8,128)(2,1)S(1)}, u32[]{:S(2)}, u32[]{:S(2)}) collective-permute-start(bf16[128,1024]{1,0:T(8,128)(2,1)S(1)} %slice_bitcast_fusion.6), channel_id=1, source_target_pairs={{0,96},{16,112},{32,0},{48,16},{64,32},{80,48},{96,64},{112,80},{1... | collective-permute-start | bytes 786440 | tf_op jit(solution)/shard_map/ppermute | solution.py:58
  52.5 8.0 %collective-permute-start.2 = (bf16[128,1024]{1,0:T(8,128)(2,1)S(1)}, bf16[128,1024]{1,0:T(8,128)(2,1)S(1)}, u32[]{:S(2)}, u32[]{:S(2)}) collective-permute-start(bf16[128,1024]{1,0:T(8,128)(2,1)S(1)} %get-tuple-element.71), channel_id=1, source_target_pairs={{0,0},{1,1},{2,16},{3,17},{4,32},{5,33},{6,48},{7,49},{8,64},{9,65... | collective-permute-start | bytes 786440 | tf_op jit(solution)/shard_map/ppermute | solution.py:47
  63.1 22.6 %collective-permute-start.8 = (bf16[2,128,1024]{2,1,0:T(8,128)(2,1)S(1)}, bf16[2,128,1024]{2,1,0:T(8,128)(2,1)S(1)}, u32[]{:S(2)}, u32[]{:S(2)}) collective-permute-start(bf16[2,128,1024]{2,1,0:T(8,128)(2,1)S(1)} %collective-permute-done.7.refs_4_), channel_id=1, source_target_pairs={{0,16},{16,0},{32,48},{48,32},{64,80},{80,64},{96,112},{112,96},{1... | collective-permute-start | bytes 1572872 | tf_op jit(solution)/shard_map/ppermute | solution.py:62
  88.8 14.7 %shard_map.137 = bf16[16,2048,128]{2,1,0:T(8,128)(2,1)} custom-call(bf16[2,128,1024]{2,1,0:T(8,128)(2,1)S(1)} %pad_maximum_fusion.1.refs_0_, bf16[2,128,1024]{2,1,0:T(8,128)(2,1)S(1)} %collective-permute-done.4.refs_1_, bf16[2,128,1024]{2,1,0:T(8,128)(2,1)S(1)} %collective-permute-done.5.refs_2_, bf16[2,128,1024]{2,1,0:T(8,128)(2,1)} %copy-done.20, ...), custom_call_target="tpu_custom_call" | custom-call | flops 8589934592 | bytes 16777216 | tf_op jit(solution)/shard_map/pallas_call | solution.py:140
  107.8 2.6 collective-permute-start.15
  112.0 9.7 %collective-permute-done.13 = bf16[2,128,1024]{2,1,0:T(8,128)(2,1)} collective-permute-done((bf16[2,128,1024]{2,1,0:T(8,128)(2,1)S(1)}, bf16[2,128,1024]{2,1,0:T(8,128)(2,1)}, u32[]{:S(2)}, u32[]{:S(2)}) %collective-permute-start.13) | collective-permute-done | bytes 524320 | tf_op jit(solution)/shard_map/ppermute | solution.py:55
  123.8 2.9 %collective-permute-start.18 = (bf16[128,1024]{1,0:T(8,128)(2,1)S(1)}, bf16[128,1024]{1,0:T(8,128)(2,1)S(1)}, u32[]{:S(2)}, u32[]{:S(2)}) collective-permute-start(bf16[128,1024]{1,0:T(8,128)(2,1)S(1)} %slice_bitcast_fusion.4), channel_id=1, source_target_pairs={{0,96},{16,112},{32,0},{48,16},{64,32},{80,48},{96,64},{112,80},{1... | collective-permute-start | bytes 786440 | tf_op jit(solution)/shard_map/ppermute | solution.py:58
  135.0 2.7 shard_map.143
  138.7 6.4 %all-to-all-start = ((bf16[16,144,128]{2,1,0:T(8,128)(2,1)}), bf16[16,144,128]{2,1,0:T(8,128)(2,1)}, u32[]{:S(2)}, u32[]{:S(2)}) async-start(bf16[16,144,128]{2,1,0:T(8,128)(2,1)} %fusion.1), calls=%async_computation | async-start | bytes 1179648 | tf_op jit(solution)/shard_map/all_to_all | solution.py:351
  145.1 2.5 collective-permute-start.29
  152.9 2.8 shard_map.139
  158.3 10.3 %collective-permute-done.27.refs_2_ = bf16[4,64,1024]{2,1,0:T(8,128)(2,1)S(1)} collective-permute-done((bf16[4,64,1024]{2,1,0:T(8,128)(2,1)}, bf16[4,64,1024]{2,1,0:T(8,128)(2,1)S(1)}, u32[]{:S(2)}, u32[]{:S(2)}) %collective-permute-start.27) | collective-permute-done | bytes 524320 | tf_op jit(solution)/shard_map/ppermute | solution.py:176
  168.6 2.8 shard_map.144
  171.4 4.1 %collective-permute-done.29.refs_2_ = bf16[4,64,1024]{2,1,0:T(8,128)(2,1)S(1)} collective-permute-done((bf16[4,64,1024]{2,1,0:T(8,128)(2,1)}, bf16[4,64,1024]{2,1,0:T(8,128)(2,1)S(1)}, u32[]{:S(2)}, u32[]{:S(2)}) %collective-permute-start.29) | collective-permute-done | bytes 524320 | tf_op jit(solution)/shard_map/ppermute | solution.py:176
  175.5 2.8 shard_map.145
  191.4 2.8 shard_map.141
  197.4 3.6 %all-to-all-start.2 = ((bf16[16,128,128]{2,1,0:T(8,128)(2,1)}), bf16[16,128,128]{2,1,0:T(8,128)(2,1)S(1)}, u32[]{:S(2)}, u32[]{:S(2)}) async-start(bf16[16,128,128]{2,1,0:T(8,128)(2,1)} %broadcast_select_fusion), calls=%async_computation.3 | async-start | bytes 1048576 | tf_op jit(solution)/shard_map/all_to_all | solution.py:354
  201.0 3.2 %collective-permute-done.28.refs_2_ = bf16[4,128,1024]{2,1,0:T(8,128)(2,1)} collective-permute-done((bf16[4,128,1024]{2,1,0:T(8,128)(2,1)}, bf16[4,128,1024]{2,1,0:T(8,128)(2,1)}, u32[]{:S(2)}, u32[]{:S(2)}) %collective-permute-start.28) | collective-permute-done | bytes 1048608 | tf_op jit(solution)/shard_map/ppermute | solution.py:176
  204.2 7.2 %collective-permute-done.30.refs_3_ = bf16[4,128,1024]{2,1,0:T(8,128)(2,1)} collective-permute-done((bf16[4,128,1024]{2,1,0:T(8,128)(2,1)}, bf16[4,128,1024]{2,1,0:T(8,128)(2,1)}, u32[]{:S(2)}, u32[]{:S(2)}) %collective-permute-start.30) | collective-permute-done | bytes 1048608 | tf_op jit(solution)/shard_map/ppermute | solution.py:176
  215.8 2.8 shard_map.146
  223.9 2.8 shard_map.142
  233.4 5.7 %all-to-all-start.1 = ((bf16[16,2,128,128]{3,2,1,0:T(8,128)(2,1)}), bf16[16,2,128,128]{3,2,1,0:T(8,128)(2,1)S(1)}, u32[]{:S(2)}, u32[]{:S(2)}) async-start(bf16[16,2,128,128]{3,2,1,0:T(8,128)(2,1)} %shard_map.138), calls=%async_computation.2 | async-start | bytes 2097152 | tf_op jit(solution)/shard_map/all_to_all | solution.py:377
  239.2 2.6 collective-permute-start.25
  243.1 13.0 %collective-permute-done.25 = bf16[128,1024]{1,0:T(8,128)(2,1)S(1)} collective-permute-done((bf16[128,1024]{1,0:T(8,128)(2,1)S(1)}, bf16[128,1024]{1,0:T(8,128)(2,1)S(1)}, u32[]{:S(2)}, u32[]{:S(2)}) %collective-permute-start.25) | collective-permute-done | bytes 262176 | tf_op jit(solution)/shard_map/ppermute | solution.py:176
  256.2 3.6 %collective-permute-done.24 = bf16[128,1024]{1,0:T(8,128)(2,1)S(1)} collective-permute-done((bf16[128,1024]{1,0:T(8,128)(2,1)S(1)}, bf16[128,1024]{1,0:T(8,128)(2,1)S(1)}, u32[]{:S(2)}, u32[]{:S(2)}) %collective-permute-start.24) | collective-permute-done | bytes 262176 | tf_op jit(solution)/shard_map/ppermute | solution.py:176
  267.0 3.3 %collective-permute-start.35 = (bf16[4,128,128]{2,1,0:T(8,128)(2,1)S(1)}, bf16[4,128,128]{2,1,0:T(8,128)(2,1)S(1)}, u32[]{:S(2)}, u32[]{:S(2)}) collective-permute-start(bf16[4,128,128]{2,1,0:T(8,128)(2,1)S(1)} %add_convert_fusion.a), channel_id=1, source_target_pairs={{0,96},{16,112},{32,0},{48,16},{64,32},{80,48},{96,64},{112,80},{1... | collective-permute-start | bytes 393224 | tf_op jit(solution)/shard_map/ppermute | solution.py:194
  271.8 3.8 %collective-permute-done.35.b = bf16[4,128,128]{2,1,0:T(8,128)(2,1)S(1)} collective-permute-done((bf16[4,128,128]{2,1,0:T(8,128)(2,1)S(1)}, bf16[4,128,128]{2,1,0:T(8,128)(2,1)S(1)}, u32[]{:S(2)}, u32[]{:S(2)}) %collective-permute-start.35) | collective-permute-done | bytes 131104 | tf_op jit(solution)/shard_map/ppermute | solution.py:194
  276.3 3.2 %collective-permute-done.37.d = bf16[4,128,128]{2,1,0:T(8,128)(2,1)S(1)} collective-permute-done((bf16[4,128,128]{2,1,0:T(8,128)(2,1)S(1)}, bf16[4,128,128]{2,1,0:T(8,128)(2,1)S(1)}, u32[]{:S(2)}, u32[]{:S(2)}) %collective-permute-start.37) | collective-permute-done | bytes 131104 | tf_op jit(solution)/shard_map/ppermute | solution.py:194
  (169 shorter events, 80.4 us)
Async XLA Ops:
  7.2 222.6 %reduce-scatter.2.cloned.1.call-start = ((), (), s32[]{:S(2)}) async-start(), calls=%async_computation.4 | async-start | bytes 8912896 | tf_op jit(solution)/shard_map/reduce_scatter | solution.py:339
  10.0 11.9 %collective-permute-start = (bf16[128,1024]{1,0:T(8,128)(2,1)S(1)}, bf16[128,1024]{1,0:T(8,128)(2,1)S(1)}, u32[]{:S(2)}, u32[]{:S(2)}) collective-permute-start(bf16[128,1024]{1,0:T(8,128)(2,1)S(1)} %get-tuple-element.75), channel_id=1, source_target_pairs={{0,0},{1,1},{2,16},{3,17},{4,32},{5,33},{6,48},{7,49},{8,64},{9,65... | collective-permute-start | bytes 786440 | tf_op jit(solution)/shard_map/ppermute | solution.py:47
  24.6 24.3 %collective-permute-start.7 = (bf16[2,128,1024]{2,1,0:T(8,128)(2,1)S(1)}, bf16[2,128,1024]{2,1,0:T(8,128)(2,1)S(1)}, u32[]{:S(2)}, u32[]{:S(2)}) collective-permute-start(bf16[2,128,1024]{2,1,0:T(8,128)(2,1)S(1)} %pad_maximum_fusion.1.refs_0_), channel_id=1, source_target_pairs={{0,96},{16,112},{32,0},{48,16},{64,32},{80,48},{96,64},{112,80},{1... | collective-permute-start | bytes 1572872 | tf_op jit(solution)/shard_map/ppermute | solution.py:56
  40.0 12.4 %collective-permute-start.5 = (bf16[2,128,1024]{2,1,0:T(8,128)(2,1)S(1)}, bf16[2,128,1024]{2,1,0:T(8,128)(2,1)S(1)}, u32[]{:S(2)}, u32[]{:S(2)}) collective-permute-start(bf16[2,128,1024]{2,1,0:T(8,128)(2,1)S(1)} %pad_maximum_fusion.1.refs_0_), channel_id=1, source_target_pairs={{0,32},{16,48},{32,64},{48,80},{64,96},{80,112},{96,0},{112,16},{1... | collective-permute-start | bytes 1572872 | tf_op jit(solution)/shard_map/ppermute | solution.py:55
  48.9 11.8 %collective-permute-start.10 = (bf16[128,1024]{1,0:T(8,128)(2,1)S(1)}, bf16[128,1024]{1,0:T(8,128)(2,1)S(1)}, u32[]{:S(2)}, u32[]{:S(2)}) collective-permute-start(bf16[128,1024]{1,0:T(8,128)(2,1)S(1)} %slice_bitcast_fusion.6), channel_id=1, source_target_pairs={{0,96},{16,112},{32,0},{48,16},{64,32},{80,48},{96,64},{112,80},{1... | collective-permute-start | bytes 786440 | tf_op jit(solution)/shard_map/ppermute | solution.py:58
  52.4 10.7 %collective-permute-start.9 = (bf16[128,1024]{1,0:T(8,128)(2,1)S(1)}, bf16[128,1024]{1,0:T(8,128)(2,1)S(1)}, u32[]{:S(2)}, u32[]{:S(2)}) collective-permute-start(bf16[128,1024]{1,0:T(8,128)(2,1)S(1)} %slice_bitcast_fusion.7), channel_id=1, source_target_pairs={{0,32},{16,48},{32,64},{48,80},{64,96},{80,112},{96,0},{112,16},{1... | collective-permute-start | bytes 786440 | tf_op jit(solution)/shard_map/ppermute | solution.py:58
  52.5 33.2 %collective-permute-start.2 = (bf16[128,1024]{1,0:T(8,128)(2,1)S(1)}, bf16[128,1024]{1,0:T(8,128)(2,1)S(1)}, u32[]{:S(2)}, u32[]{:S(2)}) collective-permute-start(bf16[128,1024]{1,0:T(8,128)(2,1)S(1)} %get-tuple-element.71), channel_id=1, source_target_pairs={{0,0},{1,1},{2,16},{3,17},{4,32},{5,33},{6,48},{7,49},{8,64},{9,65... | collective-permute-start | bytes 786440 | tf_op jit(solution)/shard_map/ppermute | solution.py:47
  60.5 25.5 %collective-permute-start.4 = (bf16[2,128,1024]{2,1,0:T(8,128)(2,1)S(1)}, bf16[2,128,1024]{2,1,0:T(8,128)(2,1)S(1)}, u32[]{:S(2)}, u32[]{:S(2)}) collective-permute-start(bf16[2,128,1024]{2,1,0:T(8,128)(2,1)S(1)} %pad_maximum_fusion.1.refs_0_), channel_id=1, source_target_pairs={{0,16},{16,0},{32,48},{48,32},{64,80},{80,64},{96,112},{112,96},{1... | collective-permute-start | bytes 1572872 | tf_op jit(solution)/shard_map/ppermute | solution.py:62
  60.6 25.2 %collective-permute-start.3 = (bf16[128,1024]{1,0:T(8,128)(2,1)S(1)}, bf16[128,1024]{1,0:T(8,128)(2,1)S(1)}, u32[]{:S(2)}, u32[]{:S(2)}) collective-permute-start(bf16[128,1024]{1,0:T(8,128)(2,1)S(1)} %get-tuple-element.72), channel_id=1, source_target_pairs={{0,1},{1,0},{2,17},{3,16},{4,33},{5,32},{6,49},{7,48},{8,65},{9,64... | collective-permute-start | bytes 786440 | tf_op jit(solution)/shard_map/ppermute | solution.py:47
  60.7 25.3 %collective-permute-start.6 = (bf16[2,128,1024]{2,1,0:T(8,128)(2,1)S(1)}, bf16[2,128,1024]{2,1,0:T(8,128)(2,1)S(1)}, u32[]{:S(2)}, u32[]{:S(2)}) collective-permute-start(bf16[2,128,1024]{2,1,0:T(8,128)(2,1)S(1)} %collective-permute-done.5.refs_2_), channel_id=1, source_target_pairs={{0,16},{16,0},{32,48},{48,32},{64,80},{80,64},{96,112},{112,96},{1... | collective-permute-start | bytes 1572872 | tf_op jit(solution)/shard_map/ppermute | solution.py:62
  63.1 24.1 %collective-permute-start.8 = (bf16[2,128,1024]{2,1,0:T(8,128)(2,1)S(1)}, bf16[2,128,1024]{2,1,0:T(8,128)(2,1)S(1)}, u32[]{:S(2)}, u32[]{:S(2)}) collective-permute-start(bf16[2,128,1024]{2,1,0:T(8,128)(2,1)S(1)} %collective-permute-done.7.refs_4_), channel_id=1, source_target_pairs={{0,16},{16,0},{32,48},{48,32},{64,80},{80,64},{96,112},{112,96},{1... | collective-permute-start | bytes 1572872 | tf_op jit(solution)/shard_map/ppermute | solution.py:62
  104.9 16.8 %collective-permute-start.13 = (bf16[2,128,1024]{2,1,0:T(8,128)(2,1)S(1)}, bf16[2,128,1024]{2,1,0:T(8,128)(2,1)}, u32[]{:S(2)}, u32[]{:S(2)}) collective-permute-start(bf16[2,128,1024]{2,1,0:T(8,128)(2,1)S(1)} %pad_maximum_fusion.2), channel_id=1, source_target_pairs={{0,32},{16,48},{32,64},{48,80},{64,96},{80,112},{96,0},{112,16},{1... | collective-permute-start | bytes 1572872 | tf_op jit(solution)/shard_map/ppermute | solution.py:55
  107.8 15.9 %collective-permute-start.15 = (bf16[2,128,1024]{2,1,0:T(8,128)(2,1)S(1)}, bf16[2,128,1024]{2,1,0:T(8,128)(2,1)S(1)}, u32[]{:S(2)}, u32[]{:S(2)}) collective-permute-start(bf16[2,128,1024]{2,1,0:T(8,128)(2,1)S(1)} %pad_maximum_fusion.2), channel_id=1, source_target_pairs={{0,96},{16,112},{32,0},{48,16},{64,32},{80,48},{96,64},{112,80},{1... | collective-permute-start | bytes 1572872 | tf_op jit(solution)/shard_map/ppermute | solution.py:56
  111.1 16.0 %collective-permute-start.12 = (bf16[2,128,1024]{2,1,0:T(8,128)(2,1)S(1)}, bf16[2,128,1024]{2,1,0:T(8,128)(2,1)S(1)}, u32[]{:S(2)}, u32[]{:S(2)}) collective-permute-start(bf16[2,128,1024]{2,1,0:T(8,128)(2,1)S(1)} %pad_maximum_fusion.2), channel_id=1, source_target_pairs={{0,16},{16,0},{32,48},{48,32},{64,80},{80,64},{96,112},{112,96},{1... | collective-permute-start | bytes 1572872 | tf_op jit(solution)/shard_map/ppermute | solution.py:62
  122.8 10.6 %collective-permute-start.14 = (bf16[2,128,1024]{2,1,0:T(8,128)(2,1)}, bf16[2,128,1024]{2,1,0:T(8,128)(2,1)S(1)}, u32[]{:S(2)}, u32[]{:S(2)}) collective-permute-start(bf16[2,128,1024]{2,1,0:T(8,128)(2,1)} %collective-permute-done.13), channel_id=1, source_target_pairs={{0,16},{16,0},{32,48},{48,32},{64,80},{80,64},{96,112},{112,96},{1... | collective-permute-start | bytes 1572872 | tf_op jit(solution)/shard_map/ppermute | solution.py:62
  137.7 30.9 %collective-permute-start.27 = (bf16[4,64,1024]{2,1,0:T(8,128)(2,1)}, bf16[4,64,1024]{2,1,0:T(8,128)(2,1)S(1)}, u32[]{:S(2)}, u32[]{:S(2)}) collective-permute-start(bf16[4,64,1024]{2,1,0:T(8,128)(2,1)} %get-tuple-element.50), channel_id=1, source_target_pairs={{0,4},{1,5},{2,6},{3,7},{4,8},{5,9},{6,10},{7,11},{8,12},{9,13},{1... | collective-permute-start | bytes 1572872 | tf_op jit(solution)/shard_map/ppermute | solution.py:176
  138.7 41.8 %all-to-all-start = ((bf16[16,144,128]{2,1,0:T(8,128)(2,1)}), bf16[16,144,128]{2,1,0:T(8,128)(2,1)}, u32[]{:S(2)}, u32[]{:S(2)}) async-start(bf16[16,144,128]{2,1,0:T(8,128)(2,1)} %fusion.1), calls=%async_computation | async-start | bytes 1179648 | tf_op jit(solution)/shard_map/all_to_all | solution.py:351
  145.1 30.5 %collective-permute-start.29 = (bf16[4,64,1024]{2,1,0:T(8,128)(2,1)}, bf16[4,64,1024]{2,1,0:T(8,128)(2,1)S(1)}, u32[]{:S(2)}, u32[]{:S(2)}) collective-permute-start(bf16[4,64,1024]{2,1,0:T(8,128)(2,1)} %get-tuple-element.51), channel_id=1, source_target_pairs={{0,12},{1,13},{2,14},{3,15},{4,0},{5,1},{6,2},{7,3},{8,4},{9,5},{1... | collective-permute-start | bytes 1572872 | tf_op jit(solution)/shard_map/ppermute | solution.py:176
  155.6 28.2 %collective-permute-start.20 = (bf16[4,64,1024]{2,1,0:T(8,128)(2,1)}, bf16[4,64,1024]{2,1,0:T(8,128)(2,1)S(1)}, u32[]{:S(2)}, u32[]{:S(2)}) collective-permute-start(bf16[4,64,1024]{2,1,0:T(8,128)(2,1)} %get-tuple-element.45), channel_id=1, source_target_pairs={{0,1},{1,2},{2,3},{3,0},{4,5},{5,6},{6,7},{7,4},{8,9},{9,10},{10,1... | collective-permute-start | bytes 1572872 | tf_op jit(solution)/shard_map/ppermute | solution.py:176
  157.0 34.5 %collective-permute-start.22 = (bf16[4,64,1024]{2,1,0:T(8,128)(2,1)}, bf16[4,64,1024]{2,1,0:T(8,128)(2,1)S(1)}, u32[]{:S(2)}, u32[]{:S(2)}) collective-permute-start(bf16[4,64,1024]{2,1,0:T(8,128)(2,1)} %get-tuple-element.46), channel_id=1, source_target_pairs={{0,3},{1,0},{2,1},{3,2},{4,7},{5,4},{6,5},{7,6},{8,11},{9,8},{10,9... | collective-permute-start | bytes 1572872 | tf_op jit(solution)/shard_map/ppermute | solution.py:176
  171.4 32.8 %collective-permute-start.28 = (bf16[4,128,1024]{2,1,0:T(8,128)(2,1)}, bf16[4,128,1024]{2,1,0:T(8,128)(2,1)}, u32[]{:S(2)}, u32[]{:S(2)}) collective-permute-start(bf16[4,128,1024]{2,1,0:T(8,128)(2,1)} %shard_map.144), channel_id=1, source_target_pairs={{0,4},{1,5},{2,6},{3,7},{4,8},{5,9},{6,10},{7,11},{8,12},{9,13},{1... | collective-permute-start | bytes 3145736 | tf_op jit(solution)/shard_map/ppermute | solution.py:176
  178.3 33.1 %collective-permute-start.30 = (bf16[4,128,1024]{2,1,0:T(8,128)(2,1)}, bf16[4,128,1024]{2,1,0:T(8,128)(2,1)}, u32[]{:S(2)}, u32[]{:S(2)}) collective-permute-start(bf16[4,128,1024]{2,1,0:T(8,128)(2,1)} %shard_map.145), channel_id=1, source_target_pairs={{0,12},{1,13},{2,14},{3,15},{4,0},{5,1},{6,2},{7,3},{8,4},{9,5},{1... | collective-permute-start | bytes 3145736 | tf_op jit(solution)/shard_map/ppermute | solution.py:176
  190.3 33.7 %collective-permute-start.21 = (bf16[4,128,1024]{2,1,0:T(8,128)(2,1)S(1)}, bf16[4,128,1024]{2,1,0:T(8,128)(2,1)}, u32[]{:S(2)}, u32[]{:S(2)}) collective-permute-start(bf16[4,128,1024]{2,1,0:T(8,128)(2,1)S(1)} %shard_map.140), channel_id=1, source_target_pairs={{0,1},{1,2},{2,3},{3,0},{4,5},{5,6},{6,7},{7,4},{8,9},{9,10},{10,1... | collective-permute-start | bytes 3145736 | tf_op jit(solution)/shard_map/ppermute | solution.py:176
  194.2 29.8 %collective-permute-start.23 = (bf16[4,128,1024]{2,1,0:T(8,128)(2,1)}, bf16[4,128,1024]{2,1,0:T(8,128)(2,1)}, u32[]{:S(2)}, u32[]{:S(2)}) collective-permute-start(bf16[4,128,1024]{2,1,0:T(8,128)(2,1)} %shard_map.141), channel_id=1, source_target_pairs={{0,3},{1,0},{2,1},{3,2},{4,7},{5,4},{6,5},{7,6},{8,11},{9,8},{10,9... | collective-permute-start | bytes 3145736 | tf_op jit(solution)/shard_map/ppermute | solution.py:176
  197.4 35.2 %all-to-all-start.2 = ((bf16[16,128,128]{2,1,0:T(8,128)(2,1)}), bf16[16,128,128]{2,1,0:T(8,128)(2,1)S(1)}, u32[]{:S(2)}, u32[]{:S(2)}) async-start(bf16[16,128,128]{2,1,0:T(8,128)(2,1)} %broadcast_select_fusion), calls=%async_computation.3 | async-start | bytes 1048576 | tf_op jit(solution)/shard_map/all_to_all | solution.py:354
  219.4 22.4 %collective-permute-start.33 = (bf16[128,1024]{1,0:T(8,128)(2,1)}, bf16[128,1024]{1,0:T(8,128)(2,1)S(1)}, u32[]{:S(2)}, u32[]{:S(2)}) collective-permute-start(bf16[128,1024]{1,0:T(8,128)(2,1)} %pad_maximum_fusion.6), channel_id=1, source_target_pairs={{0,2},{1,3},{2,0},{3,1},{4,6},{5,7},{6,4},{7,5},{8,10},{9,11},{10,... | collective-permute-start | bytes 786440 | tf_op jit(solution)/shard_map/ppermute | solution.py:176
  222.5 19.3 %collective-permute-start.32 = (bf16[128,1024]{1,0:T(8,128)(2,1)}, bf16[128,1024]{1,0:T(8,128)(2,1)S(1)}, u32[]{:S(2)}, u32[]{:S(2)}) collective-permute-start(bf16[128,1024]{1,0:T(8,128)(2,1)} %get-tuple-element.68), channel_id=1, source_target_pairs={{0,3},{1,0},{2,1},{3,2},{4,7},{5,4},{6,5},{7,6},{8,11},{9,8},{10,9... | collective-permute-start | bytes 786440 | tf_op jit(solution)/shard_map/ppermute | solution.py:176
  223.9 17.9 %collective-permute-start.31 = (bf16[128,1024]{1,0:T(8,128)(2,1)}, bf16[128,1024]{1,0:T(8,128)(2,1)}, u32[]{:S(2)}, u32[]{:S(2)}) collective-permute-start(bf16[128,1024]{1,0:T(8,128)(2,1)} %get-tuple-element.67), channel_id=1, source_target_pairs={{0,1},{1,2},{2,3},{3,0},{4,5},{5,6},{6,7},{7,4},{8,9},{9,10},{10,1... | collective-permute-start | bytes 786440 | tf_op jit(solution)/shard_map/ppermute | solution.py:176
  227.6 15.5 %collective-permute-start.26 = (bf16[128,1024]{1,0:T(8,128)(2,1)}, bf16[128,1024]{1,0:T(8,128)(2,1)}, u32[]{:S(2)}, u32[]{:S(2)}) collective-permute-start(bf16[128,1024]{1,0:T(8,128)(2,1)} %pad_maximum_fusion.5), channel_id=1, source_target_pairs={{0,8},{1,9},{2,10},{3,11},{4,12},{5,13},{6,14},{7,15},{8,0},{9,1},... | collective-permute-start | bytes 786440 | tf_op jit(solution)/shard_map/ppermute | solution.py:176
  233.4 27.7 %all-to-all-start.1 = ((bf16[16,2,128,128]{3,2,1,0:T(8,128)(2,1)}), bf16[16,2,128,128]{3,2,1,0:T(8,128)(2,1)S(1)}, u32[]{:S(2)}, u32[]{:S(2)}) async-start(bf16[16,2,128,128]{3,2,1,0:T(8,128)(2,1)} %shard_map.138), calls=%async_computation.2 | async-start | bytes 2097152 | tf_op jit(solution)/shard_map/all_to_all | solution.py:377
  239.2 17.0 %collective-permute-start.25 = (bf16[128,1024]{1,0:T(8,128)(2,1)S(1)}, bf16[128,1024]{1,0:T(8,128)(2,1)S(1)}, u32[]{:S(2)}, u32[]{:S(2)}) collective-permute-start(bf16[128,1024]{1,0:T(8,128)(2,1)S(1)} %get-tuple-element.66), channel_id=1, source_target_pairs={{0,12},{1,13},{2,14},{3,15},{4,0},{5,1},{6,2},{7,3},{8,4},{9,5},{1... | collective-permute-start | bytes 786440 | tf_op jit(solution)/shard_map/ppermute | solution.py:176
  241.8 17.9 %collective-permute-start.24 = (bf16[128,1024]{1,0:T(8,128)(2,1)S(1)}, bf16[128,1024]{1,0:T(8,128)(2,1)S(1)}, u32[]{:S(2)}, u32[]{:S(2)}) collective-permute-start(bf16[128,1024]{1,0:T(8,128)(2,1)S(1)} %get-tuple-element.65), channel_id=1, source_target_pairs={{0,4},{1,5},{2,6},{3,7},{4,8},{5,9},{6,10},{7,11},{8,12},{9,13},{1... | collective-permute-start | bytes 786440 | tf_op jit(solution)/shard_map/ppermute | solution.py:176
  (33 other events, 239.5 us)
Sparse Core Ops, SparseCore 0:
  103.7 104.9 reduce-scatter.1
where the time goes:
time: 289 us; the launch traced here: 288 us
  starting transfers between devices  109 us (38%)
  waiting for transfers between devices  83.8 us (29%)
  Pallas kernels  41.2 us (14%)
  local copies, waits for them, and re-layouts  27.5 us (10%)
  between operations  15.3 us (5%)
  other arithmetic  10.6 us (4%)
    ppermute x14, waiting for transfers between devices, send(): return lax.ppermute(value.astype(jnp.bfloat16), 'col', step)  41.5 us
    ppermute x8, starting transfers between devices, all_panels(): found += [held, lax.ppermute(held, 'row', CORE_SWAP)]  28.1 us
    pallas_call x8, Pallas kernels, ring_kernel(): pl.pallas_call(kernel, out_shape=[jax.ShapeDtypeStruct(*o) for o in outs]...  21.3 us
    unnamed x54, local copies, waits for them, and re-layouts  19.6 us
    ppermute x14, starting transfers between devices, send(): return lax.ppermute(value.astype(jnp.bfloat16), 'col', step)  18.3 us
    ppermute x2, starting transfers between devices, all_panels(): above = lax.ppermute(own, 'row', z_step(-1))  18 us
    ppermute x4, starting transfers between devices, own_panels(): pieces.append(lax.ppermute(part, ('row', 'col'), turn(k)))  14.8 us
    pallas_call x1, Pallas kernels, by_column(): pl.pallas_call(kernel, out_shape=jax.ShapeDtypeStruct((width // block, st...  14.7 us
  transfers between devices with their start and end apart: 42, of which 19 were waited for; matrix products, arithmetic and copies ran while one was open for 6% of the time, Pallas kernels for 8%

commit v1 on v0

--- a/solution.py
+++ b/solution.py
@@ -8,6 +8,7 @@
 SIDE = 4
 CORES = 2
 F32 = jnp.float32
+RING_VMEM = 18 * 2**20
 
 
 def x_step(d):
@@ -111,7 +112,7 @@
         out_shape=[jax.ShapeDtypeStruct(*o) for o in outs],
         in_specs=[whole(pltpu.SMEM)] + [whole()] * (len(operands) + len(adds)),
         out_specs=[whole()] * len(outs),
-        compiler_params=pltpu.CompilerParams(vmem_limit_bytes=32 * 2**20),
+        compiler_params=pltpu.CompilerParams(vmem_limit_bytes=RING_VMEM),
         cost_estimate=pl.CostEstimate(
             flops=2 * SIDE * rows * columns * depth,
             bytes_accessed=2 * SIDE * rows * columns,
@@ -181,11 +182,14 @@
     (to_ahead,) = step_of(orders[1], [(from_behind, 0)], False)
     (to_behind,) = step_of(orders[3], [(from_ahead, half)], False)
     one, two = send(to_ahead, first(1)), send(to_behind, first(-1))
-    low, high, rest = step_of(orders[0], [(one, 0), (two, 0)], True)
-
-    far = jnp.concatenate([low, high], 0)
-    terms = [send(rest[1], second(1)), send(rest[2], second(-1)), send(far, second(2))]
-    return rest[0] + sum(v.astype(F32) for v in terms)
+
+    def finish(one, two):
+        low, high, rest = step_of(orders[0], [(one, 0), (two, 0)], True)
+        far = jnp.concatenate([low, high], 0)
+        terms = [send(rest[1], second(1)), send(rest[2], second(-1)), send(far, second(2))]
+        return rest[0] + sum(v.astype(F32) for v in terms)
+
+    return one, two, finish
 
 
 def row_parts(values):
@@ -328,12 +332,9 @@
     masked_one = apply_pattern(level_one_panels, level_one_pattern, block)
     masked_two = apply_pattern(level_two_panels, level_two_pattern, block)
 
-    own_one = own_panels(masked_one)
-    later_two, _ = lax.optimization_barrier((masked_two, own_one))
+    found_one = all_panels(own_panels(masked_one))
+    later_two, found_one = lax.optimization_barrier((masked_two, found_one))
     own_two = own_panels(later_two)
-    found_one = all_panels(own_one)
-    own_two, found_one = lax.optimization_barrier((own_two, found_one))
-    found_two = all_panels(own_two)
     product_one = by_column(found_one, ancestor_inverse, block)
     later_one, product_one = lax.optimization_barrier((masked_one, product_one))
     first_sum = lax.psum_scatter(
@@ -349,11 +350,13 @@
     ).astype(bf16)
     cut = jnp.swapaxes(later_one.reshape(block, count, block), 0, 1)
     cut = lax.all_to_all(jnp.concatenate([cut, facts], 1), "col", 0, 0, tiled=True)
+    own_two, cut = lax.optimization_barrier((own_two, cut))
     cut_pattern = cut[:, block, 0].astype(jnp.int32)
     readers = cut[:, block + 8, 0].astype(jnp.int32)
     parent_panels = lax.all_to_all(
         jnp.take(cut[:, :block], readers, axis=0), "col", 0, 0, tiled=True
     )
+    found_two, parent_panels = lax.optimization_barrier((all_panels(own_two), parent_panels))
 
     steps = jnp.arange(count, dtype=jnp.int32)
     place = arrival(steps)
@@ -371,12 +374,12 @@
             second,
         )
 
-    second_sum = jnp.concatenate(
-        [two_part(0, x_major, x_step, y_step), two_part(1, y_major, y_step, x_step)], 1
-    )
-    back = lax.all_to_all(
-        outgoing(place, readers, cut_pattern, first_sum), "col", 0, 0, tiled=True
-    )
+    one_a, two_a, finish_a = two_part(0, x_major, x_step, y_step)
+    one_b, two_b, finish_b = two_part(1, y_major, y_step, x_step)
+    going = outgoing(place, readers, cut_pattern, first_sum)
+    back = lax.all_to_all(going, "col", 0, 0, tiled=True)
+    one_a, two_a, one_b, two_b, _ = lax.optimization_barrier((one_a, two_a, one_b, two_b, going))
+    second_sum = jnp.concatenate([finish_a(one_a, two_a), finish_b(one_b, two_b)], 1)
     level_one_rows, level_two_rows, sums = finish_rows(
         level_two_pattern, back, parent_panels, masked_one, masked_two, second_sum, parent_lead
     )

time: 289 us -> 291 us (level)
  waiting for transfers between devices: 83.8 us -> 100 us
  local copies, waits for them, and re-layouts: 27.5 us -> 18.5 us
  other arithmetic: 10.6 us -> 6.33 us
    all_to_all x1, waiting for transfers between devices: 0.01 us -> 16.2 us  [per_device(): lax.all_to_all(jnp.concatenate([cut, facts], 1), 'col', 0, 0, tiled=True)]
    ppermute x2, waiting for transfers between devices: 8.89 us -> 19.2 us  [all_panels(): above = lax.ppermute(own, 'row', z_step(-1))]
    ppermute x2, waiting for transfers between devices: 9.74 us -> 0.01 us  [all_panels(): below = lax.ppermute(own, 'row', z_step(1))]
    all_to_all x1, waiting for transfers between devices: 0.01 us -> 8.64 us  [per_device(): lax.all_to_all(jnp.take(cut[:, :block], readers, axis=0), 'col', 0, 0, ti...]
    unnamed x54 -> x43, local copies, waits for them, and re-layouts: 19.6 us -> 12.4 us
    ppermute x1, starting transfers between devices: 1.43 us -> 7.8 us  [row_parts(): values = values + lax.ppermute(values, 'row', CORE_SWAP)]
    ppermute x8, starting transfers between devices: 28.1 us -> 24.2 us  [all_panels(): found += [held, lax.ppermute(held, 'row', CORE_SWAP)]]
    ppermute x14, waiting for transfers between devices: 41.5 us -> 38 us  [send(): return lax.ppermute(value.astype(jnp.bfloat16), 'col', step)]
  transfers between devices with their start and end apart: 42 -> 42, of which waited for: 19 -> 19; matrix products, arithmetic and copies ran while one was open for 6% -> 5% of each run, Pallas kernels for 8% -> 7%
where the time goes in v1:
time: 291 us; the launch traced here: 290 us
  starting transfers between devices  111 us (38%)
  waiting for transfers between devices  100 us (34%)
  Pallas kernels  39.5 us (14%)
  local copies, waits for them, and re-layouts  18.5 us (6%)
  between operations  15.4 us (5%)
  other arithmetic  6.33 us (2%)
    ppermute x14, waiting for transfers between devices, send(): return lax.ppermute(value.astype(jnp.bfloat16), 'col', step)  38 us
    ppermute x8, starting transfers between devices, all_panels(): found += [held, lax.ppermute(held, 'row', CORE_SWAP)]  24.2 us
    pallas_call x8, Pallas kernels, ring_kernel(): pl.pallas_call(kernel, out_shape=[jax.ShapeDtypeStruct(*o) for o in outs]...  19.4 us
    ppermute x2, waiting for transfers between devices, all_panels(): above = lax.ppermute(own, 'row', z_step(-1))  19.2 us
    ppermute x14, starting transfers between devices, send(): return lax.ppermute(value.astype(jnp.bfloat16), 'col', step)  18.4 us
    ppermute x2, starting transfers between devices, all_panels(): above = lax.ppermute(own, 'row', z_step(-1))  18.1 us
    all_to_all x1, waiting for transfers between devices, per_device(): lax.all_to_all(jnp.concatenate([cut, facts], 1), 'col', 0, 0, tiled=True)  16.2 us
    pallas_call x1, Pallas kernels, by_column(): pl.pallas_call(kernel, out_shape=jax.ShapeDtypeStruct((width // block, st...  14.8 us
  transfers between devices with their start and end apart: 42, of which 19 were waited for; matrix products, arithmetic and copies ran while one was open for 5% of the time, Pallas kernels for 7%

profile of v1, /device:TPU:1, one launch (start us, length us, event | category | flops | bytes accessed | tf_op | source)
XLA Modules:
  0.0 290.4 jit_solution(7026709927323687601)
XLA Ops:
  9.2 6.0 %collective-permute-start = (bf16[128,1024]{1,0:T(8,128)(2,1)S(1)}, bf16[128,1024]{1,0:T(8,128)(2,1)S(1)}, u32[]{:S(2)}, u32[]{:S(2)}) collective-permute-start(bf16[128,1024]{1,0:T(8,128)(2,1)S(1)} %get-tuple-element.103), channel_id=1, source_target_pairs={{0,0},{1,1},{2,16},{3,17},{4,32},{5,33},{6,48},{7,49},{8,64},{9,65... | collective-permute-start | bytes 786440 | tf_op jit(solution)/shard_map/ppermute | solution.py:48
  15.9 5.2 %collective-permute-done = bf16[128,1024]{1,0:T(8,128)(2,1)S(1)} collective-permute-done((bf16[128,1024]{1,0:T(8,128)(2,1)S(1)}, bf16[128,1024]{1,0:T(8,128)(2,1)S(1)}, u32[]{:S(2)}, u32[]{:S(2)}) %collective-permute-start) | collective-permute-done | bytes 262176 | tf_op jit(solution)/shard_map/ppermute | solution.py:48
  23.7 15.4 %collective-permute-start.5 = (bf16[2,128,1024]{2,1,0:T(8,128)(2,1)S(1)}, bf16[2,128,1024]{2,1,0:T(8,128)(2,1)S(1)}, u32[]{:S(2)}, u32[]{:S(2)}) collective-permute-start(bf16[2,128,1024]{2,1,0:T(8,128)(2,1)S(1)} %pad_maximum_fusion.1.refs_0_), channel_id=1, source_target_pairs={{0,96},{16,112},{32,0},{48,16},{64,32},{80,48},{96,64},{112,80},{1... | collective-permute-start | bytes 1572872 | tf_op jit(solution)/shard_map/ppermute | solution.py:57
  39.1 8.9 %collective-permute-done.5.refs_4_ = bf16[2,128,1024]{2,1,0:T(8,128)(2,1)S(1)} collective-permute-done((bf16[2,128,1024]{2,1,0:T(8,128)(2,1)S(1)}, bf16[2,128,1024]{2,1,0:T(8,128)(2,1)S(1)}, u32[]{:S(2)}, u32[]{:S(2)}) %collective-permute-start.5) | collective-permute-done | bytes 524320 | tf_op jit(solution)/shard_map/ppermute | solution.py:57
  48.0 3.5 %collective-permute-start.8 = (bf16[128,1024]{1,0:T(8,128)(2,1)S(1)}, bf16[128,1024]{1,0:T(8,128)(2,1)S(1)}, u32[]{:S(2)}, u32[]{:S(2)}) collective-permute-start(bf16[128,1024]{1,0:T(8,128)(2,1)S(1)} %slice_bitcast_fusion.6), channel_id=1, source_target_pairs={{0,96},{16,112},{32,0},{48,16},{64,32},{80,48},{96,64},{112,80},{1... | collective-permute-start | bytes 786440 | tf_op jit(solution)/shard_map/ppermute | solution.py:59
  51.6 6.9 %collective-permute-start.2 = (bf16[2,128,1024]{2,1,0:T(8,128)(2,1)S(1)}, bf16[2,128,1024]{2,1,0:T(8,128)(2,1)S(1)}, u32[]{:S(2)}, u32[]{:S(2)}) collective-permute-start(bf16[2,128,1024]{2,1,0:T(8,128)(2,1)S(1)} %pad_maximum_fusion.1.refs_0_), channel_id=1, source_target_pairs={{0,16},{16,0},{32,48},{48,32},{64,80},{80,64},{96,112},{112,96},{1... | collective-permute-start | bytes 1572872 | tf_op jit(solution)/shard_map/ppermute | solution.py:63
  59.1 7.0 %collective-permute-start.9 = (bf16[2,128,1024]{2,1,0:T(8,128)(2,1)S(1)}, bf16[2,128,1024]{2,1,0:T(8,128)(2,1)S(1)}, u32[]{:S(2)}, u32[]{:S(2)}) collective-permute-start(bf16[2,128,1024]{2,1,0:T(8,128)(2,1)S(1)} %pad_maximum_fusion.2.refs_6_), channel_id=1, source_target_pairs={{0,16},{16,0},{32,48},{48,32},{64,80},{80,64},{96,112},{112,96},{1... | collective-permute-start | bytes 1572872 | tf_op jit(solution)/shard_map/ppermute | solution.py:63
  68.5 14.8 %shard_map.137 = bf16[16,2048,128]{2,1,0:T(8,128)(2,1)} custom-call(bf16[2,128,1024]{2,1,0:T(8,128)(2,1)S(1)} %pad_maximum_fusion.1.refs_0_, bf16[2,128,1024]{2,1,0:T(8,128)(2,1)S(1)} %collective-permute-done.2.refs_1_, bf16[2,128,1024]{2,1,0:T(8,128)(2,1)S(1)} %collective-permute-done.3.refs_2_, bf16[2,128,1024]{2,1,0:T(8,128)(2,1)} %copy-done.15, ...), custom_call_target="tpu_custom_call" | custom-call | flops 8589934592 | bytes 16777216 | tf_op jit(solution)/shard_map/pallas_call | solution.py:141
  84.8 4.3 %collective-permute-start.10 = (bf16[128,1024]{1,0:T(8,128)(2,1)S(1)}, bf16[128,1024]{1,0:T(8,128)(2,1)S(1)}, u32[]{:S(2)}, u32[]{:S(2)}) collective-permute-start(bf16[128,1024]{1,0:T(8,128)(2,1)S(1)} %get-tuple-element.99), channel_id=1, source_target_pairs={{0,0},{1,1},{2,16},{3,17},{4,32},{5,33},{6,48},{7,49},{8,64},{9,65... | collective-permute-start | bytes 786440 | tf_op jit(solution)/shard_map/ppermute | solution.py:48
  91.8 8.6 %all-to-all-start = ((bf16[16,144,128]{2,1,0:T(8,128)(2,1)}), bf16[16,144,128]{2,1,0:T(8,128)(2,1)S(1)}, u32[]{:S(2)}, u32[]{:S(2)}) async-start(bf16[16,144,128]{2,1,0:T(8,128)(2,1)} %fusion.1), calls=%async_computation | async-start | bytes 1179648 | tf_op jit(solution)/shard_map/all_to_all | solution.py:352
  100.6 16.2 %all-to-all-done = bf16[16,144,128]{2,1,0:T(8,128)(2,1)S(1)} async-done(((bf16[16,144,128]{2,1,0:T(8,128)(2,1)}), bf16[16,144,128]{2,1,0:T(8,128)(2,1)S(1)}, u32[]{:S(2)}, u32[]{:S(2)}) %all-to-all-start) | async-done | bytes 589856 | tf_op jit(solution)/shard_map/all_to_all | solution.py:352
  116.8 6.9 %collective-permute-start.12 = (bf16[2,128,1024]{2,1,0:T(8,128)(2,1)S(1)}, bf16[2,128,1024]{2,1,0:T(8,128)(2,1)}, u32[]{:S(2)}, u32[]{:S(2)}) collective-permute-start(bf16[2,128,1024]{2,1,0:T(8,128)(2,1)S(1)} %pad_maximum_fusion.3), channel_id=1, source_target_pairs={{0,16},{16,0},{32,48},{48,32},{64,80},{80,64},{96,112},{112,96},{1... | collective-permute-start | bytes 1572872 | tf_op jit(solution)/shard_map/ppermute | solution.py:63
  123.6 2.7 collective-permute-start.15
  127.0 10.3 %collective-permute-done.15 = bf16[2,128,1024]{2,1,0:T(8,128)(2,1)S(1)} collective-permute-done((bf16[2,128,1024]{2,1,0:T(8,128)(2,1)S(1)}, bf16[2,128,1024]{2,1,0:T(8,128)(2,1)S(1)}, u32[]{:S(2)}, u32[]{:S(2)}) %collective-permute-start.15) | collective-permute-done | bytes 524320 | tf_op jit(solution)/shard_map/ppermute | solution.py:57
  137.4 3.5 %collective-permute-start.18 = (bf16[128,1024]{1,0:T(8,128)(2,1)S(1)}, bf16[128,1024]{1,0:T(8,128)(2,1)}, u32[]{:S(2)}, u32[]{:S(2)}) collective-permute-start(bf16[128,1024]{1,0:T(8,128)(2,1)S(1)} %slice_bitcast_fusion.4), channel_id=1, source_target_pairs={{0,96},{16,112},{32,0},{48,16},{64,32},{80,48},{96,64},{112,80},{1... | collective-permute-start | bytes 786440 | tf_op jit(solution)/shard_map/ppermute | solution.py:59
  143.4 5.7 %all-to-all-start.2 = ((bf16[16,128,128]{2,1,0:T(8,128)(2,1)}), bf16[16,128,128]{2,1,0:T(8,128)(2,1)S(1)}, u32[]{:S(2)}, u32[]{:S(2)}) async-start(bf16[16,128,128]{2,1,0:T(8,128)(2,1)} %broadcast_select_fusion), calls=%async_computation.3 | async-start | bytes 1048576 | tf_op jit(solution)/shard_map/all_to_all | solution.py:356
  154.5 8.6 %all-to-all-done.2.panels_ref = bf16[16,128,128]{2,1,0:T(8,128)(2,1)S(1)} async-done(((bf16[16,128,128]{2,1,0:T(8,128)(2,1)}), bf16[16,128,128]{2,1,0:T(8,128)(2,1)S(1)}, u32[]{:S(2)}, u32[]{:S(2)}) %all-to-all-start.2) | async-done | bytes 524320 | tf_op jit(solution)/shard_map/all_to_all | solution.py:356
  178.4 7.4 %collective-permute-done.20.refs_2_ = bf16[4,64,1024]{2,1,0:T(8,128)(2,1)S(1)} collective-permute-done((bf16[4,64,1024]{2,1,0:T(8,128)(2,1)S(1)}, bf16[4,64,1024]{2,1,0:T(8,128)(2,1)S(1)}, u32[]{:S(2)}, u32[]{:S(2)}) %collective-permute-start.20) | collective-permute-done | bytes 524320 | tf_op jit(solution)/shard_map/ppermute | solution.py:177
  189.6 2.8 shard_map.141
  194.7 3.1 %collective-permute-done.24.refs_2_ = bf16[4,64,1024]{2,1,0:T(8,128)(2,1)S(1)} collective-permute-done((bf16[4,64,1024]{2,1,0:T(8,128)(2,1)S(1)}, bf16[4,64,1024]{2,1,0:T(8,128)(2,1)S(1)}, u32[]{:S(2)}, u32[]{:S(2)}) %collective-permute-start.24) | collective-permute-done | bytes 524320 | tf_op jit(solution)/shard_map/ppermute | solution.py:177
  197.8 2.8 shard_map.143
  200.6 2.8 shard_map.144
  208.9 3.7 %all-to-all-start.1 = ((bf16[16,2,128,128]{3,2,1,0:T(8,128)(2,1)}), bf16[16,2,128,128]{3,2,1,0:T(8,128)(2,1)S(1)}, u32[]{:S(2)}, u32[]{:S(2)}) async-start(bf16[16,2,128,128]{3,2,1,0:T(8,128)(2,1)} %shard_map.138), calls=%async_computation.2 | async-start | bytes 2097152 | tf_op jit(solution)/shard_map/all_to_all | solution.py:380
  212.6 19.5 %collective-permute-done.25.refs_2_ = bf16[4,128,1024]{2,1,0:T(8,128)(2,1)} collective-permute-done((bf16[4,128,1024]{2,1,0:T(8,128)(2,1)}, bf16[4,128,1024]{2,1,0:T(8,128)(2,1)}, u32[]{:S(2)}, u32[]{:S(2)}) %collective-permute-start.25) | collective-permute-done | bytes 1048608 | tf_op jit(solution)/shard_map/ppermute | solution.py:177
  238.2 2.8 shard_map.146
  242.9 2.8 shard_map.145
  246.2 3.3 %collective-permute-start.29 = (bf16[128,1024]{1,0:T(8,128)(2,1)S(1)}, bf16[128,1024]{1,0:T(8,128)(2,1)S(1)}, u32[]{:S(2)}, u32[]{:S(2)}) collective-permute-start(bf16[128,1024]{1,0:T(8,128)(2,1)S(1)} %get-tuple-element.94), channel_id=1, source_target_pairs={{0,12},{1,13},{2,14},{3,15},{4,0},{5,1},{6,2},{7,3},{8,4},{9,5},{1... | collective-permute-start | bytes 786440 | tf_op jit(solution)/shard_map/ppermute | solution.py:177
  252.9 3.9 %collective-permute-done.29 = bf16[128,1024]{1,0:T(8,128)(2,1)S(1)} collective-permute-done((bf16[128,1024]{1,0:T(8,128)(2,1)S(1)}, bf16[128,1024]{1,0:T(8,128)(2,1)S(1)}, u32[]{:S(2)}, u32[]{:S(2)}) %collective-permute-start.29) | collective-permute-done | bytes 262176 | tf_op jit(solution)/shard_map/ppermute | solution.py:177
  260.2 7.8 %collective-permute-start.34 = (f32[4,128,128]{2,1,0:T(8,128)S(1)}, f32[4,128,128]{2,1,0:T(8,128)S(1)}, u32[]{:S(2)}, u32[]{:S(2)}) collective-permute-start(f32[4,128,128]{2,1,0:T(8,128)S(1)} %get-tuple-element.84), channel_id=1, source_target_pairs={{0,16},{16,0},{32,48},{48,32},{64,80},{80,64},{96,112},{112,96},{1... | collective-permute-start | bytes 786440 | tf_op jit(solution)/shard_map/ppermute | solution.py:196
  269.2 4.0 %collective-permute-start.35 = (bf16[4,128,128]{2,1,0:T(8,128)(2,1)S(1)}, bf16[4,128,128]{2,1,0:T(8,128)(2,1)S(1)}, u32[]{:S(2)}, u32[]{:S(2)}) collective-permute-start(bf16[4,128,128]{2,1,0:T(8,128)(2,1)S(1)} %add_convert_fusion.a), channel_id=1, source_target_pairs={{0,96},{16,112},{32,0},{48,16},{64,32},{80,48},{96,64},{112,80},{1... | collective-permute-start | bytes 393224 | tf_op jit(solution)/shard_map/ppermute | solution.py:198
  274.8 4.1 %collective-permute-done.35.b = bf16[4,128,128]{2,1,0:T(8,128)(2,1)S(1)} collective-permute-done((bf16[4,128,128]{2,1,0:T(8,128)(2,1)S(1)}, bf16[4,128,128]{2,1,0:T(8,128)(2,1)S(1)}, u32[]{:S(2)}, u32[]{:S(2)}) %collective-permute-start.35) | collective-permute-done | bytes 131104 | tf_op jit(solution)/shard_map/ppermute | solution.py:198
  279.2 3.2 %collective-permute-done.37.d = bf16[4,128,128]{2,1,0:T(8,128)(2,1)S(1)} collective-permute-done((bf16[4,128,128]{2,1,0:T(8,128)(2,1)S(1)}, bf16[4,128,128]{2,1,0:T(8,128)(2,1)S(1)}, u32[]{:S(2)}, u32[]{:S(2)}) %collective-permute-start.37) | collective-permute-done | bytes 131104 | tf_op jit(solution)/shard_map/ppermute | solution.py:198
  (159 shorter events, 66.6 us)
Async XLA Ops:
  7.2 198.8 %reduce-scatter.2.cloned.1.call-start = ((), (), s32[]{:S(2)}) async-start(), calls=%async_computation.4 | async-start | bytes 8912896 | tf_op jit(solution)/shard_map/reduce_scatter | solution.py:340
  9.2 11.9 %collective-permute-start = (bf16[128,1024]{1,0:T(8,128)(2,1)S(1)}, bf16[128,1024]{1,0:T(8,128)(2,1)S(1)}, u32[]{:S(2)}, u32[]{:S(2)}) collective-permute-start(bf16[128,1024]{1,0:T(8,128)(2,1)S(1)} %get-tuple-element.103), channel_id=1, source_target_pairs={{0,0},{1,1},{2,16},{3,17},{4,32},{5,33},{6,48},{7,49},{8,64},{9,65... | collective-permute-start | bytes 786440 | tf_op jit(solution)/shard_map/ppermute | solution.py:48
  23.7 24.3 %collective-permute-start.5 = (bf16[2,128,1024]{2,1,0:T(8,128)(2,1)S(1)}, bf16[2,128,1024]{2,1,0:T(8,128)(2,1)S(1)}, u32[]{:S(2)}, u32[]{:S(2)}) collective-permute-start(bf16[2,128,1024]{2,1,0:T(8,128)(2,1)S(1)} %pad_maximum_fusion.1.refs_0_), channel_id=1, source_target_pairs={{0,96},{16,112},{32,0},{48,16},{64,32},{80,48},{96,64},{112,80},{1... | collective-permute-start | bytes 1572872 | tf_op jit(solution)/shard_map/ppermute | solution.py:57
  39.1 12.4 %collective-permute-start.3 = (bf16[2,128,1024]{2,1,0:T(8,128)(2,1)S(1)}, bf16[2,128,1024]{2,1,0:T(8,128)(2,1)S(1)}, u32[]{:S(2)}, u32[]{:S(2)}) collective-permute-start(bf16[2,128,1024]{2,1,0:T(8,128)(2,1)S(1)} %pad_maximum_fusion.1.refs_0_), channel_id=1, source_target_pairs={{0,32},{16,48},{32,64},{48,80},{64,96},{80,112},{96,0},{112,16},{1... | collective-permute-start | bytes 1572872 | tf_op jit(solution)/shard_map/ppermute | solution.py:56
  48.0 11.0 %collective-permute-start.8 = (bf16[128,1024]{1,0:T(8,128)(2,1)S(1)}, bf16[128,1024]{1,0:T(8,128)(2,1)S(1)}, u32[]{:S(2)}, u32[]{:S(2)}) collective-permute-start(bf16[128,1024]{1,0:T(8,128)(2,1)S(1)} %slice_bitcast_fusion.6), channel_id=1, source_target_pairs={{0,96},{16,112},{32,0},{48,16},{64,32},{80,48},{96,64},{112,80},{1... | collective-permute-start | bytes 786440 | tf_op jit(solution)/shard_map/ppermute | solution.py:59
  51.6 14.7 %collective-permute-start.2 = (bf16[2,128,1024]{2,1,0:T(8,128)(2,1)S(1)}, bf16[2,128,1024]{2,1,0:T(8,128)(2,1)S(1)}, u32[]{:S(2)}, u32[]{:S(2)}) collective-permute-start(bf16[2,128,1024]{2,1,0:T(8,128)(2,1)S(1)} %pad_maximum_fusion.1.refs_0_), channel_id=1, source_target_pairs={{0,16},{16,0},{32,48},{48,32},{64,80},{80,64},{96,112},{112,96},{1... | collective-permute-start | bytes 1572872 | tf_op jit(solution)/shard_map/ppermute | solution.py:63
  84.8 15.6 %collective-permute-start.10 = (bf16[128,1024]{1,0:T(8,128)(2,1)S(1)}, bf16[128,1024]{1,0:T(8,128)(2,1)S(1)}, u32[]{:S(2)}, u32[]{:S(2)}) collective-permute-start(bf16[128,1024]{1,0:T(8,128)(2,1)S(1)} %get-tuple-element.99), channel_id=1, source_target_pairs={{0,0},{1,1},{2,16},{3,17},{4,32},{5,33},{6,48},{7,49},{8,64},{9,65... | collective-permute-start | bytes 786440 | tf_op jit(solution)/shard_map/ppermute | solution.py:48
  89.1 11.3 %collective-permute-start.11 = (bf16[128,1024]{1,0:T(8,128)(2,1)S(1)}, bf16[128,1024]{1,0:T(8,128)(2,1)S(1)}, u32[]{:S(2)}, u32[]{:S(2)}) collective-permute-start(bf16[128,1024]{1,0:T(8,128)(2,1)S(1)} %get-tuple-element.100), channel_id=1, source_target_pairs={{0,1},{1,0},{2,17},{3,16},{4,33},{5,32},{6,49},{7,48},{8,65},{9,64... | collective-permute-start | bytes 786440 | tf_op jit(solution)/shard_map/ppermute | solution.py:48
  91.8 25.0 %all-to-all-start = ((bf16[16,144,128]{2,1,0:T(8,128)(2,1)}), bf16[16,144,128]{2,1,0:T(8,128)(2,1)S(1)}, u32[]{:S(2)}, u32[]{:S(2)}) async-start(bf16[16,144,128]{2,1,0:T(8,128)(2,1)} %fusion.1), calls=%async_computation | async-start | bytes 1179648 | tf_op jit(solution)/shard_map/all_to_all | solution.py:352
  116.8 46.4 %collective-permute-start.12 = (bf16[2,128,1024]{2,1,0:T(8,128)(2,1)S(1)}, bf16[2,128,1024]{2,1,0:T(8,128)(2,1)}, u32[]{:S(2)}, u32[]{:S(2)}) collective-permute-start(bf16[2,128,1024]{2,1,0:T(8,128)(2,1)S(1)} %pad_maximum_fusion.3), channel_id=1, source_target_pairs={{0,16},{16,0},{32,48},{48,32},{64,80},{80,64},{96,112},{112,96},{1... | collective-permute-start | bytes 1572872 | tf_op jit(solution)/shard_map/ppermute | solution.py:63
  123.6 17.2 %collective-permute-start.13 = (bf16[2,128,1024]{2,1,0:T(8,128)(2,1)S(1)}, bf16[2,128,1024]{2,1,0:T(8,128)(2,1)S(1)}, u32[]{:S(2)}, u32[]{:S(2)}) collective-permute-start(bf16[2,128,1024]{2,1,0:T(8,128)(2,1)S(1)} %pad_maximum_fusion.3), channel_id=1, source_target_pairs={{0,32},{16,48},{32,64},{48,80},{64,96},{80,112},{96,0},{112,16},{1... | collective-permute-start | bytes 1572872 | tf_op jit(solution)/shard_map/ppermute | solution.py:56
  123.6 13.7 %collective-permute-start.15 = (bf16[2,128,1024]{2,1,0:T(8,128)(2,1)S(1)}, bf16[2,128,1024]{2,1,0:T(8,128)(2,1)S(1)}, u32[]{:S(2)}, u32[]{:S(2)}) collective-permute-start(bf16[2,128,1024]{2,1,0:T(8,128)(2,1)S(1)} %pad_maximum_fusion.3), channel_id=1, source_target_pairs={{0,96},{16,112},{32,0},{48,16},{64,32},{80,48},{96,64},{112,80},{1... | collective-permute-start | bytes 1572872 | tf_op jit(solution)/shard_map/ppermute | solution.py:57
  137.4 14.0 %collective-permute-start.18 = (bf16[128,1024]{1,0:T(8,128)(2,1)S(1)}, bf16[128,1024]{1,0:T(8,128)(2,1)}, u32[]{:S(2)}, u32[]{:S(2)}) collective-permute-start(bf16[128,1024]{1,0:T(8,128)(2,1)S(1)} %slice_bitcast_fusion.4), channel_id=1, source_target_pairs={{0,96},{16,112},{32,0},{48,16},{64,32},{80,48},{96,64},{112,80},{1... | collective-permute-start | bytes 786440 | tf_op jit(solution)/shard_map/ppermute | solution.py:59
  141.6 9.8 %collective-permute-start.17 = (bf16[128,1024]{1,0:T(8,128)(2,1)}, bf16[128,1024]{1,0:T(8,128)(2,1)}, u32[]{:S(2)}, u32[]{:S(2)}) collective-permute-start(bf16[128,1024]{1,0:T(8,128)(2,1)} %slice_bitcast_fusion.5), channel_id=1, source_target_pairs={{0,32},{16,48},{32,64},{48,80},{64,96},{80,112},{96,0},{112,16},{1... | collective-permute-start | bytes 786440 | tf_op jit(solution)/shard_map/ppermute | solution.py:59
  143.4 19.8 %all-to-all-start.2 = ((bf16[16,128,128]{2,1,0:T(8,128)(2,1)}), bf16[16,128,128]{2,1,0:T(8,128)(2,1)S(1)}, u32[]{:S(2)}, u32[]{:S(2)}) async-start(bf16[16,128,128]{2,1,0:T(8,128)(2,1)} %broadcast_select_fusion), calls=%async_computation.3 | async-start | bytes 1048576 | tf_op jit(solution)/shard_map/all_to_all | solution.py:356
  149.1 14.1 %collective-permute-start.14 = (bf16[2,128,1024]{2,1,0:T(8,128)(2,1)}, bf16[2,128,1024]{2,1,0:T(8,128)(2,1)}, u32[]{:S(2)}, u32[]{:S(2)}) collective-permute-start(bf16[2,128,1024]{2,1,0:T(8,128)(2,1)} %copy-done.11), channel_id=1, source_target_pairs={{0,16},{16,0},{32,48},{48,32},{64,80},{80,64},{96,112},{112,96},{1... | collective-permute-start | bytes 1572872 | tf_op jit(solution)/shard_map/ppermute | solution.py:63
  151.3 11.9 %collective-permute-start.16 = (bf16[2,128,1024]{2,1,0:T(8,128)(2,1)S(1)}, bf16[2,128,1024]{2,1,0:T(8,128)(2,1)}, u32[]{:S(2)}, u32[]{:S(2)}) collective-permute-start(bf16[2,128,1024]{2,1,0:T(8,128)(2,1)S(1)} %collective-permute-done.15), channel_id=1, source_target_pairs={{0,16},{16,0},{32,48},{48,32},{64,80},{80,64},{96,112},{112,96},{1... | collective-permute-start | bytes 1572872 | tf_op jit(solution)/shard_map/ppermute | solution.py:63
  152.5 10.7 %collective-permute-start.19 = (bf16[2,128,1024]{2,1,0:T(8,128)(2,1)S(1)}, bf16[2,128,1024]{2,1,0:T(8,128)(2,1)}, u32[]{:S(2)}, u32[]{:S(2)}) collective-permute-start(bf16[2,128,1024]{2,1,0:T(8,128)(2,1)S(1)} %pad_maximum_fusion.4), channel_id=1, source_target_pairs={{0,16},{16,0},{32,48},{48,32},{64,80},{80,64},{96,112},{112,96},{1... | collective-permute-start | bytes 1572872 | tf_op jit(solution)/shard_map/ppermute | solution.py:63
  171.1 14.8 %collective-permute-start.20 = (bf16[4,64,1024]{2,1,0:T(8,128)(2,1)S(1)}, bf16[4,64,1024]{2,1,0:T(8,128)(2,1)S(1)}, u32[]{:S(2)}, u32[]{:S(2)}) collective-permute-start(bf16[4,64,1024]{2,1,0:T(8,128)(2,1)S(1)} %get-tuple-element.69), channel_id=1, source_target_pairs={{0,1},{1,2},{2,3},{3,0},{4,5},{5,6},{6,7},{7,4},{8,9},{9,10},{10,1... | collective-permute-start | bytes 1572872 | tf_op jit(solution)/shard_map/ppermute | solution.py:177
  172.5 17.1 %collective-permute-start.22 = (bf16[4,64,1024]{2,1,0:T(8,128)(2,1)S(1)}, bf16[4,64,1024]{2,1,0:T(8,128)(2,1)S(1)}, u32[]{:S(2)}, u32[]{:S(2)}) collective-permute-start(bf16[4,64,1024]{2,1,0:T(8,128)(2,1)S(1)} %get-tuple-element.70), channel_id=1, source_target_pairs={{0,3},{1,0},{2,1},{3,2},{4,7},{5,4},{6,5},{7,6},{8,11},{9,8},{10,9... | collective-permute-start | bytes 1572872 | tf_op jit(solution)/shard_map/ppermute | solution.py:177
  175.7 22.1 %collective-permute-start.24 = (bf16[4,64,1024]{2,1,0:T(8,128)(2,1)S(1)}, bf16[4,64,1024]{2,1,0:T(8,128)(2,1)S(1)}, u32[]{:S(2)}, u32[]{:S(2)}) collective-permute-start(bf16[4,64,1024]{2,1,0:T(8,128)(2,1)S(1)} %get-tuple-element.71), channel_id=1, source_target_pairs={{0,4},{1,5},{2,6},{3,7},{4,8},{5,9},{6,10},{7,11},{8,12},{9,13},{1... | collective-permute-start | bytes 1572872 | tf_op jit(solution)/shard_map/ppermute | solution.py:177
  176.9 23.6 %collective-permute-start.26 = (bf16[4,64,1024]{2,1,0:T(8,128)(2,1)S(1)}, bf16[4,64,1024]{2,1,0:T(8,128)(2,1)S(1)}, u32[]{:S(2)}, u32[]{:S(2)}) collective-permute-start(bf16[4,64,1024]{2,1,0:T(8,128)(2,1)S(1)} %get-tuple-element.72), channel_id=1, source_target_pairs={{0,12},{1,13},{2,14},{3,15},{4,0},{5,1},{6,2},{7,3},{8,4},{9,5},{1... | collective-permute-start | bytes 1572872 | tf_op jit(solution)/shard_map/ppermute | solution.py:177
  187.7 24.9 %collective-permute-start.21 = (bf16[4,128,1024]{2,1,0:T(8,128)(2,1)S(1)}, bf16[4,128,1024]{2,1,0:T(8,128)(2,1)}, u32[]{:S(2)}, u32[]{:S(2)}) collective-permute-start(bf16[4,128,1024]{2,1,0:T(8,128)(2,1)S(1)} %shard_map.140), channel_id=1, source_target_pairs={{0,1},{1,2},{2,3},{3,0},{4,5},{5,6},{6,7},{7,4},{8,9},{9,10},{10,1... | collective-permute-start | bytes 3145736 | tf_op jit(solution)/shard_map/ppermute | solution.py:177
  192.4 20.1 %collective-permute-start.23 = (bf16[4,128,1024]{2,1,0:T(8,128)(2,1)}, bf16[4,128,1024]{2,1,0:T(8,128)(2,1)}, u32[]{:S(2)}, u32[]{:S(2)}) collective-permute-start(bf16[4,128,1024]{2,1,0:T(8,128)(2,1)} %shard_map.141), channel_id=1, source_target_pairs={{0,3},{1,0},{2,1},{3,2},{4,7},{5,4},{6,5},{7,6},{8,11},{9,8},{10,9... | collective-permute-start | bytes 3145736 | tf_op jit(solution)/shard_map/ppermute | solution.py:177
  200.5 31.5 %collective-permute-start.25 = (bf16[4,128,1024]{2,1,0:T(8,128)(2,1)}, bf16[4,128,1024]{2,1,0:T(8,128)(2,1)}, u32[]{:S(2)}, u32[]{:S(2)}) collective-permute-start(bf16[4,128,1024]{2,1,0:T(8,128)(2,1)} %shard_map.143), channel_id=1, source_target_pairs={{0,4},{1,5},{2,6},{3,7},{4,8},{5,9},{6,10},{7,11},{8,12},{9,13},{1... | collective-permute-start | bytes 3145736 | tf_op jit(solution)/shard_map/ppermute | solution.py:177
  203.4 30.5 %collective-permute-start.27 = (bf16[4,128,1024]{2,1,0:T(8,128)(2,1)}, bf16[4,128,1024]{2,1,0:T(8,128)(2,1)}, u32[]{:S(2)}, u32[]{:S(2)}) collective-permute-start(bf16[4,128,1024]{2,1,0:T(8,128)(2,1)} %shard_map.144), channel_id=1, source_target_pairs={{0,12},{1,13},{2,14},{3,15},{4,0},{5,1},{6,2},{7,3},{8,4},{9,5},{1... | collective-permute-start | bytes 3145736 | tf_op jit(solution)/shard_map/ppermute | solution.py:177
  208.9 48.1 %all-to-all-start.1 = ((bf16[16,2,128,128]{3,2,1,0:T(8,128)(2,1)}), bf16[16,2,128,128]{3,2,1,0:T(8,128)(2,1)S(1)}, u32[]{:S(2)}, u32[]{:S(2)}) async-start(bf16[16,2,128,128]{3,2,1,0:T(8,128)(2,1)} %shard_map.138), calls=%async_computation.2 | async-start | bytes 2097152 | tf_op jit(solution)/shard_map/all_to_all | solution.py:380
  241.4 9.0 %collective-permute-start.32 = (bf16[128,1024]{1,0:T(8,128)(2,1)S(1)}, bf16[128,1024]{1,0:T(8,128)(2,1)S(1)}, u32[]{:S(2)}, u32[]{:S(2)}) collective-permute-start(bf16[128,1024]{1,0:T(8,128)(2,1)S(1)} %get-tuple-element.96), channel_id=1, source_target_pairs={{0,3},{1,0},{2,1},{3,2},{4,7},{5,4},{6,5},{7,6},{8,11},{9,8},{10,9... | collective-permute-start | bytes 786440 | tf_op jit(solution)/shard_map/ppermute | solution.py:177
  241.4 9.3 %collective-permute-start.31 = (bf16[128,1024]{1,0:T(8,128)(2,1)S(1)}, bf16[128,1024]{1,0:T(8,128)(2,1)S(1)}, u32[]{:S(2)}, u32[]{:S(2)}) collective-permute-start(bf16[128,1024]{1,0:T(8,128)(2,1)S(1)} %get-tuple-element.95), channel_id=1, source_target_pairs={{0,1},{1,2},{2,3},{3,0},{4,5},{5,6},{6,7},{7,4},{8,9},{9,10},{10,1... | collective-permute-start | bytes 786440 | tf_op jit(solution)/shard_map/ppermute | solution.py:177
  246.2 10.5 %collective-permute-start.29 = (bf16[128,1024]{1,0:T(8,128)(2,1)S(1)}, bf16[128,1024]{1,0:T(8,128)(2,1)S(1)}, u32[]{:S(2)}, u32[]{:S(2)}) collective-permute-start(bf16[128,1024]{1,0:T(8,128)(2,1)S(1)} %get-tuple-element.94), channel_id=1, source_target_pairs={{0,12},{1,13},{2,14},{3,15},{4,0},{5,1},{6,2},{7,3},{8,4},{9,5},{1... | collective-permute-start | bytes 786440 | tf_op jit(solution)/shard_map/ppermute | solution.py:177
  269.2 9.6 %collective-permute-start.35 = (bf16[4,128,128]{2,1,0:T(8,128)(2,1)S(1)}, bf16[4,128,128]{2,1,0:T(8,128)(2,1)S(1)}, u32[]{:S(2)}, u32[]{:S(2)}) collective-permute-start(bf16[4,128,128]{2,1,0:T(8,128)(2,1)S(1)} %add_convert_fusion.a), channel_id=1, source_target_pairs={{0,96},{16,112},{32,0},{48,16},{64,32},{80,48},{96,64},{112,80},{1... | collective-permute-start | bytes 393224 | tf_op jit(solution)/shard_map/ppermute | solution.py:198
  273.2 9.1 %collective-permute-start.37 = (bf16[4,128,128]{2,1,0:T(8,128)(2,1)S(1)}, bf16[4,128,128]{2,1,0:T(8,128)(2,1)S(1)}, u32[]{:S(2)}, u32[]{:S(2)}) collective-permute-start(bf16[4,128,128]{2,1,0:T(8,128)(2,1)S(1)} %add_convert_fusion.a), channel_id=1, source_target_pairs={{0,32},{16,48},{32,64},{48,80},{64,96},{80,112},{96,0},{112,16},{1... | collective-permute-start | bytes 393224 | tf_op jit(solution)/shard_map/ppermute | solution.py:198
  (28 other events, 307.0 us)
Sparse Core Ops, SparseCore 0:
  83.4 114.6 reduce-scatter.1

commit v2 on v1

--- a/solution.py
+++ b/solution.py
@@ -70,55 +70,6 @@
     source = supernode // 2
     slot = jnp.array([0, 2, 3, 1], jnp.int32)[(source // CORES - z) % SIDE]
     return slot * 4 + (source + core) % CORES * 2 + supernode % 2
-
-
-def ring_kernel(order, dots, operands, adds, last, shape):
-    rows, columns = shape
-    half = rows // 2
-    kind = jnp.bfloat16
-    split = not adds
-    if last:
-        outs = [((half, columns), kind)] * 2 + [((SIDE - 1, rows, columns), F32)]
-    elif split:
-        outs = [((SIDE, half, columns), kind)] * 2
-    else:
-        outs = [((SIDE, rows, columns), kind)]
-
-    def kernel(order_ref, *refs):
-        given = refs[: len(operands)]
-        sums = refs[len(operands) : len(operands) + len(adds)]
-        out = refs[len(operands) + len(adds) :]
-        for j, start, term in dots(order_ref, *given):
-            size = term.shape[0]
-            for lo in range(start, start + size, min(size, half)):
-                n = min(size, half)
-                value = term[lo - start : lo - start + n]
-                for ref, (_, first) in zip(sums, adds, strict=True):
-                    if first <= lo < first + ref.shape[1]:
-                        value = value + ref[j, lo - first : lo - first + n].astype(F32)
-                side, at = lo // half, lo % half
-                if last and j == 2:
-                    out[side][at : at + n] = value.astype(kind)
-                elif last:
-                    out[2][min(j, 2), lo : lo + n] = value
-                elif split:
-                    out[side][j, at : at + n] = value.astype(kind)
-                else:
-                    out[0][j, lo : lo + n] = value.astype(kind)
-
-    depth = operands[0].shape[-1]
-    return pl.pallas_call(
-        kernel,
-        out_shape=[jax.ShapeDtypeStruct(*o) for o in outs],
-        in_specs=[whole(pltpu.SMEM)] + [whole()] * (len(operands) + len(adds)),
-        out_specs=[whole()] * len(outs),
-        compiler_params=pltpu.CompilerParams(vmem_limit_bytes=RING_VMEM),
-        cost_estimate=pl.CostEstimate(
-            flops=2 * SIDE * rows * columns * depth,
-            bytes_accessed=2 * SIDE * rows * columns,
-            transcendentals=0,
-        ),
-    )(order, *operands, *[v for v, _ in adds])
 
 
 def by_column(pieces, matrix, block):
@@ -155,41 +106,57 @@
     )(*pieces, matrix)
 
 
-def by_supernode(rows, matrix, part):
-    block = rows.shape[1]
+def by_supernode(order, rows, matrix, part):
+    block, depth = rows.shape[1:]
     width = matrix.shape[1] // 2
-
-    def dots(order_ref, rows_ref, matrix_ref):
-        left = jnp.concatenate([rows_ref[order_ref[j]] for j in range(SIDE)], 0)
-        total = jnp.dot(
-            left, matrix_ref[:, part * width : (part + 1) * width], preferred_element_type=F32
-        )
-        for j in range(SIDE):
-            yield j, 0, total[j * block : (j + 1) * block]
-
-    return lambda order, adds, last: ring_kernel(
-        order, dots, [rows, matrix], adds, last, (block, width)
-    )
-
-
-def scatter_sum(step_of, orders, first, second):
-    def send(value, step):
-        return lax.ppermute(value.astype(jnp.bfloat16), "col", step)
-
-    low, high = step_of(orders[2], [], False)
-    half = low.shape[1]
-    from_behind, from_ahead = send(low, first(1)), send(high, first(-1))
-    (to_ahead,) = step_of(orders[1], [(from_behind, 0)], False)
-    (to_behind,) = step_of(orders[3], [(from_ahead, half)], False)
-    one, two = send(to_ahead, first(1)), send(to_behind, first(-1))
-
-    def finish(one, two):
-        low, high, rest = step_of(orders[0], [(one, 0), (two, 0)], True)
-        far = jnp.concatenate([low, high], 0)
-        terms = [send(rest[1], second(1)), send(rest[2], second(-1)), send(far, second(2))]
-        return rest[0] + sum(v.astype(F32) for v in terms)
-
-    return one, two, finish
+    groups = order.shape[0] // SIDE
+
+    def kernel(order_ref, rows_ref, matrix_ref, out_ref):
+        right = matrix_ref[:, part * width : (part + 1) * width]
+        for g in range(groups):
+            left = jnp.concatenate([rows_ref[order_ref[SIDE * g + j]] for j in range(SIDE)], 0)
+            total = jnp.dot(left, right, preferred_element_type=F32)
+            out_ref[g] = total.reshape(SIDE, block, width).astype(out_ref.dtype)
+
+    return pl.pallas_call(
+        kernel,
+        out_shape=jax.ShapeDtypeStruct((groups, SIDE, block, width), rows.dtype),
+        in_specs=[whole(pltpu.SMEM), whole(), whole()],
+        out_specs=whole(),
+        compiler_params=pltpu.CompilerParams(vmem_limit_bytes=RING_VMEM),
+        cost_estimate=pl.CostEstimate(
+            flops=2 * groups * SIDE * block * depth * width,
+            bytes_accessed=2 * groups * SIDE * block * (depth + width),
+            transcendentals=0,
+        ),
+    )(order, rows, matrix)
+
+
+def send(value, step):
+    return lax.ppermute(value.astype(jnp.bfloat16), "col", step)
+
+
+def first_sends(product, order, step):
+    far = product(order[2])[0]
+    half = far.shape[1] // 2
+    arriving = send(far[:, :half], step(1)), send(far[:, half:], step(-1))
+    near = product(jnp.concatenate([order[1], order[3], order[0]]))
+    return arriving, near
+
+
+def second_sends(arriving, near, step):
+    from_behind, from_ahead = [v.astype(F32) for v in arriving]
+    half = from_behind.shape[1]
+    wide = near.astype(F32)
+    to_ahead = jnp.concatenate([wide[0, :, :half] + from_behind, wide[0, :, half:]], 1)
+    to_behind = jnp.concatenate([wide[1, :, :half], wide[1, :, half:] + from_ahead], 1)
+    return send(to_ahead, step(1)), send(to_behind, step(-1))
+
+
+def third_sends(arriving, near, step):
+    total = near[2].astype(F32) + arriving[0].astype(F32) + arriving[1].astype(F32)
+    terms = [send(total[d], step(d)) for d in range(1, SIDE)]
+    return total[0] + sum(v.astype(F32) for v in terms)
 
 
 def row_parts(values):
@@ -335,8 +302,8 @@
     found_one = all_panels(own_panels(masked_one))
     later_two, found_one = lax.optimization_barrier((masked_two, found_one))
     own_two = own_panels(later_two)
+    later_one, own_two = lax.optimization_barrier((masked_one, own_two))
     product_one = by_column(found_one, ancestor_inverse, block)
-    later_one, product_one = lax.optimization_barrier((masked_one, product_one))
     first_sum = lax.psum_scatter(
         product_one.reshape(count * count * block, block), "col", scatter_dimension=0, tiled=True
     ).reshape(count, block, block)
@@ -350,13 +317,12 @@
     ).astype(bf16)
     cut = jnp.swapaxes(later_one.reshape(block, count, block), 0, 1)
     cut = lax.all_to_all(jnp.concatenate([cut, facts], 1), "col", 0, 0, tiled=True)
-    own_two, cut = lax.optimization_barrier((own_two, cut))
     cut_pattern = cut[:, block, 0].astype(jnp.int32)
     readers = cut[:, block + 8, 0].astype(jnp.int32)
     parent_panels = lax.all_to_all(
         jnp.take(cut[:, :block], readers, axis=0), "col", 0, 0, tiled=True
     )
-    found_two, parent_panels = lax.optimization_barrier((all_panels(own_two), parent_panels))
+    found_two = all_panels(own_two)
 
     steps = jnp.arange(count, dtype=jnp.int32)
     place = arrival(steps)
@@ -366,20 +332,20 @@
 
     rows_two = jnp.concatenate(found_two, 0)
 
-    def two_part(part, order, first, second):
-        return scatter_sum(
-            by_supernode(rows_two, ancestor_inverse, part),
-            place[order].reshape(SIDE, SIDE),
-            first,
-            second,
-        )
-
-    one_a, two_a, finish_a = two_part(0, x_major, x_step, y_step)
-    one_b, two_b, finish_b = two_part(1, y_major, y_step, x_step)
+    def product(part):
+        return lambda order: by_supernode(order, rows_two, ancestor_inverse, part)
+
+    first_a, near_a = first_sends(product(0), place[x_major].reshape(SIDE, SIDE), x_step)
+    first_b, near_b = first_sends(product(1), place[y_major].reshape(SIDE, SIDE), y_step)
+    first_a, first_b, parent_panels = lax.optimization_barrier((first_a, first_b, parent_panels))
+    second_a = second_sends(first_a, near_a, x_step)
+    second_b = second_sends(first_b, near_b, y_step)
     going = outgoing(place, readers, cut_pattern, first_sum)
     back = lax.all_to_all(going, "col", 0, 0, tiled=True)
-    one_a, two_a, one_b, two_b, _ = lax.optimization_barrier((one_a, two_a, one_b, two_b, going))
-    second_sum = jnp.concatenate([finish_a(one_a, two_a), finish_b(one_b, two_b)], 1)
+    second_a, second_b, _ = lax.optimization_barrier((second_a, second_b, going))
+    second_sum = jnp.concatenate(
+        [third_sends(second_a, near_a, y_step), third_sends(second_b, near_b, x_step)], 1
+    )
     level_one_rows, level_two_rows, sums = finish_rows(
         level_two_pattern, back, parent_panels, masked_one, masked_two, second_sum, parent_lead
     )

time: 291 us -> 291 us (level)
  waiting for transfers between devices: 100 us -> 78.3 us
  other arithmetic: 6.33 us -> 25.7 us
  local copies, waits for them, and re-layouts: 18.5 us -> 27.4 us
  Pallas kernels: 39.5 us -> 31.1 us
    all_to_all x1, waiting for transfers between devices: 16.2 us -> 5.72 us  [per_device(): lax.all_to_all(jnp.concatenate([cut, facts], 1), 'col', 0, 0, tiled=True)]
    ppermute x2, starting transfers between devices: 0.01 us -> 9.52 us  [all_panels(): below = lax.ppermute(own, 'row', z_step(1))]
    another operation x2 -> x4, other arithmetic: 0.22 us -> 9.16 us
    ppermute x4, waiting for transfers between devices: 7.79 us -> 16.7 us  [own_panels(): pieces.append(lax.ppermute(part, ('row', 'col'), turn(k)))]
    all_to_all x1, waiting for transfers between devices: 8.64 us -> 0.01 us  [per_device(): lax.all_to_all(jnp.take(cut[:, :block], readers, axis=0), 'col', 0, 0, ti...]
    ppermute x2, waiting for transfers between devices: 19.2 us -> 10.7 us  [all_panels(): above = lax.ppermute(own, 'row', z_step(-1))]
    pallas_call x8 -> x4, Pallas kernels: 19.4 us -> 11.5 us  [by_supernode(): pl.pallas_call(kernel, out_shape=jax.ShapeDtypeStruct((groups, SIDE, bloc...]
    convert_element_type x0 -> x2, other arithmetic: none -> 7.17 us  [second_sends(): wide = near.astype(F32)]
  transfers between devices with their start and end apart: 42 -> 42, of which waited for: 19 -> 21; matrix products, arithmetic and copies ran while one was open for 5% -> 16% of each run, Pallas kernels for 7% -> 4%
where the time goes in v2:
time: 291 us; the launch traced here: 290 us
  starting transfers between devices  112 us (38%)
  waiting for transfers between devices  78.3 us (27%)
  Pallas kernels  31.1 us (11%)
  local copies, waits for them, and re-layouts  27.4 us (9%)
  other arithmetic  25.7 us (9%)
  between operations  15.4 us (5%)
    ppermute x14, waiting for transfers between devices, send(): return lax.ppermute(value.astype(jnp.bfloat16), 'col', step)  35.1 us
    ppermute x2, starting transfers between devices, all_panels(): above = lax.ppermute(own, 'row', z_step(-1))  22 us
    ppermute x8, starting transfers between devices, all_panels(): found += [held, lax.ppermute(held, 'row', CORE_SWAP)]  20.2 us
    ppermute x4, waiting for transfers between devices, own_panels(): pieces.append(lax.ppermute(part, ('row', 'col'), turn(k)))  16.7 us
    ppermute x14, starting transfers between devices, send(): return lax.ppermute(value.astype(jnp.bfloat16), 'col', step)  16.4 us
    unnamed x56, local copies, waits for them, and re-layouts  16.3 us
    pallas_call x1, Pallas kernels, by_column(): pl.pallas_call(kernel, out_shape=jax.ShapeDtypeStruct((width // block, st...  14.8 us
    ppermute x4, starting transfers between devices, own_panels(): pieces.append(lax.ppermute(part, ('row', 'col'), turn(k)))  12.6 us
  transfers between devices with their start and end apart: 42, of which 21 were waited for; matrix products, arithmetic and copies ran while one was open for 16% of the time, Pallas kernels for 4%

profile of v2, /device:TPU:1, one launch (start us, length us, event | category | flops | bytes accessed | tf_op | source)
XLA Modules:
  0.0 289.9 jit_solution(13713629180767271928)
XLA Ops:
  9.2 6.0 %collective-permute-start = (bf16[128,1024]{1,0:T(8,128)(2,1)S(1)}, bf16[128,1024]{1,0:T(8,128)(2,1)S(1)}, u32[]{:S(2)}, u32[]{:S(2)}) collective-permute-start(bf16[128,1024]{1,0:T(8,128)(2,1)S(1)} %get-tuple-element.89), channel_id=1, source_target_pairs={{0,0},{1,1},{2,16},{3,17},{4,32},{5,33},{6,48},{7,49},{8,64},{9,65... | collective-permute-start | bytes 786440 | tf_op jit(solution)/shard_map/ppermute | solution.py:48
  15.9 5.2 %collective-permute-done = bf16[128,1024]{1,0:T(8,128)(2,1)S(1)} collective-permute-done((bf16[128,1024]{1,0:T(8,128)(2,1)S(1)}, bf16[128,1024]{1,0:T(8,128)(2,1)S(1)}, u32[]{:S(2)}, u32[]{:S(2)}) %collective-permute-start) | collective-permute-done | bytes 262176 | tf_op jit(solution)/shard_map/ppermute | solution.py:48
  23.7 15.4 %collective-permute-start.5 = (bf16[2,128,1024]{2,1,0:T(8,128)(2,1)S(1)}, bf16[2,128,1024]{2,1,0:T(8,128)(2,1)S(1)}, u32[]{:S(2)}, u32[]{:S(2)}) collective-permute-start(bf16[2,128,1024]{2,1,0:T(8,128)(2,1)S(1)} %pad_maximum_fusion.5.refs_0_), channel_id=1, source_target_pairs={{0,96},{16,112},{32,0},{48,16},{64,32},{80,48},{96,64},{112,80},{1... | collective-permute-start | bytes 1572872 | tf_op jit(solution)/shard_map/ppermute | solution.py:57
  39.1 8.9 %collective-permute-done.5.refs_4_ = bf16[2,128,1024]{2,1,0:T(8,128)(2,1)S(1)} collective-permute-done((bf16[2,128,1024]{2,1,0:T(8,128)(2,1)S(1)}, bf16[2,128,1024]{2,1,0:T(8,128)(2,1)S(1)}, u32[]{:S(2)}, u32[]{:S(2)}) %collective-permute-start.5) | collective-permute-done | bytes 524320 | tf_op jit(solution)/shard_map/ppermute | solution.py:57
  48.0 3.5 %collective-permute-start.8 = (bf16[128,1024]{1,0:T(8,128)(2,1)S(1)}, bf16[128,1024]{1,0:T(8,128)(2,1)S(1)}, u32[]{:S(2)}, u32[]{:S(2)}) collective-permute-start(bf16[128,1024]{1,0:T(8,128)(2,1)S(1)} %slice_bitcast_fusion.20), channel_id=1, source_target_pairs={{0,96},{16,112},{32,0},{48,16},{64,32},{80,48},{96,64},{112,80},{1... | collective-permute-start | bytes 786440 | tf_op jit(solution)/shard_map/ppermute | solution.py:59
  51.7 6.9 %collective-permute-start.2 = (bf16[2,128,1024]{2,1,0:T(8,128)(2,1)S(1)}, bf16[2,128,1024]{2,1,0:T(8,128)(2,1)S(1)}, u32[]{:S(2)}, u32[]{:S(2)}) collective-permute-start(bf16[2,128,1024]{2,1,0:T(8,128)(2,1)S(1)} %pad_maximum_fusion.5.refs_0_), channel_id=1, source_target_pairs={{0,16},{16,0},{32,48},{48,32},{64,80},{80,64},{96,112},{112,96},{1... | collective-permute-start | bytes 1572872 | tf_op jit(solution)/shard_map/ppermute | solution.py:63
  59.2 7.0 %collective-permute-start.9 = (bf16[2,128,1024]{2,1,0:T(8,128)(2,1)S(1)}, bf16[2,128,1024]{2,1,0:T(8,128)(2,1)S(1)}, u32[]{:S(2)}, u32[]{:S(2)}) collective-permute-start(bf16[2,128,1024]{2,1,0:T(8,128)(2,1)S(1)} %pad_maximum_fusion.6.refs_6_), channel_id=1, source_target_pairs={{0,16},{16,0},{32,48},{48,32},{64,80},{80,64},{96,112},{112,96},{1... | collective-permute-start | bytes 1572872 | tf_op jit(solution)/shard_map/ppermute | solution.py:63
  68.5 14.8 %shard_map.137 = bf16[16,2048,128]{2,1,0:T(8,128)(2,1)} custom-call(bf16[2,128,1024]{2,1,0:T(8,128)(2,1)S(1)} %pad_maximum_fusion.5.refs_0_, bf16[2,128,1024]{2,1,0:T(8,128)(2,1)S(1)} %collective-permute-done.2.refs_1_, bf16[2,128,1024]{2,1,0:T(8,128)(2,1)S(1)} %collective-permute-done.3.refs_2_, bf16[2,128,1024]{2,1,0:T(8,128)(2,1)} %copy-done.21, ...), custom_call_target="tpu_custom_call" | custom-call | flops 8589934592 | bytes 16777216 | tf_op jit(solution)/shard_map/pallas_call | solution.py:92
  85.4 4.3 %collective-permute-start.10 = (bf16[128,1024]{1,0:T(8,128)(2,1)S(1)}, bf16[128,1024]{1,0:T(8,128)(2,1)S(1)}, u32[]{:S(2)}, u32[]{:S(2)}) collective-permute-start(bf16[128,1024]{1,0:T(8,128)(2,1)S(1)} %get-tuple-element.85), channel_id=1, source_target_pairs={{0,0},{1,1},{2,16},{3,17},{4,32},{5,33},{6,48},{7,49},{8,64},{9,65... | collective-permute-start | bytes 786440 | tf_op jit(solution)/shard_map/ppermute | solution.py:48
  92.1 5.1 %collective-permute-done.10 = bf16[128,1024]{1,0:T(8,128)(2,1)S(1)} collective-permute-done((bf16[128,1024]{1,0:T(8,128)(2,1)S(1)}, bf16[128,1024]{1,0:T(8,128)(2,1)S(1)}, u32[]{:S(2)}, u32[]{:S(2)}) %collective-permute-start.10) | collective-permute-done | bytes 262176 | tf_op jit(solution)/shard_map/ppermute | solution.py:48
  97.2 3.9 %collective-permute-done.11 = bf16[128,1024]{1,0:T(8,128)(2,1)S(1)} collective-permute-done((bf16[128,1024]{1,0:T(8,128)(2,1)S(1)}, bf16[128,1024]{1,0:T(8,128)(2,1)S(1)}, u32[]{:S(2)}, u32[]{:S(2)}) %collective-permute-start.11) | collective-permute-done | bytes 262176 | tf_op jit(solution)/shard_map/ppermute | solution.py:48
  101.2 9.5 %collective-permute-start.13 = (bf16[2,128,1024]{2,1,0:T(8,128)(2,1)S(1)}, bf16[2,128,1024]{2,1,0:T(8,128)(2,1)S(1)}, u32[]{:S(2)}, u32[]{:S(2)}) collective-permute-start(bf16[2,128,1024]{2,1,0:T(8,128)(2,1)S(1)} %pad_maximum_fusion.7), channel_id=1, source_target_pairs={{0,32},{16,48},{32,64},{48,80},{64,96},{80,112},{96,0},{112,16},{1... | collective-permute-start | bytes 1572872 | tf_op jit(solution)/shard_map/ppermute | solution.py:56
  114.0 6.6 %collective-permute-start.15 = (bf16[2,128,1024]{2,1,0:T(8,128)(2,1)S(1)}, bf16[2,128,1024]{2,1,0:T(8,128)(2,1)}, u32[]{:S(2)}, u32[]{:S(2)}) collective-permute-start(bf16[2,128,1024]{2,1,0:T(8,128)(2,1)S(1)} %pad_maximum_fusion.7), channel_id=1, source_target_pairs={{0,96},{16,112},{32,0},{48,16},{64,32},{80,48},{96,64},{112,80},{1... | collective-permute-start | bytes 1572872 | tf_op jit(solution)/shard_map/ppermute | solution.py:57
  122.6 7.4 %all-to-all-start = ((bf16[16,144,128]{2,1,0:T(8,128)(2,1)}), bf16[16,144,128]{2,1,0:T(8,128)(2,1)S(1)}, u32[]{:S(2)}, u32[]{:S(2)}) async-start(bf16[16,144,128]{2,1,0:T(8,128)(2,1)} %fusion.11), calls=%async_computation | async-start | bytes 1179648 | tf_op jit(solution)/shard_map/all_to_all | solution.py:319
  133.6 3.5 %collective-permute-start.18 = (bf16[128,1024]{1,0:T(8,128)(2,1)}, bf16[128,1024]{1,0:T(8,128)(2,1)S(1)}, u32[]{:S(2)}, u32[]{:S(2)}) collective-permute-start(bf16[128,1024]{1,0:T(8,128)(2,1)} %slice_bitcast_fusion.18), channel_id=1, source_target_pairs={{0,96},{16,112},{32,0},{48,16},{64,32},{80,48},{96,64},{112,80},{1... | collective-permute-start | bytes 786440 | tf_op jit(solution)/shard_map/ppermute | solution.py:59
  140.9 5.7 %all-to-all-done = bf16[16,144,128]{2,1,0:T(8,128)(2,1)S(1)} async-done(((bf16[16,144,128]{2,1,0:T(8,128)(2,1)}), bf16[16,144,128]{2,1,0:T(8,128)(2,1)S(1)}, u32[]{:S(2)}, u32[]{:S(2)}) %all-to-all-start) | async-done | bytes 589856 | tf_op jit(solution)/shard_map/all_to_all | solution.py:319
  149.0 4.2 %all-to-all-start.2 = ((bf16[16,128,128]{2,1,0:T(8,128)(2,1)}), bf16[16,128,128]{2,1,0:T(8,128)(2,1)}, u32[]{:S(2)}, u32[]{:S(2)}) async-start(bf16[16,128,128]{2,1,0:T(8,128)(2,1)} %broadcast_select_fusion), calls=%async_computation.3 | async-start | bytes 1048576 | tf_op jit(solution)/shard_map/all_to_all | solution.py:322
  176.7 4.0 %shard_map.141 = bf16[3,4,128,1024]{3,2,1,0:T(8,128)(2,1)S(1)} custom-call(s32[12]{0:T(128)S(1)} %pad_add_fusion.order_ref, bf16[16,128,1024]{2,1,0:T(8,128)(2,1)S(1)} %copy-done, bf16[1024,2048]{1,0:T(8,128)(2,1)S(1)} %copy-done.2), custom_call_target="tpu_custom_call" | custom-call | flops 3221225472 | bytes 6291456 | tf_op jit(solution)/shard_map/pallas_call | solution.py:121
  180.7 3.5 %convert_element_type.122 = f32[3,4,128,1024]{3,2,1,0:T(8,128)} convert(bf16[3,4,128,1024]{3,2,1,0:T(8,128)(2,1)S(1)} %shard_map.141) | non-fusion elementwise | flops 1572864 | bytes 9437184 | tf_op jit(solution)/shard_map/convert_element_type | solution.py:150
  184.2 4.0 %shard_map.142 = bf16[3,4,128,1024]{3,2,1,0:T(8,128)(2,1)S(1)} custom-call(s32[12]{0:T(128)S(1)} %pad_add_fusion.1.order_ref, bf16[16,128,1024]{2,1,0:T(8,128)(2,1)S(1)} %copy-done.1, bf16[1024,2048]{1,0:T(8,128)(2,1)S(1)} %copy-done.2), custom_call_target="tpu_custom_call" | custom-call | flops 3221225472 | bytes 6291456 | tf_op jit(solution)/shard_map/pallas_call | solution.py:121
  188.2 3.7 %convert_element_type.125 = f32[3,4,128,1024]{3,2,1,0:T(8,128)} convert(bf16[3,4,128,1024]{3,2,1,0:T(8,128)(2,1)S(1)} %shard_map.142) | non-fusion elementwise | flops 1572864 | bytes 9437184 | tf_op jit(solution)/shard_map/convert_element_type | solution.py:150
  194.1 2.6 collective-permute-done.22
  202.0 2.7 collective-permute-start.25
  214.5 4.3 %all-to-all-start.1 = ((bf16[16,2,128,128]{3,2,1,0:T(8,128)(2,1)}), bf16[16,2,128,128]{3,2,1,0:T(8,128)(2,1)}, u32[]{:S(2)}, u32[]{:S(2)}) async-start(bf16[16,2,128,128]{3,2,1,0:T(8,128)(2,1)} %copy-done.8), calls=%async_computation.2 | async-start | bytes 2097152 | tf_op jit(solution)/shard_map/all_to_all | solution.py:344
  218.9 9.2 %collective-permute-done.24 = bf16[4,128,1024]{2,1,0:T(8,128)(2,1)} collective-permute-done((bf16[4,128,1024]{2,1,0:T(8,128)(2,1)}, bf16[4,128,1024]{2,1,0:T(8,128)(2,1)}, u32[]{:S(2)}, u32[]{:S(2)}) %collective-permute-start.24) | collective-permute-done | bytes 1048608 | tf_op jit(solution)/shard_map/ppermute | solution.py:136
  228.1 13.1 %collective-permute-done.26 = bf16[4,128,1024]{2,1,0:T(8,128)(2,1)} collective-permute-done((bf16[4,128,1024]{2,1,0:T(8,128)(2,1)}, bf16[4,128,1024]{2,1,0:T(8,128)(2,1)}, u32[]{:S(2)}, u32[]{:S(2)}) %collective-permute-start.26) | collective-permute-done | bytes 1048608 | tf_op jit(solution)/shard_map/ppermute | solution.py:136
  241.9 2.6 fusion.36
  248.6 3.2 %collective-permute-start.30 = (bf16[128,1024]{1,0:T(8,128)(2,1)S(1)}, bf16[128,1024]{1,0:T(8,128)(2,1)S(1)}, u32[]{:S(2)}, u32[]{:S(2)}) collective-permute-start(bf16[128,1024]{1,0:T(8,128)(2,1)S(1)} %get-tuple-element.74), channel_id=1, source_target_pairs={{0,12},{1,13},{2,14},{3,15},{4,0},{5,1},{6,2},{7,3},{8,4},{9,5},{1... | collective-permute-start | bytes 786440 | tf_op jit(solution)/shard_map/ppermute | solution.py:136
  252.5 5.3 %collective-permute-done.31 = bf16[128,1024]{1,0:T(8,128)(2,1)S(1)} collective-permute-done((bf16[128,1024]{1,0:T(8,128)(2,1)S(1)}, bf16[128,1024]{1,0:T(8,128)(2,1)S(1)}, u32[]{:S(2)}, u32[]{:S(2)}) %collective-permute-start.31) | collective-permute-done | bytes 262176 | tf_op jit(solution)/shard_map/ppermute | solution.py:136
  261.4 2.8 shard_map.143
  264.2 6.5 %collective-permute-start.34 = (f32[4,128,128]{2,1,0:T(8,128)S(1)}, f32[4,128,128]{2,1,0:T(8,128)S(1)}, u32[]{:S(2)}, u32[]{:S(2)}) collective-permute-start(f32[4,128,128]{2,1,0:T(8,128)S(1)} %get-tuple-element.52), channel_id=1, source_target_pairs={{0,16},{16,0},{32,48},{48,32},{64,80},{80,64},{96,112},{112,96},{1... | collective-permute-start | bytes 786440 | tf_op jit(solution)/shard_map/ppermute | solution.py:163
  278.3 3.5 %collective-permute-done.37.d = bf16[4,128,128]{2,1,0:T(8,128)(2,1)S(1)} collective-permute-done((bf16[4,128,128]{2,1,0:T(8,128)(2,1)S(1)}, bf16[4,128,128]{2,1,0:T(8,128)(2,1)S(1)}, u32[]{:S(2)}, u32[]{:S(2)}) %collective-permute-start.37) | collective-permute-done | bytes 131104 | tf_op jit(solution)/shard_map/ppermute | solution.py:165
  (180 shorter events, 85.5 us)
Async XLA Ops:
  7.2 204.5 %reduce-scatter.2.cloned.1.call-start = ((), (), s32[]{:S(2)}) async-start(), calls=%async_computation.4 | async-start | bytes 8912896 | tf_op jit(solution)/shard_map/reduce_scatter | solution.py:307
  9.2 11.9 %collective-permute-start = (bf16[128,1024]{1,0:T(8,128)(2,1)S(1)}, bf16[128,1024]{1,0:T(8,128)(2,1)S(1)}, u32[]{:S(2)}, u32[]{:S(2)}) collective-permute-start(bf16[128,1024]{1,0:T(8,128)(2,1)S(1)} %get-tuple-element.89), channel_id=1, source_target_pairs={{0,0},{1,1},{2,16},{3,17},{4,32},{5,33},{6,48},{7,49},{8,64},{9,65... | collective-permute-start | bytes 786440 | tf_op jit(solution)/shard_map/ppermute | solution.py:48
  23.7 24.3 %collective-permute-start.5 = (bf16[2,128,1024]{2,1,0:T(8,128)(2,1)S(1)}, bf16[2,128,1024]{2,1,0:T(8,128)(2,1)S(1)}, u32[]{:S(2)}, u32[]{:S(2)}) collective-permute-start(bf16[2,128,1024]{2,1,0:T(8,128)(2,1)S(1)} %pad_maximum_fusion.5.refs_0_), channel_id=1, source_target_pairs={{0,96},{16,112},{32,0},{48,16},{64,32},{80,48},{96,64},{112,80},{1... | collective-permute-start | bytes 1572872 | tf_op jit(solution)/shard_map/ppermute | solution.py:57
  39.1 12.4 %collective-permute-start.3 = (bf16[2,128,1024]{2,1,0:T(8,128)(2,1)S(1)}, bf16[2,128,1024]{2,1,0:T(8,128)(2,1)S(1)}, u32[]{:S(2)}, u32[]{:S(2)}) collective-permute-start(bf16[2,128,1024]{2,1,0:T(8,128)(2,1)S(1)} %pad_maximum_fusion.5.refs_0_), channel_id=1, source_target_pairs={{0,32},{16,48},{32,64},{48,80},{64,96},{80,112},{96,0},{112,16},{1... | collective-permute-start | bytes 1572872 | tf_op jit(solution)/shard_map/ppermute | solution.py:56
  48.0 11.0 %collective-permute-start.8 = (bf16[128,1024]{1,0:T(8,128)(2,1)S(1)}, bf16[128,1024]{1,0:T(8,128)(2,1)S(1)}, u32[]{:S(2)}, u32[]{:S(2)}) collective-permute-start(bf16[128,1024]{1,0:T(8,128)(2,1)S(1)} %slice_bitcast_fusion.20), channel_id=1, source_target_pairs={{0,96},{16,112},{32,0},{48,16},{64,32},{80,48},{96,64},{112,80},{1... | collective-permute-start | bytes 786440 | tf_op jit(solution)/shard_map/ppermute | solution.py:59
  51.7 14.7 %collective-permute-start.2 = (bf16[2,128,1024]{2,1,0:T(8,128)(2,1)S(1)}, bf16[2,128,1024]{2,1,0:T(8,128)(2,1)S(1)}, u32[]{:S(2)}, u32[]{:S(2)}) collective-permute-start(bf16[2,128,1024]{2,1,0:T(8,128)(2,1)S(1)} %pad_maximum_fusion.5.refs_0_), channel_id=1, source_target_pairs={{0,16},{16,0},{32,48},{48,32},{64,80},{80,64},{96,112},{112,96},{1... | collective-permute-start | bytes 1572872 | tf_op jit(solution)/shard_map/ppermute | solution.py:63
  59.2 8.6 %collective-permute-start.9 = (bf16[2,128,1024]{2,1,0:T(8,128)(2,1)S(1)}, bf16[2,128,1024]{2,1,0:T(8,128)(2,1)S(1)}, u32[]{:S(2)}, u32[]{:S(2)}) collective-permute-start(bf16[2,128,1024]{2,1,0:T(8,128)(2,1)S(1)} %pad_maximum_fusion.6.refs_6_), channel_id=1, source_target_pairs={{0,16},{16,0},{32,48},{48,32},{64,80},{80,64},{96,112},{112,96},{1... | collective-permute-start | bytes 1572872 | tf_op jit(solution)/shard_map/ppermute | solution.py:63
  85.4 11.8 %collective-permute-start.10 = (bf16[128,1024]{1,0:T(8,128)(2,1)S(1)}, bf16[128,1024]{1,0:T(8,128)(2,1)S(1)}, u32[]{:S(2)}, u32[]{:S(2)}) collective-permute-start(bf16[128,1024]{1,0:T(8,128)(2,1)S(1)} %get-tuple-element.85), channel_id=1, source_target_pairs={{0,0},{1,1},{2,16},{3,17},{4,32},{5,33},{6,48},{7,49},{8,64},{9,65... | collective-permute-start | bytes 786440 | tf_op jit(solution)/shard_map/ppermute | solution.py:48
  89.8 11.3 %collective-permute-start.11 = (bf16[128,1024]{1,0:T(8,128)(2,1)S(1)}, bf16[128,1024]{1,0:T(8,128)(2,1)S(1)}, u32[]{:S(2)}, u32[]{:S(2)}) collective-permute-start(bf16[128,1024]{1,0:T(8,128)(2,1)S(1)} %get-tuple-element.86), channel_id=1, source_target_pairs={{0,1},{1,0},{2,17},{3,16},{4,33},{5,32},{6,49},{7,48},{8,65},{9,64... | collective-permute-start | bytes 786440 | tf_op jit(solution)/shard_map/ppermute | solution.py:48
  101.2 28.8 %collective-permute-start.13 = (bf16[2,128,1024]{2,1,0:T(8,128)(2,1)S(1)}, bf16[2,128,1024]{2,1,0:T(8,128)(2,1)S(1)}, u32[]{:S(2)}, u32[]{:S(2)}) collective-permute-start(bf16[2,128,1024]{2,1,0:T(8,128)(2,1)S(1)} %pad_maximum_fusion.7), channel_id=1, source_target_pairs={{0,32},{16,48},{32,64},{48,80},{64,96},{80,112},{96,0},{112,16},{1... | collective-permute-start | bytes 1572872 | tf_op jit(solution)/shard_map/ppermute | solution.py:56
  111.5 26.8 %collective-permute-start.12 = (bf16[2,128,1024]{2,1,0:T(8,128)(2,1)S(1)}, bf16[2,128,1024]{2,1,0:T(8,128)(2,1)}, u32[]{:S(2)}, u32[]{:S(2)}) collective-permute-start(bf16[2,128,1024]{2,1,0:T(8,128)(2,1)S(1)} %pad_maximum_fusion.7), channel_id=1, source_target_pairs={{0,16},{16,0},{32,48},{48,32},{64,80},{80,64},{96,112},{112,96},{1... | collective-permute-start | bytes 1572872 | tf_op jit(solution)/shard_map/ppermute | solution.py:63
  114.0 17.9 %collective-permute-start.15 = (bf16[2,128,1024]{2,1,0:T(8,128)(2,1)S(1)}, bf16[2,128,1024]{2,1,0:T(8,128)(2,1)}, u32[]{:S(2)}, u32[]{:S(2)}) collective-permute-start(bf16[2,128,1024]{2,1,0:T(8,128)(2,1)S(1)} %pad_maximum_fusion.7), channel_id=1, source_target_pairs={{0,96},{16,112},{32,0},{48,16},{64,32},{80,48},{96,64},{112,80},{1... | collective-permute-start | bytes 1572872 | tf_op jit(solution)/shard_map/ppermute | solution.py:57
  122.6 24.1 %all-to-all-start = ((bf16[16,144,128]{2,1,0:T(8,128)(2,1)}), bf16[16,144,128]{2,1,0:T(8,128)(2,1)S(1)}, u32[]{:S(2)}, u32[]{:S(2)}) async-start(bf16[16,144,128]{2,1,0:T(8,128)(2,1)} %fusion.11), calls=%async_computation | async-start | bytes 1179648 | tf_op jit(solution)/shard_map/all_to_all | solution.py:319
  130.0 23.2 %collective-permute-start.17 = (bf16[128,1024]{1,0:T(8,128)(2,1)S(1)}, bf16[128,1024]{1,0:T(8,128)(2,1)S(1)}, u32[]{:S(2)}, u32[]{:S(2)}) collective-permute-start(bf16[128,1024]{1,0:T(8,128)(2,1)S(1)} %slice_bitcast_fusion.19), channel_id=1, source_target_pairs={{0,32},{16,48},{32,64},{48,80},{64,96},{80,112},{96,0},{112,16},{1... | collective-permute-start | bytes 786440 | tf_op jit(solution)/shard_map/ppermute | solution.py:59
  133.6 19.7 %collective-permute-start.18 = (bf16[128,1024]{1,0:T(8,128)(2,1)}, bf16[128,1024]{1,0:T(8,128)(2,1)S(1)}, u32[]{:S(2)}, u32[]{:S(2)}) collective-permute-start(bf16[128,1024]{1,0:T(8,128)(2,1)} %slice_bitcast_fusion.18), channel_id=1, source_target_pairs={{0,96},{16,112},{32,0},{48,16},{64,32},{80,48},{96,64},{112,80},{1... | collective-permute-start | bytes 786440 | tf_op jit(solution)/shard_map/ppermute | solution.py:59
  137.1 18.4 %collective-permute-start.14 = (bf16[2,128,1024]{2,1,0:T(8,128)(2,1)S(1)}, bf16[2,128,1024]{2,1,0:T(8,128)(2,1)}, u32[]{:S(2)}, u32[]{:S(2)}) collective-permute-start(bf16[2,128,1024]{2,1,0:T(8,128)(2,1)S(1)} %collective-permute-done.13), channel_id=1, source_target_pairs={{0,16},{16,0},{32,48},{48,32},{64,80},{80,64},{96,112},{112,96},{1... | collective-permute-start | bytes 1572872 | tf_op jit(solution)/shard_map/ppermute | solution.py:63
  138.2 21.0 %collective-permute-start.16 = (bf16[2,128,1024]{2,1,0:T(8,128)(2,1)}, bf16[2,128,1024]{2,1,0:T(8,128)(2,1)}, u32[]{:S(2)}, u32[]{:S(2)}) collective-permute-start(bf16[2,128,1024]{2,1,0:T(8,128)(2,1)} %collective-permute-done.15), channel_id=1, source_target_pairs={{0,16},{16,0},{32,48},{48,32},{64,80},{80,64},{96,112},{112,96},{1... | collective-permute-start | bytes 1572872 | tf_op jit(solution)/shard_map/ppermute | solution.py:63
  149.0 45.0 %all-to-all-start.2 = ((bf16[16,128,128]{2,1,0:T(8,128)(2,1)}), bf16[16,128,128]{2,1,0:T(8,128)(2,1)}, u32[]{:S(2)}, u32[]{:S(2)}) async-start(bf16[16,128,128]{2,1,0:T(8,128)(2,1)} %broadcast_select_fusion), calls=%async_computation.3 | async-start | bytes 1048576 | tf_op jit(solution)/shard_map/all_to_all | solution.py:322
  153.3 9.3 %collective-permute-start.19 = (bf16[2,128,1024]{2,1,0:T(8,128)(2,1)S(1)}, bf16[2,128,1024]{2,1,0:T(8,128)(2,1)S(1)}, u32[]{:S(2)}, u32[]{:S(2)}) collective-permute-start(bf16[2,128,1024]{2,1,0:T(8,128)(2,1)S(1)} %pad_maximum_fusion.8), channel_id=1, source_target_pairs={{0,16},{16,0},{32,48},{48,32},{64,80},{80,64},{96,112},{112,96},{1... | collective-permute-start | bytes 1572872 | tf_op jit(solution)/shard_map/ppermute | solution.py:63
  168.5 25.5 %collective-permute-start.20 = (bf16[4,64,1024]{2,1,0:T(8,128)(2,1)}, bf16[4,64,1024]{2,1,0:T(8,128)(2,1)}, u32[]{:S(2)}, u32[]{:S(2)}) collective-permute-start(bf16[4,64,1024]{2,1,0:T(8,128)(2,1)} %get-tuple-element.82), channel_id=1, source_target_pairs={{0,1},{1,2},{2,3},{3,0},{4,5},{5,6},{6,7},{7,4},{8,9},{9,10},{10,1... | collective-permute-start | bytes 1572872 | tf_op jit(solution)/shard_map/ppermute | solution.py:136
  170.0 24.1 %collective-permute-start.21 = (bf16[4,64,1024]{2,1,0:T(8,128)(2,1)}, bf16[4,64,1024]{2,1,0:T(8,128)(2,1)}, u32[]{:S(2)}, u32[]{:S(2)}) collective-permute-start(bf16[4,64,1024]{2,1,0:T(8,128)(2,1)} %get-tuple-element.81), channel_id=1, source_target_pairs={{0,3},{1,0},{2,1},{3,2},{4,7},{5,4},{6,5},{7,6},{8,11},{9,8},{10,9... | collective-permute-start | bytes 1572872 | tf_op jit(solution)/shard_map/ppermute | solution.py:136
  174.0 22.6 %collective-permute-start.22 = (bf16[4,64,1024]{2,1,0:T(8,128)(2,1)}, bf16[4,64,1024]{2,1,0:T(8,128)(2,1)}, u32[]{:S(2)}, u32[]{:S(2)}) collective-permute-start(bf16[4,64,1024]{2,1,0:T(8,128)(2,1)} %get-tuple-element.80), channel_id=1, source_target_pairs={{0,4},{1,5},{2,6},{3,7},{4,8},{5,9},{6,10},{7,11},{8,12},{9,13},{1... | collective-permute-start | bytes 1572872 | tf_op jit(solution)/shard_map/ppermute | solution.py:136
  175.4 22.3 %collective-permute-start.23 = (bf16[4,64,1024]{2,1,0:T(8,128)(2,1)}, bf16[4,64,1024]{2,1,0:T(8,128)(2,1)}, u32[]{:S(2)}, u32[]{:S(2)}) collective-permute-start(bf16[4,64,1024]{2,1,0:T(8,128)(2,1)} %get-tuple-element.79), channel_id=1, source_target_pairs={{0,12},{1,13},{2,14},{3,15},{4,0},{5,1},{6,2},{7,3},{8,4},{9,5},{1... | collective-permute-start | bytes 1572872 | tf_op jit(solution)/shard_map/ppermute | solution.py:136
  201.0 27.1 %collective-permute-start.24 = (bf16[4,128,1024]{2,1,0:T(8,128)(2,1)}, bf16[4,128,1024]{2,1,0:T(8,128)(2,1)}, u32[]{:S(2)}, u32[]{:S(2)}) collective-permute-start(bf16[4,128,1024]{2,1,0:T(8,128)(2,1)} %pad_maximum_fusion), channel_id=1, source_target_pairs={{0,1},{1,2},{2,3},{3,0},{4,5},{5,6},{6,7},{7,4},{8,9},{9,10},{10,1... | collective-permute-start | bytes 3145736 | tf_op jit(solution)/shard_map/ppermute | solution.py:136
  202.0 26.0 %collective-permute-start.25 = (bf16[4,128,1024]{2,1,0:T(8,128)(2,1)}, bf16[4,128,1024]{2,1,0:T(8,128)(2,1)}, u32[]{:S(2)}, u32[]{:S(2)}) collective-permute-start(bf16[4,128,1024]{2,1,0:T(8,128)(2,1)} %pad_maximum_fusion.1), channel_id=1, source_target_pairs={{0,3},{1,0},{2,1},{3,2},{4,7},{5,4},{6,5},{7,6},{8,11},{9,8},{10,9... | collective-permute-start | bytes 3145736 | tf_op jit(solution)/shard_map/ppermute | solution.py:136
  208.0 33.2 %collective-permute-start.26 = (bf16[4,128,1024]{2,1,0:T(8,128)(2,1)}, bf16[4,128,1024]{2,1,0:T(8,128)(2,1)}, u32[]{:S(2)}, u32[]{:S(2)}) collective-permute-start(bf16[4,128,1024]{2,1,0:T(8,128)(2,1)} %pad_maximum_fusion.2), channel_id=1, source_target_pairs={{0,4},{1,5},{2,6},{3,7},{4,8},{5,9},{6,10},{7,11},{8,12},{9,13},{1... | collective-permute-start | bytes 3145736 | tf_op jit(solution)/shard_map/ppermute | solution.py:136
  210.2 31.7 %collective-permute-start.27 = (bf16[4,128,1024]{2,1,0:T(8,128)(2,1)}, bf16[4,128,1024]{2,1,0:T(8,128)(2,1)}, u32[]{:S(2)}, u32[]{:S(2)}) collective-permute-start(bf16[4,128,1024]{2,1,0:T(8,128)(2,1)} %pad_maximum_fusion.3), channel_id=1, source_target_pairs={{0,12},{1,13},{2,14},{3,15},{4,0},{5,1},{6,2},{7,3},{8,4},{9,5},{1... | collective-permute-start | bytes 3145736 | tf_op jit(solution)/shard_map/ppermute | solution.py:136
  214.5 46.8 %all-to-all-start.1 = ((bf16[16,2,128,128]{3,2,1,0:T(8,128)(2,1)}), bf16[16,2,128,128]{3,2,1,0:T(8,128)(2,1)}, u32[]{:S(2)}, u32[]{:S(2)}) async-start(bf16[16,2,128,128]{3,2,1,0:T(8,128)(2,1)} %copy-done.8), calls=%async_computation.2 | async-start | bytes 2097152 | tf_op jit(solution)/shard_map/all_to_all | solution.py:344
  245.4 12.4 %collective-permute-start.31 = (bf16[128,1024]{1,0:T(8,128)(2,1)S(1)}, bf16[128,1024]{1,0:T(8,128)(2,1)S(1)}, u32[]{:S(2)}, u32[]{:S(2)}) collective-permute-start(bf16[128,1024]{1,0:T(8,128)(2,1)S(1)} %get-tuple-element.76), channel_id=1, source_target_pairs={{0,1},{1,2},{2,3},{3,0},{4,5},{5,6},{6,7},{7,4},{8,9},{9,10},{10,1... | collective-permute-start | bytes 786440 | tf_op jit(solution)/shard_map/ppermute | solution.py:136
  248.6 9.6 %collective-permute-start.30 = (bf16[128,1024]{1,0:T(8,128)(2,1)S(1)}, bf16[128,1024]{1,0:T(8,128)(2,1)S(1)}, u32[]{:S(2)}, u32[]{:S(2)}) collective-permute-start(bf16[128,1024]{1,0:T(8,128)(2,1)S(1)} %get-tuple-element.74), channel_id=1, source_target_pairs={{0,12},{1,13},{2,14},{3,15},{4,0},{5,1},{6,2},{7,3},{8,4},{9,5},{1... | collective-permute-start | bytes 786440 | tf_op jit(solution)/shard_map/ppermute | solution.py:136
  251.9 9.2 %collective-permute-start.28 = (bf16[128,1024]{1,0:T(8,128)(2,1)S(1)}, bf16[128,1024]{1,0:T(8,128)(2,1)S(1)}, u32[]{:S(2)}, u32[]{:S(2)}) collective-permute-start(bf16[128,1024]{1,0:T(8,128)(2,1)S(1)} %get-tuple-element.73), channel_id=1, source_target_pairs={{0,4},{1,5},{2,6},{3,7},{4,8},{5,9},{6,10},{7,11},{8,12},{9,13},{1... | collective-permute-start | bytes 786440 | tf_op jit(solution)/shard_map/ppermute | solution.py:136
  272.1 9.7 %collective-permute-start.37 = (bf16[4,128,128]{2,1,0:T(8,128)(2,1)S(1)}, bf16[4,128,128]{2,1,0:T(8,128)(2,1)S(1)}, u32[]{:S(2)}, u32[]{:S(2)}) collective-permute-start(bf16[4,128,128]{2,1,0:T(8,128)(2,1)S(1)} %add_convert_fusion.a), channel_id=1, source_target_pairs={{0,32},{16,48},{32,64},{48,80},{64,96},{80,112},{96,0},{112,16},{1... | collective-permute-start | bytes 393224 | tf_op jit(solution)/shard_map/ppermute | solution.py:165
  (34 other events, 445.3 us)
Sparse Core Ops, SparseCore 0:
  83.4 114.1 reduce-scatter.1

commit v3 on v2

--- a/solution.py
+++ b/solution.py
@@ -8,7 +8,7 @@
 SIDE = 4
 CORES = 2
 F32 = jnp.float32
-RING_VMEM = 18 * 2**20
+RING_VMEM = 28 * 2**20
 
 
 def x_step(d):
@@ -39,14 +39,15 @@
     return (shaped * pattern.astype(panels.dtype)[:, None, :, None]).reshape(panels.shape)
 
 
-def own_panels(masked):
+def turned_panels(masked, k):
     col = lax.axis_index("col")
     half = masked.shape[1] // 2
-    pieces = []
-    for k in range(2):
-        part = lax.dynamic_slice_in_dim(masked, (col + k) % 2 * half, half, 1)
-        pieces.append(lax.ppermute(part, ("row", "col"), turn(k)))
-    even = col % 2 == 0
+    part = lax.dynamic_slice_in_dim(masked, (col + k) % 2 * half, half, 1)
+    return lax.ppermute(part, ("row", "col"), turn(k))
+
+
+def in_order(pieces):
+    even = lax.axis_index("col") % 2 == 0
     return jnp.stack(
         [jnp.where(even, pieces[0], pieces[1]), jnp.where(even, pieces[1], pieces[0])]
     )
@@ -106,57 +107,92 @@
     )(*pieces, matrix)
 
 
-def by_supernode(order, rows, matrix, part):
+def grouped_dot(rows_ref, order_ref, first, matrix_ref, part):
+    width = matrix_ref.shape[1] // 2
+    left = jnp.concatenate([rows_ref[order_ref[part, first + j]] for j in range(SIDE)], 0)
+    total = jnp.dot(
+        left, matrix_ref[:, part * width : (part + 1) * width], preferred_element_type=F32
+    )
+    return total.reshape(SIDE, -1, width)
+
+
+def ring_call(kernel, shapes, scalars, arrays, flops=0):
+    return pl.pallas_call(
+        kernel,
+        out_shape=[jax.ShapeDtypeStruct(shape, kind) for shape, kind in shapes],
+        in_specs=[whole(pltpu.SMEM)] * len(scalars) + [whole()] * len(arrays),
+        out_specs=[whole()] * len(shapes),
+        compiler_params=pltpu.CompilerParams(vmem_limit_bytes=RING_VMEM),
+        cost_estimate=pl.CostEstimate(flops=flops, bytes_accessed=2**22, transcendentals=0),
+    )(*scalars, *arrays)
+
+
+def ring_far(order, rows, matrix):
+    block, depth = rows.shape[1:]
+    half, width = block // 2, matrix.shape[1] // 2
+
+    def kernel(order_ref, rows_ref, matrix_ref, *out):
+        for part in range(2):
+            total = grouped_dot(rows_ref, order_ref, 2 * SIDE, matrix_ref, part)
+            out[2 * part][...] = total[:, :half].astype(rows.dtype)
+            out[2 * part + 1][...] = total[:, half:].astype(rows.dtype)
+
+    shape = ((SIDE, half, width), rows.dtype)
+    flops = 4 * SIDE * block * depth * width
+    return ring_call(kernel, [shape] * 4, [order], [rows, matrix], flops)
+
+
+def ring_near(order, rows, matrix):
     block, depth = rows.shape[1:]
     width = matrix.shape[1] // 2
-    groups = order.shape[0] // SIDE
-
-    def kernel(order_ref, rows_ref, matrix_ref, out_ref):
-        right = matrix_ref[:, part * width : (part + 1) * width]
-        for g in range(groups):
-            left = jnp.concatenate([rows_ref[order_ref[SIDE * g + j]] for j in range(SIDE)], 0)
-            total = jnp.dot(left, right, preferred_element_type=F32)
-            out_ref[g] = total.reshape(SIDE, block, width).astype(out_ref.dtype)
-
-    return pl.pallas_call(
-        kernel,
-        out_shape=jax.ShapeDtypeStruct((groups, SIDE, block, width), rows.dtype),
-        in_specs=[whole(pltpu.SMEM), whole(), whole()],
-        out_specs=whole(),
-        compiler_params=pltpu.CompilerParams(vmem_limit_bytes=RING_VMEM),
-        cost_estimate=pl.CostEstimate(
-            flops=2 * groups * SIDE * block * depth * width,
-            bytes_accessed=2 * groups * SIDE * block * (depth + width),
-            transcendentals=0,
-        ),
-    )(order, rows, matrix)
+
+    def kernel(order_ref, rows_ref, matrix_ref, *out):
+        for part in range(2):
+            for g, d in enumerate((1, 3, 0)):
+                total = grouped_dot(rows_ref, order_ref, d * SIDE, matrix_ref, part)
+                out[3 * part + g][...] = total.astype(rows.dtype)
+
+    shape = ((SIDE, block, width), rows.dtype)
+    flops = 12 * SIDE * block * depth * width
+    return ring_call(kernel, [shape] * 6, [order], [rows, matrix], flops)
 
 
 def send(value, step):
-    return lax.ppermute(value.astype(jnp.bfloat16), "col", step)
-
-
-def first_sends(product, order, step):
-    far = product(order[2])[0]
-    half = far.shape[1] // 2
-    arriving = send(far[:, :half], step(1)), send(far[:, half:], step(-1))
-    near = product(jnp.concatenate([order[1], order[3], order[0]]))
-    return arriving, near
+    return lax.ppermute(value, "col", step)
 
 
 def second_sends(arriving, near, step):
-    from_behind, from_ahead = [v.astype(F32) for v in arriving]
-    half = from_behind.shape[1]
-    wide = near.astype(F32)
-    to_ahead = jnp.concatenate([wide[0, :, :half] + from_behind, wide[0, :, half:]], 1)
-    to_behind = jnp.concatenate([wide[1, :, :half], wide[1, :, half:] + from_ahead], 1)
-    return send(to_ahead, step(1)), send(to_behind, step(-1))
+    half = arriving[0].shape[1]
+
+    def kernel(low_ref, high_ref, ahead_ref, behind_ref, ahead_out, behind_out):
+        kind = ahead_out.dtype
+        ahead_out[:, :half] = (ahead_ref[:, :half].astype(F32) + low_ref[...].astype(F32)).astype(kind)
+        ahead_out[:, half:] = ahead_ref[:, half:]
+        behind_out[:, :half] = behind_ref[:, :half]
+        behind_out[:, half:] = (behind_ref[:, half:].astype(F32) + high_ref[...].astype(F32)).astype(kind)
+
+    shape = (near[0].shape, near[0].dtype)
+    ahead, behind = ring_call(kernel, [shape] * 2, [], [*arriving, near[0], near[1]])
+    return send(ahead, step(1)), send(behind, step(-1))
 
 
 def third_sends(arriving, near, step):
-    total = near[2].astype(F32) + arriving[0].astype(F32) + arriving[1].astype(F32)
-    terms = [send(total[d], step(d)) for d in range(1, SIDE)]
-    return total[0] + sum(v.astype(F32) for v in terms)
+    _, block, width = near[2].shape
+    kind = near[2].dtype
+
+    def kernel(one_ref, two_ref, own_ref, own_out, *out):
+        for d in range(SIDE):
+            total = own_ref[d].astype(F32) + one_ref[d].astype(F32) + two_ref[d].astype(F32)
+            if d:
+                out[d - 1][...] = total.astype(kind)
+            else:
+                own_out[...] = total
+
+    shape = (block, width)
+    own, *others = ring_call(
+        kernel, [(shape, F32)] + [(shape, kind)] * 3, [], [*arriving, near[2]]
+    )
+    return [own] + [send(v, step(d + 1)) for d, v in enumerate(others)]
 
 
 def row_parts(values):
@@ -197,7 +233,7 @@
     )[0]
 
 
-def finish_rows(pattern, back, parent_panels, masked_one, masked_two, second, lead):
+def finish_rows(pattern, back, parent_panels, masked_one, masked_two, lead, second):
     count, _, block, _ = back.shape
     width = count * block
     kind = back.dtype
@@ -206,9 +242,10 @@
         return lax.dot_general(a, b, (((1,), (1,)), ((), ())), preferred_element_type=F32)
 
     def kernel(
-        pattern_ref, back_ref, panels_ref, one_ref, two_ref, second_ref, lead_ref,
-        rows_one_ref, rows_two_ref, sums_ref, chosen, panels,
+        pattern_ref, back_ref, panels_ref, one_ref, two_ref, lead_ref, *refs
     ):
+        terms = [refs[: len(second) // 2], refs[len(second) // 2 : len(second)]]
+        rows_one_ref, rows_two_ref, sums_ref, chosen, panels = refs[len(second) :]
         for i in range(count):
             part = pl.ds(i * block, block)
             rows_one_ref[:, part] = back_ref[i, 0]
@@ -216,9 +253,10 @@
             panels[:, part] = panels_ref[i]
         for i in range(count):
             part = pl.ds(i * block, block)
-            total = second_ref[:, part].astype(F32) + jnp.dot(
-                lead_ref[...], chosen[:, part], preferred_element_type=F32
-            )
+            side, first = i * 2 // count, i % (count // 2) * block
+            total = jnp.dot(lead_ref[...], chosen[:, part], preferred_element_type=F32)
+            for ref in terms[side]:
+                total = total + ref[:, first : first + block].astype(F32)
             rows_two_ref[:, part] = (-(total * pattern_ref[0, i].astype(F32))).astype(kind)
         sums_ref[0] = over(one_ref[...], rows_one_ref[...])
         sums_ref[1] = over(two_ref[...], chosen[...])
@@ -229,7 +267,7 @@
         kernel,
         [((block, width), kind), ((block, width), kind), ((4, block, block), F32)],
         [pattern],
-        [back, parent_panels, masked_one, masked_two, second, lead],
+        [back, parent_panels, masked_one, masked_two, lead, *second],
         [pltpu.VMEM((block, width), kind), pltpu.VMEM((block, width), kind)],
     )
 
@@ -299,11 +337,14 @@
     masked_one = apply_pattern(level_one_panels, level_one_pattern, block)
     masked_two = apply_pattern(level_two_panels, level_two_pattern, block)
 
-    found_one = all_panels(own_panels(masked_one))
-    later_two, found_one = lax.optimization_barrier((masked_two, found_one))
-    own_two = own_panels(later_two)
+    found_one = all_panels(in_order([turned_panels(masked_one, k) for k in range(2)]))
+    later_two, _ = lax.optimization_barrier((masked_two, found_one[2:6:2]))
+    early_two = turned_panels(later_two, 0)
+    early_two, found_one = lax.optimization_barrier((early_two, found_one))
+    product_one = by_column(found_one, ancestor_inverse, block)
+    later_two, product_one = lax.optimization_barrier((masked_two, product_one))
+    own_two = in_order([early_two, turned_panels(later_two, 1)])
     later_one, own_two = lax.optimization_barrier((masked_one, own_two))
-    product_one = by_column(found_one, ancestor_inverse, block)
     first_sum = lax.psum_scatter(
         product_one.reshape(count * count * block, block), "col", scatter_dimension=0, tiled=True
     ).reshape(count, block, block)
@@ -322,7 +363,7 @@
     parent_panels = lax.all_to_all(
         jnp.take(cut[:, :block], readers, axis=0), "col", 0, 0, tiled=True
     )
-    found_two = all_panels(own_two)
+    rows_two = lax.all_gather(own_two, "row", axis=0, tiled=True)
 
     steps = jnp.arange(count, dtype=jnp.int32)
     place = arrival(steps)
@@ -330,24 +371,20 @@
     x_major = (y + inner) % SIDE * SIDE + (x + outer) % SIDE
     y_major = (y + outer) % SIDE * SIDE + (x + inner) % SIDE
 
-    rows_two = jnp.concatenate(found_two, 0)
-
-    def product(part):
-        return lambda order: by_supernode(order, rows_two, ancestor_inverse, part)
-
-    first_a, near_a = first_sends(product(0), place[x_major].reshape(SIDE, SIDE), x_step)
-    first_b, near_b = first_sends(product(1), place[y_major].reshape(SIDE, SIDE), y_step)
+    order = jnp.stack([x_major, y_major])
+    low_a, high_a, low_b, high_b = ring_far(order, rows_two, ancestor_inverse)
+    first_a = send(low_a, x_step(1)), send(high_a, x_step(-1))
+    first_b = send(low_b, y_step(1)), send(high_b, y_step(-1))
+    near = ring_near(order, rows_two, ancestor_inverse)
     first_a, first_b, parent_panels = lax.optimization_barrier((first_a, first_b, parent_panels))
-    second_a = second_sends(first_a, near_a, x_step)
-    second_b = second_sends(first_b, near_b, y_step)
+    second_a = second_sends(first_a, near[:3], x_step)
+    second_b = second_sends(first_b, near[3:], y_step)
     going = outgoing(place, readers, cut_pattern, first_sum)
     back = lax.all_to_all(going, "col", 0, 0, tiled=True)
     second_a, second_b, _ = lax.optimization_barrier((second_a, second_b, going))
-    second_sum = jnp.concatenate(
-        [third_sends(second_a, near_a, y_step), third_sends(second_b, near_b, x_step)], 1
-    )
+    second_sum = third_sends(second_a, near[:3], y_step) + third_sends(second_b, near[3:], x_step)
     level_one_rows, level_two_rows, sums = finish_rows(
-        level_two_pattern, back, parent_panels, masked_one, masked_two, second_sum, parent_lead
+        level_two_pattern, back, parent_panels, masked_one, masked_two, parent_lead, second_sum
     )
 
     diag_blocks = level_one_diag.reshape(count, block, block)

time: 291 us -> 292 us (level)
  other arithmetic: 25.7 us -> 5.41 us
  waiting for transfers between devices: 78.3 us -> 97.4 us
  Pallas kernels: 31.1 us -> 40.7 us
  starting transfers between devices: 112 us -> 103 us
    reduce_scatter x1, waiting for transfers between devices: 0.01 us -> 23 us  [per_device(): lax.psum_scatter(product_one.reshape(count * count * block, block), 'col'...]
    all_to_all x1, starting transfers between devices: 7.41 us -> 22.6 us  [per_device(): lax.all_to_all(jnp.concatenate([cut, facts], 1), 'col', 0, 0, tiled=True)]
    ppermute x18, waiting for transfers between devices: 51.8 us -> 39.2 us  [the longest x14 20.9 us: send(): return lax.ppermute(value, 'col', step)]
    unnamed x56 -> x74, local copies, waits for them, and re-layouts: 16.3 us -> 26 us
    ppermute x2 -> x1, starting transfers between devices: 9.52 us -> 0.01 us  [all_panels(): below = lax.ppermute(own, 'row', z_step(1))]
    pallas_call x4 -> x6, Pallas kernels: 11.5 us -> 20.5 us  [ring_call(): pl.pallas_call(kernel, out_shape=[jax.ShapeDtypeStruct(shape, kind) for s...]
    another operation x8 -> x5, other arithmetic: 9.34 us -> 1.01 us  [the longest x4 1 us: in_order(): jnp.stack([jnp.where(even, pieces[0], pieces[1]), jnp.where(even, pieces[...]
    all_to_all x1, waiting for transfers between devices: 5.72 us -> 13.5 us  [per_device(): lax.all_to_all(jnp.concatenate([cut, facts], 1), 'col', 0, 0, tiled=True)]
  transfers between devices with their start and end apart: 42 -> 35, of which waited for: 21 -> 16; matrix products, arithmetic and copies ran while one was open for 16% -> 2% of each run, Pallas kernels for 4% -> 8%
where the time goes in v3:
time: 292 us; the launch traced here: 291 us
  starting transfers between devices  103 us (35%)
  waiting for transfers between devices  97.4 us (33%)
  Pallas kernels  40.7 us (14%)
  local copies, waits for them, and re-layouts  28.7 us (10%)
  between operations  16.6 us (6%)
  other arithmetic  5.41 us (2%)
    unnamed x74, local copies, waits for them, and re-layouts  26 us
    reduce_scatter x1, waiting for transfers between devices, per_device(): lax.psum_scatter(product_one.reshape(count * count * block, block), 'col'...  23 us
    all_to_all x1, starting transfers between devices, per_device(): lax.all_to_all(jnp.concatenate([cut, facts], 1), 'col', 0, 0, tiled=True)  22.6 us
    ppermute x14, starting transfers between devices, send(): return lax.ppermute(value, 'col', step)  21 us
    ppermute x14, waiting for transfers between devices, send(): return lax.ppermute(value, 'col', step)  20.9 us
    pallas_call x6, Pallas kernels, ring_call(): pl.pallas_call(kernel, out_shape=[jax.ShapeDtypeStruct(shape, kind) for s...  20.5 us
    ppermute x4, waiting for transfers between devices, turned_panels(): return lax.ppermute(part, ('row', 'col'), turn(k))  18.3 us
    ppermute x1, starting transfers between devices, all_panels(): above = lax.ppermute(own, 'row', z_step(-1))  15.4 us
  transfers between devices with their start and end apart: 35, of which 16 were waited for; matrix products, arithmetic and copies ran while one was open for 2% of the time, Pallas kernels for 8%

profile of v3, /device:TPU:1, one launch (start us, length us, event | category | flops | bytes accessed | tf_op | source)
XLA Modules:
  0.0 291.4 jit_solution(11907778500783898138)
XLA Ops:
  10.0 6.0 %collective-permute-start = (bf16[128,1024]{1,0:T(8,128)(2,1)S(1)}, bf16[128,1024]{1,0:T(8,128)(2,1)S(1)}, u32[]{:S(2)}, u32[]{:S(2)}) collective-permute-start(bf16[128,1024]{1,0:T(8,128)(2,1)S(1)} %get-tuple-element.115), channel_id=1, source_target_pairs={{0,0},{1,1},{2,16},{3,17},{4,32},{5,33},{6,48},{7,49},{8,64},{9,65... | collective-permute-start | bytes 786440 | tf_op jit(solution)/shard_map/ppermute | solution.py:46
  16.7 5.2 %collective-permute-done = bf16[128,1024]{1,0:T(8,128)(2,1)S(1)} collective-permute-done((bf16[128,1024]{1,0:T(8,128)(2,1)S(1)}, bf16[128,1024]{1,0:T(8,128)(2,1)S(1)}, u32[]{:S(2)}, u32[]{:S(2)}) %collective-permute-start) | collective-permute-done | bytes 262176 | tf_op jit(solution)/shard_map/ppermute | solution.py:46
  21.9 2.5 collective-permute-done.1
  24.5 15.4 %collective-permute-start.3 = (bf16[2,128,1024]{2,1,0:T(8,128)(2,1)S(1)}, bf16[2,128,1024]{2,1,0:T(8,128)(2,1)S(1)}, u32[]{:S(2)}, u32[]{:S(2)}) collective-permute-start(bf16[2,128,1024]{2,1,0:T(8,128)(2,1)S(1)} %pad_maximum_fusion.refs_0_), channel_id=1, source_target_pairs={{0,96},{16,112},{32,0},{48,16},{64,32},{80,48},{96,64},{112,80},{1... | collective-permute-start | bytes 1572872 | tf_op jit(solution)/shard_map/ppermute | solution.py:58
  39.9 8.8 %collective-permute-done.3.refs_4_ = bf16[2,128,1024]{2,1,0:T(8,128)(2,1)S(1)} collective-permute-done((bf16[2,128,1024]{2,1,0:T(8,128)(2,1)S(1)}, bf16[2,128,1024]{2,1,0:T(8,128)(2,1)S(1)}, u32[]{:S(2)}, u32[]{:S(2)}) %collective-permute-start.3) | collective-permute-done | bytes 524320 | tf_op jit(solution)/shard_map/ppermute | solution.py:58
  48.8 3.5 %collective-permute-start.9 = (bf16[128,1024]{1,0:T(8,128)(2,1)S(1)}, bf16[128,1024]{1,0:T(8,128)(2,1)S(1)}, u32[]{:S(2)}, u32[]{:S(2)}) collective-permute-start(bf16[128,1024]{1,0:T(8,128)(2,1)S(1)} %slice_bitcast_fusion), channel_id=1, source_target_pairs={{0,96},{16,112},{32,0},{48,16},{64,32},{80,48},{96,64},{112,80},{1... | collective-permute-start | bytes 786440 | tf_op jit(solution)/shard_map/ppermute | solution.py:60
  52.5 6.9 %collective-permute-start.5 = (bf16[2,128,1024]{2,1,0:T(8,128)(2,1)S(1)}, bf16[2,128,1024]{2,1,0:T(8,128)(2,1)S(1)}, u32[]{:S(2)}, u32[]{:S(2)}) collective-permute-start(bf16[2,128,1024]{2,1,0:T(8,128)(2,1)S(1)} %pad_maximum_fusion.refs_0_), channel_id=1, source_target_pairs={{0,16},{16,0},{32,48},{48,32},{64,80},{80,64},{96,112},{112,96},{1... | collective-permute-start | bytes 1572872 | tf_op jit(solution)/shard_map/ppermute | solution.py:64
  59.9 7.0 %collective-permute-start.10 = (bf16[2,128,1024]{2,1,0:T(8,128)(2,1)S(1)}, bf16[2,128,1024]{2,1,0:T(8,128)(2,1)S(1)}, u32[]{:S(2)}, u32[]{:S(2)}) collective-permute-start(bf16[2,128,1024]{2,1,0:T(8,128)(2,1)S(1)} %pad_maximum_fusion.1.refs_6_), channel_id=1, source_target_pairs={{0,16},{16,0},{32,48},{48,32},{64,80},{80,64},{96,112},{112,96},{1... | collective-permute-start | bytes 1572872 | tf_op jit(solution)/shard_map/ppermute | solution.py:64
  67.0 4.1 %collective-permute-start.4 = (bf16[128,1024]{1,0:T(8,128)(2,1)S(1)}, bf16[128,1024]{1,0:T(8,128)(2,1)S(1)}, u32[]{:S(2)}, u32[]{:S(2)}) collective-permute-start(bf16[128,1024]{1,0:T(8,128)(2,1)S(1)} %constant_dynamic-slice_fusion.1), channel_id=1, source_target_pairs={{0,0},{1,1},{2,16},{3,17},{4,32},{5,33},{6,48},{7,49},{8,64},{9,65... | collective-permute-start | bytes 786440 | tf_op jit(solution)/shard_map/ppermute | solution.py:46
  71.1 5.1 %collective-permute-done.4 = bf16[128,1024]{1,0:T(8,128)(2,1)S(1)} collective-permute-done((bf16[128,1024]{1,0:T(8,128)(2,1)S(1)}, bf16[128,1024]{1,0:T(8,128)(2,1)S(1)}, u32[]{:S(2)}, u32[]{:S(2)}) %collective-permute-start.4) | collective-permute-done | bytes 262176 | tf_op jit(solution)/shard_map/ppermute | solution.py:46
  78.0 14.7 %shard_map.137 = bf16[16,2048,128]{2,1,0:T(8,128)(2,1)} custom-call(bf16[2,128,1024]{2,1,0:T(8,128)(2,1)S(1)} %pad_maximum_fusion.refs_0_, bf16[2,128,1024]{2,1,0:T(8,128)(2,1)S(1)} %collective-permute-done.5.refs_1_, bf16[2,128,1024]{2,1,0:T(8,128)(2,1)S(1)} %collective-permute-done.2.refs_2_, bf16[2,128,1024]{2,1,0:T(8,128)(2,1)} %copy-done.34, ...), custom_call_target="tpu_custom_call" | custom-call | flops 8589934592 | bytes 16777216 | tf_op jit(solution)/shard_map/pallas_call | solution.py:93
  94.4 5.4 %collective-permute-done.11 = bf16[128,1024]{1,0:T(8,128)(2,1)S(1)} collective-permute-done((bf16[128,1024]{1,0:T(8,128)(2,1)S(1)}, bf16[128,1024]{1,0:T(8,128)(2,1)S(1)}, u32[]{:S(2)}, u32[]{:S(2)}) %collective-permute-start.11) | collective-permute-done | bytes 262176 | tf_op jit(solution)/shard_map/ppermute | solution.py:46
  103.1 22.6 %all-to-all-start = ((bf16[16,144,128]{2,1,0:T(8,128)(2,1)}), bf16[16,144,128]{2,1,0:T(8,128)(2,1)S(1)}, u32[]{:S(2)}, u32[]{:S(2)}) async-start(bf16[16,144,128]{2,1,0:T(8,128)(2,1)} %fusion.1), calls=%async_computation | async-start | bytes 1179648 | tf_op jit(solution)/shard_map/all_to_all | solution.py:360
  125.8 13.5 %all-to-all-done = bf16[16,144,128]{2,1,0:T(8,128)(2,1)S(1)} async-done(((bf16[16,144,128]{2,1,0:T(8,128)(2,1)}), bf16[16,144,128]{2,1,0:T(8,128)(2,1)S(1)}, u32[]{:S(2)}, u32[]{:S(2)}) %all-to-all-start) | async-done | bytes 589856 | tf_op jit(solution)/shard_map/all_to_all | solution.py:360
  141.7 3.6 %all-to-all-start.2 = ((bf16[16,128,128]{2,1,0:T(8,128)(2,1)}), bf16[16,128,128]{2,1,0:T(8,128)(2,1)S(1)}, u32[]{:S(2)}, u32[]{:S(2)}) async-start(bf16[16,128,128]{2,1,0:T(8,128)(2,1)} %broadcast_select_fusion), calls=%async_computation.3 | async-start | bytes 1048576 | tf_op jit(solution)/shard_map/all_to_all | solution.py:363
  145.2 3.3 %all-gather.2.cloned.1.call-done.rows_ref = bf16[16,128,1024]{2,1,0:T(8,128)(2,1)} async-done(((bf16[2,128,1024]{2,1,0:T(8,128)(2,1)}), bf16[16,128,1024]{2,1,0:T(8,128)(2,1)}) %all-gather.2.cloned.1.call-update) | async-done | bytes 4194320 | tf_op jit(solution)/shard_map/all_gather | solution.py:366
  153.0 3.9 %shard_map.139 = (bf16[4,64,1024]{2,1,0:T(8,128)(2,1)}, bf16[4,64,1024]{2,1,0:T(8,128)(2,1)}, bf16[4,64,1024]{2,1,0:T(8,128)(2,1)}, bf16[4,64,1024]{2,1,0:T(8,128)(2,1)}) custom-call(s32[2,16]{1,0:T(2,128)S(1)} %pad_add_fusion.order_ref, bf16[16,128,1024]{2,1,0:T(8,128)(2,1)S(1)} %copy-done.1, bf16[1024,2048]{1,0:T(8,128)(2,1)S(1)} %copy-done), custom_call_target="tpu_custom_call" | custom-call | flops 2147483648 | bytes 4194304 | tf_op jit(solution)/shard_map/pallas_call | solution.py:120
  162.2 7.2 %shard_map.140 = (bf16[4,128,1024]{2,1,0:T(8,128)(2,1)S(1)}, bf16[4,128,1024]{2,1,0:T(8,128)(2,1)S(1)}, bf16[4,128,1024]{2,1,0:T(8,128)(2,1)S(1)}, bf16[4,128,10...) custom-call(s32[2,16]{1,0:T(2,128)S(1)} %pad_add_fusion.order_ref, ...), custom_call_target="tpu_custom_call" | custom-call | flops 6442450944 | bytes 4194304 | tf_op jit(solution)/shard_map/pallas_call | solution.py:120
  174.4 8.7 %collective-permute-done.12.low_ref = bf16[4,64,1024]{2,1,0:T(8,128)(2,1)} collective-permute-done((bf16[4,64,1024]{2,1,0:T(8,128)(2,1)}, bf16[4,64,1024]{2,1,0:T(8,128)(2,1)}, u32[]{:S(2)}, u32[]{:S(2)}) %collective-permute-start.12) | collective-permute-done | bytes 524320 | tf_op jit(solution)/shard_map/ppermute | solution.py:161
  187.6 2.9 %shard_map.141 = (bf16[4,128,1024]{2,1,0:T(8,128)(2,1)}, bf16[4,128,1024]{2,1,0:T(8,128)(2,1)}) custom-call(bf16[4,64,1024]{2,1,0:T(8,128)(2,1)} %collective-permute-done.12.low_ref, bf16[4,64,1024]{2,1,0:T(8,128)(2,1)} %collective-permute-done.13.high_ref, bf16[4,128,1024]{2,1,0:T(8,128)(2,1)S(1)} %copy-done.11, bf16[4,128,1024]{2,1,0:T(8,128)(2,1)S(1)} %copy-done.13), custom_call_target="tpu_custom_call" | custom-call | bytes 4194304 | tf_op jit(solution)/shard_map/pallas_call | solution.py:120
  190.5 2.7 collective-permute-start.17
  193.2 2.5 shard_map.142
  195.7 2.6 collective-permute-start.19
  199.1 23.0 %reduce-scatter.2.cloned.1.call-done = bf16[2048,128]{1,0:T(8,128)(2,1)} async-done(((bf16[32768,128]{1,0:T(8,128)(2,1)}), bf16[2048,128]{1,0:T(8,128)(2,1)}) %reduce-scatter.2.cloned.1.call-update) | async-done | bytes 524304 | tf_op jit(solution)/shard_map/reduce_scatter | solution.py:348
  224.9 5.2 %all-to-all-start.1 = ((bf16[16,2,128,128]{3,2,1,0:T(8,128)(2,1)}), bf16[16,2,128,128]{3,2,1,0:T(8,128)(2,1)S(1)}, u32[]{:S(2)}, u32[]{:S(2)}) async-start(bf16[16,2,128,128]{3,2,1,0:T(8,128)(2,1)} %shard_map.138), calls=%async_computation.2 | async-start | bytes 2097152 | tf_op jit(solution)/shard_map/all_to_all | solution.py:383
  234.9 2.4 collective-permute-start.21
  244.8 6.7 %collective-permute-done.20.refs_1_ = bf16[128,1024]{1,0:T(8,128)(2,1)S(1)} collective-permute-done((bf16[128,1024]{1,0:T(8,128)(2,1)S(1)}, bf16[128,1024]{1,0:T(8,128)(2,1)S(1)}, u32[]{:S(2)}, u32[]{:S(2)}) %collective-permute-start.20) | collective-permute-done | bytes 262176 | tf_op jit(solution)/shard_map/ppermute | solution.py:161
  253.1 3.5 %collective-permute-done.21.refs_2_ = bf16[128,1024]{1,0:T(8,128)(2,1)S(1)} collective-permute-done((bf16[128,1024]{1,0:T(8,128)(2,1)S(1)}, bf16[128,1024]{1,0:T(8,128)(2,1)S(1)}, u32[]{:S(2)}, u32[]{:S(2)}) %collective-permute-start.21) | collective-permute-done | bytes 262176 | tf_op jit(solution)/shard_map/ppermute | solution.py:161
  266.0 2.4 shard_map.145
  270.3 2.7 collective-permute-start.27
  274.9 3.3 %collective-permute-done.27.b = bf16[4,128,128]{2,1,0:T(8,128)(2,1)S(1)} collective-permute-done((bf16[4,128,128]{2,1,0:T(8,128)(2,1)S(1)}, bf16[4,128,128]{2,1,0:T(8,128)(2,1)S(1)}, u32[]{:S(2)}, u32[]{:S(2)}) %collective-permute-start.27) | collective-permute-done | bytes 131104 | tf_op jit(solution)/shard_map/ppermute | solution.py:201
  278.9 3.8 %collective-permute-done.29.d = bf16[4,128,128]{2,1,0:T(8,128)(2,1)S(1)} collective-permute-done((bf16[4,128,128]{2,1,0:T(8,128)(2,1)S(1)}, bf16[4,128,128]{2,1,0:T(8,128)(2,1)S(1)}, u32[]{:S(2)}, u32[]{:S(2)}) %collective-permute-start.29) | collective-permute-done | bytes 131104 | tf_op jit(solution)/shard_map/ppermute | solution.py:201
  (158 shorter events, 63.5 us)
Async XLA Ops:
  8.0 140.5 %all-gather.2.cloned.1.call-start = ((), (), s32[]{:S(2)}) async-start(), calls=%async_computation.5 | async-start | bytes 4718592 | tf_op jit(solution)/shard_map/all_gather | solution.py:366
  10.0 11.9 %collective-permute-start = (bf16[128,1024]{1,0:T(8,128)(2,1)S(1)}, bf16[128,1024]{1,0:T(8,128)(2,1)S(1)}, u32[]{:S(2)}, u32[]{:S(2)}) collective-permute-start(bf16[128,1024]{1,0:T(8,128)(2,1)S(1)} %get-tuple-element.115), channel_id=1, source_target_pairs={{0,0},{1,1},{2,16},{3,17},{4,32},{5,33},{6,48},{7,49},{8,64},{9,65... | collective-permute-start | bytes 786440 | tf_op jit(solution)/shard_map/ppermute | solution.py:46
  16.0 8.4 %collective-permute-start.1 = (bf16[128,1024]{1,0:T(8,128)(2,1)S(1)}, bf16[128,1024]{1,0:T(8,128)(2,1)S(1)}, u32[]{:S(2)}, u32[]{:S(2)}) collective-permute-start(bf16[128,1024]{1,0:T(8,128)(2,1)S(1)} %get-tuple-element.116), channel_id=1, source_target_pairs={{0,1},{1,0},{2,17},{3,16},{4,33},{5,32},{6,49},{7,48},{8,65},{9,64... | collective-permute-start | bytes 786440 | tf_op jit(solution)/shard_map/ppermute | solution.py:46
  24.5 24.2 %collective-permute-start.3 = (bf16[2,128,1024]{2,1,0:T(8,128)(2,1)S(1)}, bf16[2,128,1024]{2,1,0:T(8,128)(2,1)S(1)}, u32[]{:S(2)}, u32[]{:S(2)}) collective-permute-start(bf16[2,128,1024]{2,1,0:T(8,128)(2,1)S(1)} %pad_maximum_fusion.refs_0_), channel_id=1, source_target_pairs={{0,96},{16,112},{32,0},{48,16},{64,32},{80,48},{96,64},{112,80},{1... | collective-permute-start | bytes 1572872 | tf_op jit(solution)/shard_map/ppermute | solution.py:58
  39.9 12.3 %collective-permute-start.2 = (bf16[2,128,1024]{2,1,0:T(8,128)(2,1)S(1)}, bf16[2,128,1024]{2,1,0:T(8,128)(2,1)S(1)}, u32[]{:S(2)}, u32[]{:S(2)}) collective-permute-start(bf16[2,128,1024]{2,1,0:T(8,128)(2,1)S(1)} %pad_maximum_fusion.refs_0_), channel_id=1, source_target_pairs={{0,32},{16,48},{32,64},{48,80},{64,96},{80,112},{96,0},{112,16},{1... | collective-permute-start | bytes 1572872 | tf_op jit(solution)/shard_map/ppermute | solution.py:57
  48.8 11.1 %collective-permute-start.9 = (bf16[128,1024]{1,0:T(8,128)(2,1)S(1)}, bf16[128,1024]{1,0:T(8,128)(2,1)S(1)}, u32[]{:S(2)}, u32[]{:S(2)}) collective-permute-start(bf16[128,1024]{1,0:T(8,128)(2,1)S(1)} %slice_bitcast_fusion), channel_id=1, source_target_pairs={{0,96},{16,112},{32,0},{48,16},{64,32},{80,48},{96,64},{112,80},{1... | collective-permute-start | bytes 786440 | tf_op jit(solution)/shard_map/ppermute | solution.py:60
  52.3 7.6 %collective-permute-start.8 = (bf16[128,1024]{1,0:T(8,128)(2,1)S(1)}, bf16[128,1024]{1,0:T(8,128)(2,1)S(1)}, u32[]{:S(2)}, u32[]{:S(2)}) collective-permute-start(bf16[128,1024]{1,0:T(8,128)(2,1)S(1)} %slice_bitcast_fusion.1), channel_id=1, source_target_pairs={{0,32},{16,48},{32,64},{48,80},{64,96},{80,112},{96,0},{112,16},{1... | collective-permute-start | bytes 786440 | tf_op jit(solution)/shard_map/ppermute | solution.py:60
  52.5 18.7 %collective-permute-start.5 = (bf16[2,128,1024]{2,1,0:T(8,128)(2,1)S(1)}, bf16[2,128,1024]{2,1,0:T(8,128)(2,1)S(1)}, u32[]{:S(2)}, u32[]{:S(2)}) collective-permute-start(bf16[2,128,1024]{2,1,0:T(8,128)(2,1)S(1)} %pad_maximum_fusion.refs_0_), channel_id=1, source_target_pairs={{0,16},{16,0},{32,48},{48,32},{64,80},{80,64},{96,112},{112,96},{1... | collective-permute-start | bytes 1572872 | tf_op jit(solution)/shard_map/ppermute | solution.py:64
  59.4 16.9 %collective-permute-start.6 = (bf16[2,128,1024]{2,1,0:T(8,128)(2,1)S(1)}, bf16[2,128,1024]{2,1,0:T(8,128)(2,1)S(1)}, u32[]{:S(2)}, u32[]{:S(2)}) collective-permute-start(bf16[2,128,1024]{2,1,0:T(8,128)(2,1)S(1)} %collective-permute-done.2.refs_2_), channel_id=1, source_target_pairs={{0,16},{16,0},{32,48},{48,32},{64,80},{80,64},{96,112},{112,96},{1... | collective-permute-start | bytes 1572872 | tf_op jit(solution)/shard_map/ppermute | solution.py:64
  59.5 16.8 %collective-permute-start.7 = (bf16[2,128,1024]{2,1,0:T(8,128)(2,1)S(1)}, bf16[2,128,1024]{2,1,0:T(8,128)(2,1)S(1)}, u32[]{:S(2)}, u32[]{:S(2)}) collective-permute-start(bf16[2,128,1024]{2,1,0:T(8,128)(2,1)S(1)} %collective-permute-done.3.refs_4_), channel_id=1, source_target_pairs={{0,16},{16,0},{32,48},{48,32},{64,80},{80,64},{96,112},{112,96},{1... | collective-permute-start | bytes 1572872 | tf_op jit(solution)/shard_map/ppermute | solution.py:64
  59.9 16.3 %collective-permute-start.10 = (bf16[2,128,1024]{2,1,0:T(8,128)(2,1)S(1)}, bf16[2,128,1024]{2,1,0:T(8,128)(2,1)S(1)}, u32[]{:S(2)}, u32[]{:S(2)}) collective-permute-start(bf16[2,128,1024]{2,1,0:T(8,128)(2,1)S(1)} %pad_maximum_fusion.1.refs_6_), channel_id=1, source_target_pairs={{0,16},{16,0},{32,48},{48,32},{64,80},{80,64},{96,112},{112,96},{1... | collective-permute-start | bytes 1572872 | tf_op jit(solution)/shard_map/ppermute | solution.py:64
  67.0 9.2 %collective-permute-start.4 = (bf16[128,1024]{1,0:T(8,128)(2,1)S(1)}, bf16[128,1024]{1,0:T(8,128)(2,1)S(1)}, u32[]{:S(2)}, u32[]{:S(2)}) collective-permute-start(bf16[128,1024]{1,0:T(8,128)(2,1)S(1)} %constant_dynamic-slice_fusion.1), channel_id=1, source_target_pairs={{0,0},{1,1},{2,16},{3,17},{4,32},{5,33},{6,48},{7,49},{8,64},{9,65... | collective-permute-start | bytes 786440 | tf_op jit(solution)/shard_map/ppermute | solution.py:46
  100.8 121.3 %reduce-scatter.2.cloned.1.call-start = ((), (), s32[]{:S(2)}) async-start(), calls=%async_computation.4 | async-start | bytes 8912896 | tf_op jit(solution)/shard_map/reduce_scatter | solution.py:348
  103.1 36.2 %all-to-all-start = ((bf16[16,144,128]{2,1,0:T(8,128)(2,1)}), bf16[16,144,128]{2,1,0:T(8,128)(2,1)S(1)}, u32[]{:S(2)}, u32[]{:S(2)}) async-start(bf16[16,144,128]{2,1,0:T(8,128)(2,1)} %fusion.1), calls=%async_computation | async-start | bytes 1179648 | tf_op jit(solution)/shard_map/all_to_all | solution.py:360
  141.7 32.8 %all-to-all-start.2 = ((bf16[16,128,128]{2,1,0:T(8,128)(2,1)}), bf16[16,128,128]{2,1,0:T(8,128)(2,1)S(1)}, u32[]{:S(2)}, u32[]{:S(2)}) async-start(bf16[16,128,128]{2,1,0:T(8,128)(2,1)} %broadcast_select_fusion), calls=%async_computation.3 | async-start | bytes 1048576 | tf_op jit(solution)/shard_map/all_to_all | solution.py:363
  156.8 26.3 %collective-permute-start.12 = (bf16[4,64,1024]{2,1,0:T(8,128)(2,1)}, bf16[4,64,1024]{2,1,0:T(8,128)(2,1)}, u32[]{:S(2)}, u32[]{:S(2)}) collective-permute-start(bf16[4,64,1024]{2,1,0:T(8,128)(2,1)} %get-tuple-element.70), channel_id=1, source_target_pairs={{0,1},{1,2},{2,3},{3,0},{4,5},{5,6},{6,7},{7,4},{8,9},{9,10},{10,1... | collective-permute-start | bytes 1572872 | tf_op jit(solution)/shard_map/ppermute | solution.py:161
  158.1 25.1 %collective-permute-start.13 = (bf16[4,64,1024]{2,1,0:T(8,128)(2,1)}, bf16[4,64,1024]{2,1,0:T(8,128)(2,1)}, u32[]{:S(2)}, u32[]{:S(2)}) collective-permute-start(bf16[4,64,1024]{2,1,0:T(8,128)(2,1)} %get-tuple-element.71), channel_id=1, source_target_pairs={{0,3},{1,0},{2,1},{3,2},{4,7},{5,4},{6,5},{7,6},{8,11},{9,8},{10,9... | collective-permute-start | bytes 1572872 | tf_op jit(solution)/shard_map/ppermute | solution.py:161
  159.5 25.6 %collective-permute-start.14 = (bf16[4,64,1024]{2,1,0:T(8,128)(2,1)}, bf16[4,64,1024]{2,1,0:T(8,128)(2,1)S(1)}, u32[]{:S(2)}, u32[]{:S(2)}) collective-permute-start(bf16[4,64,1024]{2,1,0:T(8,128)(2,1)} %get-tuple-element.72), channel_id=1, source_target_pairs={{0,4},{1,5},{2,6},{3,7},{4,8},{5,9},{6,10},{7,11},{8,12},{9,13},{1... | collective-permute-start | bytes 1572872 | tf_op jit(solution)/shard_map/ppermute | solution.py:161
  160.8 24.3 %collective-permute-start.15 = (bf16[4,64,1024]{2,1,0:T(8,128)(2,1)}, bf16[4,64,1024]{2,1,0:T(8,128)(2,1)}, u32[]{:S(2)}, u32[]{:S(2)}) collective-permute-start(bf16[4,64,1024]{2,1,0:T(8,128)(2,1)} %get-tuple-element.73), channel_id=1, source_target_pairs={{0,12},{1,13},{2,14},{3,15},{4,0},{5,1},{6,2},{7,3},{8,4},{9,5},{1... | collective-permute-start | bytes 1572872 | tf_op jit(solution)/shard_map/ppermute | solution.py:161
  190.5 39.6 %collective-permute-start.16 = (bf16[4,128,1024]{2,1,0:T(8,128)(2,1)}, bf16[4,128,1024]{2,1,0:T(8,128)(2,1)}, u32[]{:S(2)}, u32[]{:S(2)}) collective-permute-start(bf16[4,128,1024]{2,1,0:T(8,128)(2,1)} %get-tuple-element.79), channel_id=1, source_target_pairs={{0,1},{1,2},{2,3},{3,0},{4,5},{5,6},{6,7},{7,4},{8,9},{9,10},{10,1... | collective-permute-start | bytes 3145736 | tf_op jit(solution)/shard_map/ppermute | solution.py:161
  190.5 39.6 %collective-permute-start.17 = (bf16[4,128,1024]{2,1,0:T(8,128)(2,1)}, bf16[4,128,1024]{2,1,0:T(8,128)(2,1)}, u32[]{:S(2)}, u32[]{:S(2)}) collective-permute-start(bf16[4,128,1024]{2,1,0:T(8,128)(2,1)} %get-tuple-element.80), channel_id=1, source_target_pairs={{0,3},{1,0},{2,1},{3,2},{4,7},{5,4},{6,5},{7,6},{8,11},{9,8},{10,9... | collective-permute-start | bytes 3145736 | tf_op jit(solution)/shard_map/ppermute | solution.py:161
  195.7 34.5 %collective-permute-start.18 = (bf16[4,128,1024]{2,1,0:T(8,128)(2,1)}, bf16[4,128,1024]{2,1,0:T(8,128)(2,1)}, u32[]{:S(2)}, u32[]{:S(2)}) collective-permute-start(bf16[4,128,1024]{2,1,0:T(8,128)(2,1)} %get-tuple-element.85), channel_id=1, source_target_pairs={{0,4},{1,5},{2,6},{3,7},{4,8},{5,9},{6,10},{7,11},{8,12},{9,13},{1... | collective-permute-start | bytes 3145736 | tf_op jit(solution)/shard_map/ppermute | solution.py:161
  195.7 34.4 %collective-permute-start.19 = (bf16[4,128,1024]{2,1,0:T(8,128)(2,1)}, bf16[4,128,1024]{2,1,0:T(8,128)(2,1)}, u32[]{:S(2)}, u32[]{:S(2)}) collective-permute-start(bf16[4,128,1024]{2,1,0:T(8,128)(2,1)} %get-tuple-element.86), channel_id=1, source_target_pairs={{0,12},{1,13},{2,14},{3,15},{4,0},{5,1},{6,2},{7,3},{8,4},{9,5},{1... | collective-permute-start | bytes 3145736 | tf_op jit(solution)/shard_map/ppermute | solution.py:161
  224.9 35.3 %all-to-all-start.1 = ((bf16[16,2,128,128]{3,2,1,0:T(8,128)(2,1)}), bf16[16,2,128,128]{3,2,1,0:T(8,128)(2,1)S(1)}, u32[]{:S(2)}, u32[]{:S(2)}) async-start(bf16[16,2,128,128]{3,2,1,0:T(8,128)(2,1)} %shard_map.138), calls=%async_computation.2 | async-start | bytes 2097152 | tf_op jit(solution)/shard_map/all_to_all | solution.py:383
  233.4 18.0 %collective-permute-start.20 = (bf16[128,1024]{1,0:T(8,128)(2,1)S(1)}, bf16[128,1024]{1,0:T(8,128)(2,1)S(1)}, u32[]{:S(2)}, u32[]{:S(2)}) collective-permute-start(bf16[128,1024]{1,0:T(8,128)(2,1)S(1)} %get-tuple-element.91), channel_id=1, source_target_pairs={{0,4},{1,5},{2,6},{3,7},{4,8},{5,9},{6,10},{7,11},{8,12},{9,13},{1... | collective-permute-start | bytes 786440 | tf_op jit(solution)/shard_map/ppermute | solution.py:161
  234.9 21.8 %collective-permute-start.21 = (bf16[128,1024]{1,0:T(8,128)(2,1)S(1)}, bf16[128,1024]{1,0:T(8,128)(2,1)S(1)}, u32[]{:S(2)}, u32[]{:S(2)}) collective-permute-start(bf16[128,1024]{1,0:T(8,128)(2,1)S(1)} %get-tuple-element.92), channel_id=1, source_target_pairs={{0,8},{1,9},{2,10},{3,11},{4,12},{5,13},{6,14},{7,15},{8,0},{9,1},... | collective-permute-start | bytes 786440 | tf_op jit(solution)/shard_map/ppermute | solution.py:161
  237.3 20.1 %collective-permute-start.22 = (bf16[128,1024]{1,0:T(8,128)(2,1)S(1)}, bf16[128,1024]{1,0:T(8,128)(2,1)S(1)}, u32[]{:S(2)}, u32[]{:S(2)}) collective-permute-start(bf16[128,1024]{1,0:T(8,128)(2,1)S(1)} %get-tuple-element.93), channel_id=1, source_target_pairs={{0,12},{1,13},{2,14},{3,15},{4,0},{5,1},{6,2},{7,3},{8,4},{9,5},{1... | collective-permute-start | bytes 786440 | tf_op jit(solution)/shard_map/ppermute | solution.py:161
  241.2 16.9 %collective-permute-start.23 = (bf16[128,1024]{1,0:T(8,128)(2,1)S(1)}, bf16[128,1024]{1,0:T(8,128)(2,1)S(1)}, u32[]{:S(2)}, u32[]{:S(2)}) collective-permute-start(bf16[128,1024]{1,0:T(8,128)(2,1)S(1)} %get-tuple-element.98), channel_id=1, source_target_pairs={{0,1},{1,2},{2,3},{3,0},{4,5},{5,6},{6,7},{7,4},{8,9},{9,10},{10,1... | collective-permute-start | bytes 786440 | tf_op jit(solution)/shard_map/ppermute | solution.py:161
  242.4 16.4 %collective-permute-start.24 = (bf16[128,1024]{1,0:T(8,128)(2,1)S(1)}, bf16[128,1024]{1,0:T(8,128)(2,1)S(1)}, u32[]{:S(2)}, u32[]{:S(2)}) collective-permute-start(bf16[128,1024]{1,0:T(8,128)(2,1)S(1)} %get-tuple-element.99), channel_id=1, source_target_pairs={{0,2},{1,3},{2,0},{3,1},{4,6},{5,7},{6,4},{7,5},{8,10},{9,11},{10,... | collective-permute-start | bytes 786440 | tf_op jit(solution)/shard_map/ppermute | solution.py:161
  251.4 8.0 %collective-permute-start.25 = (bf16[128,1024]{1,0:T(8,128)(2,1)S(1)}, bf16[128,1024]{1,0:T(8,128)(2,1)S(1)}, u32[]{:S(2)}, u32[]{:S(2)}) collective-permute-start(bf16[128,1024]{1,0:T(8,128)(2,1)S(1)} %get-tuple-element.100), channel_id=1, source_target_pairs={{0,3},{1,0},{2,1},{3,2},{4,7},{5,4},{6,5},{7,6},{8,11},{9,8},{10,9... | collective-permute-start | bytes 786440 | tf_op jit(solution)/shard_map/ppermute | solution.py:161
  270.3 7.9 %collective-permute-start.27 = (bf16[4,128,128]{2,1,0:T(8,128)(2,1)S(1)}, bf16[4,128,128]{2,1,0:T(8,128)(2,1)S(1)}, u32[]{:S(2)}, u32[]{:S(2)}) collective-permute-start(bf16[4,128,128]{2,1,0:T(8,128)(2,1)S(1)} %add_convert_fusion.a), channel_id=1, source_target_pairs={{0,96},{16,112},{32,0},{48,16},{64,32},{80,48},{96,64},{112,80},{1... | collective-permute-start | bytes 393224 | tf_op jit(solution)/shard_map/ppermute | solution.py:201
  273.4 9.3 %collective-permute-start.29 = (bf16[4,128,128]{2,1,0:T(8,128)(2,1)S(1)}, bf16[4,128,128]{2,1,0:T(8,128)(2,1)S(1)}, u32[]{:S(2)}, u32[]{:S(2)}) collective-permute-start(bf16[4,128,128]{2,1,0:T(8,128)(2,1)S(1)} %add_convert_fusion.a), channel_id=1, source_target_pairs={{0,32},{16,48},{32,64},{48,80},{64,96},{80,112},{96,0},{112,16},{1... | collective-permute-start | bytes 393224 | tf_op jit(solution)/shard_map/ppermute | solution.py:201
  (40 other events, 224.7 us)
Sparse Core Ops, SparseCore 0:
  100.9 47.5 all-gather.1
Sparse Core Ops, SparseCore 1:
  104.7 117.4 reduce-scatter.1

commit v4 on v3

--- a/solution.py
+++ b/solution.py
@@ -8,7 +8,8 @@
 SIDE = 4
 CORES = 2
 F32 = jnp.float32
-RING_VMEM = 28 * 2**20
+LONG_CHAIN = 10**11
+RING_VMEM = 52 * 2**20
 
 
 def x_step(d):
@@ -107,54 +108,41 @@
     )(*pieces, matrix)
 
 
-def grouped_dot(rows_ref, order_ref, first, matrix_ref, part):
-    width = matrix_ref.shape[1] // 2
-    left = jnp.concatenate([rows_ref[order_ref[part, first + j]] for j in range(SIDE)], 0)
-    total = jnp.dot(
-        left, matrix_ref[:, part * width : (part + 1) * width], preferred_element_type=F32
-    )
-    return total.reshape(SIDE, -1, width)
-
-
-def ring_call(kernel, shapes, scalars, arrays, flops=0):
-    return pl.pallas_call(
-        kernel,
-        out_shape=[jax.ShapeDtypeStruct(shape, kind) for shape, kind in shapes],
-        in_specs=[whole(pltpu.SMEM)] * len(scalars) + [whole()] * len(arrays),
-        out_specs=[whole()] * len(shapes),
-        compiler_params=pltpu.CompilerParams(vmem_limit_bytes=RING_VMEM),
-        cost_estimate=pl.CostEstimate(flops=flops, bytes_accessed=2**22, transcendentals=0),
-    )(*scalars, *arrays)
-
-
-def ring_far(order, rows, matrix):
-    block, depth = rows.shape[1:]
-    half, width = block // 2, matrix.shape[1] // 2
-
-    def kernel(order_ref, rows_ref, matrix_ref, *out):
-        for part in range(2):
-            total = grouped_dot(rows_ref, order_ref, 2 * SIDE, matrix_ref, part)
-            out[2 * part][...] = total[:, :half].astype(rows.dtype)
-            out[2 * part + 1][...] = total[:, half:].astype(rows.dtype)
-
-    shape = ((SIDE, half, width), rows.dtype)
-    flops = 4 * SIDE * block * depth * width
-    return ring_call(kernel, [shape] * 4, [order], [rows, matrix], flops)
-
-
-def ring_near(order, rows, matrix):
+def by_supernode(order, rows, matrix, part, split):
     block, depth = rows.shape[1:]
     width = matrix.shape[1] // 2
-
-    def kernel(order_ref, rows_ref, matrix_ref, *out):
-        for part in range(2):
-            for g, d in enumerate((1, 3, 0)):
-                total = grouped_dot(rows_ref, order_ref, d * SIDE, matrix_ref, part)
-                out[3 * part + g][...] = total.astype(rows.dtype)
-
-    shape = ((SIDE, block, width), rows.dtype)
-    flops = 12 * SIDE * block * depth * width
-    return ring_call(kernel, [shape] * 6, [order], [rows, matrix], flops)
+    groups = order.shape[0] // SIDE
+    outs = 2 if split else 1
+    size = block // outs
+
+    def kernel(order_ref, a_ref, b_ref, c_ref, d_ref, matrix_ref, *out):
+        left = jnp.concatenate([a_ref[0], b_ref[0], c_ref[0], d_ref[0]], 0)
+        total = jnp.dot(left, matrix_ref[...], preferred_element_type=F32)
+        total = total.reshape(SIDE, block, width)
+        for i, ref in enumerate(out):
+            ref[0] = total[:, i * size : (i + 1) * size].astype(ref.dtype)
+
+    def pick(j):
+        return pl.BlockSpec((1, block, depth), lambda i, order_ref: (order_ref[SIDE * i + j], 0, 0))
+
+    return pl.pallas_call(
+        kernel,
+        out_shape=[jax.ShapeDtypeStruct((groups, SIDE, size, width), rows.dtype)] * outs,
+        grid_spec=pltpu.PrefetchScalarGridSpec(
+            num_scalar_prefetch=1,
+            grid=(groups,),
+            in_specs=[pick(j) for j in range(SIDE)]
+            + [pl.BlockSpec((depth, width), lambda i, order_ref: (0, part))],
+            out_specs=[pl.BlockSpec((1, SIDE, size, width), lambda i, order_ref: (i, 0, 0, 0))]
+            * outs,
+        ),
+        compiler_params=pltpu.CompilerParams(vmem_limit_bytes=RING_VMEM),
+        cost_estimate=pl.CostEstimate(
+            flops=2 * groups * SIDE * block * depth * width,
+            bytes_accessed=2 * groups * SIDE * block * (depth + width),
+            transcendentals=0,
+        ),
+    )(order, rows, rows, rows, rows, matrix)
 
 
 def send(value, step):
@@ -162,36 +150,58 @@
 
 
 def second_sends(arriving, near, step):
-    half = arriving[0].shape[1]
+    _, _, block, width = near.shape
+    half = block // 2
 
     def kernel(low_ref, high_ref, ahead_ref, behind_ref, ahead_out, behind_out):
         kind = ahead_out.dtype
-        ahead_out[:, :half] = (ahead_ref[:, :half].astype(F32) + low_ref[...].astype(F32)).astype(kind)
-        ahead_out[:, half:] = ahead_ref[:, half:]
-        behind_out[:, :half] = behind_ref[:, :half]
-        behind_out[:, half:] = (behind_ref[:, half:].astype(F32) + high_ref[...].astype(F32)).astype(kind)
-
-    shape = (near[0].shape, near[0].dtype)
-    ahead, behind = ring_call(kernel, [shape] * 2, [], [*arriving, near[0], near[1]])
+        low = ahead_ref[0, 0, :half].astype(F32) + low_ref[0].astype(F32)
+        high = behind_ref[0, 0, half:].astype(F32) + high_ref[0].astype(F32)
+        ahead_out[0, :half] = low.astype(kind)
+        ahead_out[0, half:] = ahead_ref[0, 0, half:]
+        behind_out[0, :half] = behind_ref[0, 0, :half]
+        behind_out[0, half:] = high.astype(kind)
+
+    part = pl.BlockSpec((1, half, width), lambda i: (i, 0, 0))
+    own = [pl.BlockSpec((1, 1, block, width), lambda i, g=g: (g, i, 0, 0)) for g in range(2)]
+    full = pl.BlockSpec((1, block, width), lambda i: (i, 0, 0))
+    ahead, behind = pl.pallas_call(
+        kernel,
+        out_shape=[jax.ShapeDtypeStruct((SIDE, block, width), near.dtype)] * 2,
+        grid=(SIDE,),
+        in_specs=[part, part, *own],
+        out_specs=[full, full],
+        compiler_params=pltpu.CompilerParams(vmem_limit_bytes=RING_VMEM),
+        cost_estimate=pl.CostEstimate(flops=0, bytes_accessed=2**22, transcendentals=0),
+    )(*arriving, near, near)
     return send(ahead, step(1)), send(behind, step(-1))
 
 
 def third_sends(arriving, near, step):
-    _, block, width = near[2].shape
-    kind = near[2].dtype
+    _, _, block, width = near.shape
+    kind = near.dtype
+    tile = width // SIDE
 
     def kernel(one_ref, two_ref, own_ref, own_out, *out):
         for d in range(SIDE):
-            total = own_ref[d].astype(F32) + one_ref[d].astype(F32) + two_ref[d].astype(F32)
+            total = own_ref[0, d].astype(F32) + one_ref[d].astype(F32) + two_ref[d].astype(F32)
             if d:
                 out[d - 1][...] = total.astype(kind)
             else:
                 own_out[...] = total
 
-    shape = (block, width)
-    own, *others = ring_call(
-        kernel, [(shape, F32)] + [(shape, kind)] * 3, [], [*arriving, near[2]]
-    )
+    four = pl.BlockSpec((SIDE, block, tile), lambda i: (0, 0, i))
+    one = pl.BlockSpec((block, tile), lambda i: (0, i))
+    own, *others = pl.pallas_call(
+        kernel,
+        out_shape=[jax.ShapeDtypeStruct((block, width), F32)]
+        + [jax.ShapeDtypeStruct((block, width), kind)] * 3,
+        grid=(SIDE,),
+        in_specs=[four, four, pl.BlockSpec((1, SIDE, block, tile), lambda i: (2, 0, 0, i))],
+        out_specs=[one] * 4,
+        compiler_params=pltpu.CompilerParams(vmem_limit_bytes=RING_VMEM),
+        cost_estimate=pl.CostEstimate(flops=0, bytes_accessed=2**22, transcendentals=0),
+    )(*arriving, near)
     return [own] + [send(v, step(d + 1)) for d, v in enumerate(others)]
 
 
@@ -201,18 +211,21 @@
     return [values] + [lax.ppermute(values, "row", z_step(-d)) for d in range(1, SIDE)]
 
 
-def whole(space=None):
-    return pl.BlockSpec(memory_space=space or pltpu.VMEM)
-
-
-def small_call(kernel, shapes, scalars, arrays, scratch=()):
+def whole(shape):
+    return pl.BlockSpec(shape, lambda i: (0,) * len(shape))
+
+
+def small_call(kernel, shapes, scalars, arrays, scratch=(), flops=0):
     return pl.pallas_call(
         kernel,
         out_shape=[jax.ShapeDtypeStruct(shape, kind) for shape, kind in shapes],
-        in_specs=[whole(pltpu.SMEM)] * len(scalars) + [whole()] * len(arrays),
-        out_specs=[whole()] * len(shapes),
+        grid=(1,),
+        in_specs=[pl.BlockSpec(memory_space=pltpu.SMEM)] * len(scalars)
+        + [whole(v.shape) for v in arrays],
+        out_specs=[whole(shape) for shape, _ in shapes],
         scratch_shapes=list(scratch),
-        compiler_params=pltpu.CompilerParams(vmem_limit_bytes=24 * 2**20),
+        compiler_params=pltpu.CompilerParams(vmem_limit_bytes=RING_VMEM),
+        cost_estimate=pl.CostEstimate(flops=flops, bytes_accessed=2**20, transcendentals=0),
     )(*scalars, *arrays)
 
 
@@ -230,6 +243,7 @@
         [((count, 2, block, block), jnp.bfloat16)],
         [place, readers, pattern],
         [total],
+        flops=LONG_CHAIN,
     )[0]
 
 
@@ -371,18 +385,22 @@
     x_major = (y + inner) % SIDE * SIDE + (x + outer) % SIDE
     y_major = (y + outer) % SIDE * SIDE + (x + inner) % SIDE
 
-    order = jnp.stack([x_major, y_major])
-    low_a, high_a, low_b, high_b = ring_far(order, rows_two, ancestor_inverse)
-    first_a = send(low_a, x_step(1)), send(high_a, x_step(-1))
-    first_b = send(low_b, y_step(1)), send(high_b, y_step(-1))
-    near = ring_near(order, rows_two, ancestor_inverse)
+    def ring(order, part, step):
+        order = order.reshape(SIDE, -1)
+        low, high = by_supernode(order[2], rows_two, ancestor_inverse, part, True)
+        arriving = send(low[0], step(1)), send(high[0], step(-1))
+        rest = jnp.concatenate([order[1], order[3], order[0]])
+        return arriving, by_supernode(rest, rows_two, ancestor_inverse, part, False)[0]
+
+    first_a, near_a = ring(x_major, 0, x_step)
+    first_b, near_b = ring(y_major, 1, y_step)
     first_a, first_b, parent_panels = lax.optimization_barrier((first_a, first_b, parent_panels))
-    second_a = second_sends(first_a, near[:3], x_step)
-    second_b = second_sends(first_b, near[3:], y_step)
+    second_a = second_sends(first_a, near_a, x_step)
+    second_b = second_sends(first_b, near_b, y_step)
     going = outgoing(place, readers, cut_pattern, first_sum)
     back = lax.all_to_all(going, "col", 0, 0, tiled=True)
     second_a, second_b, _ = lax.optimization_barrier((second_a, second_b, going))
-    second_sum = third_sends(second_a, near[:3], y_step) + third_sends(second_b, near[3:], x_step)
+    second_sum = third_sends(second_a, near_a, y_step) + third_sends(second_b, near_b, x_step)
     level_one_rows, level_two_rows, sums = finish_rows(
         level_two_pattern, back, parent_panels, masked_one, masked_two, parent_lead, second_sum
     )

time: 292 us -> 288 us (0.986)
  local copies, waits for them, and re-layouts: 28.7 us -> 9.2 us
  Pallas kernels: 40.7 us -> 58.6 us
  waiting for transfers between devices: 97.4 us -> 91.1 us
  starting transfers between devices: 103 us -> 106 us
    unnamed x74 -> x36, local copies, waits for them, and re-layouts: 26 us -> 6.34 us
    pallas_call x6 -> x8, Pallas kernels: 20.5 us -> 37.2 us  [the longest x4 24 us: by_supernode(): pl.pallas_call(kernel, out_shape=[jax.ShapeDtypeStruct((groups, SIDE, siz...]
    ppermute x3, waiting for transfers between devices: 7.8 us -> 3.66 us  [row_parts(): lax.ppermute(values, 'row', z_step(-d))]
  transfers between devices with their start and end apart: 35 -> 35, of which waited for: 16 -> 19; matrix products, arithmetic and copies ran while one was open for 2% -> 2% of each run, Pallas kernels for 8% -> 14%
where the time goes in v4:
time: 288 us; the launch traced here: 287 us
  starting transfers between devices  106 us (37%)
  waiting for transfers between devices  91.1 us (32%)
  Pallas kernels  58.6 us (20%)
  between operations  16.6 us (6%)
  local copies, waits for them, and re-layouts  9.2 us (3%)
  other arithmetic  5.6 us (2%)
    reduce_scatter x1, waiting for transfers between devices, per_device(): lax.psum_scatter(product_one.reshape(count * count * block, block), 'col'...  24.6 us
    pallas_call x4, Pallas kernels, by_supernode(): pl.pallas_call(kernel, out_shape=[jax.ShapeDtypeStruct((groups, SIDE, siz...  24 us
    all_to_all x1, starting transfers between devices, per_device(): lax.all_to_all(jnp.concatenate([cut, facts], 1), 'col', 0, 0, tiled=True)  22.6 us
    ppermute x14, starting transfers between devices, send(): return lax.ppermute(value, 'col', step)  21.4 us
    ppermute x14, waiting for transfers between devices, send(): return lax.ppermute(value, 'col', step)  18.9 us
    ppermute x4, waiting for transfers between devices, turned_panels(): return lax.ppermute(part, ('row', 'col'), turn(k))  18.3 us
    ppermute x1, starting transfers between devices, all_panels(): above = lax.ppermute(own, 'row', z_step(-1))  15.4 us
    pallas_call x1, Pallas kernels, by_column(): pl.pallas_call(kernel, out_shape=jax.ShapeDtypeStruct((width // block, st...  14.7 us
  transfers between devices with their start and end apart: 35, of which 19 were waited for; matrix products, arithmetic and copies ran while one was open for 2% of the time, Pallas kernels for 14%

profile of v4, /device:TPU:1, one launch (start us, length us, event | category | flops | bytes accessed | tf_op | source)
XLA Modules:
  0.0 286.7 jit_solution(10415405263038047466)
XLA Ops:
  10.0 6.0 %collective-permute-start = (bf16[128,1024]{1,0:T(8,128)(2,1)S(1)}, bf16[128,1024]{1,0:T(8,128)(2,1)S(1)}, u32[]{:S(2)}, u32[]{:S(2)}) collective-permute-start(bf16[128,1024]{1,0:T(8,128)(2,1)S(1)} %get-tuple-element.103), channel_id=1, source_target_pairs={{0,0},{1,1},{2,16},{3,17},{4,32},{5,33},{6,48},{7,49},{8,64},{9,65... | collective-permute-start | bytes 786440 | tf_op jit(solution)/shard_map/ppermute | solution.py:47
  16.7 5.2 %collective-permute-done = bf16[128,1024]{1,0:T(8,128)(2,1)S(1)} collective-permute-done((bf16[128,1024]{1,0:T(8,128)(2,1)S(1)}, bf16[128,1024]{1,0:T(8,128)(2,1)S(1)}, u32[]{:S(2)}, u32[]{:S(2)}) %collective-permute-start) | collective-permute-done | bytes 262176 | tf_op jit(solution)/shard_map/ppermute | solution.py:47
  24.6 15.4 %collective-permute-start.3 = (bf16[2,128,1024]{2,1,0:T(8,128)(2,1)S(1)}, bf16[2,128,1024]{2,1,0:T(8,128)(2,1)S(1)}, u32[]{:S(2)}, u32[]{:S(2)}) collective-permute-start(bf16[2,128,1024]{2,1,0:T(8,128)(2,1)S(1)} %pad_maximum_fusion.refs_0_), channel_id=1, source_target_pairs={{0,96},{16,112},{32,0},{48,16},{64,32},{80,48},{96,64},{112,80},{1... | collective-permute-start | bytes 1572872 | tf_op jit(solution)/shard_map/ppermute | solution.py:59
  40.0 8.9 %collective-permute-done.3.refs_4_ = bf16[2,128,1024]{2,1,0:T(8,128)(2,1)S(1)} collective-permute-done((bf16[2,128,1024]{2,1,0:T(8,128)(2,1)S(1)}, bf16[2,128,1024]{2,1,0:T(8,128)(2,1)S(1)}, u32[]{:S(2)}, u32[]{:S(2)}) %collective-permute-start.3) | collective-permute-done | bytes 524320 | tf_op jit(solution)/shard_map/ppermute | solution.py:59
  48.9 3.5 %collective-permute-start.9 = (bf16[128,1024]{1,0:T(8,128)(2,1)S(1)}, bf16[128,1024]{1,0:T(8,128)(2,1)S(1)}, u32[]{:S(2)}, u32[]{:S(2)}) collective-permute-start(bf16[128,1024]{1,0:T(8,128)(2,1)S(1)} %slice_bitcast_fusion), channel_id=1, source_target_pairs={{0,96},{16,112},{32,0},{48,16},{64,32},{80,48},{96,64},{112,80},{1... | collective-permute-start | bytes 786440 | tf_op jit(solution)/shard_map/ppermute | solution.py:61
  52.5 6.9 %collective-permute-start.5 = (bf16[2,128,1024]{2,1,0:T(8,128)(2,1)S(1)}, bf16[2,128,1024]{2,1,0:T(8,128)(2,1)S(1)}, u32[]{:S(2)}, u32[]{:S(2)}) collective-permute-start(bf16[2,128,1024]{2,1,0:T(8,128)(2,1)S(1)} %pad_maximum_fusion.refs_0_), channel_id=1, source_target_pairs={{0,16},{16,0},{32,48},{48,32},{64,80},{80,64},{96,112},{112,96},{1... | collective-permute-start | bytes 1572872 | tf_op jit(solution)/shard_map/ppermute | solution.py:65
  60.0 7.0 %collective-permute-start.10 = (bf16[2,128,1024]{2,1,0:T(8,128)(2,1)S(1)}, bf16[2,128,1024]{2,1,0:T(8,128)(2,1)S(1)}, u32[]{:S(2)}, u32[]{:S(2)}) collective-permute-start(bf16[2,128,1024]{2,1,0:T(8,128)(2,1)S(1)} %pad_maximum_fusion.1.refs_6_), channel_id=1, source_target_pairs={{0,16},{16,0},{32,48},{48,32},{64,80},{80,64},{96,112},{112,96},{1... | collective-permute-start | bytes 1572872 | tf_op jit(solution)/shard_map/ppermute | solution.py:65
  67.1 4.1 %collective-permute-start.4 = (bf16[128,1024]{1,0:T(8,128)(2,1)S(1)}, bf16[128,1024]{1,0:T(8,128)(2,1)S(1)}, u32[]{:S(2)}, u32[]{:S(2)}) collective-permute-start(bf16[128,1024]{1,0:T(8,128)(2,1)S(1)} %constant_dynamic-slice_fusion.1), channel_id=1, source_target_pairs={{0,0},{1,1},{2,16},{3,17},{4,32},{5,33},{6,48},{7,49},{8,64},{9,65... | collective-permute-start | bytes 786440 | tf_op jit(solution)/shard_map/ppermute | solution.py:47
  71.2 5.1 %collective-permute-done.4 = bf16[128,1024]{1,0:T(8,128)(2,1)S(1)} collective-permute-done((bf16[128,1024]{1,0:T(8,128)(2,1)S(1)}, bf16[128,1024]{1,0:T(8,128)(2,1)S(1)}, u32[]{:S(2)}, u32[]{:S(2)}) %collective-permute-start.4) | collective-permute-done | bytes 262176 | tf_op jit(solution)/shard_map/ppermute | solution.py:47
  78.1 14.7 %shard_map.137 = bf16[16,2048,128]{2,1,0:T(8,128)(2,1)} custom-call(bf16[2,128,1024]{2,1,0:T(8,128)(2,1)S(1)} %pad_maximum_fusion.refs_0_, bf16[2,128,1024]{2,1,0:T(8,128)(2,1)S(1)} %collective-permute-done.5.refs_1_, bf16[2,128,1024]{2,1,0:T(8,128)(2,1)S(1)} %collective-permute-done.2.refs_2_, bf16[2,128,1024]{2,1,0:T(8,128)(2,1)} %copy-done.16, ...), custom_call_target="tpu_custom_call" | custom-call | flops 8589934592 | bytes 16777216 | tf_op jit(solution)/shard_map/pallas_call | solution.py:94
  94.5 5.4 %collective-permute-done.11 = bf16[128,1024]{1,0:T(8,128)(2,1)S(1)} collective-permute-done((bf16[128,1024]{1,0:T(8,128)(2,1)S(1)}, bf16[128,1024]{1,0:T(8,128)(2,1)S(1)}, u32[]{:S(2)}, u32[]{:S(2)}) %collective-permute-start.11) | collective-permute-done | bytes 262176 | tf_op jit(solution)/shard_map/ppermute | solution.py:47
  104.1 22.6 %all-to-all-start = ((bf16[16,144,128]{2,1,0:T(8,128)(2,1)}), bf16[16,144,128]{2,1,0:T(8,128)(2,1)S(1)}, u32[]{:S(2)}, u32[]{:S(2)}) async-start(bf16[16,144,128]{2,1,0:T(8,128)(2,1)} %fusion.1), calls=%async_computation | async-start | bytes 1179648 | tf_op jit(solution)/shard_map/all_to_all | solution.py:374
  126.9 14.1 %all-to-all-done = bf16[16,144,128]{2,1,0:T(8,128)(2,1)S(1)} async-done(((bf16[16,144,128]{2,1,0:T(8,128)(2,1)}), bf16[16,144,128]{2,1,0:T(8,128)(2,1)S(1)}, u32[]{:S(2)}, u32[]{:S(2)}) %all-to-all-start) | async-done | bytes 589856 | tf_op jit(solution)/shard_map/all_to_all | solution.py:374
  143.3 4.3 %all-to-all-start.2 = ((bf16[16,128,128]{2,1,0:T(8,128)(2,1)}), bf16[16,128,128]{2,1,0:T(8,128)(2,1)}, u32[]{:S(2)}, u32[]{:S(2)}) async-start(bf16[16,128,128]{2,1,0:T(8,128)(2,1)} %broadcast_select_fusion), calls=%async_computation.3 | async-start | bytes 1048576 | tf_op jit(solution)/shard_map/all_to_all | solution.py:377
  148.6 3.7 %shard_map.140 = (bf16[1,4,64,1024]{3,2,1,0:T(8,128)(2,1)S(1)}, bf16[1,4,64,1024]{3,2,1,0:T(8,128)(2,1)S(1)}) custom-call(s32[4]{0:T(128)S(1)} %get-tuple-element.108.order_ref, bf16[16,128,1024]{2,1,0:T(8,128)(2,1)} %all-gather.2.cloned.1.call-done.a_ref.b_ref.c_ref.d_ref, bf16[16,128,1024]{2,1,0:T(8,128)(2,1)} %all-gather.2.cloned.1.call-done.a_ref.b_ref.c_ref.d_ref, ...), custom_call_target="tpu_custom_call" | custom-call | flops 1073741824 | bytes 2097152 | tf_op jit(solution)/shard_map/pallas_call | solution.py:128
  154.8 4.7 %shard_map.139 = (bf16[1,4,64,1024]{3,2,1,0:T(8,128)(2,1)}, bf16[1,4,64,1024]{3,2,1,0:T(8,128)(2,1)}) custom-call(s32[4]{0:T(128)S(1)} %get-tuple-element.112.order_ref, bf16[16,128,1024]{2,1,0:T(8,128)(2,1)} %all-gather.2.cloned.1.call-done.a_ref.b_ref.c_ref.d_ref, bf16[16,128,1024]{2,1,0:T(8,128)(2,1)} %all-gather.2.cloned.1.call-done.a_ref.b_ref.c_ref.d_ref, ...), custom_call_target="tpu_custom_call" | custom-call | flops 1073741824 | bytes 2097152 | tf_op jit(solution)/shard_map/pallas_call | solution.py:128
  162.0 7.9 %shard_map.143.ahead_ref.behind_ref.own_ref = bf16[3,4,128,1024]{3,2,1,0:T(8,128)(2,1)} custom-call(s32[12]{0:T(128)S(1)} %pad_add_fusion.1.order_ref, bf16[16,128,1024]{2,1,0:T(8,128)(2,1)} %all-gather.2.cloned.1.call-done.a_ref.b_ref.c_ref.d_ref, bf16[16,128,1024]{2,1,0:T(8,128)(2,1)} %all-gather.2.cloned.1.call-done.a_ref.b_ref.c_ref.d_ref, ...), custom_call_target="tpu_custom_call" | custom-call | flops 3221225472 | bytes 6291456 | tf_op jit(solution)/shard_map/pallas_call | solution.py:128
  169.8 7.7 %shard_map.141.ahead_ref.behind_ref.own_ref = bf16[3,4,128,1024]{3,2,1,0:T(8,128)(2,1)} custom-call(s32[12]{0:T(128)S(1)} %pad_add_fusion.order_ref, bf16[16,128,1024]{2,1,0:T(8,128)(2,1)} %all-gather.2.cloned.1.call-done.a_ref.b_ref.c_ref.d_ref, bf16[16,128,1024]{2,1,0:T(8,128)(2,1)} %all-gather.2.cloned.1.call-done.a_ref.b_ref.c_ref.d_ref, ...), custom_call_target="tpu_custom_call" | custom-call | flops 3221225472 | bytes 6291456 | tf_op jit(solution)/shard_map/pallas_call | solution.py:128
  183.7 3.2 %collective-permute-done.12.low_ref = bf16[4,64,1024]{2,1,0:T(8,128)(2,1)S(1)} collective-permute-done((bf16[4,64,1024]{2,1,0:T(8,128)(2,1)}, bf16[4,64,1024]{2,1,0:T(8,128)(2,1)S(1)}, u32[]{:S(2)}, u32[]{:S(2)}) %collective-permute-start.12) | collective-permute-done | bytes 524320 | tf_op jit(solution)/shard_map/ppermute | solution.py:149
  186.9 3.8 %shard_map.144 = (bf16[4,128,1024]{2,1,0:T(8,128)(2,1)}, bf16[4,128,1024]{2,1,0:T(8,128)(2,1)}) custom-call(bf16[4,64,1024]{2,1,0:T(8,128)(2,1)S(1)} %collective-permute-done.14.low_ref, bf16[4,64,1024]{2,1,0:T(8,128)(2,1)S(1)} %collective-permute-done.15.high_ref, bf16[3,4,128,1024]{3,2,1,0:T(8,128)(2,1)} %shard_map.143.ahead_ref.behind_ref.own_ref, ...), custom_call_target="tpu_custom_call" | custom-call | bytes 4194304 | tf_op jit(solution)/shard_map/pallas_call | solution.py:168
  190.7 2.7 collective-permute-start.19
  193.3 3.8 %shard_map.142 = (bf16[4,128,1024]{2,1,0:T(8,128)(2,1)}, bf16[4,128,1024]{2,1,0:T(8,128)(2,1)}) custom-call(bf16[4,64,1024]{2,1,0:T(8,128)(2,1)S(1)} %collective-permute-done.12.low_ref, bf16[4,64,1024]{2,1,0:T(8,128)(2,1)S(1)} %collective-permute-done.13.high_ref, bf16[3,4,128,1024]{3,2,1,0:T(8,128)(2,1)} %shard_map.141.ahead_ref.behind_ref.own_ref, ...), custom_call_target="tpu_custom_call" | custom-call | bytes 4194304 | tf_op jit(solution)/shard_map/pallas_call | solution.py:168
  197.1 2.7 collective-permute-start.17
  199.8 24.6 %reduce-scatter.2.cloned.1.call-done = bf16[2048,128]{1,0:T(8,128)(2,1)} async-done(((bf16[32768,128]{1,0:T(8,128)(2,1)}), bf16[2048,128]{1,0:T(8,128)(2,1)}) %reduce-scatter.2.cloned.1.call-update) | async-done | bytes 524304 | tf_op jit(solution)/shard_map/reduce_scatter | solution.py:362
  227.3 5.2 %all-to-all-start.1 = ((bf16[16,2,128,128]{3,2,1,0:T(8,128)(2,1)}), bf16[16,2,128,128]{3,2,1,0:T(8,128)(2,1)S(1)}, u32[]{:S(2)}, u32[]{:S(2)}) async-start(bf16[16,2,128,128]{3,2,1,0:T(8,128)(2,1)} %shard_map.138), calls=%async_computation.2 | async-start | bytes 2097152 | tf_op jit(solution)/shard_map/all_to_all | solution.py:401
  233.5 2.8 shard_map.145
  242.0 2.8 shard_map.146
  249.3 4.3 %collective-permute-done.20.refs_1_ = bf16[128,1024]{1,0:T(8,128)(2,1)S(1)} collective-permute-done((bf16[128,1024]{1,0:T(8,128)(2,1)S(1)}, bf16[128,1024]{1,0:T(8,128)(2,1)S(1)}, u32[]{:S(2)}, u32[]{:S(2)}) %collective-permute-start.20) | collective-permute-done | bytes 262176 | tf_op jit(solution)/shard_map/ppermute | solution.py:149
  256.1 3.0 %collective-permute-done.21.refs_2_ = bf16[128,1024]{1,0:T(8,128)(2,1)S(1)} collective-permute-done((bf16[128,1024]{1,0:T(8,128)(2,1)S(1)}, bf16[128,1024]{1,0:T(8,128)(2,1)S(1)}, u32[]{:S(2)}, u32[]{:S(2)}) %collective-permute-start.21) | collective-permute-done | bytes 262176 | tf_op jit(solution)/shard_map/ppermute | solution.py:149
  262.3 3.6 %shard_map.147 = (bf16[128,2048]{1,0:T(8,128)(2,1)}, bf16[128,2048]{1,0:T(8,128)(2,1)}, f32[4,128,128]{2,1,0:T(8,128)S(1)}) custom-call(s32[1,16]{1,0:T(1,128)S(1)} %copy-done.5, bf16[16,2,128,128]{3,2,1,0:T(8,128)(2,1)} %copy-done.10, bf16[16,128,128]{2,1,0:T(8,128)(2,1)} %all-to-all-done.2.panels_ref, bf16[128,2048]{1,0:T(8,128)(2,1)} %copy-done.8, ...), custom_call_target="tpu_custom_call" | custom-call | bytes 1048576 | tf_op jit(solution)/shard_map/pallas_call | solution.py:219
  268.5 3.4 %collective-permute-start.28 = (bf16[4,128,128]{2,1,0:T(8,128)(2,1)S(1)}, bf16[4,128,128]{2,1,0:T(8,128)(2,1)S(1)}, u32[]{:S(2)}, u32[]{:S(2)}) collective-permute-start(bf16[4,128,128]{2,1,0:T(8,128)(2,1)S(1)} %add_convert_fusion.a), channel_id=1, source_target_pairs={{0,64},{16,80},{32,96},{48,112},{64,0},{80,16},{96,32},{112,48},{1... | collective-permute-start | bytes 393224 | tf_op jit(solution)/shard_map/ppermute | solution.py:211
  274.4 3.6 %collective-permute-done.28.c = bf16[4,128,128]{2,1,0:T(8,128)(2,1)S(1)} collective-permute-done((bf16[4,128,128]{2,1,0:T(8,128)(2,1)S(1)}, bf16[4,128,128]{2,1,0:T(8,128)(2,1)S(1)}, u32[]{:S(2)}, u32[]{:S(2)}) %collective-permute-start.28) | collective-permute-done | bytes 131104 | tf_op jit(solution)/shard_map/ppermute | solution.py:211
  (125 shorter events, 53.5 us)
Async XLA Ops:
  8.0 140.5 %all-gather.2.cloned.1.call-start = ((), (), s32[]{:S(2)}) async-start(), calls=%async_computation.5 | async-start | bytes 4718592 | tf_op jit(solution)/shard_map/all_gather | solution.py:380
  10.0 11.9 %collective-permute-start = (bf16[128,1024]{1,0:T(8,128)(2,1)S(1)}, bf16[128,1024]{1,0:T(8,128)(2,1)S(1)}, u32[]{:S(2)}, u32[]{:S(2)}) collective-permute-start(bf16[128,1024]{1,0:T(8,128)(2,1)S(1)} %get-tuple-element.103), channel_id=1, source_target_pairs={{0,0},{1,1},{2,16},{3,17},{4,32},{5,33},{6,48},{7,49},{8,64},{9,65... | collective-permute-start | bytes 786440 | tf_op jit(solution)/shard_map/ppermute | solution.py:47
  16.1 8.4 %collective-permute-start.1 = (bf16[128,1024]{1,0:T(8,128)(2,1)S(1)}, bf16[128,1024]{1,0:T(8,128)(2,1)S(1)}, u32[]{:S(2)}, u32[]{:S(2)}) collective-permute-start(bf16[128,1024]{1,0:T(8,128)(2,1)S(1)} %get-tuple-element.104), channel_id=1, source_target_pairs={{0,1},{1,0},{2,17},{3,16},{4,33},{5,32},{6,49},{7,48},{8,65},{9,64... | collective-permute-start | bytes 786440 | tf_op jit(solution)/shard_map/ppermute | solution.py:47
  24.6 24.3 %collective-permute-start.3 = (bf16[2,128,1024]{2,1,0:T(8,128)(2,1)S(1)}, bf16[2,128,1024]{2,1,0:T(8,128)(2,1)S(1)}, u32[]{:S(2)}, u32[]{:S(2)}) collective-permute-start(bf16[2,128,1024]{2,1,0:T(8,128)(2,1)S(1)} %pad_maximum_fusion.refs_0_), channel_id=1, source_target_pairs={{0,96},{16,112},{32,0},{48,16},{64,32},{80,48},{96,64},{112,80},{1... | collective-permute-start | bytes 1572872 | tf_op jit(solution)/shard_map/ppermute | solution.py:59
  40.0 12.4 %collective-permute-start.2 = (bf16[2,128,1024]{2,1,0:T(8,128)(2,1)S(1)}, bf16[2,128,1024]{2,1,0:T(8,128)(2,1)S(1)}, u32[]{:S(2)}, u32[]{:S(2)}) collective-permute-start(bf16[2,128,1024]{2,1,0:T(8,128)(2,1)S(1)} %pad_maximum_fusion.refs_0_), channel_id=1, source_target_pairs={{0,32},{16,48},{32,64},{48,80},{64,96},{80,112},{96,0},{112,16},{1... | collective-permute-start | bytes 1572872 | tf_op jit(solution)/shard_map/ppermute | solution.py:58
  48.9 11.1 %collective-permute-start.9 = (bf16[128,1024]{1,0:T(8,128)(2,1)S(1)}, bf16[128,1024]{1,0:T(8,128)(2,1)S(1)}, u32[]{:S(2)}, u32[]{:S(2)}) collective-permute-start(bf16[128,1024]{1,0:T(8,128)(2,1)S(1)} %slice_bitcast_fusion), channel_id=1, source_target_pairs={{0,96},{16,112},{32,0},{48,16},{64,32},{80,48},{96,64},{112,80},{1... | collective-permute-start | bytes 786440 | tf_op jit(solution)/shard_map/ppermute | solution.py:61
  52.4 7.6 %collective-permute-start.8 = (bf16[128,1024]{1,0:T(8,128)(2,1)S(1)}, bf16[128,1024]{1,0:T(8,128)(2,1)S(1)}, u32[]{:S(2)}, u32[]{:S(2)}) collective-permute-start(bf16[128,1024]{1,0:T(8,128)(2,1)S(1)} %slice_bitcast_fusion.1), channel_id=1, source_target_pairs={{0,32},{16,48},{32,64},{48,80},{64,96},{80,112},{96,0},{112,16},{1... | collective-permute-start | bytes 786440 | tf_op jit(solution)/shard_map/ppermute | solution.py:61
  52.5 18.6 %collective-permute-start.5 = (bf16[2,128,1024]{2,1,0:T(8,128)(2,1)S(1)}, bf16[2,128,1024]{2,1,0:T(8,128)(2,1)S(1)}, u32[]{:S(2)}, u32[]{:S(2)}) collective-permute-start(bf16[2,128,1024]{2,1,0:T(8,128)(2,1)S(1)} %pad_maximum_fusion.refs_0_), channel_id=1, source_target_pairs={{0,16},{16,0},{32,48},{48,32},{64,80},{80,64},{96,112},{112,96},{1... | collective-permute-start | bytes 1572872 | tf_op jit(solution)/shard_map/ppermute | solution.py:65
  59.4 16.9 %collective-permute-start.7 = (bf16[2,128,1024]{2,1,0:T(8,128)(2,1)S(1)}, bf16[2,128,1024]{2,1,0:T(8,128)(2,1)S(1)}, u32[]{:S(2)}, u32[]{:S(2)}) collective-permute-start(bf16[2,128,1024]{2,1,0:T(8,128)(2,1)S(1)} %collective-permute-done.3.refs_4_), channel_id=1, source_target_pairs={{0,16},{16,0},{32,48},{48,32},{64,80},{80,64},{96,112},{112,96},{1... | collective-permute-start | bytes 1572872 | tf_op jit(solution)/shard_map/ppermute | solution.py:65
  59.5 16.8 %collective-permute-start.6 = (bf16[2,128,1024]{2,1,0:T(8,128)(2,1)S(1)}, bf16[2,128,1024]{2,1,0:T(8,128)(2,1)S(1)}, u32[]{:S(2)}, u32[]{:S(2)}) collective-permute-start(bf16[2,128,1024]{2,1,0:T(8,128)(2,1)S(1)} %collective-permute-done.2.refs_2_), channel_id=1, source_target_pairs={{0,16},{16,0},{32,48},{48,32},{64,80},{80,64},{96,112},{112,96},{1... | collective-permute-start | bytes 1572872 | tf_op jit(solution)/shard_map/ppermute | solution.py:65
  60.0 16.3 %collective-permute-start.10 = (bf16[2,128,1024]{2,1,0:T(8,128)(2,1)S(1)}, bf16[2,128,1024]{2,1,0:T(8,128)(2,1)S(1)}, u32[]{:S(2)}, u32[]{:S(2)}) collective-permute-start(bf16[2,128,1024]{2,1,0:T(8,128)(2,1)S(1)} %pad_maximum_fusion.1.refs_6_), channel_id=1, source_target_pairs={{0,16},{16,0},{32,48},{48,32},{64,80},{80,64},{96,112},{112,96},{1... | collective-permute-start | bytes 1572872 | tf_op jit(solution)/shard_map/ppermute | solution.py:65
  67.1 9.2 %collective-permute-start.4 = (bf16[128,1024]{1,0:T(8,128)(2,1)S(1)}, bf16[128,1024]{1,0:T(8,128)(2,1)S(1)}, u32[]{:S(2)}, u32[]{:S(2)}) collective-permute-start(bf16[128,1024]{1,0:T(8,128)(2,1)S(1)} %constant_dynamic-slice_fusion.1), channel_id=1, source_target_pairs={{0,0},{1,1},{2,16},{3,17},{4,32},{5,33},{6,48},{7,49},{8,64},{9,65... | collective-permute-start | bytes 786440 | tf_op jit(solution)/shard_map/ppermute | solution.py:47
  92.8 7.1 %collective-permute-start.11 = (bf16[128,1024]{1,0:T(8,128)(2,1)S(1)}, bf16[128,1024]{1,0:T(8,128)(2,1)S(1)}, u32[]{:S(2)}, u32[]{:S(2)}) collective-permute-start(bf16[128,1024]{1,0:T(8,128)(2,1)S(1)} %constant_dynamic-slice_fusion), channel_id=1, source_target_pairs={{0,1},{1,0},{2,17},{3,16},{4,33},{5,32},{6,49},{7,48},{8,65},{9,64... | collective-permute-start | bytes 786440 | tf_op jit(solution)/shard_map/ppermute | solution.py:47
  100.8 123.6 %reduce-scatter.2.cloned.1.call-start = ((), (), s32[]{:S(2)}) async-start(), calls=%async_computation.4 | async-start | bytes 8912896 | tf_op jit(solution)/shard_map/reduce_scatter | solution.py:362
  104.1 36.9 %all-to-all-start = ((bf16[16,144,128]{2,1,0:T(8,128)(2,1)}), bf16[16,144,128]{2,1,0:T(8,128)(2,1)S(1)}, u32[]{:S(2)}, u32[]{:S(2)}) async-start(bf16[16,144,128]{2,1,0:T(8,128)(2,1)} %fusion.1), calls=%async_computation | async-start | bytes 1179648 | tf_op jit(solution)/shard_map/all_to_all | solution.py:374
  143.3 34.2 %all-to-all-start.2 = ((bf16[16,128,128]{2,1,0:T(8,128)(2,1)}), bf16[16,128,128]{2,1,0:T(8,128)(2,1)}, u32[]{:S(2)}, u32[]{:S(2)}) async-start(bf16[16,128,128]{2,1,0:T(8,128)(2,1)} %broadcast_select_fusion), calls=%async_computation.3 | async-start | bytes 1048576 | tf_op jit(solution)/shard_map/all_to_all | solution.py:377
  152.3 26.6 %collective-permute-start.15 = (bf16[4,64,1024]{2,1,0:T(8,128)(2,1)S(1)}, bf16[4,64,1024]{2,1,0:T(8,128)(2,1)S(1)}, u32[]{:S(2)}, u32[]{:S(2)}) collective-permute-start(bf16[4,64,1024]{2,1,0:T(8,128)(2,1)S(1)} %bitcast.54), channel_id=1, source_target_pairs={{0,12},{1,13},{2,14},{3,15},{4,0},{5,1},{6,2},{7,3},{8,4},{9,5},{1... | collective-permute-start | bytes 1572872 | tf_op jit(solution)/shard_map/ppermute | solution.py:149
  154.8 26.7 %collective-permute-start.14 = (bf16[4,64,1024]{2,1,0:T(8,128)(2,1)S(1)}, bf16[4,64,1024]{2,1,0:T(8,128)(2,1)S(1)}, u32[]{:S(2)}, u32[]{:S(2)}) collective-permute-start(bf16[4,64,1024]{2,1,0:T(8,128)(2,1)S(1)} %bitcast.53), channel_id=1, source_target_pairs={{0,4},{1,5},{2,6},{3,7},{4,8},{5,9},{6,10},{7,11},{8,12},{9,13},{1... | collective-permute-start | bytes 1572872 | tf_op jit(solution)/shard_map/ppermute | solution.py:149
  159.5 24.2 %collective-permute-start.13 = (bf16[4,64,1024]{2,1,0:T(8,128)(2,1)}, bf16[4,64,1024]{2,1,0:T(8,128)(2,1)S(1)}, u32[]{:S(2)}, u32[]{:S(2)}) collective-permute-start(bf16[4,64,1024]{2,1,0:T(8,128)(2,1)} %bitcast.18), channel_id=1, source_target_pairs={{0,3},{1,0},{2,1},{3,2},{4,7},{5,4},{6,5},{7,6},{8,11},{9,8},{10,9... | collective-permute-start | bytes 1572872 | tf_op jit(solution)/shard_map/ppermute | solution.py:149
  162.0 24.9 %collective-permute-start.12 = (bf16[4,64,1024]{2,1,0:T(8,128)(2,1)}, bf16[4,64,1024]{2,1,0:T(8,128)(2,1)S(1)}, u32[]{:S(2)}, u32[]{:S(2)}) collective-permute-start(bf16[4,64,1024]{2,1,0:T(8,128)(2,1)} %bitcast.17), channel_id=1, source_target_pairs={{0,1},{1,2},{2,3},{3,0},{4,5},{5,6},{6,7},{7,4},{8,9},{9,10},{10,1... | collective-permute-start | bytes 1572872 | tf_op jit(solution)/shard_map/ppermute | solution.py:149
  190.6 41.8 %collective-permute-start.18 = (bf16[4,128,1024]{2,1,0:T(8,128)(2,1)}, bf16[4,128,1024]{2,1,0:T(8,128)(2,1)}, u32[]{:S(2)}, u32[]{:S(2)}) collective-permute-start(bf16[4,128,1024]{2,1,0:T(8,128)(2,1)} %get-tuple-element.75), channel_id=1, source_target_pairs={{0,4},{1,5},{2,6},{3,7},{4,8},{5,9},{6,10},{7,11},{8,12},{9,13},{1... | collective-permute-start | bytes 3145736 | tf_op jit(solution)/shard_map/ppermute | solution.py:149
  190.7 41.8 %collective-permute-start.19 = (bf16[4,128,1024]{2,1,0:T(8,128)(2,1)}, bf16[4,128,1024]{2,1,0:T(8,128)(2,1)}, u32[]{:S(2)}, u32[]{:S(2)}) collective-permute-start(bf16[4,128,1024]{2,1,0:T(8,128)(2,1)} %get-tuple-element.76), channel_id=1, source_target_pairs={{0,12},{1,13},{2,14},{3,15},{4,0},{5,1},{6,2},{7,3},{8,4},{9,5},{1... | collective-permute-start | bytes 3145736 | tf_op jit(solution)/shard_map/ppermute | solution.py:149
  197.1 35.3 %collective-permute-start.16 = (bf16[4,128,1024]{2,1,0:T(8,128)(2,1)}, bf16[4,128,1024]{2,1,0:T(8,128)(2,1)S(1)}, u32[]{:S(2)}, u32[]{:S(2)}) collective-permute-start(bf16[4,128,1024]{2,1,0:T(8,128)(2,1)} %get-tuple-element.71), channel_id=1, source_target_pairs={{0,1},{1,2},{2,3},{3,0},{4,5},{5,6},{6,7},{7,4},{8,9},{9,10},{10,1... | collective-permute-start | bytes 3145736 | tf_op jit(solution)/shard_map/ppermute | solution.py:149
  197.1 35.4 %collective-permute-start.17 = (bf16[4,128,1024]{2,1,0:T(8,128)(2,1)}, bf16[4,128,1024]{2,1,0:T(8,128)(2,1)}, u32[]{:S(2)}, u32[]{:S(2)}) collective-permute-start(bf16[4,128,1024]{2,1,0:T(8,128)(2,1)} %get-tuple-element.72), channel_id=1, source_target_pairs={{0,3},{1,0},{2,1},{3,2},{4,7},{5,4},{6,5},{7,6},{8,11},{9,8},{10,9... | collective-permute-start | bytes 3145736 | tf_op jit(solution)/shard_map/ppermute | solution.py:149
  227.3 34.0 %all-to-all-start.1 = ((bf16[16,2,128,128]{3,2,1,0:T(8,128)(2,1)}), bf16[16,2,128,128]{3,2,1,0:T(8,128)(2,1)S(1)}, u32[]{:S(2)}, u32[]{:S(2)}) async-start(bf16[16,2,128,128]{3,2,1,0:T(8,128)(2,1)} %shard_map.138), calls=%async_computation.2 | async-start | bytes 2097152 | tf_op jit(solution)/shard_map/all_to_all | solution.py:401
  237.1 16.5 %collective-permute-start.20 = (bf16[128,1024]{1,0:T(8,128)(2,1)S(1)}, bf16[128,1024]{1,0:T(8,128)(2,1)S(1)}, u32[]{:S(2)}, u32[]{:S(2)}) collective-permute-start(bf16[128,1024]{1,0:T(8,128)(2,1)S(1)} %get-tuple-element.80), channel_id=1, source_target_pairs={{0,4},{1,5},{2,6},{3,7},{4,8},{5,9},{6,10},{7,11},{8,12},{9,13},{1... | collective-permute-start | bytes 786440 | tf_op jit(solution)/shard_map/ppermute | solution.py:149
  238.5 20.7 %collective-permute-start.21 = (bf16[128,1024]{1,0:T(8,128)(2,1)S(1)}, bf16[128,1024]{1,0:T(8,128)(2,1)S(1)}, u32[]{:S(2)}, u32[]{:S(2)}) collective-permute-start(bf16[128,1024]{1,0:T(8,128)(2,1)S(1)} %get-tuple-element.81), channel_id=1, source_target_pairs={{0,8},{1,9},{2,10},{3,11},{4,12},{5,13},{6,14},{7,15},{8,0},{9,1},... | collective-permute-start | bytes 786440 | tf_op jit(solution)/shard_map/ppermute | solution.py:149
  240.9 18.3 %collective-permute-start.22 = (bf16[128,1024]{1,0:T(8,128)(2,1)S(1)}, bf16[128,1024]{1,0:T(8,128)(2,1)S(1)}, u32[]{:S(2)}, u32[]{:S(2)}) collective-permute-start(bf16[128,1024]{1,0:T(8,128)(2,1)S(1)} %get-tuple-element.82), channel_id=1, source_target_pairs={{0,12},{1,13},{2,14},{3,15},{4,0},{5,1},{6,2},{7,3},{8,4},{9,5},{1... | collective-permute-start | bytes 786440 | tf_op jit(solution)/shard_map/ppermute | solution.py:149
  245.7 13.4 %collective-permute-start.23 = (bf16[128,1024]{1,0:T(8,128)(2,1)S(1)}, bf16[128,1024]{1,0:T(8,128)(2,1)S(1)}, u32[]{:S(2)}, u32[]{:S(2)}) collective-permute-start(bf16[128,1024]{1,0:T(8,128)(2,1)S(1)} %get-tuple-element.86), channel_id=1, source_target_pairs={{0,1},{1,2},{2,3},{3,0},{4,5},{5,6},{6,7},{7,4},{8,9},{9,10},{10,1... | collective-permute-start | bytes 786440 | tf_op jit(solution)/shard_map/ppermute | solution.py:149
  246.9 12.5 %collective-permute-start.24 = (bf16[128,1024]{1,0:T(8,128)(2,1)S(1)}, bf16[128,1024]{1,0:T(8,128)(2,1)S(1)}, u32[]{:S(2)}, u32[]{:S(2)}) collective-permute-start(bf16[128,1024]{1,0:T(8,128)(2,1)S(1)} %get-tuple-element.87), channel_id=1, source_target_pairs={{0,2},{1,3},{2,0},{3,1},{4,6},{5,7},{6,4},{7,5},{8,10},{9,11},{10,... | collective-permute-start | bytes 786440 | tf_op jit(solution)/shard_map/ppermute | solution.py:149
  253.6 7.7 %collective-permute-start.25 = (bf16[128,1024]{1,0:T(8,128)(2,1)S(1)}, bf16[128,1024]{1,0:T(8,128)(2,1)S(1)}, u32[]{:S(2)}, u32[]{:S(2)}) collective-permute-start(bf16[128,1024]{1,0:T(8,128)(2,1)S(1)} %get-tuple-element.88), channel_id=1, source_target_pairs={{0,3},{1,0},{2,1},{3,2},{4,7},{5,4},{6,5},{7,6},{8,11},{9,8},{10,9... | collective-permute-start | bytes 786440 | tf_op jit(solution)/shard_map/ppermute | solution.py:149
  268.5 9.5 %collective-permute-start.28 = (bf16[4,128,128]{2,1,0:T(8,128)(2,1)S(1)}, bf16[4,128,128]{2,1,0:T(8,128)(2,1)S(1)}, u32[]{:S(2)}, u32[]{:S(2)}) collective-permute-start(bf16[4,128,128]{2,1,0:T(8,128)(2,1)S(1)} %add_convert_fusion.a), channel_id=1, source_target_pairs={{0,64},{16,80},{32,96},{48,112},{64,0},{80,16},{96,32},{112,48},{1... | collective-permute-start | bytes 393224 | tf_op jit(solution)/shard_map/ppermute | solution.py:211
  (21 other events, 371.0 us)
Sparse Core Ops, SparseCore 0:
  100.9 47.5 all-gather.1
Sparse Core Ops, SparseCore 1:
  104.7 119.7 reduce-scatter.1

commit v5 on v4

--- a/solution.py
+++ b/solution.py
@@ -8,7 +8,6 @@
 SIDE = 4
 CORES = 2
 F32 = jnp.float32
-LONG_CHAIN = 10**11
 RING_VMEM = 52 * 2**20
 
 
@@ -74,38 +73,45 @@
     return slot * 4 + (source + core) % CORES * 2 + supernode % 2
 
 
-def by_column(pieces, matrix, block):
-    rows, depth = pieces[0].shape[0] * pieces[0].shape[1], pieces[0].shape[2]
-    width = matrix.shape[1]
-    steps = len(pieces)
-
-    def kernel(*refs):
-        matrix_ref, out_ref, held = refs[steps:]
-        for i in range(steps):
-
-            @pl.when(pl.program_id(0) == i)
-            def _():
-                held[...] = refs[i][...].reshape(rows, depth)
-
-        total = jnp.dot(held[...], matrix_ref[...], preferred_element_type=F32)
-        for d in range(width // block):
-            out_ref[d] = total[:, d * block : (d + 1) * block].astype(out_ref.dtype)
+def by_column(order, pieces, matrix, split):
+    block, depth = pieces[0].shape[1:]
+    each = 2 * block
+    rows = len(pieces) * each
+    groups = order.shape[0] // SIDE
+    outs = 2 if split else 1
+    size = rows // outs
+
+    def kernel(order_ref, *refs):
+        right = jnp.concatenate([ref[...] for ref in refs[:SIDE]], 1)
+        held, out = refs[SIDE : SIDE + len(pieces)], refs[SIDE + len(pieces) :]
+        for i, piece in enumerate(held):
+            left = piece[...].reshape(each, depth)
+            total = jnp.dot(left, right, preferred_element_type=F32)
+            ref, first = out[i * each // size], i * each % size
+            for j in range(SIDE):
+                ref[0, j, first : first + each] = total[:, j * block : (j + 1) * block].astype(ref.dtype)
+
+    def pick(j):
+        return pl.BlockSpec((depth, block), lambda i, order_ref: (0, order_ref[SIDE * i + j]))
 
     return pl.pallas_call(
         kernel,
-        out_shape=jax.ShapeDtypeStruct((width // block, steps * rows, block), matrix.dtype),
-        grid=(steps,),
-        in_specs=[pl.BlockSpec(v.shape, lambda i: (0, 0, 0)) for v in pieces]
-        + [pl.BlockSpec((depth, width), lambda i: (0, 0))],
-        out_specs=pl.BlockSpec((width // block, rows, block), lambda i: (0, i, 0)),
-        scratch_shapes=[pltpu.VMEM((rows, depth), matrix.dtype)],
-        compiler_params=pltpu.CompilerParams(vmem_limit_bytes=52 * 2**20),
+        out_shape=[jax.ShapeDtypeStruct((groups, SIDE, size, block), matrix.dtype)] * outs,
+        grid_spec=pltpu.PrefetchScalarGridSpec(
+            num_scalar_prefetch=1,
+            grid=(groups,),
+            in_specs=[pick(j) for j in range(SIDE)]
+            + [pl.BlockSpec(v.shape, lambda i, order_ref: (0, 0, 0)) for v in pieces],
+            out_specs=[pl.BlockSpec((1, SIDE, size, block), lambda i, order_ref: (i, 0, 0, 0))]
+            * outs,
+        ),
+        compiler_params=pltpu.CompilerParams(vmem_limit_bytes=RING_VMEM),
         cost_estimate=pl.CostEstimate(
-            flops=2 * steps * rows * depth * width,
-            bytes_accessed=2 * (steps * rows * (depth + width) + depth * width),
+            flops=2 * groups * SIDE * block * depth * rows,
+            bytes_accessed=2 * groups * SIDE * block * (depth + rows),
             transcendentals=0,
         ),
-    )(*pieces, matrix)
+    )(order, *[matrix] * SIDE, *pieces)
 
 
 def by_supernode(order, rows, matrix, part, split):
@@ -180,7 +186,7 @@
 def third_sends(arriving, near, step):
     _, _, block, width = near.shape
     kind = near.dtype
-    tile = width // SIDE
+    tile = block // SIDE
 
     def kernel(one_ref, two_ref, own_ref, own_out, *out):
         for d in range(SIDE):
@@ -190,14 +196,14 @@
             else:
                 own_out[...] = total
 
-    four = pl.BlockSpec((SIDE, block, tile), lambda i: (0, 0, i))
-    one = pl.BlockSpec((block, tile), lambda i: (0, i))
+    four = pl.BlockSpec((SIDE, tile, width), lambda i: (0, i, 0))
+    one = pl.BlockSpec((tile, width), lambda i: (i, 0))
     own, *others = pl.pallas_call(
         kernel,
         out_shape=[jax.ShapeDtypeStruct((block, width), F32)]
         + [jax.ShapeDtypeStruct((block, width), kind)] * 3,
         grid=(SIDE,),
-        in_specs=[four, four, pl.BlockSpec((1, SIDE, block, tile), lambda i: (2, 0, 0, i))],
+        in_specs=[four, four, pl.BlockSpec((1, SIDE, tile, width), lambda i: (2, 0, i, 0))],
         out_specs=[one] * 4,
         compiler_params=pltpu.CompilerParams(vmem_limit_bytes=RING_VMEM),
         cost_estimate=pl.CostEstimate(flops=0, bytes_accessed=2**22, transcendentals=0),
@@ -215,7 +221,7 @@
     return pl.BlockSpec(shape, lambda i: (0,) * len(shape))
 
 
-def small_call(kernel, shapes, scalars, arrays, scratch=(), flops=0):
+def small_call(kernel, shapes, scalars, arrays, scratch=()):
     return pl.pallas_call(
         kernel,
         out_shape=[jax.ShapeDtypeStruct(shape, kind) for shape, kind in shapes],
@@ -225,25 +231,32 @@
         out_specs=[whole(shape) for shape, _ in shapes],
         scratch_shapes=list(scratch),
         compiler_params=pltpu.CompilerParams(vmem_limit_bytes=RING_VMEM),
-        cost_estimate=pl.CostEstimate(flops=flops, bytes_accessed=2**20, transcendentals=0),
+        cost_estimate=pl.CostEstimate(flops=0, bytes_accessed=2**20, transcendentals=0),
     )(*scalars, *arrays)
 
 
-def outgoing(place, readers, pattern, total):
-    count, block = total.shape[:2]
-
-    def kernel(place_ref, readers_ref, pattern_ref, total_ref, out_ref):
+def outgoing(place, readers, pattern, terms):
+    count = place.shape[0]
+    block = terms[0].shape[1]
+    middle = count // 2
+
+    def kernel(place_ref, readers_ref, pattern_ref, *refs):
+        out_ref, total = refs[len(terms) :]
+        half = len(terms) // 2
+        for side in range(2):
+            value = sum(ref[...].astype(F32) for ref in refs[side * half : (side + 1) * half])
+            total[side * middle : (side + 1) * middle] = value.reshape(middle, block, block)
         for d in range(count):
             for j, k in enumerate((d, readers_ref[d])):
-                value = total_ref[place_ref[k]].astype(F32) * pattern_ref[k].astype(F32)
+                value = total[place_ref[k]] * pattern_ref[k].astype(F32)
                 out_ref[d, j] = (-value).astype(out_ref.dtype)
 
     return small_call(
         kernel,
         [((count, 2, block, block), jnp.bfloat16)],
         [place, readers, pattern],
-        [total],
-        flops=LONG_CHAIN,
+        terms,
+        [pltpu.VMEM((count, block, block), F32)],
     )[0]
 
 
@@ -351,18 +364,35 @@
     masked_one = apply_pattern(level_one_panels, level_one_pattern, block)
     masked_two = apply_pattern(level_two_panels, level_two_pattern, block)
 
+    steps = jnp.arange(count, dtype=jnp.int32)
+    place = arrival(steps)
+    outer, inner = steps // SIDE, steps % SIDE
+    x_major = (y + inner) % SIDE * SIDE + (x + outer) % SIDE
+    y_major = (y + outer) % SIDE * SIDE + (x + inner) % SIDE
+
+    def ring(product, order, step):
+        order = order.reshape(SIDE, -1)
+        low, high = product(order[2], True)
+        arriving = send(low[0], step(1)), send(high[0], step(-1))
+        return arriving, product(jnp.concatenate([order[1], order[3], order[0]]), False)[0]
+
     found_one = all_panels(in_order([turned_panels(masked_one, k) for k in range(2)]))
-    later_two, _ = lax.optimization_barrier((masked_two, found_one[2:6:2]))
-    early_two = turned_panels(later_two, 0)
-    early_two, found_one = lax.optimization_barrier((early_two, found_one))
-    product_one = by_column(found_one, ancestor_inverse, block)
-    later_two, product_one = lax.optimization_barrier((masked_two, product_one))
-    own_two = in_order([early_two, turned_panels(later_two, 1)])
-    later_one, own_two = lax.optimization_barrier((masked_one, own_two))
-    first_sum = lax.psum_scatter(
-        product_one.reshape(count * count * block, block), "col", scatter_dimension=0, tiled=True
-    ).reshape(count, block, block)
-
+    later_two, found_one = lax.optimization_barrier((masked_two, found_one))
+    own_two = in_order([turned_panels(later_two, k) for k in range(2)])
+
+    def one_part(pieces):
+        return lambda order, split: by_column(order, pieces, ancestor_inverse, split)
+
+    first_a, near_a = ring(one_part(found_one[:4]), x_major, x_step)
+    first_b, near_b = ring(one_part(found_one[4:]), y_major, y_step)
+    first_a, first_b, own_two = lax.optimization_barrier((first_a, first_b, own_two))
+    second_a = second_sends(first_a, near_a, x_step)
+    second_b = second_sends(first_b, near_b, y_step)
+    rows_two = jnp.concatenate(all_panels(own_two), 0)
+    second_a, second_b, rows_two = lax.optimization_barrier((second_a, second_b, rows_two))
+    first_sum = third_sends(second_a, near_a, y_step) + third_sends(second_b, near_b, x_step)
+
+    later_one, _ = lax.optimization_barrier((masked_one, own_two))
     facts = jnp.concatenate(
         [
             jnp.broadcast_to(level_one_pattern.reshape(count, 1, 1), (count, 8, block)),
@@ -377,29 +407,22 @@
     parent_panels = lax.all_to_all(
         jnp.take(cut[:, :block], readers, axis=0), "col", 0, 0, tiled=True
     )
-    rows_two = lax.all_gather(own_two, "row", axis=0, tiled=True)
-
-    steps = jnp.arange(count, dtype=jnp.int32)
-    place = arrival(steps)
-    outer, inner = steps // SIDE, steps % SIDE
-    x_major = (y + inner) % SIDE * SIDE + (x + outer) % SIDE
-    y_major = (y + outer) % SIDE * SIDE + (x + inner) % SIDE
-
-    def ring(order, part, step):
-        order = order.reshape(SIDE, -1)
-        low, high = by_supernode(order[2], rows_two, ancestor_inverse, part, True)
-        arriving = send(low[0], step(1)), send(high[0], step(-1))
-        rest = jnp.concatenate([order[1], order[3], order[0]])
-        return arriving, by_supernode(rest, rows_two, ancestor_inverse, part, False)[0]
-
-    first_a, near_a = ring(x_major, 0, x_step)
-    first_b, near_b = ring(y_major, 1, y_step)
-    first_a, first_b, parent_panels = lax.optimization_barrier((first_a, first_b, parent_panels))
+    back = lax.all_to_all(
+        outgoing(place, readers, cut_pattern, first_sum), "col", 0, 0, tiled=True
+    )
+
+    def two_part(part):
+        return lambda order, split: by_supernode(
+            place[order], rows_two, ancestor_inverse, part, split
+        )
+
+    first_a, near_a = ring(two_part(0), x_major, x_step)
+    first_b, near_b = ring(two_part(1), y_major, y_step)
     second_a = second_sends(first_a, near_a, x_step)
     second_b = second_sends(first_b, near_b, y_step)
-    going = outgoing(place, readers, cut_pattern, first_sum)
-    back = lax.all_to_all(going, "col", 0, 0, tiled=True)
-    second_a, second_b, _ = lax.optimization_barrier((second_a, second_b, going))
+    second_a, second_b, back, parent_panels = lax.optimization_barrier(
+        (second_a, second_b, back, parent_panels)
+    )
     second_sum = third_sends(second_a, near_a, y_step) + third_sends(second_b, near_b, x_step)
     level_one_rows, level_two_rows, sums = finish_rows(
         level_two_pattern, back, parent_panels, masked_one, masked_two, parent_lead, second_sum

time: 288 us -> 324 us (1.12)
  waiting for transfers between devices: 91.1 us -> 61.5 us
  blocking collectives: 0 us -> 24.2 us
  Pallas kernels: 58.6 us -> 79.7 us
  starting transfers between devices: 106 us -> 123 us
  local copies, waits for them, and re-layouts: 9.2 us -> 24.7 us
  between operations: 16.6 us -> 1.84 us
    reduce_scatter x1 -> x0, waiting for transfers between devices: 24.6 us -> none  [per_device(): lax.psum_scatter(product_one.reshape(count * count * block, block), 'col'...]
    all_to_all x0 -> x1, blocking collectives: none -> 24.2 us  [per_device(): lax.all_to_all(outgoing(place, readers, cut_pattern, first_sum), 'col', 0...]
    ppermute x14 -> x28, starting transfers between devices: 21.4 us -> 40.4 us  [send(): return lax.ppermute(value, 'col', step)]
    all_to_all x1, starting transfers between devices: 22.6 us -> 6.92 us  [per_device(): lax.all_to_all(jnp.concatenate([cut, facts], 1), 'col', 0, 0, tiled=True)]
    ppermute x4, waiting for transfers between devices: 18.3 us -> 6.03 us  [turned_panels(): return lax.ppermute(part, ('row', 'col'), turn(k))]
    ppermute x14 -> x28, waiting for transfers between devices: 18.9 us -> 30.6 us  [send(): return lax.ppermute(value, 'col', step)]
    unnamed x36 -> x54, local copies, waits for them, and re-layouts: 6.34 us -> 15.5 us
    ppermute x1, starting transfers between devices: 1.36 us -> 9.78 us  [row_parts(): values = values + lax.ppermute(values, 'row', CORE_SWAP)]
  transfers between devices with their start and end apart: 35 -> 54, of which waited for: 19 -> 14; matrix products, arithmetic and copies ran while one was open for 2% -> 7% of each run, Pallas kernels for 14% -> 21%
where the time goes in v5:
time: 324 us; the launch traced here: 322 us
  starting transfers between devices  123 us (38%)
  Pallas kernels  79.7 us (25%)
  waiting for transfers between devices  61.5 us (19%)
  local copies, waits for them, and re-layouts  24.7 us (8%)
  blocking collectives  24.2 us (7%)
  other arithmetic  7.12 us (2%)
    ppermute x28, starting transfers between devices, send(): return lax.ppermute(value, 'col', step)  40.4 us
    ppermute x28, waiting for transfers between devices, send(): return lax.ppermute(value, 'col', step)  30.6 us
    pallas_call x4, Pallas kernels, by_supernode(): pl.pallas_call(kernel, out_shape=[jax.ShapeDtypeStruct((groups, SIDE, siz...  24.5 us
    all_to_all x1, blocking collectives, per_device(): lax.all_to_all(outgoing(place, readers, cut_pattern, first_sum), 'col', 0...  24.2 us
    pallas_call x4, Pallas kernels, by_column(): pl.pallas_call(kernel, out_shape=[jax.ShapeDtypeStruct((groups, SIDE, siz...  21.5 us
    ppermute x2, starting transfers between devices, all_panels(): above = lax.ppermute(own, 'row', z_step(-1))  20.2 us
    ppermute x8, starting transfers between devices, all_panels(): found += [held, lax.ppermute(held, 'row', CORE_SWAP)]  17.7 us
    unnamed x54, local copies, waits for them, and re-layouts  15.5 us
  transfers between devices with their start and end apart: 54, of which 14 were waited for; matrix products, arithmetic and copies ran while one was open for 7% of the time, Pallas kernels for 21%

profile of v5, /device:TPU:1, one launch (start us, length us, event | category | flops | bytes accessed | tf_op | source)
XLA Modules:
  0.0 322.4 jit_solution(14893203799073311268)
XLA Ops:
  3.3 6.0 %collective-permute-start = (bf16[128,1024]{1,0:T(8,128)(2,1)S(1)}, bf16[128,1024]{1,0:T(8,128)(2,1)S(1)}, u32[]{:S(2)}, u32[]{:S(2)}) collective-permute-start(bf16[128,1024]{1,0:T(8,128)(2,1)S(1)} %get-tuple-element.143), channel_id=1, source_target_pairs={{0,0},{1,1},{2,16},{3,17},{4,32},{5,33},{6,48},{7,49},{8,64},{9,65... | collective-permute-start | bytes 786440 | tf_op jit(solution)/shard_map/ppermute | solution.py:46
  11.8 3.5 %collective-permute-done = bf16[128,1024]{1,0:T(8,128)(2,1)S(1)} collective-permute-done((bf16[128,1024]{1,0:T(8,128)(2,1)S(1)}, bf16[128,1024]{1,0:T(8,128)(2,1)S(1)}, u32[]{:S(2)}, u32[]{:S(2)}) %collective-permute-start) | collective-permute-done | bytes 262176 | tf_op jit(solution)/shard_map/ppermute | solution.py:46
  17.9 15.4 %collective-permute-start.5 = (bf16[2,128,1024]{2,1,0:T(8,128)(2,1)S(1)}, bf16[2,128,1024]{2,1,0:T(8,128)(2,1)S(1)}, u32[]{:S(2)}, u32[]{:S(2)}) collective-permute-start(bf16[2,128,1024]{2,1,0:T(8,128)(2,1)S(1)} %pad_maximum_fusion.refs_4_), channel_id=1, source_target_pairs={{0,96},{16,112},{32,0},{48,16},{64,32},{80,48},{96,64},{112,80},{1... | collective-permute-start | bytes 1572872 | tf_op jit(solution)/shard_map/ppermute | solution.py:58
  33.3 8.8 %collective-permute-done.5.refs_4_ = bf16[2,128,1024]{2,1,0:T(8,128)(2,1)S(1)} collective-permute-done((bf16[2,128,1024]{2,1,0:T(8,128)(2,1)S(1)}, bf16[2,128,1024]{2,1,0:T(8,128)(2,1)S(1)}, u32[]{:S(2)}, u32[]{:S(2)}) %collective-permute-start.5) | collective-permute-done | bytes 524320 | tf_op jit(solution)/shard_map/ppermute | solution.py:58
  42.2 3.5 %collective-permute-start.8 = (bf16[128,1024]{1,0:T(8,128)(2,1)S(1)}, bf16[128,1024]{1,0:T(8,128)(2,1)S(1)}, u32[]{:S(2)}, u32[]{:S(2)}) collective-permute-start(bf16[128,1024]{1,0:T(8,128)(2,1)S(1)} %slice_bitcast_fusion.2), channel_id=1, source_target_pairs={{0,96},{16,112},{32,0},{48,16},{64,32},{80,48},{96,64},{112,80},{1... | collective-permute-start | bytes 786440 | tf_op jit(solution)/shard_map/ppermute | solution.py:60
  45.9 6.9 %collective-permute-start.2 = (bf16[2,128,1024]{2,1,0:T(8,128)(2,1)S(1)}, bf16[2,128,1024]{2,1,0:T(8,128)(2,1)S(1)}, u32[]{:S(2)}, u32[]{:S(2)}) collective-permute-start(bf16[2,128,1024]{2,1,0:T(8,128)(2,1)S(1)} %pad_maximum_fusion.refs_4_), channel_id=1, source_target_pairs={{0,16},{16,0},{32,48},{48,32},{64,80},{80,64},{96,112},{112,96},{1... | collective-permute-start | bytes 1572872 | tf_op jit(solution)/shard_map/ppermute | solution.py:64
  53.3 7.0 %collective-permute-start.9 = (bf16[2,128,1024]{2,1,0:T(8,128)(2,1)S(1)}, bf16[2,128,1024]{2,1,0:T(8,128)(2,1)}, u32[]{:S(2)}, u32[]{:S(2)}) collective-permute-start(bf16[2,128,1024]{2,1,0:T(8,128)(2,1)S(1)} %pad_maximum_fusion.1.refs_6_), channel_id=1, source_target_pairs={{0,16},{16,0},{32,48},{48,32},{64,80},{80,64},{96,112},{112,96},{1... | collective-permute-start | bytes 1572872 | tf_op jit(solution)/shard_map/ppermute | solution.py:64
  64.9 4.0 %collective-permute-start.14 = (bf16[128,1024]{1,0:T(8,128)(2,1)S(1)}, bf16[128,1024]{1,0:T(8,128)(2,1)S(1)}, u32[]{:S(2)}, u32[]{:S(2)}) collective-permute-start(bf16[128,1024]{1,0:T(8,128)(2,1)S(1)} %get-tuple-element.139), channel_id=1, source_target_pairs={{0,0},{1,1},{2,16},{3,17},{4,32},{5,33},{6,48},{7,49},{8,64},{9,65... | collective-permute-start | bytes 786440 | tf_op jit(solution)/shard_map/ppermute | solution.py:46
  70.8 3.5 %shard_map.138 = (bf16[1,4,512,128]{3,2,1,0:T(8,128)(2,1)S(1)}, bf16[1,4,512,128]{3,2,1,0:T(8,128)(2,1)S(1)}) custom-call(s32[4]{0:T(128)S(1)} %get-tuple-element.152.order_ref, bf16[1024,2048]{1,0:T(8,128)(2,1)} %matrix_ref.7, bf16[1024,2048]{1,0:T(8,128)(2,1)} %matrix_ref.7, bf16[1024,2048]{1,0:T(8,128)(2,1)} %matrix_ref.7, bf16[1024,2048]{1,0:T(8,128)(2,1)} %matrix_ref.7, ...), custom_call_target="tpu_custom_call" | custom-call | flops 1073741824 | bytes 2097152 | tf_op jit(solution)/shard_map/pallas_call | solution.py:97
  77.1 3.5 %shard_map.137 = (bf16[1,4,512,128]{3,2,1,0:T(8,128)(2,1)S(1)}, bf16[1,4,512,128]{3,2,1,0:T(8,128)(2,1)S(1)}) custom-call(s32[4]{0:T(128)S(1)} %get-tuple-element.160.order_ref, bf16[1024,2048]{1,0:T(8,128)(2,1)} %matrix_ref.7, bf16[1024,2048]{1,0:T(8,128)(2,1)} %matrix_ref.7, bf16[1024,2048]{1,0:T(8,128)(2,1)} %matrix_ref.7, bf16[1024,2048]{1,0:T(8,128)(2,1)} %matrix_ref.7, ...), custom_call_target="tpu_custom_call" | custom-call | flops 1073741824 | bytes 2097152 | tf_op jit(solution)/shard_map/pallas_call | solution.py:97
  83.4 7.2 %shard_map.141.ahead_ref.behind_ref.own_ref = bf16[3,4,1024,128]{3,2,1,0:T(8,128)(2,1)} custom-call(s32[12]{0:T(128)S(1)} %pad_add_fusion.1.order_ref, bf16[1024,2048]{1,0:T(8,128)(2,1)} %matrix_ref.7, bf16[1024,2048]{1,0:T(8,128)(2,1)} %matrix_ref.7, bf16[1024,2048]{1,0:T(8,128)(2,1)} %matrix_ref.7, bf16[1024,2048]{1,0:T(8,128)(2,1)} %matrix_ref.7, ...), custom_call_target="tpu_custom_call" | custom-call | flops 3221225472 | bytes 6291456 | tf_op jit(solution)/shard_map/pallas_call | solution.py:97
  90.6 10.1 %collective-permute-done.12.low_ref = bf16[4,512,128]{2,1,0:T(8,128)(2,1)S(1)} collective-permute-done((bf16[4,512,128]{2,1,0:T(8,128)(2,1)S(1)}, bf16[4,512,128]{2,1,0:T(8,128)(2,1)S(1)}, u32[]{:S(2)}, u32[]{:S(2)}) %collective-permute-start.12) | collective-permute-done | bytes 524320 | tf_op jit(solution)/shard_map/ppermute | solution.py:155
  103.6 7.3 %shard_map.139.ahead_ref.behind_ref.own_ref = bf16[3,4,1024,128]{3,2,1,0:T(8,128)(2,1)} custom-call(s32[12]{0:T(128)S(1)} %pad_add_fusion.order_ref, bf16[1024,2048]{1,0:T(8,128)(2,1)} %matrix_ref.7, bf16[1024,2048]{1,0:T(8,128)(2,1)} %matrix_ref.7, bf16[1024,2048]{1,0:T(8,128)(2,1)} %matrix_ref.7, bf16[1024,2048]{1,0:T(8,128)(2,1)} %matrix_ref.7, ...), custom_call_target="tpu_custom_call" | custom-call | flops 3221225472 | bytes 6291456 | tf_op jit(solution)/shard_map/pallas_call | solution.py:97
  110.8 4.8 %collective-permute-start.23 = (bf16[2,128,1024]{2,1,0:T(8,128)(2,1)S(1)}, bf16[2,128,1024]{2,1,0:T(8,128)(2,1)S(1)}, u32[]{:S(2)}, u32[]{:S(2)}) collective-permute-start(bf16[2,128,1024]{2,1,0:T(8,128)(2,1)S(1)} %pad_maximum_fusion.2), channel_id=1, source_target_pairs={{0,96},{16,112},{32,0},{48,16},{64,32},{80,48},{96,64},{112,80},{1... | collective-permute-start | bytes 1572872 | tf_op jit(solution)/shard_map/ppermute | solution.py:58
  115.7 3.8 %shard_map.142 = (bf16[4,1024,128]{2,1,0:T(8,128)(2,1)}, bf16[4,1024,128]{2,1,0:T(8,128)(2,1)}) custom-call(bf16[4,512,128]{2,1,0:T(8,128)(2,1)S(1)} %collective-permute-done.12.low_ref, bf16[4,512,128]{2,1,0:T(8,128)(2,1)S(1)} %collective-permute-done.13.high_ref, bf16[3,4,1024,128]{3,2,1,0:T(8,128)(2,1)} %shard_map.141.ahead_ref.behind_ref.own_ref, ...), custom_call_target="tpu_custom_call" | custom-call | bytes 4194304 | tf_op jit(solution)/shard_map/pallas_call | solution.py:174
  123.5 6.9 %all-to-all-start = ((bf16[16,144,128]{2,1,0:T(8,128)(2,1)}), bf16[16,144,128]{2,1,0:T(8,128)(2,1)S(1)}, u32[]{:S(2)}, u32[]{:S(2)}) async-start(bf16[16,144,128]{2,1,0:T(8,128)(2,1)} %fusion.1), calls=%async_computation | async-start | bytes 1179648 | tf_op jit(solution)/shard_map/all_to_all | solution.py:404
  130.4 3.8 %shard_map.140 = (bf16[4,1024,128]{2,1,0:T(8,128)(2,1)}, bf16[4,1024,128]{2,1,0:T(8,128)(2,1)}) custom-call(bf16[4,512,128]{2,1,0:T(8,128)(2,1)S(1)} %collective-permute-done.10.low_ref, bf16[4,512,128]{2,1,0:T(8,128)(2,1)S(1)} %collective-permute-done.11.high_ref, bf16[3,4,1024,128]{3,2,1,0:T(8,128)(2,1)} %shard_map.139.ahead_ref.behind_ref.own_ref, ...), custom_call_target="tpu_custom_call" | custom-call | bytes 4194304 | tf_op jit(solution)/shard_map/pallas_call | solution.py:174
  143.8 8.0 %all-to-all-done = bf16[16,144,128]{2,1,0:T(8,128)(2,1)S(1)} async-done(((bf16[16,144,128]{2,1,0:T(8,128)(2,1)}), bf16[16,144,128]{2,1,0:T(8,128)(2,1)S(1)}, u32[]{:S(2)}, u32[]{:S(2)}) %all-to-all-start) | async-done | bytes 589856 | tf_op jit(solution)/shard_map/all_to_all | solution.py:404
  154.1 4.7 %collective-permute-start.16 = (bf16[4,1024,128]{2,1,0:T(8,128)(2,1)}, bf16[4,1024,128]{2,1,0:T(8,128)(2,1)S(1)}, u32[]{:S(2)}, u32[]{:S(2)}) collective-permute-start(bf16[4,1024,128]{2,1,0:T(8,128)(2,1)} %get-tuple-element.84), channel_id=1, source_target_pairs={{0,1},{1,2},{2,3},{3,0},{4,5},{5,6},{6,7},{7,4},{8,9},{9,10},{10,1... | collective-permute-start | bytes 3145736 | tf_op jit(solution)/shard_map/ppermute | solution.py:155
  167.4 9.8 %collective-permute-done.19.two_ref = bf16[4,1024,128]{2,1,0:T(8,128)(2,1)S(1)} collective-permute-done((bf16[4,1024,128]{2,1,0:T(8,128)(2,1)}, bf16[4,1024,128]{2,1,0:T(8,128)(2,1)S(1)}, u32[]{:S(2)}, u32[]{:S(2)}) %collective-permute-start.19) | collective-permute-done | bytes 1048608 | tf_op jit(solution)/shard_map/ppermute | solution.py:155
  181.9 4.5 %shard_map.146 = (bf16[1,4,64,1024]{3,2,1,0:T(8,128)(2,1)}, bf16[1,4,64,1024]{3,2,1,0:T(8,128)(2,1)S(1)}) custom-call(s32[4]{0:T(128)S(1)} %gather_fusion.3, bf16[16,128,1024]{2,1,0:T(8,128)(2,1)} %constant_dynamic-update-slice_fusion.a_ref.b_ref.c_ref.d_ref, bf16[16,128,1024]{2,1,0:T(8,128)(2,1)} %constant_dynamic-update-slice_fusion.a_ref.b_ref.c_ref.d_ref, ...), custom_call_target="tpu_custom_call" | custom-call | flops 1073741824 | bytes 2097152 | tf_op jit(solution)/shard_map/pallas_call | solution.py:134
  189.1 4.5 %shard_map.143 = (bf16[1,4,64,1024]{3,2,1,0:T(8,128)(2,1)}, bf16[1,4,64,1024]{3,2,1,0:T(8,128)(2,1)S(1)}) custom-call(s32[4]{0:T(128)S(1)} %gather_fusion.1, bf16[16,128,1024]{2,1,0:T(8,128)(2,1)} %constant_dynamic-update-slice_fusion.a_ref.b_ref.c_ref.d_ref, bf16[16,128,1024]{2,1,0:T(8,128)(2,1)} %constant_dynamic-update-slice_fusion.a_ref.b_ref.c_ref.d_ref, ...), custom_call_target="tpu_custom_call" | custom-call | flops 1073741824 | bytes 2097152 | tf_op jit(solution)/shard_map/pallas_call | solution.py:134
  197.2 4.2 %all-to-all-start.2 = ((bf16[16,128,128]{2,1,0:T(8,128)(2,1)}), bf16[16,128,128]{2,1,0:T(8,128)(2,1)}, u32[]{:S(2)}, u32[]{:S(2)}) async-start(bf16[16,128,128]{2,1,0:T(8,128)(2,1)} %broadcast_select_fusion), calls=%async_computation.2 | async-start | bytes 1048576 | tf_op jit(solution)/shard_map/all_to_all | solution.py:407
  206.2 7.7 %shard_map.147.ahead_ref.behind_ref.own_ref = bf16[3,4,128,1024]{3,2,1,0:T(8,128)(2,1)} custom-call(s32[12]{0:T(128)S(1)} %gather_fusion.4, bf16[16,128,1024]{2,1,0:T(8,128)(2,1)} %constant_dynamic-update-slice_fusion.a_ref.b_ref.c_ref.d_ref, bf16[16,128,1024]{2,1,0:T(8,128)(2,1)} %constant_dynamic-update-slice_fusion.a_ref.b_ref.c_ref.d_ref, ...), custom_call_target="tpu_custom_call" | custom-call | flops 3221225472 | bytes 6291456 | tf_op jit(solution)/shard_map/pallas_call | solution.py:134
  225.9 7.8 %shard_map.144.ahead_ref.behind_ref.own_ref = bf16[3,4,128,1024]{3,2,1,0:T(8,128)(2,1)} custom-call(s32[12]{0:T(128)S(1)} %gather_fusion.2, bf16[16,128,1024]{2,1,0:T(8,128)(2,1)} %constant_dynamic-update-slice_fusion.a_ref.b_ref.c_ref.d_ref, bf16[16,128,1024]{2,1,0:T(8,128)(2,1)} %constant_dynamic-update-slice_fusion.a_ref.b_ref.c_ref.d_ref, ...), custom_call_target="tpu_custom_call" | custom-call | flops 3221225472 | bytes 6291456 | tf_op jit(solution)/shard_map/pallas_call | solution.py:134
  233.6 3.8 %shard_map.148 = (bf16[4,128,1024]{2,1,0:T(8,128)(2,1)}, bf16[4,128,1024]{2,1,0:T(8,128)(2,1)}) custom-call(bf16[4,64,1024]{2,1,0:T(8,128)(2,1)S(1)} %collective-permute-done.32.low_ref, bf16[4,64,1024]{2,1,0:T(8,128)(2,1)S(1)} %collective-permute-done.33.high_ref, bf16[3,4,128,1024]{3,2,1,0:T(8,128)(2,1)} %shard_map.147.ahead_ref.behind_ref.own_ref, ...), custom_call_target="tpu_custom_call" | custom-call | bytes 4194304 | tf_op jit(solution)/shard_map/pallas_call | solution.py:174
  237.4 3.8 %shard_map.145 = (bf16[4,128,1024]{2,1,0:T(8,128)(2,1)}, bf16[4,128,1024]{2,1,0:T(8,128)(2,1)}) custom-call(bf16[4,64,1024]{2,1,0:T(8,128)(2,1)S(1)} %collective-permute-done.28.low_ref, bf16[4,64,1024]{2,1,0:T(8,128)(2,1)S(1)} %collective-permute-done.29.high_ref, bf16[3,4,128,1024]{3,2,1,0:T(8,128)(2,1)} %shard_map.144.ahead_ref.behind_ref.own_ref, ...), custom_call_target="tpu_custom_call" | custom-call | bytes 4194304 | tf_op jit(solution)/shard_map/pallas_call | solution.py:174
  249.6 24.2 %all_to_all.15.back_ref = bf16[16,2,128,128]{3,2,1,0:T(8,128)(2,1)} all-to-all(bf16[16,2,128,128]{3,2,1,0:T(8,128)(2,1)} %shard_map.151), channel_id=1, replica_groups=mesh['row'=8,'col'=16] {'col'}, dimensions={0} | all-to-all | bytes 2097152 | tf_op jit(solution)/shard_map/all_to_all | solution.py:410
  289.6 6.3 %collective-permute-done.42.refs_1_ = bf16[128,1024]{1,0:T(8,128)(2,1)S(1)} collective-permute-done((bf16[128,1024]{1,0:T(8,128)(2,1)S(1)}, bf16[128,1024]{1,0:T(8,128)(2,1)S(1)}, u32[]{:S(2)}, u32[]{:S(2)}) %collective-permute-start.42) | collective-permute-done | bytes 262176 | tf_op jit(solution)/shard_map/ppermute | solution.py:155
  296.6 3.6 %shard_map.154 = (bf16[128,2048]{1,0:T(8,128)(2,1)}, bf16[128,2048]{1,0:T(8,128)(2,1)}, f32[4,128,128]{2,1,0:T(8,128)S(1)}) custom-call(s32[1,16]{1,0:T(1,128)S(1)} %copy-done.14, bf16[16,2,128,128]{3,2,1,0:T(8,128)(2,1)} %all_to_all.15.back_ref, bf16[16,128,128]{2,1,0:T(8,128)(2,1)} %all-to-all-done.2.panels_ref, bf16[128,2048]{1,0:T(8,128)(2,1)} %copy-done.15, ...), custom_call_target="tpu_custom_call" | custom-call | bytes 1048576 | tf_op jit(solution)/shard_map/pallas_call | solution.py:225
  300.2 9.8 %collective-permute-start.48 = (f32[4,128,128]{2,1,0:T(8,128)S(1)}, f32[4,128,128]{2,1,0:T(8,128)S(1)}, u32[]{:S(2)}, u32[]{:S(2)}) collective-permute-start(f32[4,128,128]{2,1,0:T(8,128)S(1)} %get-tuple-element.128), channel_id=1, source_target_pairs={{0,16},{16,0},{32,48},{48,32},{64,80},{80,64},{96,112},{112,96},{1... | collective-permute-start | bytes 786440 | tf_op jit(solution)/shard_map/ppermute | solution.py:215
  317.3 3.8 %collective-permute-done.51.d = bf16[4,128,128]{2,1,0:T(8,128)(2,1)S(1)} collective-permute-done((bf16[4,128,128]{2,1,0:T(8,128)(2,1)S(1)}, bf16[4,128,128]{2,1,0:T(8,128)(2,1)S(1)}, u32[]{:S(2)}, u32[]{:S(2)}) %collective-permute-start.51) | collective-permute-done | bytes 131104 | tf_op jit(solution)/shard_map/ppermute | solution.py:217
  (200 shorter events, 107.8 us)
Async XLA Ops:
  17.9 24.3 %collective-permute-start.5 = (bf16[2,128,1024]{2,1,0:T(8,128)(2,1)S(1)}, bf16[2,128,1024]{2,1,0:T(8,128)(2,1)S(1)}, u32[]{:S(2)}, u32[]{:S(2)}) collective-permute-start(bf16[2,128,1024]{2,1,0:T(8,128)(2,1)S(1)} %pad_maximum_fusion.refs_4_), channel_id=1, source_target_pairs={{0,96},{16,112},{32,0},{48,16},{64,32},{80,48},{96,64},{112,80},{1... | collective-permute-start | bytes 1572872 | tf_op jit(solution)/shard_map/ppermute | solution.py:58
  45.9 18.9 %collective-permute-start.2 = (bf16[2,128,1024]{2,1,0:T(8,128)(2,1)S(1)}, bf16[2,128,1024]{2,1,0:T(8,128)(2,1)S(1)}, u32[]{:S(2)}, u32[]{:S(2)}) collective-permute-start(bf16[2,128,1024]{2,1,0:T(8,128)(2,1)S(1)} %pad_maximum_fusion.refs_4_), channel_id=1, source_target_pairs={{0,16},{16,0},{32,48},{48,32},{64,80},{80,64},{96,112},{112,96},{1... | collective-permute-start | bytes 1572872 | tf_op jit(solution)/shard_map/ppermute | solution.py:64
  69.0 21.5 %collective-permute-start.15 = (bf16[128,1024]{1,0:T(8,128)(2,1)S(1)}, bf16[128,1024]{1,0:T(8,128)(2,1)S(1)}, u32[]{:S(2)}, u32[]{:S(2)}) collective-permute-start(bf16[128,1024]{1,0:T(8,128)(2,1)S(1)} %get-tuple-element.140), channel_id=1, source_target_pairs={{0,1},{1,0},{2,17},{3,16},{4,33},{5,32},{6,49},{7,48},{8,65},{9,64... | collective-permute-start | bytes 786440 | tf_op jit(solution)/shard_map/ppermute | solution.py:46
  74.3 26.4 %collective-permute-start.12 = (bf16[4,512,128]{2,1,0:T(8,128)(2,1)S(1)}, bf16[4,512,128]{2,1,0:T(8,128)(2,1)S(1)}, u32[]{:S(2)}, u32[]{:S(2)}) collective-permute-start(bf16[4,512,128]{2,1,0:T(8,128)(2,1)S(1)} %bitcast.81), channel_id=1, source_target_pairs={{0,4},{1,5},{2,6},{3,7},{4,8},{5,9},{6,10},{7,11},{8,12},{9,13},{1... | collective-permute-start | bytes 1572872 | tf_op jit(solution)/shard_map/ppermute | solution.py:155
  76.1 24.6 %collective-permute-start.13 = (bf16[4,512,128]{2,1,0:T(8,128)(2,1)S(1)}, bf16[4,512,128]{2,1,0:T(8,128)(2,1)S(1)}, u32[]{:S(2)}, u32[]{:S(2)}) collective-permute-start(bf16[4,512,128]{2,1,0:T(8,128)(2,1)S(1)} %bitcast.80), channel_id=1, source_target_pairs={{0,12},{1,13},{2,14},{3,15},{4,0},{5,1},{6,2},{7,3},{8,4},{9,5},{1... | collective-permute-start | bytes 1572872 | tf_op jit(solution)/shard_map/ppermute | solution.py:155
  80.6 20.1 %collective-permute-start.10 = (bf16[4,512,128]{2,1,0:T(8,128)(2,1)S(1)}, bf16[4,512,128]{2,1,0:T(8,128)(2,1)S(1)}, u32[]{:S(2)}, u32[]{:S(2)}) collective-permute-start(bf16[4,512,128]{2,1,0:T(8,128)(2,1)S(1)} %bitcast.83), channel_id=1, source_target_pairs={{0,1},{1,2},{2,3},{3,0},{4,5},{5,6},{6,7},{7,4},{8,9},{9,10},{10,1... | collective-permute-start | bytes 1572872 | tf_op jit(solution)/shard_map/ppermute | solution.py:155
  80.7 20.0 %collective-permute-start.11 = (bf16[4,512,128]{2,1,0:T(8,128)(2,1)S(1)}, bf16[4,512,128]{2,1,0:T(8,128)(2,1)S(1)}, u32[]{:S(2)}, u32[]{:S(2)}) collective-permute-start(bf16[4,512,128]{2,1,0:T(8,128)(2,1)S(1)} %bitcast.82), channel_id=1, source_target_pairs={{0,3},{1,0},{2,1},{3,2},{4,7},{5,4},{6,5},{7,6},{8,11},{9,8},{10,9... | collective-permute-start | bytes 1572872 | tf_op jit(solution)/shard_map/ppermute | solution.py:155
  100.7 33.4 %collective-permute-start.21 = (bf16[2,128,1024]{2,1,0:T(8,128)(2,1)S(1)}, bf16[2,128,1024]{2,1,0:T(8,128)(2,1)}, u32[]{:S(2)}, u32[]{:S(2)}) collective-permute-start(bf16[2,128,1024]{2,1,0:T(8,128)(2,1)S(1)} %pad_maximum_fusion.2), channel_id=1, source_target_pairs={{0,32},{16,48},{32,64},{48,80},{64,96},{80,112},{96,0},{112,16},{1... | collective-permute-start | bytes 1572872 | tf_op jit(solution)/shard_map/ppermute | solution.py:57
  110.8 29.2 %collective-permute-start.20 = (bf16[2,128,1024]{2,1,0:T(8,128)(2,1)S(1)}, bf16[2,128,1024]{2,1,0:T(8,128)(2,1)}, u32[]{:S(2)}, u32[]{:S(2)}) collective-permute-start(bf16[2,128,1024]{2,1,0:T(8,128)(2,1)S(1)} %pad_maximum_fusion.2), channel_id=1, source_target_pairs={{0,16},{16,0},{32,48},{48,32},{64,80},{80,64},{96,112},{112,96},{1... | collective-permute-start | bytes 1572872 | tf_op jit(solution)/shard_map/ppermute | solution.py:64
  110.8 25.0 %collective-permute-start.23 = (bf16[2,128,1024]{2,1,0:T(8,128)(2,1)S(1)}, bf16[2,128,1024]{2,1,0:T(8,128)(2,1)S(1)}, u32[]{:S(2)}, u32[]{:S(2)}) collective-permute-start(bf16[2,128,1024]{2,1,0:T(8,128)(2,1)S(1)} %pad_maximum_fusion.2), channel_id=1, source_target_pairs={{0,96},{16,112},{32,0},{48,16},{64,32},{80,48},{96,64},{112,80},{1... | collective-permute-start | bytes 1572872 | tf_op jit(solution)/shard_map/ppermute | solution.py:58
  119.5 47.9 %collective-permute-start.18 = (bf16[4,1024,128]{2,1,0:T(8,128)(2,1)}, bf16[4,1024,128]{2,1,0:T(8,128)(2,1)}, u32[]{:S(2)}, u32[]{:S(2)}) collective-permute-start(bf16[4,1024,128]{2,1,0:T(8,128)(2,1)} %get-tuple-element.88), channel_id=1, source_target_pairs={{0,4},{1,5},{2,6},{3,7},{4,8},{5,9},{6,10},{7,11},{8,12},{9,13},{1... | collective-permute-start | bytes 3145736 | tf_op jit(solution)/shard_map/ppermute | solution.py:155
  123.5 28.4 %all-to-all-start = ((bf16[16,144,128]{2,1,0:T(8,128)(2,1)}), bf16[16,144,128]{2,1,0:T(8,128)(2,1)S(1)}, u32[]{:S(2)}, u32[]{:S(2)}) async-start(bf16[16,144,128]{2,1,0:T(8,128)(2,1)} %fusion.1), calls=%async_computation | async-start | bytes 1179648 | tf_op jit(solution)/shard_map/all_to_all | solution.py:404
  135.8 18.3 %collective-permute-start.26 = (bf16[128,1024]{1,0:T(8,128)(2,1)S(1)}, bf16[128,1024]{1,0:T(8,128)(2,1)}, u32[]{:S(2)}, u32[]{:S(2)}) collective-permute-start(bf16[128,1024]{1,0:T(8,128)(2,1)S(1)} %slice_bitcast_fusion), channel_id=1, source_target_pairs={{0,96},{16,112},{32,0},{48,16},{64,32},{80,48},{96,64},{112,80},{1... | collective-permute-start | bytes 786440 | tf_op jit(solution)/shard_map/ppermute | solution.py:60
  138.6 20.2 %collective-permute-start.22 = (bf16[2,128,1024]{2,1,0:T(8,128)(2,1)}, bf16[2,128,1024]{2,1,0:T(8,128)(2,1)S(1)}, u32[]{:S(2)}, u32[]{:S(2)}) collective-permute-start(bf16[2,128,1024]{2,1,0:T(8,128)(2,1)} %collective-permute-done.21), channel_id=1, source_target_pairs={{0,16},{16,0},{32,48},{48,32},{64,80},{80,64},{96,112},{112,96},{1... | collective-permute-start | bytes 1572872 | tf_op jit(solution)/shard_map/ppermute | solution.py:64
  140.1 21.4 %collective-permute-start.24 = (bf16[2,128,1024]{2,1,0:T(8,128)(2,1)S(1)}, bf16[2,128,1024]{2,1,0:T(8,128)(2,1)S(1)}, u32[]{:S(2)}, u32[]{:S(2)}) collective-permute-start(bf16[2,128,1024]{2,1,0:T(8,128)(2,1)S(1)} %collective-permute-done.23), channel_id=1, source_target_pairs={{0,16},{16,0},{32,48},{48,32},{64,80},{80,64},{96,112},{112,96},{1... | collective-permute-start | bytes 1572872 | tf_op jit(solution)/shard_map/ppermute | solution.py:64
  154.0 23.2 %collective-permute-start.19 = (bf16[4,1024,128]{2,1,0:T(8,128)(2,1)}, bf16[4,1024,128]{2,1,0:T(8,128)(2,1)S(1)}, u32[]{:S(2)}, u32[]{:S(2)}) collective-permute-start(bf16[4,1024,128]{2,1,0:T(8,128)(2,1)} %get-tuple-element.89), channel_id=1, source_target_pairs={{0,12},{1,13},{2,14},{3,15},{4,0},{5,1},{6,2},{7,3},{8,4},{9,5},{1... | collective-permute-start | bytes 3145736 | tf_op jit(solution)/shard_map/ppermute | solution.py:155
  154.1 25.9 %collective-permute-start.16 = (bf16[4,1024,128]{2,1,0:T(8,128)(2,1)}, bf16[4,1024,128]{2,1,0:T(8,128)(2,1)S(1)}, u32[]{:S(2)}, u32[]{:S(2)}) collective-permute-start(bf16[4,1024,128]{2,1,0:T(8,128)(2,1)} %get-tuple-element.84), channel_id=1, source_target_pairs={{0,1},{1,2},{2,3},{3,0},{4,5},{5,6},{6,7},{7,4},{8,9},{9,10},{10,1... | collective-permute-start | bytes 3145736 | tf_op jit(solution)/shard_map/ppermute | solution.py:155
  158.8 23.1 %collective-permute-start.17 = (bf16[4,1024,128]{2,1,0:T(8,128)(2,1)}, bf16[4,1024,128]{2,1,0:T(8,128)(2,1)}, u32[]{:S(2)}, u32[]{:S(2)}) collective-permute-start(bf16[4,1024,128]{2,1,0:T(8,128)(2,1)} %get-tuple-element.85), channel_id=1, source_target_pairs={{0,3},{1,0},{2,1},{3,2},{4,7},{5,4},{6,5},{7,6},{8,11},{9,8},{10,9... | collective-permute-start | bytes 3145736 | tf_op jit(solution)/shard_map/ppermute | solution.py:155
  186.5 33.4 %collective-permute-start.32 = (bf16[4,64,1024]{2,1,0:T(8,128)(2,1)}, bf16[4,64,1024]{2,1,0:T(8,128)(2,1)S(1)}, u32[]{:S(2)}, u32[]{:S(2)}) collective-permute-start(bf16[4,64,1024]{2,1,0:T(8,128)(2,1)} %bitcast.27), channel_id=1, source_target_pairs={{0,4},{1,5},{2,6},{3,7},{4,8},{5,9},{6,10},{7,11},{8,12},{9,13},{1... | collective-permute-start | bytes 1572872 | tf_op jit(solution)/shard_map/ppermute | solution.py:155
  187.6 33.4 %collective-permute-start.33 = (bf16[4,64,1024]{2,1,0:T(8,128)(2,1)S(1)}, bf16[4,64,1024]{2,1,0:T(8,128)(2,1)S(1)}, u32[]{:S(2)}, u32[]{:S(2)}) collective-permute-start(bf16[4,64,1024]{2,1,0:T(8,128)(2,1)S(1)} %bitcast.79), channel_id=1, source_target_pairs={{0,12},{1,13},{2,14},{3,15},{4,0},{5,1},{6,2},{7,3},{8,4},{9,5},{1... | collective-permute-start | bytes 1572872 | tf_op jit(solution)/shard_map/ppermute | solution.py:155
  193.7 28.6 %collective-permute-start.28 = (bf16[4,64,1024]{2,1,0:T(8,128)(2,1)}, bf16[4,64,1024]{2,1,0:T(8,128)(2,1)S(1)}, u32[]{:S(2)}, u32[]{:S(2)}) collective-permute-start(bf16[4,64,1024]{2,1,0:T(8,128)(2,1)} %bitcast.21), channel_id=1, source_target_pairs={{0,1},{1,2},{2,3},{3,0},{4,5},{5,6},{6,7},{7,4},{8,9},{9,10},{10,1... | collective-permute-start | bytes 1572872 | tf_op jit(solution)/shard_map/ppermute | solution.py:155
  195.9 28.8 %collective-permute-start.29 = (bf16[4,64,1024]{2,1,0:T(8,128)(2,1)S(1)}, bf16[4,64,1024]{2,1,0:T(8,128)(2,1)S(1)}, u32[]{:S(2)}, u32[]{:S(2)}) collective-permute-start(bf16[4,64,1024]{2,1,0:T(8,128)(2,1)S(1)} %bitcast.78), channel_id=1, source_target_pairs={{0,3},{1,0},{2,1},{3,2},{4,7},{5,4},{6,5},{7,6},{8,11},{9,8},{10,9... | collective-permute-start | bytes 1572872 | tf_op jit(solution)/shard_map/ppermute | solution.py:155
  197.2 52.4 %all-to-all-start.2 = ((bf16[16,128,128]{2,1,0:T(8,128)(2,1)}), bf16[16,128,128]{2,1,0:T(8,128)(2,1)}, u32[]{:S(2)}, u32[]{:S(2)}) async-start(bf16[16,128,128]{2,1,0:T(8,128)(2,1)} %broadcast_select_fusion), calls=%async_computation.2 | async-start | bytes 1048576 | tf_op jit(solution)/shard_map/all_to_all | solution.py:407
  217.4 23.8 %collective-permute-start.40 = (bf16[1024,128]{1,0:T(8,128)(2,1)S(1)}, bf16[1024,128]{1,0:T(8,128)(2,1)S(1)}, u32[]{:S(2)}, u32[]{:S(2)}) collective-permute-start(bf16[1024,128]{1,0:T(8,128)(2,1)S(1)} %get-tuple-element.111), channel_id=1, source_target_pairs={{0,2},{1,3},{2,0},{3,1},{4,6},{5,7},{6,4},{7,5},{8,10},{9,11},{10,... | collective-permute-start | bytes 786440 | tf_op jit(solution)/shard_map/ppermute | solution.py:155
  219.9 21.9 %collective-permute-start.41 = (bf16[1024,128]{1,0:T(8,128)(2,1)S(1)}, bf16[1024,128]{1,0:T(8,128)(2,1)S(1)}, u32[]{:S(2)}, u32[]{:S(2)}) collective-permute-start(bf16[1024,128]{1,0:T(8,128)(2,1)S(1)} %get-tuple-element.112), channel_id=1, source_target_pairs={{0,3},{1,0},{2,1},{3,2},{4,7},{5,4},{6,5},{7,6},{8,11},{9,8},{10,9... | collective-permute-start | bytes 786440 | tf_op jit(solution)/shard_map/ppermute | solution.py:155
  221.0 23.1 %collective-permute-start.36 = (bf16[1024,128]{1,0:T(8,128)(2,1)S(1)}, bf16[1024,128]{1,0:T(8,128)(2,1)S(1)}, u32[]{:S(2)}, u32[]{:S(2)}) collective-permute-start(bf16[1024,128]{1,0:T(8,128)(2,1)S(1)} %get-tuple-element.104), channel_id=1, source_target_pairs={{0,4},{1,5},{2,6},{3,7},{4,8},{5,9},{6,10},{7,11},{8,12},{9,13},{1... | collective-permute-start | bytes 786440 | tf_op jit(solution)/shard_map/ppermute | solution.py:155
  222.3 22.2 %collective-permute-start.37 = (bf16[1024,128]{1,0:T(8,128)(2,1)S(1)}, bf16[1024,128]{1,0:T(8,128)(2,1)S(1)}, u32[]{:S(2)}, u32[]{:S(2)}) collective-permute-start(bf16[1024,128]{1,0:T(8,128)(2,1)S(1)} %get-tuple-element.105), channel_id=1, source_target_pairs={{0,8},{1,9},{2,10},{3,11},{4,12},{5,13},{6,14},{7,15},{8,0},{9,1},... | collective-permute-start | bytes 786440 | tf_op jit(solution)/shard_map/ppermute | solution.py:155
  224.7 22.2 %collective-permute-start.38 = (bf16[1024,128]{1,0:T(8,128)(2,1)S(1)}, bf16[1024,128]{1,0:T(8,128)(2,1)S(1)}, u32[]{:S(2)}, u32[]{:S(2)}) collective-permute-start(bf16[1024,128]{1,0:T(8,128)(2,1)S(1)} %get-tuple-element.106), channel_id=1, source_target_pairs={{0,12},{1,13},{2,14},{3,15},{4,0},{5,1},{6,2},{7,3},{8,4},{9,5},{1... | collective-permute-start | bytes 786440 | tf_op jit(solution)/shard_map/ppermute | solution.py:155
  241.3 32.6 %collective-permute-start.34 = (bf16[4,128,1024]{2,1,0:T(8,128)(2,1)}, bf16[4,128,1024]{2,1,0:T(8,128)(2,1)S(1)}, u32[]{:S(2)}, u32[]{:S(2)}) collective-permute-start(bf16[4,128,1024]{2,1,0:T(8,128)(2,1)} %get-tuple-element.98), channel_id=1, source_target_pairs={{0,4},{1,5},{2,6},{3,7},{4,8},{5,9},{6,10},{7,11},{8,12},{9,13},{1... | collective-permute-start | bytes 3145736 | tf_op jit(solution)/shard_map/ppermute | solution.py:155
  241.8 32.0 %collective-permute-start.35 = (bf16[4,128,1024]{2,1,0:T(8,128)(2,1)}, bf16[4,128,1024]{2,1,0:T(8,128)(2,1)}, u32[]{:S(2)}, u32[]{:S(2)}) collective-permute-start(bf16[4,128,1024]{2,1,0:T(8,128)(2,1)} %get-tuple-element.99), channel_id=1, source_target_pairs={{0,12},{1,13},{2,14},{3,15},{4,0},{5,1},{6,2},{7,3},{8,4},{9,5},{1... | collective-permute-start | bytes 3145736 | tf_op jit(solution)/shard_map/ppermute | solution.py:155
  244.2 29.7 %collective-permute-start.30 = (bf16[4,128,1024]{2,1,0:T(8,128)(2,1)}, bf16[4,128,1024]{2,1,0:T(8,128)(2,1)S(1)}, u32[]{:S(2)}, u32[]{:S(2)}) collective-permute-start(bf16[4,128,1024]{2,1,0:T(8,128)(2,1)} %get-tuple-element.94), channel_id=1, source_target_pairs={{0,1},{1,2},{2,3},{3,0},{4,5},{5,6},{6,7},{7,4},{8,9},{9,10},{10,1... | collective-permute-start | bytes 3145736 | tf_op jit(solution)/shard_map/ppermute | solution.py:155
  244.5 29.4 %collective-permute-start.31 = (bf16[4,128,1024]{2,1,0:T(8,128)(2,1)}, bf16[4,128,1024]{2,1,0:T(8,128)(2,1)}, u32[]{:S(2)}, u32[]{:S(2)}) collective-permute-start(bf16[4,128,1024]{2,1,0:T(8,128)(2,1)} %get-tuple-element.95), channel_id=1, source_target_pairs={{0,3},{1,0},{2,1},{3,2},{4,7},{5,4},{6,5},{7,6},{8,11},{9,8},{10,9... | collective-permute-start | bytes 3145736 | tf_op jit(solution)/shard_map/ppermute | solution.py:155
  (45 other events, 474.7 us)

commit v6 on v4

--- a/solution.py
+++ b/solution.py
@@ -8,7 +8,6 @@
 SIDE = 4
 CORES = 2
 F32 = jnp.float32
-LONG_CHAIN = 10**11
 RING_VMEM = 52 * 2**20
 
 
@@ -108,33 +107,34 @@
     )(*pieces, matrix)
 
 
-def by_supernode(order, rows, matrix, part, split):
+def by_supernode(order, rows, matrix, part):
     block, depth = rows.shape[1:]
     width = matrix.shape[1] // 2
     groups = order.shape[0] // SIDE
-    outs = 2 if split else 1
-    size = block // outs
 
     def kernel(order_ref, a_ref, b_ref, c_ref, d_ref, matrix_ref, *out):
         left = jnp.concatenate([a_ref[0], b_ref[0], c_ref[0], d_ref[0]], 0)
         total = jnp.dot(left, matrix_ref[...], preferred_element_type=F32)
-        total = total.reshape(SIDE, block, width)
-        for i, ref in enumerate(out):
-            ref[0] = total[:, i * size : (i + 1) * size].astype(ref.dtype)
+        value = total.reshape(SIDE, block, width).astype(rows.dtype)
+        for g in range(groups):
+
+            @pl.when(pl.program_id(0) == g)
+            def _():
+                out[g][...] = value
 
     def pick(j):
         return pl.BlockSpec((1, block, depth), lambda i, order_ref: (order_ref[SIDE * i + j], 0, 0))
 
     return pl.pallas_call(
         kernel,
-        out_shape=[jax.ShapeDtypeStruct((groups, SIDE, size, width), rows.dtype)] * outs,
+        out_shape=[jax.ShapeDtypeStruct((SIDE, block, width), rows.dtype)] * groups,
         grid_spec=pltpu.PrefetchScalarGridSpec(
             num_scalar_prefetch=1,
             grid=(groups,),
             in_specs=[pick(j) for j in range(SIDE)]
             + [pl.BlockSpec((depth, width), lambda i, order_ref: (0, part))],
-            out_specs=[pl.BlockSpec((1, SIDE, size, width), lambda i, order_ref: (i, 0, 0, 0))]
-            * outs,
+            out_specs=[pl.BlockSpec((SIDE, block, width), lambda i, order_ref: (0, 0, 0))]
+            * groups,
         ),
         compiler_params=pltpu.CompilerParams(vmem_limit_bytes=RING_VMEM),
         cost_estimate=pl.CostEstimate(
@@ -149,42 +149,23 @@
     return lax.ppermute(value, "col", step)
 
 
-def second_sends(arriving, near, step):
-    _, _, block, width = near.shape
-    half = block // 2
-
-    def kernel(low_ref, high_ref, ahead_ref, behind_ref, ahead_out, behind_out):
-        kind = ahead_out.dtype
-        low = ahead_ref[0, 0, :half].astype(F32) + low_ref[0].astype(F32)
-        high = behind_ref[0, 0, half:].astype(F32) + high_ref[0].astype(F32)
-        ahead_out[0, :half] = low.astype(kind)
-        ahead_out[0, half:] = ahead_ref[0, 0, half:]
-        behind_out[0, :half] = behind_ref[0, 0, :half]
-        behind_out[0, half:] = high.astype(kind)
-
-    part = pl.BlockSpec((1, half, width), lambda i: (i, 0, 0))
-    own = [pl.BlockSpec((1, 1, block, width), lambda i, g=g: (g, i, 0, 0)) for g in range(2)]
-    full = pl.BlockSpec((1, block, width), lambda i: (i, 0, 0))
-    ahead, behind = pl.pallas_call(
-        kernel,
-        out_shape=[jax.ShapeDtypeStruct((SIDE, block, width), near.dtype)] * 2,
-        grid=(SIDE,),
-        in_specs=[part, part, *own],
-        out_specs=[full, full],
-        compiler_params=pltpu.CompilerParams(vmem_limit_bytes=RING_VMEM),
-        cost_estimate=pl.CostEstimate(flops=0, bytes_accessed=2**22, transcendentals=0),
-    )(*arriving, near, near)
-    return send(ahead, step(1)), send(behind, step(-1))
-
-
-def third_sends(arriving, near, step):
-    _, _, block, width = near.shape
-    kind = near.dtype
+def first_sends(product, order, step):
+    order = order.reshape(SIDE, -1)
+    (far,) = product(order[2])
+    rest, far = lax.optimization_barrier((jnp.concatenate([order[1], order[3], order[0]]), far))
+    ahead, behind, own = product(rest)
+    return [send(far, step(2)), send(ahead, step(1)), send(behind, step(-1))], own
+
+
+def second_sends(arriving, own, step):
+    _, block, width = own.shape
+    kind = own.dtype
     tile = width // SIDE
 
-    def kernel(one_ref, two_ref, own_ref, own_out, *out):
+    def kernel(one_ref, two_ref, three_ref, own_ref, own_out, *out):
         for d in range(SIDE):
-            total = own_ref[0, d].astype(F32) + one_ref[d].astype(F32) + two_ref[d].astype(F32)
+            total = own_ref[d].astype(F32) + one_ref[d].astype(F32)
+            total = total + two_ref[d].astype(F32) + three_ref[d].astype(F32)
             if d:
                 out[d - 1][...] = total.astype(kind)
             else:
@@ -192,17 +173,17 @@
 
     four = pl.BlockSpec((SIDE, block, tile), lambda i: (0, 0, i))
     one = pl.BlockSpec((block, tile), lambda i: (0, i))
-    own, *others = pl.pallas_call(
+    kept, *others = pl.pallas_call(
         kernel,
         out_shape=[jax.ShapeDtypeStruct((block, width), F32)]
         + [jax.ShapeDtypeStruct((block, width), kind)] * 3,
         grid=(SIDE,),
-        in_specs=[four, four, pl.BlockSpec((1, SIDE, block, tile), lambda i: (2, 0, 0, i))],
+        in_specs=[four] * 4,
         out_specs=[one] * 4,
         compiler_params=pltpu.CompilerParams(vmem_limit_bytes=RING_VMEM),
         cost_estimate=pl.CostEstimate(flops=0, bytes_accessed=2**22, transcendentals=0),
-    )(*arriving, near)
-    return [own] + [send(v, step(d + 1)) for d, v in enumerate(others)]
+    )(*arriving, own)
+    return [kept] + [send(v, step(d + 1)) for d, v in enumerate(others)]
 
 
 def row_parts(values):
@@ -215,7 +196,7 @@
     return pl.BlockSpec(shape, lambda i: (0,) * len(shape))
 
 
-def small_call(kernel, shapes, scalars, arrays, scratch=(), flops=0):
+def small_call(kernel, shapes, scalars, arrays, scratch=()):
     return pl.pallas_call(
         kernel,
         out_shape=[jax.ShapeDtypeStruct(shape, kind) for shape, kind in shapes],
@@ -225,7 +206,7 @@
         out_specs=[whole(shape) for shape, _ in shapes],
         scratch_shapes=list(scratch),
         compiler_params=pltpu.CompilerParams(vmem_limit_bytes=RING_VMEM),
-        cost_estimate=pl.CostEstimate(flops=flops, bytes_accessed=2**20, transcendentals=0),
+        cost_estimate=pl.CostEstimate(flops=0, bytes_accessed=2**20, transcendentals=0),
     )(*scalars, *arrays)
 
 
@@ -243,7 +224,6 @@
         [((count, 2, block, block), jnp.bfloat16)],
         [place, readers, pattern],
         [total],
-        flops=LONG_CHAIN,
     )[0]
 
 
@@ -352,17 +332,28 @@
     masked_two = apply_pattern(level_two_panels, level_two_pattern, block)
 
     found_one = all_panels(in_order([turned_panels(masked_one, k) for k in range(2)]))
-    later_two, _ = lax.optimization_barrier((masked_two, found_one[2:6:2]))
-    early_two = turned_panels(later_two, 0)
-    early_two, found_one = lax.optimization_barrier((early_two, found_one))
+    later_two, found_one = lax.optimization_barrier((masked_two, found_one))
+    own_two = in_order([turned_panels(later_two, k) for k in range(2)])
     product_one = by_column(found_one, ancestor_inverse, block)
-    later_two, product_one = lax.optimization_barrier((masked_two, product_one))
-    own_two = in_order([early_two, turned_panels(later_two, 1)])
-    later_one, own_two = lax.optimization_barrier((masked_one, own_two))
     first_sum = lax.psum_scatter(
         product_one.reshape(count * count * block, block), "col", scatter_dimension=0, tiled=True
     ).reshape(count, block, block)
 
+    steps = jnp.arange(count, dtype=jnp.int32)
+    place = arrival(steps)
+    outer, inner = steps // SIDE, steps % SIDE
+    x_major = (y + inner) % SIDE * SIDE + (x + outer) % SIDE
+    y_major = (y + outer) % SIDE * SIDE + (x + inner) % SIDE
+
+    rows_two = jnp.concatenate(all_panels(own_two), 0)
+
+    def product(part):
+        return lambda order: by_supernode(place[order], rows_two, ancestor_inverse, part)
+
+    coming_a, own_a = first_sends(product(0), x_major, x_step)
+    coming_b, own_b = first_sends(product(1), y_major, y_step)
+
+    later_one, _ = lax.optimization_barrier((masked_one, rows_two))
     facts = jnp.concatenate(
         [
             jnp.broadcast_to(level_one_pattern.reshape(count, 1, 1), (count, 8, block)),
@@ -377,30 +368,13 @@
     parent_panels = lax.all_to_all(
         jnp.take(cut[:, :block], readers, axis=0), "col", 0, 0, tiled=True
     )
-    rows_two = lax.all_gather(own_two, "row", axis=0, tiled=True)
-
-    steps = jnp.arange(count, dtype=jnp.int32)
-    place = arrival(steps)
-    outer, inner = steps // SIDE, steps % SIDE
-    x_major = (y + inner) % SIDE * SIDE + (x + outer) % SIDE
-    y_major = (y + outer) % SIDE * SIDE + (x + inner) % SIDE
-
-    def ring(order, part, step):
-        order = order.reshape(SIDE, -1)
-        low, high = by_supernode(order[2], rows_two, ancestor_inverse, part, True)
-        arriving = send(low[0], step(1)), send(high[0], step(-1))
-        rest = jnp.concatenate([order[1], order[3], order[0]])
-        return arriving, by_supernode(rest, rows_two, ancestor_inverse, part, False)[0]
-
-    first_a, near_a = ring(x_major, 0, x_step)
-    first_b, near_b = ring(y_major, 1, y_step)
-    first_a, first_b, parent_panels = lax.optimization_barrier((first_a, first_b, parent_panels))
-    second_a = second_sends(first_a, near_a, x_step)
-    second_b = second_sends(first_b, near_b, y_step)
+
     going = outgoing(place, readers, cut_pattern, first_sum)
     back = lax.all_to_all(going, "col", 0, 0, tiled=True)
-    second_a, second_b, _ = lax.optimization_barrier((second_a, second_b, going))
-    second_sum = third_sends(second_a, near_a, y_step) + third_sends(second_b, near_b, x_step)
+    coming_a, coming_b, parent_panels, _ = lax.optimization_barrier(
+        (coming_a, coming_b, parent_panels, going)
+    )
+    second_sum = second_sends(coming_a, own_a, y_step) + second_sends(coming_b, own_b, x_step)
     level_one_rows, level_two_rows, sums = finish_rows(
         level_two_pattern, back, parent_panels, masked_one, masked_two, parent_lead, second_sum
     )

time: 288 us -> 300 us (1.042)
  starting transfers between devices: 106 us -> 119 us
  local copies, waits for them, and re-layouts: 9.2 us -> 21.7 us
  waiting for transfers between devices: 91.1 us -> 80.8 us
  Pallas kernels: 58.6 us -> 51.8 us
    all_to_all x1, starting transfers between devices: 22.6 us -> 6.09 us  [per_device(): lax.all_to_all(jnp.concatenate([cut, facts], 1), 'col', 0, 0, tiled=True)]
    all_to_all x1, waiting for transfers between devices: 0.01 us -> 15.3 us  [per_device(): lax.all_to_all(jnp.take(cut[:, :block], readers, axis=0), 'col', 0, 0, ti...]
    ppermute x4 -> x8, starting transfers between devices: 14.4 us -> 28.7 us  [all_panels(): found += [held, lax.ppermute(held, 'row', CORE_SWAP)]]
    all_to_all x1, waiting for transfers between devices: 14.1 us -> 0.01 us  [per_device(): lax.all_to_all(jnp.concatenate([cut, facts], 1), 'col', 0, 0, tiled=True)]
    ppermute x1 -> x2, starting transfers between devices: 0.01 us -> 9.68 us  [all_panels(): below = lax.ppermute(own, 'row', z_step(1))]
    ppermute x14 -> x12, waiting for transfers between devices: 18.9 us -> 9.88 us  [send(): return lax.ppermute(value, 'col', step)]
    pallas_call x8 -> x6, Pallas kernels: 37.2 us -> 30.4 us  [the longest x4 24.1 us: by_supernode(): pl.pallas_call(kernel, out_shape=[jax.ShapeDtypeStruct((SIDE, block, widt...]
    reduce_scatter x1, waiting for transfers between devices: 24.6 us -> 18.2 us  [per_device(): lax.psum_scatter(product_one.reshape(count * count * block, block), 'col'...]
  transfers between devices with their start and end apart: 35 -> 40, of which waited for: 19 -> 17; matrix products, arithmetic and copies ran while one was open for 2% -> 8% of each run, Pallas kernels for 14% -> 11%
where the time goes in v6:
time: 300 us; the launch traced here: 297 us
  starting transfers between devices  119 us (40%)
  waiting for transfers between devices  80.8 us (27%)
  Pallas kernels  51.8 us (17%)
  local copies, waits for them, and re-layouts  21.7 us (7%)
  between operations  15.2 us (5%)
  other arithmetic  8.26 us (3%)
    ppermute x8, starting transfers between devices, all_panels(): found += [held, lax.ppermute(held, 'row', CORE_SWAP)]  28.7 us
    pallas_call x4, Pallas kernels, by_supernode(): pl.pallas_call(kernel, out_shape=[jax.ShapeDtypeStruct((SIDE, block, widt...  24.1 us
    ppermute x12, starting transfers between devices, send(): return lax.ppermute(value, 'col', step)  21.7 us
    reduce_scatter x1, waiting for transfers between devices, per_device(): lax.psum_scatter(product_one.reshape(count * count * block, block), 'col'...  18.2 us
    ppermute x4, waiting for transfers between devices, turned_panels(): return lax.ppermute(part, ('row', 'col'), turn(k))  17.1 us
    ppermute x2, starting transfers between devices, all_panels(): above = lax.ppermute(own, 'row', z_step(-1))  15.5 us
    all_to_all x1, waiting for transfers between devices, per_device(): lax.all_to_all(jnp.take(cut[:, :block], readers, axis=0), 'col', 0, 0, ti...  15.3 us
    pallas_call x1, Pallas kernels, by_column(): pl.pallas_call(kernel, out_shape=jax.ShapeDtypeStruct((width // block, st...  14.7 us
  transfers between devices with their start and end apart: 40, of which 17 were waited for; matrix products, arithmetic and copies ran while one was open for 8% of the time, Pallas kernels for 11%

profile of v6, /device:TPU:1, one launch (start us, length us, event | category | flops | bytes accessed | tf_op | source)
XLA Modules:
  0.0 296.9 jit_solution(15659876951879759192)
XLA Ops:
  9.2 6.0 %collective-permute-start = (bf16[128,1024]{1,0:T(8,128)(2,1)S(1)}, bf16[128,1024]{1,0:T(8,128)(2,1)S(1)}, u32[]{:S(2)}, u32[]{:S(2)}) collective-permute-start(bf16[128,1024]{1,0:T(8,128)(2,1)S(1)} %get-tuple-element.99), channel_id=1, source_target_pairs={{0,0},{1,1},{2,16},{3,17},{4,32},{5,33},{6,48},{7,49},{8,64},{9,65... | collective-permute-start | bytes 786440 | tf_op jit(solution)/shard_map/ppermute | solution.py:46
  15.9 5.2 %collective-permute-done = bf16[128,1024]{1,0:T(8,128)(2,1)S(1)} collective-permute-done((bf16[128,1024]{1,0:T(8,128)(2,1)S(1)}, bf16[128,1024]{1,0:T(8,128)(2,1)S(1)}, u32[]{:S(2)}, u32[]{:S(2)}) %collective-permute-start) | collective-permute-done | bytes 262176 | tf_op jit(solution)/shard_map/ppermute | solution.py:46
  23.7 15.4 %collective-permute-start.5 = (bf16[2,128,1024]{2,1,0:T(8,128)(2,1)S(1)}, bf16[2,128,1024]{2,1,0:T(8,128)(2,1)S(1)}, u32[]{:S(2)}, u32[]{:S(2)}) collective-permute-start(bf16[2,128,1024]{2,1,0:T(8,128)(2,1)S(1)} %pad_maximum_fusion.refs_0_), channel_id=1, source_target_pairs={{0,96},{16,112},{32,0},{48,16},{64,32},{80,48},{96,64},{112,80},{1... | collective-permute-start | bytes 1572872 | tf_op jit(solution)/shard_map/ppermute | solution.py:58
  39.1 8.9 %collective-permute-done.5.refs_4_ = bf16[2,128,1024]{2,1,0:T(8,128)(2,1)S(1)} collective-permute-done((bf16[2,128,1024]{2,1,0:T(8,128)(2,1)S(1)}, bf16[2,128,1024]{2,1,0:T(8,128)(2,1)S(1)}, u32[]{:S(2)}, u32[]{:S(2)}) %collective-permute-start.5) | collective-permute-done | bytes 524320 | tf_op jit(solution)/shard_map/ppermute | solution.py:58
  48.0 3.5 %collective-permute-start.8 = (bf16[128,1024]{1,0:T(8,128)(2,1)S(1)}, bf16[128,1024]{1,0:T(8,128)(2,1)S(1)}, u32[]{:S(2)}, u32[]{:S(2)}) collective-permute-start(bf16[128,1024]{1,0:T(8,128)(2,1)S(1)} %slice_bitcast_fusion.2), channel_id=1, source_target_pairs={{0,96},{16,112},{32,0},{48,16},{64,32},{80,48},{96,64},{112,80},{1... | collective-permute-start | bytes 786440 | tf_op jit(solution)/shard_map/ppermute | solution.py:60
  51.6 6.9 %collective-permute-start.2 = (bf16[2,128,1024]{2,1,0:T(8,128)(2,1)S(1)}, bf16[2,128,1024]{2,1,0:T(8,128)(2,1)S(1)}, u32[]{:S(2)}, u32[]{:S(2)}) collective-permute-start(bf16[2,128,1024]{2,1,0:T(8,128)(2,1)S(1)} %pad_maximum_fusion.refs_0_), channel_id=1, source_target_pairs={{0,16},{16,0},{32,48},{48,32},{64,80},{80,64},{96,112},{112,96},{1... | collective-permute-start | bytes 1572872 | tf_op jit(solution)/shard_map/ppermute | solution.py:64
  59.2 7.0 %collective-permute-start.9 = (bf16[2,128,1024]{2,1,0:T(8,128)(2,1)S(1)}, bf16[2,128,1024]{2,1,0:T(8,128)(2,1)S(1)}, u32[]{:S(2)}, u32[]{:S(2)}) collective-permute-start(bf16[2,128,1024]{2,1,0:T(8,128)(2,1)S(1)} %pad_maximum_fusion.1.refs_6_), channel_id=1, source_target_pairs={{0,16},{16,0},{32,48},{48,32},{64,80},{80,64},{96,112},{112,96},{1... | collective-permute-start | bytes 1572872 | tf_op jit(solution)/shard_map/ppermute | solution.py:64
  68.5 14.7 %shard_map.137 = bf16[16,2048,128]{2,1,0:T(8,128)(2,1)} custom-call(bf16[2,128,1024]{2,1,0:T(8,128)(2,1)S(1)} %pad_maximum_fusion.refs_0_, bf16[2,128,1024]{2,1,0:T(8,128)(2,1)S(1)} %collective-permute-done.2.refs_1_, bf16[2,128,1024]{2,1,0:T(8,128)(2,1)S(1)} %collective-permute-done.3.refs_2_, bf16[2,128,1024]{2,1,0:T(8,128)(2,1)} %copy-done.13, ...), custom_call_target="tpu_custom_call" | custom-call | flops 8589934592 | bytes 16777216 | tf_op jit(solution)/shard_map/pallas_call | solution.py:93
  83.5 4.3 %collective-permute-start.10 = (bf16[128,1024]{1,0:T(8,128)(2,1)S(1)}, bf16[128,1024]{1,0:T(8,128)(2,1)S(1)}, u32[]{:S(2)}, u32[]{:S(2)}) collective-permute-start(bf16[128,1024]{1,0:T(8,128)(2,1)S(1)} %get-tuple-element.96), channel_id=1, source_target_pairs={{0,0},{1,1},{2,16},{3,17},{4,32},{5,33},{6,48},{7,49},{8,64},{9,65... | collective-permute-start | bytes 786440 | tf_op jit(solution)/shard_map/ppermute | solution.py:46
  90.1 3.7 %collective-permute-done.10 = bf16[128,1024]{1,0:T(8,128)(2,1)S(1)} collective-permute-done((bf16[128,1024]{1,0:T(8,128)(2,1)S(1)}, bf16[128,1024]{1,0:T(8,128)(2,1)S(1)}, u32[]{:S(2)}, u32[]{:S(2)}) %collective-permute-start.10) | collective-permute-done | bytes 262176 | tf_op jit(solution)/shard_map/ppermute | solution.py:46
  93.8 5.7 %collective-permute-done.11 = bf16[128,1024]{1,0:T(8,128)(2,1)S(1)} collective-permute-done((bf16[128,1024]{1,0:T(8,128)(2,1)S(1)}, bf16[128,1024]{1,0:T(8,128)(2,1)S(1)}, u32[]{:S(2)}, u32[]{:S(2)}) %collective-permute-start.11) | collective-permute-done | bytes 262176 | tf_op jit(solution)/shard_map/ppermute | solution.py:46
  101.0 9.7 %collective-permute-start.13 = (bf16[2,128,1024]{2,1,0:T(8,128)(2,1)S(1)}, bf16[2,128,1024]{2,1,0:T(8,128)(2,1)S(1)}, u32[]{:S(2)}, u32[]{:S(2)}) collective-permute-start(bf16[2,128,1024]{2,1,0:T(8,128)(2,1)S(1)} %pad_maximum_fusion.2), channel_id=1, source_target_pairs={{0,32},{16,48},{32,64},{48,80},{64,96},{80,112},{96,0},{112,16},{1... | collective-permute-start | bytes 1572872 | tf_op jit(solution)/shard_map/ppermute | solution.py:57
  110.9 8.9 %collective-permute-start.12 = (bf16[2,128,1024]{2,1,0:T(8,128)(2,1)S(1)}, bf16[2,128,1024]{2,1,0:T(8,128)(2,1)}, u32[]{:S(2)}, u32[]{:S(2)}) collective-permute-start(bf16[2,128,1024]{2,1,0:T(8,128)(2,1)S(1)} %pad_maximum_fusion.2), channel_id=1, source_target_pairs={{0,16},{16,0},{32,48},{48,32},{64,80},{80,64},{96,112},{112,96},{1... | collective-permute-start | bytes 1572872 | tf_op jit(solution)/shard_map/ppermute | solution.py:64
  120.1 4.7 %collective-permute-start.17 = (bf16[128,1024]{1,0:T(8,128)(2,1)S(1)}, bf16[128,1024]{1,0:T(8,128)(2,1)S(1)}, u32[]{:S(2)}, u32[]{:S(2)}) collective-permute-start(bf16[128,1024]{1,0:T(8,128)(2,1)S(1)} %slice_bitcast_fusion.1), channel_id=1, source_target_pairs={{0,32},{16,48},{32,64},{48,80},{64,96},{80,112},{96,0},{112,16},{1... | collective-permute-start | bytes 786440 | tf_op jit(solution)/shard_map/ppermute | solution.py:60
  124.9 4.1 %collective-permute-start.14 = (bf16[2,128,1024]{2,1,0:T(8,128)(2,1)S(1)}, bf16[2,128,1024]{2,1,0:T(8,128)(2,1)S(1)}, u32[]{:S(2)}, u32[]{:S(2)}) collective-permute-start(bf16[2,128,1024]{2,1,0:T(8,128)(2,1)S(1)} %collective-permute-done.13), channel_id=1, source_target_pairs={{0,16},{16,0},{32,48},{48,32},{64,80},{80,64},{96,112},{112,96},{1... | collective-permute-start | bytes 1572872 | tf_op jit(solution)/shard_map/ppermute | solution.py:64
  145.5 6.1 %all-to-all-start = ((bf16[16,144,128]{2,1,0:T(8,128)(2,1)}), bf16[16,144,128]{2,1,0:T(8,128)(2,1)}, u32[]{:S(2)}, u32[]{:S(2)}) async-start(bf16[16,144,128]{2,1,0:T(8,128)(2,1)} %fusion.1), calls=%async_computation | async-start | bytes 1179648 | tf_op jit(solution)/shard_map/all_to_all | solution.py:365
  151.6 3.8 %shard_map.139 = bf16[4,128,1024]{2,1,0:T(8,128)(2,1)S(1)} custom-call(s32[4]{0:T(128)S(1)} %gather_fusion.1, bf16[16,128,1024]{2,1,0:T(8,128)(2,1)} %constant_dynamic-update-slice_fusion.a_ref.b_ref.c_ref.d_ref, bf16[16,128,1024]{2,1,0:T(8,128)(2,1)} %constant_dynamic-update-slice_fusion.a_ref.b_ref.c_ref.d_ref, ...), custom_call_target="tpu_custom_call" | custom-call | flops 1073741824 | bytes 2097152 | tf_op jit(solution)/shard_map/pallas_call | solution.py:128
  158.9 8.1 %shard_map.140 = (bf16[4,128,1024]{2,1,0:T(8,128)(2,1)S(1)}, bf16[4,128,1024]{2,1,0:T(8,128)(2,1)}, bf16[4,128,1024]{2,1,0:T(8,128)(2,1)}) custom-call(s32[12]{0:T(128)S(1)} %gather_fusion.2, bf16[16,128,1024]{2,1,0:T(8,128)(2,1)} %constant_dynamic-update-slice_fusion.a_ref.b_ref.c_ref.d_ref, ...), custom_call_target="tpu_custom_call" | custom-call | flops 3221225472 | bytes 6291456 | tf_op jit(solution)/shard_map/pallas_call | solution.py:128
  169.7 3.7 %shard_map.141 = bf16[4,128,1024]{2,1,0:T(8,128)(2,1)S(1)} custom-call(s32[4]{0:T(128)S(1)} %gather_fusion.3, bf16[16,128,1024]{2,1,0:T(8,128)(2,1)} %constant_dynamic-update-slice_fusion.a_ref.b_ref.c_ref.d_ref, bf16[16,128,1024]{2,1,0:T(8,128)(2,1)} %constant_dynamic-update-slice_fusion.a_ref.b_ref.c_ref.d_ref, ...), custom_call_target="tpu_custom_call" | custom-call | flops 1073741824 | bytes 2097152 | tf_op jit(solution)/shard_map/pallas_call | solution.py:128
  176.9 8.4 %shard_map.142 = (bf16[4,128,1024]{2,1,0:T(8,128)(2,1)}, bf16[4,128,1024]{2,1,0:T(8,128)(2,1)}, bf16[4,128,1024]{2,1,0:T(8,128)(2,1)}) custom-call(s32[12]{0:T(128)S(1)} %gather_fusion.4, bf16[16,128,1024]{2,1,0:T(8,128)(2,1)} %constant_dynamic-update-slice_fusion.a_ref.b_ref.c_ref.d_ref, ...), custom_call_target="tpu_custom_call" | custom-call | flops 3221225472 | bytes 6291456 | tf_op jit(solution)/shard_map/pallas_call | solution.py:128
  195.8 4.2 %all-to-all-start.2 = ((bf16[16,128,128]{2,1,0:T(8,128)(2,1)}), bf16[16,128,128]{2,1,0:T(8,128)(2,1)}, u32[]{:S(2)}, u32[]{:S(2)}) async-start(bf16[16,128,128]{2,1,0:T(8,128)(2,1)} %broadcast_select_fusion), calls=%async_computation.3 | async-start | bytes 1048576 | tf_op jit(solution)/shard_map/all_to_all | solution.py:368
  200.1 18.2 %reduce-scatter.2.cloned.1.call-done = bf16[2048,128]{1,0:T(8,128)(2,1)} async-done(((bf16[32768,128]{1,0:T(8,128)(2,1)}), bf16[2048,128]{1,0:T(8,128)(2,1)}) %reduce-scatter.2.cloned.1.call-update) | async-done | bytes 524304 | tf_op jit(solution)/shard_map/reduce_scatter | solution.py:338
  221.0 15.3 %all-to-all-done.2.panels_ref = bf16[16,128,128]{2,1,0:T(8,128)(2,1)} async-done(((bf16[16,128,128]{2,1,0:T(8,128)(2,1)}), bf16[16,128,128]{2,1,0:T(8,128)(2,1)}, u32[]{:S(2)}, u32[]{:S(2)}) %all-to-all-start.2) | async-done | bytes 524320 | tf_op jit(solution)/shard_map/all_to_all | solution.py:368
  236.4 4.1 %all-to-all-start.1 = ((bf16[16,2,128,128]{3,2,1,0:T(8,128)(2,1)}), bf16[16,2,128,128]{3,2,1,0:T(8,128)(2,1)S(1)}, u32[]{:S(2)}, u32[]{:S(2)}) async-start(bf16[16,2,128,128]{3,2,1,0:T(8,128)(2,1)} %shard_map.138), calls=%async_computation.2 | async-start | bytes 2097152 | tf_op jit(solution)/shard_map/all_to_all | solution.py:373
  240.5 3.2 %shard_map.143 = (f32[128,1024]{1,0:T(8,128)S(1)}, bf16[128,1024]{1,0:T(8,128)(2,1)S(1)}, bf16[128,1024]{1,0:T(8,128)(2,1)S(1)}, bf16[128,1024]{1,0:T(8,128)(2,1)S(1)}) custom-call(bf16[4,128,1024]{2,1,0:T(8,128)(2,1)} %collective-permute-done.20.one_ref, bf16[4,128,1024]{2,1,0:T(8,128)(2,1)} %collective-permute-done.21.two_ref, ...), custom_call_target="tpu_custom_call" | custom-call | bytes 4194304 | tf_op jit(solution)/shard_map/pallas_call | solution.py:176
  249.5 3.2 %shard_map.144 = (f32[128,1024]{1,0:T(8,128)S(1)}, bf16[128,1024]{1,0:T(8,128)(2,1)S(1)}, bf16[128,1024]{1,0:T(8,128)(2,1)S(1)}, bf16[128,1024]{1,0:T(8,128)(2,1)S(1)}) custom-call(bf16[4,128,1024]{2,1,0:T(8,128)(2,1)} %collective-permute-done.23.one_ref, bf16[4,128,1024]{2,1,0:T(8,128)(2,1)} %collective-permute-done.24.two_ref, ...), custom_call_target="tpu_custom_call" | custom-call | bytes 4194304 | tf_op jit(solution)/shard_map/pallas_call | solution.py:176
  257.0 4.7 %collective-permute-done.26.refs_1_ = bf16[128,1024]{1,0:T(8,128)(2,1)S(1)} collective-permute-done((bf16[128,1024]{1,0:T(8,128)(2,1)S(1)}, bf16[128,1024]{1,0:T(8,128)(2,1)S(1)}, u32[]{:S(2)}, u32[]{:S(2)}) %collective-permute-start.26) | collective-permute-done | bytes 262176 | tf_op jit(solution)/shard_map/ppermute | solution.py:149
  263.9 3.4 %collective-permute-done.27.refs_2_ = bf16[128,1024]{1,0:T(8,128)(2,1)S(1)} collective-permute-done((bf16[128,1024]{1,0:T(8,128)(2,1)S(1)}, bf16[128,1024]{1,0:T(8,128)(2,1)S(1)}, u32[]{:S(2)}, u32[]{:S(2)}) %collective-permute-start.27) | collective-permute-done | bytes 262176 | tf_op jit(solution)/shard_map/ppermute | solution.py:149
  270.1 3.6 %shard_map.145 = (bf16[128,2048]{1,0:T(8,128)(2,1)}, bf16[128,2048]{1,0:T(8,128)(2,1)}, f32[4,128,128]{2,1,0:T(8,128)S(1)}) custom-call(s32[1,16]{1,0:T(1,128)S(1)} %copy-done.5, bf16[16,2,128,128]{3,2,1,0:T(8,128)(2,1)} %copy-done.9, bf16[16,128,128]{2,1,0:T(8,128)(2,1)} %all-to-all-done.2.panels_ref, bf16[128,2048]{1,0:T(8,128)(2,1)} %copy-done.7, ...), custom_call_target="tpu_custom_call" | custom-call | bytes 1048576 | tf_op jit(solution)/shard_map/pallas_call | solution.py:200
  276.3 3.4 %collective-permute-start.33 = (bf16[4,128,128]{2,1,0:T(8,128)(2,1)S(1)}, bf16[4,128,128]{2,1,0:T(8,128)(2,1)S(1)}, u32[]{:S(2)}, u32[]{:S(2)}) collective-permute-start(bf16[4,128,128]{2,1,0:T(8,128)(2,1)S(1)} %add_convert_fusion.a), channel_id=1, source_target_pairs={{0,96},{16,112},{32,0},{48,16},{64,32},{80,48},{96,64},{112,80},{1... | collective-permute-start | bytes 393224 | tf_op jit(solution)/shard_map/ppermute | solution.py:192
  281.2 3.8 %collective-permute-done.33.b = bf16[4,128,128]{2,1,0:T(8,128)(2,1)S(1)} collective-permute-done((bf16[4,128,128]{2,1,0:T(8,128)(2,1)S(1)}, bf16[4,128,128]{2,1,0:T(8,128)(2,1)S(1)}, u32[]{:S(2)}, u32[]{:S(2)}) %collective-permute-start.33) | collective-permute-done | bytes 131104 | tf_op jit(solution)/shard_map/ppermute | solution.py:192
  285.6 3.2 %collective-permute-done.35.d = bf16[4,128,128]{2,1,0:T(8,128)(2,1)S(1)} collective-permute-done((bf16[4,128,128]{2,1,0:T(8,128)(2,1)S(1)}, bf16[4,128,128]{2,1,0:T(8,128)(2,1)S(1)}, u32[]{:S(2)}, u32[]{:S(2)}) %collective-permute-start.35) | collective-permute-done | bytes 131104 | tf_op jit(solution)/shard_map/ppermute | solution.py:192
  (149 shorter events, 72.6 us)
Async XLA Ops:
  7.2 211.1 %reduce-scatter.2.cloned.1.call-start = ((), (), s32[]{:S(2)}) async-start(), calls=%async_computation.4 | async-start | bytes 8912896 | tf_op jit(solution)/shard_map/reduce_scatter | solution.py:338
  9.2 11.9 %collective-permute-start = (bf16[128,1024]{1,0:T(8,128)(2,1)S(1)}, bf16[128,1024]{1,0:T(8,128)(2,1)S(1)}, u32[]{:S(2)}, u32[]{:S(2)}) collective-permute-start(bf16[128,1024]{1,0:T(8,128)(2,1)S(1)} %get-tuple-element.99), channel_id=1, source_target_pairs={{0,0},{1,1},{2,16},{3,17},{4,32},{5,33},{6,48},{7,49},{8,64},{9,65... | collective-permute-start | bytes 786440 | tf_op jit(solution)/shard_map/ppermute | solution.py:46
  15.2 8.4 %collective-permute-start.1 = (bf16[128,1024]{1,0:T(8,128)(2,1)S(1)}, bf16[128,1024]{1,0:T(8,128)(2,1)S(1)}, u32[]{:S(2)}, u32[]{:S(2)}) collective-permute-start(bf16[128,1024]{1,0:T(8,128)(2,1)S(1)} %get-tuple-element.100), channel_id=1, source_target_pairs={{0,1},{1,0},{2,17},{3,16},{4,33},{5,32},{6,49},{7,48},{8,65},{9,64... | collective-permute-start | bytes 786440 | tf_op jit(solution)/shard_map/ppermute | solution.py:46
  23.7 24.3 %collective-permute-start.5 = (bf16[2,128,1024]{2,1,0:T(8,128)(2,1)S(1)}, bf16[2,128,1024]{2,1,0:T(8,128)(2,1)S(1)}, u32[]{:S(2)}, u32[]{:S(2)}) collective-permute-start(bf16[2,128,1024]{2,1,0:T(8,128)(2,1)S(1)} %pad_maximum_fusion.refs_0_), channel_id=1, source_target_pairs={{0,96},{16,112},{32,0},{48,16},{64,32},{80,48},{96,64},{112,80},{1... | collective-permute-start | bytes 1572872 | tf_op jit(solution)/shard_map/ppermute | solution.py:58
  39.1 12.4 %collective-permute-start.3 = (bf16[2,128,1024]{2,1,0:T(8,128)(2,1)S(1)}, bf16[2,128,1024]{2,1,0:T(8,128)(2,1)S(1)}, u32[]{:S(2)}, u32[]{:S(2)}) collective-permute-start(bf16[2,128,1024]{2,1,0:T(8,128)(2,1)S(1)} %pad_maximum_fusion.refs_0_), channel_id=1, source_target_pairs={{0,32},{16,48},{32,64},{48,80},{64,96},{80,112},{96,0},{112,16},{1... | collective-permute-start | bytes 1572872 | tf_op jit(solution)/shard_map/ppermute | solution.py:57
  48.0 11.0 %collective-permute-start.8 = (bf16[128,1024]{1,0:T(8,128)(2,1)S(1)}, bf16[128,1024]{1,0:T(8,128)(2,1)S(1)}, u32[]{:S(2)}, u32[]{:S(2)}) collective-permute-start(bf16[128,1024]{1,0:T(8,128)(2,1)S(1)} %slice_bitcast_fusion.2), channel_id=1, source_target_pairs={{0,96},{16,112},{32,0},{48,16},{64,32},{80,48},{96,64},{112,80},{1... | collective-permute-start | bytes 786440 | tf_op jit(solution)/shard_map/ppermute | solution.py:60
  51.6 14.7 %collective-permute-start.2 = (bf16[2,128,1024]{2,1,0:T(8,128)(2,1)S(1)}, bf16[2,128,1024]{2,1,0:T(8,128)(2,1)S(1)}, u32[]{:S(2)}, u32[]{:S(2)}) collective-permute-start(bf16[2,128,1024]{2,1,0:T(8,128)(2,1)S(1)} %pad_maximum_fusion.refs_0_), channel_id=1, source_target_pairs={{0,16},{16,0},{32,48},{48,32},{64,80},{80,64},{96,112},{112,96},{1... | collective-permute-start | bytes 1572872 | tf_op jit(solution)/shard_map/ppermute | solution.py:64
  59.2 8.6 %collective-permute-start.9 = (bf16[2,128,1024]{2,1,0:T(8,128)(2,1)S(1)}, bf16[2,128,1024]{2,1,0:T(8,128)(2,1)S(1)}, u32[]{:S(2)}, u32[]{:S(2)}) collective-permute-start(bf16[2,128,1024]{2,1,0:T(8,128)(2,1)S(1)} %pad_maximum_fusion.1.refs_6_), channel_id=1, source_target_pairs={{0,16},{16,0},{32,48},{48,32},{64,80},{80,64},{96,112},{112,96},{1... | collective-permute-start | bytes 1572872 | tf_op jit(solution)/shard_map/ppermute | solution.py:64
  83.5 10.3 %collective-permute-start.10 = (bf16[128,1024]{1,0:T(8,128)(2,1)S(1)}, bf16[128,1024]{1,0:T(8,128)(2,1)S(1)}, u32[]{:S(2)}, u32[]{:S(2)}) collective-permute-start(bf16[128,1024]{1,0:T(8,128)(2,1)S(1)} %get-tuple-element.96), channel_id=1, source_target_pairs={{0,0},{1,1},{2,16},{3,17},{4,32},{5,33},{6,48},{7,49},{8,64},{9,65... | collective-permute-start | bytes 786440 | tf_op jit(solution)/shard_map/ppermute | solution.py:46
  87.8 11.7 %collective-permute-start.11 = (bf16[128,1024]{1,0:T(8,128)(2,1)S(1)}, bf16[128,1024]{1,0:T(8,128)(2,1)S(1)}, u32[]{:S(2)}, u32[]{:S(2)}) collective-permute-start(bf16[128,1024]{1,0:T(8,128)(2,1)S(1)} %get-tuple-element.95), channel_id=1, source_target_pairs={{0,1},{1,0},{2,17},{3,16},{4,33},{5,32},{6,49},{7,48},{8,65},{9,64... | collective-permute-start | bytes 786440 | tf_op jit(solution)/shard_map/ppermute | solution.py:46
  101.0 19.1 %collective-permute-start.13 = (bf16[2,128,1024]{2,1,0:T(8,128)(2,1)S(1)}, bf16[2,128,1024]{2,1,0:T(8,128)(2,1)S(1)}, u32[]{:S(2)}, u32[]{:S(2)}) collective-permute-start(bf16[2,128,1024]{2,1,0:T(8,128)(2,1)S(1)} %pad_maximum_fusion.2), channel_id=1, source_target_pairs={{0,32},{16,48},{32,64},{48,80},{64,96},{80,112},{96,0},{112,16},{1... | collective-permute-start | bytes 1572872 | tf_op jit(solution)/shard_map/ppermute | solution.py:57
  110.7 18.3 %collective-permute-start.15 = (bf16[2,128,1024]{2,1,0:T(8,128)(2,1)S(1)}, bf16[2,128,1024]{2,1,0:T(8,128)(2,1)S(1)}, u32[]{:S(2)}, u32[]{:S(2)}) collective-permute-start(bf16[2,128,1024]{2,1,0:T(8,128)(2,1)S(1)} %pad_maximum_fusion.2), channel_id=1, source_target_pairs={{0,96},{16,112},{32,0},{48,16},{64,32},{80,48},{96,64},{112,80},{1... | collective-permute-start | bytes 1572872 | tf_op jit(solution)/shard_map/ppermute | solution.py:58
  110.9 24.0 %collective-permute-start.12 = (bf16[2,128,1024]{2,1,0:T(8,128)(2,1)S(1)}, bf16[2,128,1024]{2,1,0:T(8,128)(2,1)}, u32[]{:S(2)}, u32[]{:S(2)}) collective-permute-start(bf16[2,128,1024]{2,1,0:T(8,128)(2,1)S(1)} %pad_maximum_fusion.2), channel_id=1, source_target_pairs={{0,16},{16,0},{32,48},{48,32},{64,80},{80,64},{96,112},{112,96},{1... | collective-permute-start | bytes 1572872 | tf_op jit(solution)/shard_map/ppermute | solution.py:64
  120.1 17.5 %collective-permute-start.17 = (bf16[128,1024]{1,0:T(8,128)(2,1)S(1)}, bf16[128,1024]{1,0:T(8,128)(2,1)S(1)}, u32[]{:S(2)}, u32[]{:S(2)}) collective-permute-start(bf16[128,1024]{1,0:T(8,128)(2,1)S(1)} %slice_bitcast_fusion.1), channel_id=1, source_target_pairs={{0,32},{16,48},{32,64},{48,80},{64,96},{80,112},{96,0},{112,16},{1... | collective-permute-start | bytes 786440 | tf_op jit(solution)/shard_map/ppermute | solution.py:60
  124.9 14.7 %collective-permute-start.14 = (bf16[2,128,1024]{2,1,0:T(8,128)(2,1)S(1)}, bf16[2,128,1024]{2,1,0:T(8,128)(2,1)S(1)}, u32[]{:S(2)}, u32[]{:S(2)}) collective-permute-start(bf16[2,128,1024]{2,1,0:T(8,128)(2,1)S(1)} %collective-permute-done.13), channel_id=1, source_target_pairs={{0,16},{16,0},{32,48},{48,32},{64,80},{80,64},{96,112},{112,96},{1... | collective-permute-start | bytes 1572872 | tf_op jit(solution)/shard_map/ppermute | solution.py:64
  129.7 8.9 %collective-permute-start.18 = (bf16[128,1024]{1,0:T(8,128)(2,1)}, bf16[128,1024]{1,0:T(8,128)(2,1)S(1)}, u32[]{:S(2)}, u32[]{:S(2)}) collective-permute-start(bf16[128,1024]{1,0:T(8,128)(2,1)} %slice_bitcast_fusion), channel_id=1, source_target_pairs={{0,96},{16,112},{32,0},{48,16},{64,32},{80,48},{96,64},{112,80},{1... | collective-permute-start | bytes 786440 | tf_op jit(solution)/shard_map/ppermute | solution.py:60
  145.5 40.1 %all-to-all-start = ((bf16[16,144,128]{2,1,0:T(8,128)(2,1)}), bf16[16,144,128]{2,1,0:T(8,128)(2,1)}, u32[]{:S(2)}, u32[]{:S(2)}) async-start(bf16[16,144,128]{2,1,0:T(8,128)(2,1)} %fusion.1), calls=%async_computation | async-start | bytes 1179648 | tf_op jit(solution)/shard_map/all_to_all | solution.py:365
  155.4 36.0 %collective-permute-start.20 = (bf16[4,128,1024]{2,1,0:T(8,128)(2,1)S(1)}, bf16[4,128,1024]{2,1,0:T(8,128)(2,1)}, u32[]{:S(2)}, u32[]{:S(2)}) collective-permute-start(bf16[4,128,1024]{2,1,0:T(8,128)(2,1)S(1)} %shard_map.139), channel_id=1, source_target_pairs={{0,2},{1,3},{2,0},{3,1},{4,6},{5,7},{6,4},{7,5},{8,10},{9,11},{10,... | collective-permute-start | bytes 3145736 | tf_op jit(solution)/shard_map/ppermute | solution.py:149
  167.0 73.4 %collective-permute-start.21 = (bf16[4,128,1024]{2,1,0:T(8,128)(2,1)S(1)}, bf16[4,128,1024]{2,1,0:T(8,128)(2,1)}, u32[]{:S(2)}, u32[]{:S(2)}) collective-permute-start(bf16[4,128,1024]{2,1,0:T(8,128)(2,1)S(1)} %get-tuple-element.58), channel_id=1, source_target_pairs={{0,1},{1,2},{2,3},{3,0},{4,5},{5,6},{6,7},{7,4},{8,9},{9,10},{10,1... | collective-permute-start | bytes 3145736 | tf_op jit(solution)/shard_map/ppermute | solution.py:149
  167.3 73.1 %collective-permute-start.22 = (bf16[4,128,1024]{2,1,0:T(8,128)(2,1)}, bf16[4,128,1024]{2,1,0:T(8,128)(2,1)}, u32[]{:S(2)}, u32[]{:S(2)}) collective-permute-start(bf16[4,128,1024]{2,1,0:T(8,128)(2,1)} %get-tuple-element.59), channel_id=1, source_target_pairs={{0,3},{1,0},{2,1},{3,2},{4,7},{5,4},{6,5},{7,6},{8,11},{9,8},{10,9... | collective-permute-start | bytes 3145736 | tf_op jit(solution)/shard_map/ppermute | solution.py:149
  173.4 67.0 %collective-permute-start.23 = (bf16[4,128,1024]{2,1,0:T(8,128)(2,1)S(1)}, bf16[4,128,1024]{2,1,0:T(8,128)(2,1)}, u32[]{:S(2)}, u32[]{:S(2)}) collective-permute-start(bf16[4,128,1024]{2,1,0:T(8,128)(2,1)S(1)} %shard_map.141), channel_id=1, source_target_pairs={{0,8},{1,9},{2,10},{3,11},{4,12},{5,13},{6,14},{7,15},{8,0},{9,1},... | collective-permute-start | bytes 3145736 | tf_op jit(solution)/shard_map/ppermute | solution.py:149
  185.3 55.2 %collective-permute-start.24 = (bf16[4,128,1024]{2,1,0:T(8,128)(2,1)}, bf16[4,128,1024]{2,1,0:T(8,128)(2,1)}, u32[]{:S(2)}, u32[]{:S(2)}) collective-permute-start(bf16[4,128,1024]{2,1,0:T(8,128)(2,1)} %get-tuple-element.62), channel_id=1, source_target_pairs={{0,4},{1,5},{2,6},{3,7},{4,8},{5,9},{6,10},{7,11},{8,12},{9,13},{1... | collective-permute-start | bytes 3145736 | tf_op jit(solution)/shard_map/ppermute | solution.py:149
  191.4 49.1 %collective-permute-start.25 = (bf16[4,128,1024]{2,1,0:T(8,128)(2,1)}, bf16[4,128,1024]{2,1,0:T(8,128)(2,1)}, u32[]{:S(2)}, u32[]{:S(2)}) collective-permute-start(bf16[4,128,1024]{2,1,0:T(8,128)(2,1)} %get-tuple-element.63), channel_id=1, source_target_pairs={{0,12},{1,13},{2,14},{3,15},{4,0},{5,1},{6,2},{7,3},{8,4},{9,5},{1... | collective-permute-start | bytes 3145736 | tf_op jit(solution)/shard_map/ppermute | solution.py:149
  195.8 40.5 %all-to-all-start.2 = ((bf16[16,128,128]{2,1,0:T(8,128)(2,1)}), bf16[16,128,128]{2,1,0:T(8,128)(2,1)}, u32[]{:S(2)}, u32[]{:S(2)}) async-start(bf16[16,128,128]{2,1,0:T(8,128)(2,1)} %broadcast_select_fusion), calls=%async_computation.3 | async-start | bytes 1048576 | tf_op jit(solution)/shard_map/all_to_all | solution.py:368
  236.4 32.7 %all-to-all-start.1 = ((bf16[16,2,128,128]{3,2,1,0:T(8,128)(2,1)}), bf16[16,2,128,128]{3,2,1,0:T(8,128)(2,1)S(1)}, u32[]{:S(2)}, u32[]{:S(2)}) async-start(bf16[16,2,128,128]{3,2,1,0:T(8,128)(2,1)} %shard_map.138), calls=%async_computation.2 | async-start | bytes 2097152 | tf_op jit(solution)/shard_map/all_to_all | solution.py:373
  244.5 17.2 %collective-permute-start.26 = (bf16[128,1024]{1,0:T(8,128)(2,1)S(1)}, bf16[128,1024]{1,0:T(8,128)(2,1)S(1)}, u32[]{:S(2)}, u32[]{:S(2)}) collective-permute-start(bf16[128,1024]{1,0:T(8,128)(2,1)S(1)} %get-tuple-element.70), channel_id=1, source_target_pairs={{0,4},{1,5},{2,6},{3,7},{4,8},{5,9},{6,10},{7,11},{8,12},{9,13},{1... | collective-permute-start | bytes 786440 | tf_op jit(solution)/shard_map/ppermute | solution.py:149
  245.9 21.3 %collective-permute-start.27 = (bf16[128,1024]{1,0:T(8,128)(2,1)S(1)}, bf16[128,1024]{1,0:T(8,128)(2,1)S(1)}, u32[]{:S(2)}, u32[]{:S(2)}) collective-permute-start(bf16[128,1024]{1,0:T(8,128)(2,1)S(1)} %get-tuple-element.71), channel_id=1, source_target_pairs={{0,8},{1,9},{2,10},{3,11},{4,12},{5,13},{6,14},{7,15},{8,0},{9,1},... | collective-permute-start | bytes 786440 | tf_op jit(solution)/shard_map/ppermute | solution.py:149
  248.3 18.9 %collective-permute-start.28 = (bf16[128,1024]{1,0:T(8,128)(2,1)S(1)}, bf16[128,1024]{1,0:T(8,128)(2,1)S(1)}, u32[]{:S(2)}, u32[]{:S(2)}) collective-permute-start(bf16[128,1024]{1,0:T(8,128)(2,1)S(1)} %get-tuple-element.72), channel_id=1, source_target_pairs={{0,12},{1,13},{2,14},{3,15},{4,0},{5,1},{6,2},{7,3},{8,4},{9,5},{1... | collective-permute-start | bytes 786440 | tf_op jit(solution)/shard_map/ppermute | solution.py:149
  253.4 13.8 %collective-permute-start.29 = (bf16[128,1024]{1,0:T(8,128)(2,1)S(1)}, bf16[128,1024]{1,0:T(8,128)(2,1)S(1)}, u32[]{:S(2)}, u32[]{:S(2)}) collective-permute-start(bf16[128,1024]{1,0:T(8,128)(2,1)S(1)} %get-tuple-element.78), channel_id=1, source_target_pairs={{0,1},{1,2},{2,3},{3,0},{4,5},{5,6},{6,7},{7,4},{8,9},{9,10},{10,1... | collective-permute-start | bytes 786440 | tf_op jit(solution)/shard_map/ppermute | solution.py:149
  254.6 12.6 %collective-permute-start.30 = (bf16[128,1024]{1,0:T(8,128)(2,1)S(1)}, bf16[128,1024]{1,0:T(8,128)(2,1)S(1)}, u32[]{:S(2)}, u32[]{:S(2)}) collective-permute-start(bf16[128,1024]{1,0:T(8,128)(2,1)S(1)} %get-tuple-element.79), channel_id=1, source_target_pairs={{0,2},{1,3},{2,0},{3,1},{4,6},{5,7},{6,4},{7,5},{8,10},{9,11},{10,... | collective-permute-start | bytes 786440 | tf_op jit(solution)/shard_map/ppermute | solution.py:149
  276.3 8.7 %collective-permute-start.33 = (bf16[4,128,128]{2,1,0:T(8,128)(2,1)S(1)}, bf16[4,128,128]{2,1,0:T(8,128)(2,1)S(1)}, u32[]{:S(2)}, u32[]{:S(2)}) collective-permute-start(bf16[4,128,128]{2,1,0:T(8,128)(2,1)S(1)} %add_convert_fusion.a), channel_id=1, source_target_pairs={{0,96},{16,112},{32,0},{48,16},{64,32},{80,48},{96,64},{112,80},{1... | collective-permute-start | bytes 393224 | tf_op jit(solution)/shard_map/ppermute | solution.py:192
  279.7 9.1 %collective-permute-start.35 = (bf16[4,128,128]{2,1,0:T(8,128)(2,1)S(1)}, bf16[4,128,128]{2,1,0:T(8,128)(2,1)S(1)}, u32[]{:S(2)}, u32[]{:S(2)}) collective-permute-start(bf16[4,128,128]{2,1,0:T(8,128)(2,1)S(1)} %add_convert_fusion.a), channel_id=1, source_target_pairs={{0,32},{16,48},{32,64},{48,80},{64,96},{80,112},{96,0},{112,16},{1... | collective-permute-start | bytes 393224 | tf_op jit(solution)/shard_map/ppermute | solution.py:192
  (24 other events, 416.8 us)
Sparse Core Ops, SparseCore 0:
  83.4 134.7 reduce-scatter.1

commit v7 on v6

--- a/solution.py
+++ b/solution.py
@@ -210,24 +210,25 @@
     )(*scalars, *arrays)
 
 
-def outgoing(place, readers, pattern, total):
+def outgoing(place, readers, pattern, total, cut):
     count, block = total.shape[:2]
 
-    def kernel(place_ref, readers_ref, pattern_ref, total_ref, out_ref):
+    def kernel(place_ref, readers_ref, pattern_ref, total_ref, cut_ref, out_ref):
         for d in range(count):
             for j, k in enumerate((d, readers_ref[d])):
                 value = total_ref[place_ref[k]].astype(F32) * pattern_ref[k].astype(F32)
                 out_ref[d, j] = (-value).astype(out_ref.dtype)
+            out_ref[d, 2] = cut_ref[readers_ref[d], :block]
 
     return small_call(
         kernel,
-        [((count, 2, block, block), jnp.bfloat16)],
+        [((count, 3, block, block), jnp.bfloat16)],
         [place, readers, pattern],
-        [total],
+        [total, cut],
     )[0]
 
 
-def finish_rows(pattern, back, parent_panels, masked_one, masked_two, lead, second):
+def finish_rows(pattern, back, masked_one, masked_two, lead, second):
     count, _, block, _ = back.shape
     width = count * block
     kind = back.dtype
@@ -236,7 +237,7 @@
         return lax.dot_general(a, b, (((1,), (1,)), ((), ())), preferred_element_type=F32)
 
     def kernel(
-        pattern_ref, back_ref, panels_ref, one_ref, two_ref, lead_ref, *refs
+        pattern_ref, back_ref, one_ref, two_ref, lead_ref, *refs
     ):
         terms = [refs[: len(second) // 2], refs[len(second) // 2 : len(second)]]
         rows_one_ref, rows_two_ref, sums_ref, chosen, panels = refs[len(second) :]
@@ -244,7 +245,7 @@
             part = pl.ds(i * block, block)
             rows_one_ref[:, part] = back_ref[i, 0]
             chosen[:, part] = back_ref[i, 1]
-            panels[:, part] = panels_ref[i]
+            panels[:, part] = back_ref[i, 2]
         for i in range(count):
             part = pl.ds(i * block, block)
             side, first = i * 2 // count, i % (count // 2) * block
@@ -261,7 +262,7 @@
         kernel,
         [((block, width), kind), ((block, width), kind), ((4, block, block), F32)],
         [pattern],
-        [back, parent_panels, masked_one, masked_two, lead, *second],
+        [back, masked_one, masked_two, lead, *second],
         [pltpu.VMEM((block, width), kind), pltpu.VMEM((block, width), kind)],
     )
 
@@ -365,18 +366,12 @@
     cut = lax.all_to_all(jnp.concatenate([cut, facts], 1), "col", 0, 0, tiled=True)
     cut_pattern = cut[:, block, 0].astype(jnp.int32)
     readers = cut[:, block + 8, 0].astype(jnp.int32)
-    parent_panels = lax.all_to_all(
-        jnp.take(cut[:, :block], readers, axis=0), "col", 0, 0, tiled=True
-    )
-
-    going = outgoing(place, readers, cut_pattern, first_sum)
+    going = outgoing(place, readers, cut_pattern, first_sum, cut)
     back = lax.all_to_all(going, "col", 0, 0, tiled=True)
-    coming_a, coming_b, parent_panels, _ = lax.optimization_barrier(
-        (coming_a, coming_b, parent_panels, going)
-    )
+    coming_a, coming_b, _ = lax.optimization_barrier((coming_a, coming_b, going))
     second_sum = second_sends(coming_a, own_a, y_step) + second_sends(coming_b, own_b, x_step)
     level_one_rows, level_two_rows, sums = finish_rows(
-        level_two_pattern, back, parent_panels, masked_one, masked_two, parent_lead, second_sum
+        level_two_pattern, back, masked_one, masked_two, parent_lead, second_sum
     )
 
     diag_blocks = level_one_diag.reshape(count, block, block)

time: 300 us -> 296 us (0.987)
  local copies, waits for them, and re-layouts: 21.7 us -> 17.9 us
  starting transfers between devices: 119 us -> 122 us
    all_to_all x1 -> x0, waiting for transfers between devices: 15.3 us -> none  [per_device(): lax.all_to_all(jnp.take(cut[:, :block], readers, axis=0), 'col', 0, 0, ti...]
    reduce_scatter x1, waiting for transfers between devices: 18.2 us -> 29.6 us  [per_device(): lax.psum_scatter(product_one.reshape(count * count * block, block), 'col'...]
    ppermute x1, starting transfers between devices: 1.39 us -> 9.17 us  [row_parts(): values = values + lax.ppermute(values, 'row', CORE_SWAP)]
    ppermute x12, waiting for transfers between devices: 9.88 us -> 14.7 us  [send(): return lax.ppermute(value, 'col', step)]
    all_to_all x1 -> x0, starting transfers between devices: 4.25 us -> none  [per_device(): lax.all_to_all(jnp.take(cut[:, :block], readers, axis=0), 'col', 0, 0, ti...]
  transfers between devices with their start and end apart: 40 -> 39, of which waited for: 17 -> 17; matrix products, arithmetic and copies ran while one was open for 8% -> 6% of each run, Pallas kernels for 11% -> 11%
where the time goes in v7:
time: 296 us; the launch traced here: 295 us
  starting transfers between devices  122 us (41%)
  waiting for transfers between devices  81.4 us (28%)
  Pallas kernels  52.5 us (18%)
  local copies, waits for them, and re-layouts  17.9 us (6%)
  between operations  15.2 us (5%)
  other arithmetic  5.52 us (2%)
    reduce_scatter x1, waiting for transfers between devices, per_device(): lax.psum_scatter(product_one.reshape(count * count * block, block), 'col'...  29.6 us
    ppermute x8, starting transfers between devices, all_panels(): found += [held, lax.ppermute(held, 'row', CORE_SWAP)]  28.7 us
    pallas_call x4, Pallas kernels, by_supernode(): pl.pallas_call(kernel, out_shape=[jax.ShapeDtypeStruct((SIDE, block, widt...  24.5 us
    ppermute x12, starting transfers between devices, send(): return lax.ppermute(value, 'col', step)  21.2 us
    ppermute x4, waiting for transfers between devices, turned_panels(): return lax.ppermute(part, ('row', 'col'), turn(k))  17.1 us
    ppermute x2, starting transfers between devices, all_panels(): above = lax.ppermute(own, 'row', z_step(-1))  15.5 us
    pallas_call x1, Pallas kernels, by_column(): pl.pallas_call(kernel, out_shape=jax.ShapeDtypeStruct((width // block, st...  14.8 us
    ppermute x12, waiting for transfers between devices, send(): return lax.ppermute(value, 'col', step)  14.7 us
  transfers between devices with their start and end apart: 39, of which 17 were waited for; matrix products, arithmetic and copies ran while one was open for 6% of the time, Pallas kernels for 11%

profile of v7, /device:TPU:1, one launch (start us, length us, event | category | flops | bytes accessed | tf_op | source)
XLA Modules:
  0.0 294.9 jit_solution(2074884943344495718)
XLA Ops:
  9.2 6.0 %collective-permute-start = (bf16[128,1024]{1,0:T(8,128)(2,1)S(1)}, bf16[128,1024]{1,0:T(8,128)(2,1)S(1)}, u32[]{:S(2)}, u32[]{:S(2)}) collective-permute-start(bf16[128,1024]{1,0:T(8,128)(2,1)S(1)} %get-tuple-element.97), channel_id=1, source_target_pairs={{0,0},{1,1},{2,16},{3,17},{4,32},{5,33},{6,48},{7,49},{8,64},{9,65... | collective-permute-start | bytes 786440 | tf_op jit(solution)/shard_map/ppermute | solution.py:46
  15.9 5.2 %collective-permute-done = bf16[128,1024]{1,0:T(8,128)(2,1)S(1)} collective-permute-done((bf16[128,1024]{1,0:T(8,128)(2,1)S(1)}, bf16[128,1024]{1,0:T(8,128)(2,1)S(1)}, u32[]{:S(2)}, u32[]{:S(2)}) %collective-permute-start) | collective-permute-done | bytes 262176 | tf_op jit(solution)/shard_map/ppermute | solution.py:46
  23.7 15.4 %collective-permute-start.5 = (bf16[2,128,1024]{2,1,0:T(8,128)(2,1)S(1)}, bf16[2,128,1024]{2,1,0:T(8,128)(2,1)S(1)}, u32[]{:S(2)}, u32[]{:S(2)}) collective-permute-start(bf16[2,128,1024]{2,1,0:T(8,128)(2,1)S(1)} %pad_maximum_fusion.refs_0_), channel_id=1, source_target_pairs={{0,96},{16,112},{32,0},{48,16},{64,32},{80,48},{96,64},{112,80},{1... | collective-permute-start | bytes 1572872 | tf_op jit(solution)/shard_map/ppermute | solution.py:58
  39.1 8.9 %collective-permute-done.5.refs_4_ = bf16[2,128,1024]{2,1,0:T(8,128)(2,1)S(1)} collective-permute-done((bf16[2,128,1024]{2,1,0:T(8,128)(2,1)S(1)}, bf16[2,128,1024]{2,1,0:T(8,128)(2,1)S(1)}, u32[]{:S(2)}, u32[]{:S(2)}) %collective-permute-start.5) | collective-permute-done | bytes 524320 | tf_op jit(solution)/shard_map/ppermute | solution.py:58
  48.0 3.5 %collective-permute-start.8 = (bf16[128,1024]{1,0:T(8,128)(2,1)S(1)}, bf16[128,1024]{1,0:T(8,128)(2,1)S(1)}, u32[]{:S(2)}, u32[]{:S(2)}) collective-permute-start(bf16[128,1024]{1,0:T(8,128)(2,1)S(1)} %slice_bitcast_fusion.2), channel_id=1, source_target_pairs={{0,96},{16,112},{32,0},{48,16},{64,32},{80,48},{96,64},{112,80},{1... | collective-permute-start | bytes 786440 | tf_op jit(solution)/shard_map/ppermute | solution.py:60
  51.6 6.9 %collective-permute-start.2 = (bf16[2,128,1024]{2,1,0:T(8,128)(2,1)S(1)}, bf16[2,128,1024]{2,1,0:T(8,128)(2,1)S(1)}, u32[]{:S(2)}, u32[]{:S(2)}) collective-permute-start(bf16[2,128,1024]{2,1,0:T(8,128)(2,1)S(1)} %pad_maximum_fusion.refs_0_), channel_id=1, source_target_pairs={{0,16},{16,0},{32,48},{48,32},{64,80},{80,64},{96,112},{112,96},{1... | collective-permute-start | bytes 1572872 | tf_op jit(solution)/shard_map/ppermute | solution.py:64
  59.2 7.0 %collective-permute-start.9 = (bf16[2,128,1024]{2,1,0:T(8,128)(2,1)S(1)}, bf16[2,128,1024]{2,1,0:T(8,128)(2,1)S(1)}, u32[]{:S(2)}, u32[]{:S(2)}) collective-permute-start(bf16[2,128,1024]{2,1,0:T(8,128)(2,1)S(1)} %pad_maximum_fusion.1.refs_6_), channel_id=1, source_target_pairs={{0,16},{16,0},{32,48},{48,32},{64,80},{80,64},{96,112},{112,96},{1... | collective-permute-start | bytes 1572872 | tf_op jit(solution)/shard_map/ppermute | solution.py:64
  68.6 14.8 %shard_map.137 = bf16[16,2048,128]{2,1,0:T(8,128)(2,1)} custom-call(bf16[2,128,1024]{2,1,0:T(8,128)(2,1)S(1)} %pad_maximum_fusion.refs_0_, bf16[2,128,1024]{2,1,0:T(8,128)(2,1)S(1)} %collective-permute-done.2.refs_1_, bf16[2,128,1024]{2,1,0:T(8,128)(2,1)S(1)} %collective-permute-done.3.refs_2_, bf16[2,128,1024]{2,1,0:T(8,128)(2,1)} %copy-done.13, ...), custom_call_target="tpu_custom_call" | custom-call | flops 8589934592 | bytes 16777216 | tf_op jit(solution)/shard_map/pallas_call | solution.py:93
  83.5 4.3 %collective-permute-start.10 = (bf16[128,1024]{1,0:T(8,128)(2,1)S(1)}, bf16[128,1024]{1,0:T(8,128)(2,1)S(1)}, u32[]{:S(2)}, u32[]{:S(2)}) collective-permute-start(bf16[128,1024]{1,0:T(8,128)(2,1)S(1)} %get-tuple-element.94), channel_id=1, source_target_pairs={{0,0},{1,1},{2,16},{3,17},{4,32},{5,33},{6,48},{7,49},{8,64},{9,65... | collective-permute-start | bytes 786440 | tf_op jit(solution)/shard_map/ppermute | solution.py:46
  90.1 3.7 %collective-permute-done.10 = bf16[128,1024]{1,0:T(8,128)(2,1)S(1)} collective-permute-done((bf16[128,1024]{1,0:T(8,128)(2,1)S(1)}, bf16[128,1024]{1,0:T(8,128)(2,1)S(1)}, u32[]{:S(2)}, u32[]{:S(2)}) %collective-permute-start.10) | collective-permute-done | bytes 262176 | tf_op jit(solution)/shard_map/ppermute | solution.py:46
  93.8 5.7 %collective-permute-done.11 = bf16[128,1024]{1,0:T(8,128)(2,1)S(1)} collective-permute-done((bf16[128,1024]{1,0:T(8,128)(2,1)S(1)}, bf16[128,1024]{1,0:T(8,128)(2,1)S(1)}, u32[]{:S(2)}, u32[]{:S(2)}) %collective-permute-start.11) | collective-permute-done | bytes 262176 | tf_op jit(solution)/shard_map/ppermute | solution.py:46
  101.1 9.7 %collective-permute-start.13 = (bf16[2,128,1024]{2,1,0:T(8,128)(2,1)S(1)}, bf16[2,128,1024]{2,1,0:T(8,128)(2,1)S(1)}, u32[]{:S(2)}, u32[]{:S(2)}) collective-permute-start(bf16[2,128,1024]{2,1,0:T(8,128)(2,1)S(1)} %pad_maximum_fusion.2), channel_id=1, source_target_pairs={{0,32},{16,48},{32,64},{48,80},{64,96},{80,112},{96,0},{112,16},{1... | collective-permute-start | bytes 1572872 | tf_op jit(solution)/shard_map/ppermute | solution.py:57
  111.0 8.9 %collective-permute-start.12 = (bf16[2,128,1024]{2,1,0:T(8,128)(2,1)S(1)}, bf16[2,128,1024]{2,1,0:T(8,128)(2,1)}, u32[]{:S(2)}, u32[]{:S(2)}) collective-permute-start(bf16[2,128,1024]{2,1,0:T(8,128)(2,1)S(1)} %pad_maximum_fusion.2), channel_id=1, source_target_pairs={{0,16},{16,0},{32,48},{48,32},{64,80},{80,64},{96,112},{112,96},{1... | collective-permute-start | bytes 1572872 | tf_op jit(solution)/shard_map/ppermute | solution.py:64
  120.2 4.7 %collective-permute-start.17 = (bf16[128,1024]{1,0:T(8,128)(2,1)S(1)}, bf16[128,1024]{1,0:T(8,128)(2,1)S(1)}, u32[]{:S(2)}, u32[]{:S(2)}) collective-permute-start(bf16[128,1024]{1,0:T(8,128)(2,1)S(1)} %slice_bitcast_fusion.1), channel_id=1, source_target_pairs={{0,32},{16,48},{32,64},{48,80},{64,96},{80,112},{96,0},{112,16},{1... | collective-permute-start | bytes 786440 | tf_op jit(solution)/shard_map/ppermute | solution.py:60
  124.9 4.1 %collective-permute-start.14 = (bf16[2,128,1024]{2,1,0:T(8,128)(2,1)S(1)}, bf16[2,128,1024]{2,1,0:T(8,128)(2,1)}, u32[]{:S(2)}, u32[]{:S(2)}) collective-permute-start(bf16[2,128,1024]{2,1,0:T(8,128)(2,1)S(1)} %collective-permute-done.13), channel_id=1, source_target_pairs={{0,16},{16,0},{32,48},{48,32},{64,80},{80,64},{96,112},{112,96},{1... | collective-permute-start | bytes 1572872 | tf_op jit(solution)/shard_map/ppermute | solution.py:64
  145.7 6.1 %all-to-all-start = ((bf16[16,144,128]{2,1,0:T(8,128)(2,1)}), bf16[16,144,128]{2,1,0:T(8,128)(2,1)S(1)}, u32[]{:S(2)}, u32[]{:S(2)}) async-start(bf16[16,144,128]{2,1,0:T(8,128)(2,1)} %fusion.1), calls=%async_computation | async-start | bytes 1179648 | tf_op jit(solution)/shard_map/all_to_all | solution.py:366
  151.7 3.8 %shard_map.139 = bf16[4,128,1024]{2,1,0:T(8,128)(2,1)S(1)} custom-call(s32[4]{0:T(128)S(1)} %gather_fusion.1, bf16[16,128,1024]{2,1,0:T(8,128)(2,1)} %constant_dynamic-update-slice_fusion.a_ref.b_ref.c_ref.d_ref, bf16[16,128,1024]{2,1,0:T(8,128)(2,1)} %constant_dynamic-update-slice_fusion.a_ref.b_ref.c_ref.d_ref, ...), custom_call_target="tpu_custom_call" | custom-call | flops 1073741824 | bytes 2097152 | tf_op jit(solution)/shard_map/pallas_call | solution.py:128
  159.1 8.5 %shard_map.140 = (bf16[4,128,1024]{2,1,0:T(8,128)(2,1)}, bf16[4,128,1024]{2,1,0:T(8,128)(2,1)}, bf16[4,128,1024]{2,1,0:T(8,128)(2,1)}) custom-call(s32[12]{0:T(128)S(1)} %gather_fusion.2, bf16[16,128,1024]{2,1,0:T(8,128)(2,1)} %constant_dynamic-update-slice_fusion.a_ref.b_ref.c_ref.d_ref, ...), custom_call_target="tpu_custom_call" | custom-call | flops 3221225472 | bytes 6291456 | tf_op jit(solution)/shard_map/pallas_call | solution.py:128
  170.3 3.7 %shard_map.141 = bf16[4,128,1024]{2,1,0:T(8,128)(2,1)S(1)} custom-call(s32[4]{0:T(128)S(1)} %gather_fusion.3, bf16[16,128,1024]{2,1,0:T(8,128)(2,1)} %constant_dynamic-update-slice_fusion.a_ref.b_ref.c_ref.d_ref, bf16[16,128,1024]{2,1,0:T(8,128)(2,1)} %constant_dynamic-update-slice_fusion.a_ref.b_ref.c_ref.d_ref, ...), custom_call_target="tpu_custom_call" | custom-call | flops 1073741824 | bytes 2097152 | tf_op jit(solution)/shard_map/pallas_call | solution.py:128
  177.5 8.5 %shard_map.142 = (bf16[4,128,1024]{2,1,0:T(8,128)(2,1)}, bf16[4,128,1024]{2,1,0:T(8,128)(2,1)}, bf16[4,128,1024]{2,1,0:T(8,128)(2,1)}) custom-call(s32[12]{0:T(128)S(1)} %gather_fusion.4, bf16[16,128,1024]{2,1,0:T(8,128)(2,1)} %constant_dynamic-update-slice_fusion.a_ref.b_ref.c_ref.d_ref, ...), custom_call_target="tpu_custom_call" | custom-call | flops 3221225472 | bytes 6291456 | tf_op jit(solution)/shard_map/pallas_call | solution.py:128
  189.3 29.6 %reduce-scatter.2.cloned.1.call-done = bf16[2048,128]{1,0:T(8,128)(2,1)} async-done(((bf16[32768,128]{1,0:T(8,128)(2,1)}), bf16[2048,128]{1,0:T(8,128)(2,1)}) %reduce-scatter.2.cloned.1.call-update) | async-done | bytes 524304 | tf_op jit(solution)/shard_map/reduce_scatter | solution.py:339
  221.9 4.1 %all-to-all-start.1 = ((bf16[16,3,128,128]{3,2,1,0:T(8,128)(2,1)}), bf16[16,3,128,128]{3,2,1,0:T(8,128)(2,1)S(1)}, u32[]{:S(2)}, u32[]{:S(2)}) async-start(bf16[16,3,128,128]{3,2,1,0:T(8,128)(2,1)} %shard_map.138), calls=%async_computation.2 | async-start | bytes 3145728 | tf_op jit(solution)/shard_map/all_to_all | solution.py:370
  226.0 5.7 %collective-permute-done.24.two_ref = bf16[4,128,1024]{2,1,0:T(8,128)(2,1)} collective-permute-done((bf16[4,128,1024]{2,1,0:T(8,128)(2,1)}, bf16[4,128,1024]{2,1,0:T(8,128)(2,1)}, u32[]{:S(2)}, u32[]{:S(2)}) %collective-permute-start.24) | collective-permute-done | bytes 1048608 | tf_op jit(solution)/shard_map/ppermute | solution.py:149
  231.7 3.9 %collective-permute-done.25.three_ref = bf16[4,128,1024]{2,1,0:T(8,128)(2,1)} collective-permute-done((bf16[4,128,1024]{2,1,0:T(8,128)(2,1)}, bf16[4,128,1024]{2,1,0:T(8,128)(2,1)}, u32[]{:S(2)}, u32[]{:S(2)}) %collective-permute-start.25) | collective-permute-done | bytes 1048608 | tf_op jit(solution)/shard_map/ppermute | solution.py:149
  244.5 3.2 %shard_map.144 = (f32[128,1024]{1,0:T(8,128)S(1)}, bf16[128,1024]{1,0:T(8,128)(2,1)S(1)}, bf16[128,1024]{1,0:T(8,128)(2,1)S(1)}, bf16[128,1024]{1,0:T(8,128)(2,1)S(1)}) custom-call(bf16[4,128,1024]{2,1,0:T(8,128)(2,1)} %collective-permute-done.23.one_ref, bf16[4,128,1024]{2,1,0:T(8,128)(2,1)} %collective-permute-done.24.two_ref, ...), custom_call_target="tpu_custom_call" | custom-call | bytes 4194304 | tf_op jit(solution)/shard_map/pallas_call | solution.py:176
  250.4 4.7 %collective-permute-start.31 = (bf16[128,1024]{1,0:T(8,128)(2,1)S(1)}, bf16[128,1024]{1,0:T(8,128)(2,1)S(1)}, u32[]{:S(2)}, u32[]{:S(2)}) collective-permute-start(bf16[128,1024]{1,0:T(8,128)(2,1)S(1)} %get-tuple-element.78), channel_id=1, source_target_pairs={{0,3},{1,0},{2,1},{3,2},{4,7},{5,4},{6,5},{7,6},{8,11},{9,8},{10,9... | collective-permute-start | bytes 786440 | tf_op jit(solution)/shard_map/ppermute | solution.py:149
  255.1 3.8 %collective-permute-done.27.refs_2_ = bf16[128,1024]{1,0:T(8,128)(2,1)S(1)} collective-permute-done((bf16[128,1024]{1,0:T(8,128)(2,1)S(1)}, bf16[128,1024]{1,0:T(8,128)(2,1)S(1)}, u32[]{:S(2)}, u32[]{:S(2)}) %collective-permute-start.27) | collective-permute-done | bytes 262176 | tf_op jit(solution)/shard_map/ppermute | solution.py:149
  260.1 3.6 %shard_map.145 = (bf16[128,2048]{1,0:T(8,128)(2,1)}, bf16[128,2048]{1,0:T(8,128)(2,1)}, f32[4,128,128]{2,1,0:T(8,128)S(1)}) custom-call(s32[1,16]{1,0:T(1,128)S(1)} %copy-done.5, bf16[16,3,128,128]{3,2,1,0:T(8,128)(2,1)} %copy-done.8, bf16[128,2048]{1,0:T(8,128)(2,1)} %copy-done.7, bf16[128,2048]{1,0:T(8,128)(2,1)} %copy-done.9, ...), custom_call_target="tpu_custom_call" | custom-call | bytes 1048576 | tf_op jit(solution)/shard_map/pallas_call | solution.py:200
  263.8 9.2 %collective-permute-start.32 = (f32[4,128,128]{2,1,0:T(8,128)S(1)}, f32[4,128,128]{2,1,0:T(8,128)S(1)}, u32[]{:S(2)}, u32[]{:S(2)}) collective-permute-start(f32[4,128,128]{2,1,0:T(8,128)S(1)} %get-tuple-element.80), channel_id=1, source_target_pairs={{0,16},{16,0},{32,48},{48,32},{64,80},{80,64},{96,112},{112,96},{1... | collective-permute-start | bytes 786440 | tf_op jit(solution)/shard_map/ppermute | solution.py:190
  274.1 3.5 %collective-permute-start.33 = (bf16[4,128,128]{2,1,0:T(8,128)(2,1)S(1)}, bf16[4,128,128]{2,1,0:T(8,128)(2,1)S(1)}, u32[]{:S(2)}, u32[]{:S(2)}) collective-permute-start(bf16[4,128,128]{2,1,0:T(8,128)(2,1)S(1)} %add_convert_fusion.a), channel_id=1, source_target_pairs={{0,96},{16,112},{32,0},{48,16},{64,32},{80,48},{96,64},{112,80},{1... | collective-permute-start | bytes 393224 | tf_op jit(solution)/shard_map/ppermute | solution.py:192
  279.2 3.9 %collective-permute-done.33.b = bf16[4,128,128]{2,1,0:T(8,128)(2,1)S(1)} collective-permute-done((bf16[4,128,128]{2,1,0:T(8,128)(2,1)S(1)}, bf16[4,128,128]{2,1,0:T(8,128)(2,1)S(1)}, u32[]{:S(2)}, u32[]{:S(2)}) %collective-permute-start.33) | collective-permute-done | bytes 131104 | tf_op jit(solution)/shard_map/ppermute | solution.py:192
  283.6 3.2 %collective-permute-done.35.d = bf16[4,128,128]{2,1,0:T(8,128)(2,1)S(1)} collective-permute-done((bf16[4,128,128]{2,1,0:T(8,128)(2,1)S(1)}, bf16[4,128,128]{2,1,0:T(8,128)(2,1)S(1)}, u32[]{:S(2)}, u32[]{:S(2)}) %collective-permute-start.35) | collective-permute-done | bytes 131104 | tf_op jit(solution)/shard_map/ppermute | solution.py:192
  (141 shorter events, 62.0 us)
Async XLA Ops:
  7.2 211.6 %reduce-scatter.2.cloned.1.call-start = ((), (), s32[]{:S(2)}) async-start(), calls=%async_computation.3 | async-start | bytes 8912896 | tf_op jit(solution)/shard_map/reduce_scatter | solution.py:339
  9.2 11.9 %collective-permute-start = (bf16[128,1024]{1,0:T(8,128)(2,1)S(1)}, bf16[128,1024]{1,0:T(8,128)(2,1)S(1)}, u32[]{:S(2)}, u32[]{:S(2)}) collective-permute-start(bf16[128,1024]{1,0:T(8,128)(2,1)S(1)} %get-tuple-element.97), channel_id=1, source_target_pairs={{0,0},{1,1},{2,16},{3,17},{4,32},{5,33},{6,48},{7,49},{8,64},{9,65... | collective-permute-start | bytes 786440 | tf_op jit(solution)/shard_map/ppermute | solution.py:46
  23.7 24.3 %collective-permute-start.5 = (bf16[2,128,1024]{2,1,0:T(8,128)(2,1)S(1)}, bf16[2,128,1024]{2,1,0:T(8,128)(2,1)S(1)}, u32[]{:S(2)}, u32[]{:S(2)}) collective-permute-start(bf16[2,128,1024]{2,1,0:T(8,128)(2,1)S(1)} %pad_maximum_fusion.refs_0_), channel_id=1, source_target_pairs={{0,96},{16,112},{32,0},{48,16},{64,32},{80,48},{96,64},{112,80},{1... | collective-permute-start | bytes 1572872 | tf_op jit(solution)/shard_map/ppermute | solution.py:58
  39.1 12.4 %collective-permute-start.3 = (bf16[2,128,1024]{2,1,0:T(8,128)(2,1)S(1)}, bf16[2,128,1024]{2,1,0:T(8,128)(2,1)S(1)}, u32[]{:S(2)}, u32[]{:S(2)}) collective-permute-start(bf16[2,128,1024]{2,1,0:T(8,128)(2,1)S(1)} %pad_maximum_fusion.refs_0_), channel_id=1, source_target_pairs={{0,32},{16,48},{32,64},{48,80},{64,96},{80,112},{96,0},{112,16},{1... | collective-permute-start | bytes 1572872 | tf_op jit(solution)/shard_map/ppermute | solution.py:57
  48.0 11.0 %collective-permute-start.8 = (bf16[128,1024]{1,0:T(8,128)(2,1)S(1)}, bf16[128,1024]{1,0:T(8,128)(2,1)S(1)}, u32[]{:S(2)}, u32[]{:S(2)}) collective-permute-start(bf16[128,1024]{1,0:T(8,128)(2,1)S(1)} %slice_bitcast_fusion.2), channel_id=1, source_target_pairs={{0,96},{16,112},{32,0},{48,16},{64,32},{80,48},{96,64},{112,80},{1... | collective-permute-start | bytes 786440 | tf_op jit(solution)/shard_map/ppermute | solution.py:60
  51.6 14.7 %collective-permute-start.2 = (bf16[2,128,1024]{2,1,0:T(8,128)(2,1)S(1)}, bf16[2,128,1024]{2,1,0:T(8,128)(2,1)S(1)}, u32[]{:S(2)}, u32[]{:S(2)}) collective-permute-start(bf16[2,128,1024]{2,1,0:T(8,128)(2,1)S(1)} %pad_maximum_fusion.refs_0_), channel_id=1, source_target_pairs={{0,16},{16,0},{32,48},{48,32},{64,80},{80,64},{96,112},{112,96},{1... | collective-permute-start | bytes 1572872 | tf_op jit(solution)/shard_map/ppermute | solution.py:64
  59.2 8.6 %collective-permute-start.9 = (bf16[2,128,1024]{2,1,0:T(8,128)(2,1)S(1)}, bf16[2,128,1024]{2,1,0:T(8,128)(2,1)S(1)}, u32[]{:S(2)}, u32[]{:S(2)}) collective-permute-start(bf16[2,128,1024]{2,1,0:T(8,128)(2,1)S(1)} %pad_maximum_fusion.1.refs_6_), channel_id=1, source_target_pairs={{0,16},{16,0},{32,48},{48,32},{64,80},{80,64},{96,112},{112,96},{1... | collective-permute-start | bytes 1572872 | tf_op jit(solution)/shard_map/ppermute | solution.py:64
  83.5 10.3 %collective-permute-start.10 = (bf16[128,1024]{1,0:T(8,128)(2,1)S(1)}, bf16[128,1024]{1,0:T(8,128)(2,1)S(1)}, u32[]{:S(2)}, u32[]{:S(2)}) collective-permute-start(bf16[128,1024]{1,0:T(8,128)(2,1)S(1)} %get-tuple-element.94), channel_id=1, source_target_pairs={{0,0},{1,1},{2,16},{3,17},{4,32},{5,33},{6,48},{7,49},{8,64},{9,65... | collective-permute-start | bytes 786440 | tf_op jit(solution)/shard_map/ppermute | solution.py:46
  87.8 11.7 %collective-permute-start.11 = (bf16[128,1024]{1,0:T(8,128)(2,1)S(1)}, bf16[128,1024]{1,0:T(8,128)(2,1)S(1)}, u32[]{:S(2)}, u32[]{:S(2)}) collective-permute-start(bf16[128,1024]{1,0:T(8,128)(2,1)S(1)} %get-tuple-element.93), channel_id=1, source_target_pairs={{0,1},{1,0},{2,17},{3,16},{4,33},{5,32},{6,49},{7,48},{8,65},{9,64... | collective-permute-start | bytes 786440 | tf_op jit(solution)/shard_map/ppermute | solution.py:46
  101.1 19.1 %collective-permute-start.13 = (bf16[2,128,1024]{2,1,0:T(8,128)(2,1)S(1)}, bf16[2,128,1024]{2,1,0:T(8,128)(2,1)S(1)}, u32[]{:S(2)}, u32[]{:S(2)}) collective-permute-start(bf16[2,128,1024]{2,1,0:T(8,128)(2,1)S(1)} %pad_maximum_fusion.2), channel_id=1, source_target_pairs={{0,32},{16,48},{32,64},{48,80},{64,96},{80,112},{96,0},{112,16},{1... | collective-permute-start | bytes 1572872 | tf_op jit(solution)/shard_map/ppermute | solution.py:57
  110.8 18.3 %collective-permute-start.15 = (bf16[2,128,1024]{2,1,0:T(8,128)(2,1)S(1)}, bf16[2,128,1024]{2,1,0:T(8,128)(2,1)S(1)}, u32[]{:S(2)}, u32[]{:S(2)}) collective-permute-start(bf16[2,128,1024]{2,1,0:T(8,128)(2,1)S(1)} %pad_maximum_fusion.2), channel_id=1, source_target_pairs={{0,96},{16,112},{32,0},{48,16},{64,32},{80,48},{96,64},{112,80},{1... | collective-permute-start | bytes 1572872 | tf_op jit(solution)/shard_map/ppermute | solution.py:58
  111.0 23.4 %collective-permute-start.12 = (bf16[2,128,1024]{2,1,0:T(8,128)(2,1)S(1)}, bf16[2,128,1024]{2,1,0:T(8,128)(2,1)}, u32[]{:S(2)}, u32[]{:S(2)}) collective-permute-start(bf16[2,128,1024]{2,1,0:T(8,128)(2,1)S(1)} %pad_maximum_fusion.2), channel_id=1, source_target_pairs={{0,16},{16,0},{32,48},{48,32},{64,80},{80,64},{96,112},{112,96},{1... | collective-permute-start | bytes 1572872 | tf_op jit(solution)/shard_map/ppermute | solution.py:64
  120.2 16.9 %collective-permute-start.17 = (bf16[128,1024]{1,0:T(8,128)(2,1)S(1)}, bf16[128,1024]{1,0:T(8,128)(2,1)S(1)}, u32[]{:S(2)}, u32[]{:S(2)}) collective-permute-start(bf16[128,1024]{1,0:T(8,128)(2,1)S(1)} %slice_bitcast_fusion.1), channel_id=1, source_target_pairs={{0,32},{16,48},{32,64},{48,80},{64,96},{80,112},{96,0},{112,16},{1... | collective-permute-start | bytes 786440 | tf_op jit(solution)/shard_map/ppermute | solution.py:60
  124.9 13.8 %collective-permute-start.14 = (bf16[2,128,1024]{2,1,0:T(8,128)(2,1)S(1)}, bf16[2,128,1024]{2,1,0:T(8,128)(2,1)}, u32[]{:S(2)}, u32[]{:S(2)}) collective-permute-start(bf16[2,128,1024]{2,1,0:T(8,128)(2,1)S(1)} %collective-permute-done.13), channel_id=1, source_target_pairs={{0,16},{16,0},{32,48},{48,32},{64,80},{80,64},{96,112},{112,96},{1... | collective-permute-start | bytes 1572872 | tf_op jit(solution)/shard_map/ppermute | solution.py:64
  129.1 8.7 %collective-permute-start.18 = (bf16[128,1024]{1,0:T(8,128)(2,1)S(1)}, bf16[128,1024]{1,0:T(8,128)(2,1)S(1)}, u32[]{:S(2)}, u32[]{:S(2)}) collective-permute-start(bf16[128,1024]{1,0:T(8,128)(2,1)S(1)} %slice_bitcast_fusion), channel_id=1, source_target_pairs={{0,96},{16,112},{32,0},{48,16},{64,32},{80,48},{96,64},{112,80},{1... | collective-permute-start | bytes 786440 | tf_op jit(solution)/shard_map/ppermute | solution.py:60
  145.7 42.9 %all-to-all-start = ((bf16[16,144,128]{2,1,0:T(8,128)(2,1)}), bf16[16,144,128]{2,1,0:T(8,128)(2,1)S(1)}, u32[]{:S(2)}, u32[]{:S(2)}) async-start(bf16[16,144,128]{2,1,0:T(8,128)(2,1)} %fusion.1), calls=%async_computation | async-start | bytes 1179648 | tf_op jit(solution)/shard_map/all_to_all | solution.py:366
  155.5 30.7 %collective-permute-start.20 = (bf16[4,128,1024]{2,1,0:T(8,128)(2,1)S(1)}, bf16[4,128,1024]{2,1,0:T(8,128)(2,1)}, u32[]{:S(2)}, u32[]{:S(2)}) collective-permute-start(bf16[4,128,1024]{2,1,0:T(8,128)(2,1)S(1)} %shard_map.139), channel_id=1, source_target_pairs={{0,2},{1,3},{2,0},{3,1},{4,6},{5,7},{6,4},{7,5},{8,10},{9,11},{10,... | collective-permute-start | bytes 3145736 | tf_op jit(solution)/shard_map/ppermute | solution.py:149
  167.6 58.3 %collective-permute-start.21 = (bf16[4,128,1024]{2,1,0:T(8,128)(2,1)}, bf16[4,128,1024]{2,1,0:T(8,128)(2,1)}, u32[]{:S(2)}, u32[]{:S(2)}) collective-permute-start(bf16[4,128,1024]{2,1,0:T(8,128)(2,1)} %get-tuple-element.57), channel_id=1, source_target_pairs={{0,1},{1,2},{2,3},{3,0},{4,5},{5,6},{6,7},{7,4},{8,9},{9,10},{10,1... | collective-permute-start | bytes 3145736 | tf_op jit(solution)/shard_map/ppermute | solution.py:149
  167.9 58.1 %collective-permute-start.22 = (bf16[4,128,1024]{2,1,0:T(8,128)(2,1)}, bf16[4,128,1024]{2,1,0:T(8,128)(2,1)}, u32[]{:S(2)}, u32[]{:S(2)}) collective-permute-start(bf16[4,128,1024]{2,1,0:T(8,128)(2,1)} %get-tuple-element.58), channel_id=1, source_target_pairs={{0,3},{1,0},{2,1},{3,2},{4,7},{5,4},{6,5},{7,6},{8,11},{9,8},{10,9... | collective-permute-start | bytes 3145736 | tf_op jit(solution)/shard_map/ppermute | solution.py:149
  174.0 51.9 %collective-permute-start.23 = (bf16[4,128,1024]{2,1,0:T(8,128)(2,1)S(1)}, bf16[4,128,1024]{2,1,0:T(8,128)(2,1)}, u32[]{:S(2)}, u32[]{:S(2)}) collective-permute-start(bf16[4,128,1024]{2,1,0:T(8,128)(2,1)S(1)} %shard_map.141), channel_id=1, source_target_pairs={{0,8},{1,9},{2,10},{3,11},{4,12},{5,13},{6,14},{7,15},{8,0},{9,1},... | collective-permute-start | bytes 3145736 | tf_op jit(solution)/shard_map/ppermute | solution.py:149
  185.9 45.8 %collective-permute-start.24 = (bf16[4,128,1024]{2,1,0:T(8,128)(2,1)}, bf16[4,128,1024]{2,1,0:T(8,128)(2,1)}, u32[]{:S(2)}, u32[]{:S(2)}) collective-permute-start(bf16[4,128,1024]{2,1,0:T(8,128)(2,1)} %get-tuple-element.61), channel_id=1, source_target_pairs={{0,4},{1,5},{2,6},{3,7},{4,8},{5,9},{6,10},{7,11},{8,12},{9,13},{1... | collective-permute-start | bytes 3145736 | tf_op jit(solution)/shard_map/ppermute | solution.py:149
  186.2 49.3 %collective-permute-start.25 = (bf16[4,128,1024]{2,1,0:T(8,128)(2,1)}, bf16[4,128,1024]{2,1,0:T(8,128)(2,1)}, u32[]{:S(2)}, u32[]{:S(2)}) collective-permute-start(bf16[4,128,1024]{2,1,0:T(8,128)(2,1)} %get-tuple-element.62), channel_id=1, source_target_pairs={{0,12},{1,13},{2,14},{3,15},{4,0},{5,1},{6,2},{7,3},{8,4},{9,5},{1... | collective-permute-start | bytes 3145736 | tf_op jit(solution)/shard_map/ppermute | solution.py:149
  221.9 37.0 %all-to-all-start.1 = ((bf16[16,3,128,128]{3,2,1,0:T(8,128)(2,1)}), bf16[16,3,128,128]{3,2,1,0:T(8,128)(2,1)S(1)}, u32[]{:S(2)}, u32[]{:S(2)}) async-start(bf16[16,3,128,128]{3,2,1,0:T(8,128)(2,1)} %shard_map.138), calls=%async_computation.2 | async-start | bytes 3145728 | tf_op jit(solution)/shard_map/all_to_all | solution.py:370
  239.5 10.9 %collective-permute-start.26 = (bf16[128,1024]{1,0:T(8,128)(2,1)S(1)}, bf16[128,1024]{1,0:T(8,128)(2,1)S(1)}, u32[]{:S(2)}, u32[]{:S(2)}) collective-permute-start(bf16[128,1024]{1,0:T(8,128)(2,1)S(1)} %get-tuple-element.68), channel_id=1, source_target_pairs={{0,4},{1,5},{2,6},{3,7},{4,8},{5,9},{6,10},{7,11},{8,12},{9,13},{1... | collective-permute-start | bytes 786440 | tf_op jit(solution)/shard_map/ppermute | solution.py:149
  242.1 16.8 %collective-permute-start.27 = (bf16[128,1024]{1,0:T(8,128)(2,1)S(1)}, bf16[128,1024]{1,0:T(8,128)(2,1)S(1)}, u32[]{:S(2)}, u32[]{:S(2)}) collective-permute-start(bf16[128,1024]{1,0:T(8,128)(2,1)S(1)} %get-tuple-element.69), channel_id=1, source_target_pairs={{0,8},{1,9},{2,10},{3,11},{4,12},{5,13},{6,14},{7,15},{8,0},{9,1},... | collective-permute-start | bytes 786440 | tf_op jit(solution)/shard_map/ppermute | solution.py:149
  244.2 14.7 %collective-permute-start.28 = (bf16[128,1024]{1,0:T(8,128)(2,1)S(1)}, bf16[128,1024]{1,0:T(8,128)(2,1)S(1)}, u32[]{:S(2)}, u32[]{:S(2)}) collective-permute-start(bf16[128,1024]{1,0:T(8,128)(2,1)S(1)} %get-tuple-element.70), channel_id=1, source_target_pairs={{0,12},{1,13},{2,14},{3,15},{4,0},{5,1},{6,2},{7,3},{8,4},{9,5},{1... | collective-permute-start | bytes 786440 | tf_op jit(solution)/shard_map/ppermute | solution.py:149
  248.5 10.4 %collective-permute-start.29 = (bf16[128,1024]{1,0:T(8,128)(2,1)S(1)}, bf16[128,1024]{1,0:T(8,128)(2,1)S(1)}, u32[]{:S(2)}, u32[]{:S(2)}) collective-permute-start(bf16[128,1024]{1,0:T(8,128)(2,1)S(1)} %get-tuple-element.76), channel_id=1, source_target_pairs={{0,1},{1,2},{2,3},{3,0},{4,5},{5,6},{6,7},{7,4},{8,9},{9,10},{10,1... | collective-permute-start | bytes 786440 | tf_op jit(solution)/shard_map/ppermute | solution.py:149
  248.5 10.4 %collective-permute-start.30 = (bf16[128,1024]{1,0:T(8,128)(2,1)S(1)}, bf16[128,1024]{1,0:T(8,128)(2,1)S(1)}, u32[]{:S(2)}, u32[]{:S(2)}) collective-permute-start(bf16[128,1024]{1,0:T(8,128)(2,1)S(1)} %get-tuple-element.77), channel_id=1, source_target_pairs={{0,2},{1,3},{2,0},{3,1},{4,6},{5,7},{6,4},{7,5},{8,10},{9,11},{10,... | collective-permute-start | bytes 786440 | tf_op jit(solution)/shard_map/ppermute | solution.py:149
  250.4 8.5 %collective-permute-start.31 = (bf16[128,1024]{1,0:T(8,128)(2,1)S(1)}, bf16[128,1024]{1,0:T(8,128)(2,1)S(1)}, u32[]{:S(2)}, u32[]{:S(2)}) collective-permute-start(bf16[128,1024]{1,0:T(8,128)(2,1)S(1)} %get-tuple-element.78), channel_id=1, source_target_pairs={{0,3},{1,0},{2,1},{3,2},{4,7},{5,4},{6,5},{7,6},{8,11},{9,8},{10,9... | collective-permute-start | bytes 786440 | tf_op jit(solution)/shard_map/ppermute | solution.py:149
  263.8 10.3 %collective-permute-start.32 = (f32[4,128,128]{2,1,0:T(8,128)S(1)}, f32[4,128,128]{2,1,0:T(8,128)S(1)}, u32[]{:S(2)}, u32[]{:S(2)}) collective-permute-start(f32[4,128,128]{2,1,0:T(8,128)S(1)} %get-tuple-element.80), channel_id=1, source_target_pairs={{0,16},{16,0},{32,48},{48,32},{64,80},{80,64},{96,112},{112,96},{1... | collective-permute-start | bytes 786440 | tf_op jit(solution)/shard_map/ppermute | solution.py:190
  274.1 9.0 %collective-permute-start.33 = (bf16[4,128,128]{2,1,0:T(8,128)(2,1)S(1)}, bf16[4,128,128]{2,1,0:T(8,128)(2,1)S(1)}, u32[]{:S(2)}, u32[]{:S(2)}) collective-permute-start(bf16[4,128,128]{2,1,0:T(8,128)(2,1)S(1)} %add_convert_fusion.a), channel_id=1, source_target_pairs={{0,96},{16,112},{32,0},{48,16},{64,32},{80,48},{96,64},{112,80},{1... | collective-permute-start | bytes 393224 | tf_op jit(solution)/shard_map/ppermute | solution.py:192
  277.6 9.1 %collective-permute-start.35 = (bf16[4,128,128]{2,1,0:T(8,128)(2,1)S(1)}, bf16[4,128,128]{2,1,0:T(8,128)(2,1)S(1)}, u32[]{:S(2)}, u32[]{:S(2)}) collective-permute-start(bf16[4,128,128]{2,1,0:T(8,128)(2,1)S(1)} %add_convert_fusion.a), channel_id=1, source_target_pairs={{0,32},{16,48},{32,64},{48,80},{64,96},{80,112},{96,0},{112,16},{1... | collective-permute-start | bytes 393224 | tf_op jit(solution)/shard_map/ppermute | solution.py:192
  (23 other events, 415.4 us)
Sparse Core Ops, SparseCore 0:
  83.5 135.3 reduce-scatter.1

commit v8 on v4

--- a/solution.py
+++ b/solution.py
@@ -8,7 +8,6 @@
 SIDE = 4
 CORES = 2
 F32 = jnp.float32
-LONG_CHAIN = 10**11
 RING_VMEM = 52 * 2**20
 
 
@@ -215,7 +214,7 @@
     return pl.BlockSpec(shape, lambda i: (0,) * len(shape))
 
 
-def small_call(kernel, shapes, scalars, arrays, scratch=(), flops=0):
+def small_call(kernel, shapes, scalars, arrays, scratch=()):
     return pl.pallas_call(
         kernel,
         out_shape=[jax.ShapeDtypeStruct(shape, kind) for shape, kind in shapes],
@@ -225,29 +224,29 @@
         out_specs=[whole(shape) for shape, _ in shapes],
         scratch_shapes=list(scratch),
         compiler_params=pltpu.CompilerParams(vmem_limit_bytes=RING_VMEM),
-        cost_estimate=pl.CostEstimate(flops=flops, bytes_accessed=2**20, transcendentals=0),
+        cost_estimate=pl.CostEstimate(flops=0, bytes_accessed=2**20, transcendentals=0),
     )(*scalars, *arrays)
 
 
-def outgoing(place, readers, pattern, total):
+def outgoing(place, readers, pattern, total, cut):
     count, block = total.shape[:2]
 
-    def kernel(place_ref, readers_ref, pattern_ref, total_ref, out_ref):
+    def kernel(place_ref, readers_ref, pattern_ref, total_ref, cut_ref, out_ref):
         for d in range(count):
             for j, k in enumerate((d, readers_ref[d])):
                 value = total_ref[place_ref[k]].astype(F32) * pattern_ref[k].astype(F32)
                 out_ref[d, j] = (-value).astype(out_ref.dtype)
+            out_ref[d, 2] = cut_ref[readers_ref[d], :block]
 
     return small_call(
         kernel,
-        [((count, 2, block, block), jnp.bfloat16)],
+        [((count, 3, block, block), jnp.bfloat16)],
         [place, readers, pattern],
-        [total],
-        flops=LONG_CHAIN,
+        [total, cut],
     )[0]
 
 
-def finish_rows(pattern, back, parent_panels, masked_one, masked_two, lead, second):
+def finish_rows(pattern, back, masked_one, masked_two, lead, second):
     count, _, block, _ = back.shape
     width = count * block
     kind = back.dtype
@@ -256,7 +255,7 @@
         return lax.dot_general(a, b, (((1,), (1,)), ((), ())), preferred_element_type=F32)
 
     def kernel(
-        pattern_ref, back_ref, panels_ref, one_ref, two_ref, lead_ref, *refs
+        pattern_ref, back_ref, one_ref, two_ref, lead_ref, *refs
     ):
         terms = [refs[: len(second) // 2], refs[len(second) // 2 : len(second)]]
         rows_one_ref, rows_two_ref, sums_ref, chosen, panels = refs[len(second) :]
@@ -264,7 +263,7 @@
             part = pl.ds(i * block, block)
             rows_one_ref[:, part] = back_ref[i, 0]
             chosen[:, part] = back_ref[i, 1]
-            panels[:, part] = panels_ref[i]
+            panels[:, part] = back_ref[i, 2]
         for i in range(count):
             part = pl.ds(i * block, block)
             side, first = i * 2 // count, i % (count // 2) * block
@@ -281,7 +280,7 @@
         kernel,
         [((block, width), kind), ((block, width), kind), ((4, block, block), F32)],
         [pattern],
-        [back, parent_panels, masked_one, masked_two, lead, *second],
+        [back, masked_one, masked_two, lead, *second],
         [pltpu.VMEM((block, width), kind), pltpu.VMEM((block, width), kind)],
     )
 
@@ -352,17 +351,34 @@
     masked_two = apply_pattern(level_two_panels, level_two_pattern, block)
 
     found_one = all_panels(in_order([turned_panels(masked_one, k) for k in range(2)]))
-    later_two, _ = lax.optimization_barrier((masked_two, found_one[2:6:2]))
-    early_two = turned_panels(later_two, 0)
-    early_two, found_one = lax.optimization_barrier((early_two, found_one))
+    later_two, found_one = lax.optimization_barrier((masked_two, found_one))
+    own_two = in_order([turned_panels(later_two, k) for k in range(2)])
     product_one = by_column(found_one, ancestor_inverse, block)
-    later_two, product_one = lax.optimization_barrier((masked_two, product_one))
-    own_two = in_order([early_two, turned_panels(later_two, 1)])
-    later_one, own_two = lax.optimization_barrier((masked_one, own_two))
     first_sum = lax.psum_scatter(
         product_one.reshape(count * count * block, block), "col", scatter_dimension=0, tiled=True
     ).reshape(count, block, block)
 
+    steps = jnp.arange(count, dtype=jnp.int32)
+    place = arrival(steps)
+    outer, inner = steps // SIDE, steps % SIDE
+    x_major = (y + inner) % SIDE * SIDE + (x + outer) % SIDE
+    y_major = (y + outer) % SIDE * SIDE + (x + inner) % SIDE
+
+    rows_two = jnp.concatenate(all_panels(own_two), 0)
+
+    def ring(order, part, step):
+        order = place[order].reshape(SIDE, -1)
+        low, high = by_supernode(order[2], rows_two, ancestor_inverse, part, True)
+        arriving = send(low[0], step(1)), send(high[0], step(-1))
+        rest, low = lax.optimization_barrier((jnp.concatenate([order[1], order[3], order[0]]), low))
+        return arriving, by_supernode(rest, rows_two, ancestor_inverse, part, False)[0]
+
+    first_a, near_a = ring(x_major, 0, x_step)
+    first_b, near_b = ring(y_major, 1, y_step)
+    second_a = second_sends(first_a, near_a, x_step)
+    second_b = second_sends(first_b, near_b, y_step)
+
+    later_one, _ = lax.optimization_barrier((masked_one, rows_two))
     facts = jnp.concatenate(
         [
             jnp.broadcast_to(level_one_pattern.reshape(count, 1, 1), (count, 8, block)),
@@ -374,35 +390,12 @@
     cut = lax.all_to_all(jnp.concatenate([cut, facts], 1), "col", 0, 0, tiled=True)
     cut_pattern = cut[:, block, 0].astype(jnp.int32)
     readers = cut[:, block + 8, 0].astype(jnp.int32)
-    parent_panels = lax.all_to_all(
-        jnp.take(cut[:, :block], readers, axis=0), "col", 0, 0, tiled=True
-    )
-    rows_two = lax.all_gather(own_two, "row", axis=0, tiled=True)
-
-    steps = jnp.arange(count, dtype=jnp.int32)
-    place = arrival(steps)
-    outer, inner = steps // SIDE, steps % SIDE
-    x_major = (y + inner) % SIDE * SIDE + (x + outer) % SIDE
-    y_major = (y + outer) % SIDE * SIDE + (x + inner) % SIDE
-
-    def ring(order, part, step):
-        order = order.reshape(SIDE, -1)
-        low, high = by_supernode(order[2], rows_two, ancestor_inverse, part, True)
-        arriving = send(low[0], step(1)), send(high[0], step(-1))
-        rest = jnp.concatenate([order[1], order[3], order[0]])
-        return arriving, by_supernode(rest, rows_two, ancestor_inverse, part, False)[0]
-
-    first_a, near_a = ring(x_major, 0, x_step)
-    first_b, near_b = ring(y_major, 1, y_step)
-    first_a, first_b, parent_panels = lax.optimization_barrier((first_a, first_b, parent_panels))
-    second_a = second_sends(first_a, near_a, x_step)
-    second_b = second_sends(first_b, near_b, y_step)
-    going = outgoing(place, readers, cut_pattern, first_sum)
+    going = outgoing(place, readers, cut_pattern, first_sum, cut)
     back = lax.all_to_all(going, "col", 0, 0, tiled=True)
     second_a, second_b, _ = lax.optimization_barrier((second_a, second_b, going))
     second_sum = third_sends(second_a, near_a, y_step) + third_sends(second_b, near_b, x_step)
     level_one_rows, level_two_rows, sums = finish_rows(
-        level_two_pattern, back, parent_panels, masked_one, masked_two, parent_lead, second_sum
+        level_two_pattern, back, masked_one, masked_two, parent_lead, second_sum
     )
 
     diag_blocks = level_one_diag.reshape(count, block, block)

time: 288 us -> 288 us (level)
  waiting for transfers between devices: 91.1 us -> 71.4 us
  starting transfers between devices: 106 us -> 120 us
  local copies, waits for them, and re-layouts: 9.2 us -> 17 us
    reduce_scatter x1, waiting for transfers between devices: 24.6 us -> 0.02 us  [per_device(): lax.psum_scatter(product_one.reshape(count * count * block, block), 'col'...]
    all_to_all x1, starting transfers between devices: 22.6 us -> 5.74 us  [per_device(): lax.all_to_all(jnp.concatenate([cut, facts], 1), 'col', 0, 0, tiled=True)]
    ppermute x14, waiting for transfers between devices: 18.9 us -> 34 us  [send(): return lax.ppermute(value, 'col', step)]
    ppermute x4 -> x8, starting transfers between devices: 14.4 us -> 29 us  [all_panels(): found += [held, lax.ppermute(held, 'row', CORE_SWAP)]]
    all_to_all x1, waiting for transfers between devices: 14.1 us -> 0.01 us  [per_device(): lax.all_to_all(jnp.concatenate([cut, facts], 1), 'col', 0, 0, tiled=True)]
    ppermute x1 -> x2, starting transfers between devices: 0.01 us -> 9.74 us  [all_panels(): below = lax.ppermute(own, 'row', z_step(1))]
    ppermute x1, starting transfers between devices: 1.36 us -> 9.67 us  [row_parts(): values = values + lax.ppermute(values, 'row', CORE_SWAP)]
    unnamed x36 -> x41, local copies, waits for them, and re-layouts: 6.34 us -> 11.9 us
  transfers between devices with their start and end apart: 35 -> 41, of which waited for: 19 -> 17; matrix products, arithmetic and copies ran while one was open for 2% -> 5% of each run, Pallas kernels for 14% -> 13%
where the time goes in v8:
time: 288 us; the launch traced here: 287 us
  starting transfers between devices  120 us (42%)
  waiting for transfers between devices  71.4 us (25%)
  Pallas kernels  57.9 us (20%)
  local copies, waits for them, and re-layouts  17 us (6%)
  between operations  15.2 us (5%)
  other arithmetic  5.4 us (2%)
    ppermute x14, waiting for transfers between devices, send(): return lax.ppermute(value, 'col', step)  34 us
    ppermute x8, starting transfers between devices, all_panels(): found += [held, lax.ppermute(held, 'row', CORE_SWAP)]  29 us
    pallas_call x4, Pallas kernels, by_supernode(): pl.pallas_call(kernel, out_shape=[jax.ShapeDtypeStruct((groups, SIDE, siz...  23 us
    ppermute x14, starting transfers between devices, send(): return lax.ppermute(value, 'col', step)  18.4 us
    ppermute x4, waiting for transfers between devices, turned_panels(): return lax.ppermute(part, ('row', 'col'), turn(k))  16.1 us
    ppermute x2, starting transfers between devices, all_panels(): above = lax.ppermute(own, 'row', z_step(-1))  15.4 us
    pallas_call x1, Pallas kernels, by_column(): pl.pallas_call(kernel, out_shape=jax.ShapeDtypeStruct((width // block, st...  14.7 us
    ppermute x4, starting transfers between devices, turned_panels(): return lax.ppermute(part, ('row', 'col'), turn(k))  12.6 us
  transfers between devices with their start and end apart: 41, of which 17 were waited for; matrix products, arithmetic and copies ran while one was open for 5% of the time, Pallas kernels for 13%

profile of v8, /device:TPU:1, one launch (start us, length us, event | category | flops | bytes accessed | tf_op | source)
XLA Modules:
  0.0 286.7 jit_solution(17470471123805418118)
XLA Ops:
  9.2 6.0 %collective-permute-start = (bf16[128,1024]{1,0:T(8,128)(2,1)S(1)}, bf16[128,1024]{1,0:T(8,128)(2,1)S(1)}, u32[]{:S(2)}, u32[]{:S(2)}) collective-permute-start(bf16[128,1024]{1,0:T(8,128)(2,1)S(1)} %get-tuple-element.93), channel_id=1, source_target_pairs={{0,0},{1,1},{2,16},{3,17},{4,32},{5,33},{6,48},{7,49},{8,64},{9,65... | collective-permute-start | bytes 786440 | tf_op jit(solution)/shard_map/ppermute | solution.py:46
  15.9 5.2 %collective-permute-done = bf16[128,1024]{1,0:T(8,128)(2,1)S(1)} collective-permute-done((bf16[128,1024]{1,0:T(8,128)(2,1)S(1)}, bf16[128,1024]{1,0:T(8,128)(2,1)S(1)}, u32[]{:S(2)}, u32[]{:S(2)}) %collective-permute-start) | collective-permute-done | bytes 262176 | tf_op jit(solution)/shard_map/ppermute | solution.py:46
  23.7 15.4 %collective-permute-start.5 = (bf16[2,128,1024]{2,1,0:T(8,128)(2,1)S(1)}, bf16[2,128,1024]{2,1,0:T(8,128)(2,1)S(1)}, u32[]{:S(2)}, u32[]{:S(2)}) collective-permute-start(bf16[2,128,1024]{2,1,0:T(8,128)(2,1)S(1)} %pad_maximum_fusion.refs_0_), channel_id=1, source_target_pairs={{0,96},{16,112},{32,0},{48,16},{64,32},{80,48},{96,64},{112,80},{1... | collective-permute-start | bytes 1572872 | tf_op jit(solution)/shard_map/ppermute | solution.py:58
  39.1 8.9 %collective-permute-done.5.refs_4_ = bf16[2,128,1024]{2,1,0:T(8,128)(2,1)S(1)} collective-permute-done((bf16[2,128,1024]{2,1,0:T(8,128)(2,1)S(1)}, bf16[2,128,1024]{2,1,0:T(8,128)(2,1)S(1)}, u32[]{:S(2)}, u32[]{:S(2)}) %collective-permute-start.5) | collective-permute-done | bytes 524320 | tf_op jit(solution)/shard_map/ppermute | solution.py:58
  48.0 3.5 %collective-permute-start.8 = (bf16[128,1024]{1,0:T(8,128)(2,1)S(1)}, bf16[128,1024]{1,0:T(8,128)(2,1)S(1)}, u32[]{:S(2)}, u32[]{:S(2)}) collective-permute-start(bf16[128,1024]{1,0:T(8,128)(2,1)S(1)} %slice_bitcast_fusion.2), channel_id=1, source_target_pairs={{0,96},{16,112},{32,0},{48,16},{64,32},{80,48},{96,64},{112,80},{1... | collective-permute-start | bytes 786440 | tf_op jit(solution)/shard_map/ppermute | solution.py:60
  51.6 6.9 %collective-permute-start.2 = (bf16[2,128,1024]{2,1,0:T(8,128)(2,1)S(1)}, bf16[2,128,1024]{2,1,0:T(8,128)(2,1)S(1)}, u32[]{:S(2)}, u32[]{:S(2)}) collective-permute-start(bf16[2,128,1024]{2,1,0:T(8,128)(2,1)S(1)} %pad_maximum_fusion.refs_0_), channel_id=1, source_target_pairs={{0,16},{16,0},{32,48},{48,32},{64,80},{80,64},{96,112},{112,96},{1... | collective-permute-start | bytes 1572872 | tf_op jit(solution)/shard_map/ppermute | solution.py:64
  59.2 7.0 %collective-permute-start.9 = (bf16[2,128,1024]{2,1,0:T(8,128)(2,1)S(1)}, bf16[2,128,1024]{2,1,0:T(8,128)(2,1)S(1)}, u32[]{:S(2)}, u32[]{:S(2)}) collective-permute-start(bf16[2,128,1024]{2,1,0:T(8,128)(2,1)S(1)} %pad_maximum_fusion.1.refs_6_), channel_id=1, source_target_pairs={{0,16},{16,0},{32,48},{48,32},{64,80},{80,64},{96,112},{112,96},{1... | collective-permute-start | bytes 1572872 | tf_op jit(solution)/shard_map/ppermute | solution.py:64
  68.6 14.7 %shard_map.137 = bf16[16,2048,128]{2,1,0:T(8,128)(2,1)} custom-call(bf16[2,128,1024]{2,1,0:T(8,128)(2,1)S(1)} %pad_maximum_fusion.refs_0_, bf16[2,128,1024]{2,1,0:T(8,128)(2,1)S(1)} %collective-permute-done.2.refs_1_, bf16[2,128,1024]{2,1,0:T(8,128)(2,1)S(1)} %collective-permute-done.3.refs_2_, bf16[2,128,1024]{2,1,0:T(8,128)(2,1)} %copy-done.14, ...), custom_call_target="tpu_custom_call" | custom-call | flops 8589934592 | bytes 16777216 | tf_op jit(solution)/shard_map/pallas_call | solution.py:93
  84.7 4.3 %collective-permute-start.10 = (bf16[128,1024]{1,0:T(8,128)(2,1)S(1)}, bf16[128,1024]{1,0:T(8,128)(2,1)S(1)}, u32[]{:S(2)}, u32[]{:S(2)}) collective-permute-start(bf16[128,1024]{1,0:T(8,128)(2,1)S(1)} %get-tuple-element.90), channel_id=1, source_target_pairs={{0,0},{1,1},{2,16},{3,17},{4,32},{5,33},{6,48},{7,49},{8,64},{9,65... | collective-permute-start | bytes 786440 | tf_op jit(solution)/shard_map/ppermute | solution.py:46
  91.9 4.5 %collective-permute-done.10 = bf16[128,1024]{1,0:T(8,128)(2,1)S(1)} collective-permute-done((bf16[128,1024]{1,0:T(8,128)(2,1)S(1)}, bf16[128,1024]{1,0:T(8,128)(2,1)S(1)}, u32[]{:S(2)}, u32[]{:S(2)}) %collective-permute-start.10) | collective-permute-done | bytes 262176 | tf_op jit(solution)/shard_map/ppermute | solution.py:46
  96.4 3.9 %collective-permute-done.11 = bf16[128,1024]{1,0:T(8,128)(2,1)S(1)} collective-permute-done((bf16[128,1024]{1,0:T(8,128)(2,1)S(1)}, bf16[128,1024]{1,0:T(8,128)(2,1)S(1)}, u32[]{:S(2)}, u32[]{:S(2)}) %collective-permute-start.11) | collective-permute-done | bytes 262176 | tf_op jit(solution)/shard_map/ppermute | solution.py:46
  101.9 9.7 %collective-permute-start.13 = (bf16[2,128,1024]{2,1,0:T(8,128)(2,1)S(1)}, bf16[2,128,1024]{2,1,0:T(8,128)(2,1)S(1)}, u32[]{:S(2)}, u32[]{:S(2)}) collective-permute-start(bf16[2,128,1024]{2,1,0:T(8,128)(2,1)S(1)} %pad_maximum_fusion.2), channel_id=1, source_target_pairs={{0,32},{16,48},{32,64},{48,80},{64,96},{80,112},{96,0},{112,16},{1... | collective-permute-start | bytes 1572872 | tf_op jit(solution)/shard_map/ppermute | solution.py:57
  111.9 9.1 %collective-permute-start.12 = (bf16[2,128,1024]{2,1,0:T(8,128)(2,1)S(1)}, bf16[2,128,1024]{2,1,0:T(8,128)(2,1)}, u32[]{:S(2)}, u32[]{:S(2)}) collective-permute-start(bf16[2,128,1024]{2,1,0:T(8,128)(2,1)S(1)} %pad_maximum_fusion.2), channel_id=1, source_target_pairs={{0,16},{16,0},{32,48},{48,32},{64,80},{80,64},{96,112},{112,96},{1... | collective-permute-start | bytes 1572872 | tf_op jit(solution)/shard_map/ppermute | solution.py:64
  121.1 5.3 %collective-permute-start.17 = (bf16[128,1024]{1,0:T(8,128)(2,1)S(1)}, bf16[128,1024]{1,0:T(8,128)(2,1)S(1)}, u32[]{:S(2)}, u32[]{:S(2)}) collective-permute-start(bf16[128,1024]{1,0:T(8,128)(2,1)S(1)} %slice_bitcast_fusion.1), channel_id=1, source_target_pairs={{0,32},{16,48},{32,64},{48,80},{64,96},{80,112},{96,0},{112,16},{1... | collective-permute-start | bytes 786440 | tf_op jit(solution)/shard_map/ppermute | solution.py:60
  126.4 4.2 %collective-permute-start.14 = (bf16[2,128,1024]{2,1,0:T(8,128)(2,1)S(1)}, bf16[2,128,1024]{2,1,0:T(8,128)(2,1)S(1)}, u32[]{:S(2)}, u32[]{:S(2)}) collective-permute-start(bf16[2,128,1024]{2,1,0:T(8,128)(2,1)S(1)} %collective-permute-done.13), channel_id=1, source_target_pairs={{0,16},{16,0},{32,48},{48,32},{64,80},{80,64},{96,112},{112,96},{1... | collective-permute-start | bytes 1572872 | tf_op jit(solution)/shard_map/ppermute | solution.py:64
  147.0 5.7 %all-to-all-start = ((bf16[16,144,128]{2,1,0:T(8,128)(2,1)}), bf16[16,144,128]{2,1,0:T(8,128)(2,1)S(1)}, u32[]{:S(2)}, u32[]{:S(2)}) async-start(bf16[16,144,128]{2,1,0:T(8,128)(2,1)} %fusion.1), calls=%async_computation | async-start | bytes 1179648 | tf_op jit(solution)/shard_map/all_to_all | solution.py:390
  152.8 3.8 %shard_map.139 = (bf16[1,4,64,1024]{3,2,1,0:T(8,128)(2,1)S(1)}, bf16[1,4,64,1024]{3,2,1,0:T(8,128)(2,1)S(1)}) custom-call(s32[4]{0:T(128)S(1)} %get-tuple-element.101.order_ref, bf16[16,128,1024]{2,1,0:T(8,128)(2,1)} %constant_dynamic-update-slice_fusion.a_ref.b_ref.c_ref.d_ref, ...), custom_call_target="tpu_custom_call" | custom-call | flops 1073741824 | bytes 2097152 | tf_op jit(solution)/shard_map/pallas_call | solution.py:127
  159.3 3.7 %shard_map.142 = (bf16[1,4,64,1024]{3,2,1,0:T(8,128)(2,1)S(1)}, bf16[1,4,64,1024]{3,2,1,0:T(8,128)(2,1)S(1)}) custom-call(s32[4]{0:T(128)S(1)} %get-tuple-element.97.order_ref, bf16[16,128,1024]{2,1,0:T(8,128)(2,1)} %constant_dynamic-update-slice_fusion.a_ref.b_ref.c_ref.d_ref, ...), custom_call_target="tpu_custom_call" | custom-call | flops 1073741824 | bytes 2097152 | tf_op jit(solution)/shard_map/pallas_call | solution.py:127
  166.0 7.9 %shard_map.140.ahead_ref.behind_ref.own_ref = bf16[3,4,128,1024]{3,2,1,0:T(8,128)(2,1)} custom-call(s32[12]{0:T(128)S(1)} %pad_add_fusion.order_ref, bf16[16,128,1024]{2,1,0:T(8,128)(2,1)} %constant_dynamic-update-slice_fusion.a_ref.b_ref.c_ref.d_ref, bf16[16,128,1024]{2,1,0:T(8,128)(2,1)} %constant_dynamic-update-slice_fusion.a_ref.b_ref.c_ref.d_ref, ...), custom_call_target="tpu_custom_call" | custom-call | flops 3221225472 | bytes 6291456 | tf_op jit(solution)/shard_map/pallas_call | solution.py:127
  173.8 7.7 %shard_map.143.ahead_ref.behind_ref.own_ref = bf16[3,4,128,1024]{3,2,1,0:T(8,128)(2,1)} custom-call(s32[12]{0:T(128)S(1)} %pad_add_fusion.1.order_ref, bf16[16,128,1024]{2,1,0:T(8,128)(2,1)} %constant_dynamic-update-slice_fusion.a_ref.b_ref.c_ref.d_ref, bf16[16,128,1024]{2,1,0:T(8,128)(2,1)} %constant_dynamic-update-slice_fusion.a_ref.b_ref.c_ref.d_ref, ...), custom_call_target="tpu_custom_call" | custom-call | flops 3221225472 | bytes 6291456 | tf_op jit(solution)/shard_map/pallas_call | solution.py:127
  181.5 3.8 %shard_map.141 = (bf16[4,128,1024]{2,1,0:T(8,128)(2,1)}, bf16[4,128,1024]{2,1,0:T(8,128)(2,1)}) custom-call(bf16[4,64,1024]{2,1,0:T(8,128)(2,1)S(1)} %collective-permute-done.20.low_ref, bf16[4,64,1024]{2,1,0:T(8,128)(2,1)S(1)} %collective-permute-done.21.high_ref, bf16[3,4,128,1024]{3,2,1,0:T(8,128)(2,1)} %shard_map.140.ahead_ref.behind_ref.own_ref, ...), custom_call_target="tpu_custom_call" | custom-call | bytes 4194304 | tf_op jit(solution)/shard_map/pallas_call | solution.py:167
  188.0 3.8 %shard_map.144 = (bf16[4,128,1024]{2,1,0:T(8,128)(2,1)}, bf16[4,128,1024]{2,1,0:T(8,128)(2,1)}) custom-call(bf16[4,64,1024]{2,1,0:T(8,128)(2,1)S(1)} %collective-permute-done.24.low_ref, bf16[4,64,1024]{2,1,0:T(8,128)(2,1)S(1)} %collective-permute-done.25.high_ref, bf16[3,4,128,1024]{3,2,1,0:T(8,128)(2,1)} %shard_map.143.ahead_ref.behind_ref.own_ref, ...), custom_call_target="tpu_custom_call" | custom-call | bytes 4194304 | tf_op jit(solution)/shard_map/pallas_call | solution.py:167
  198.2 3.7 %all-to-all-start.1 = ((bf16[16,3,128,128]{3,2,1,0:T(8,128)(2,1)}), bf16[16,3,128,128]{3,2,1,0:T(8,128)(2,1)S(1)}, u32[]{:S(2)}, u32[]{:S(2)}) async-start(bf16[16,3,128,128]{3,2,1,0:T(8,128)(2,1)} %shard_map.138), calls=%async_computation.2 | async-start | bytes 3145728 | tf_op jit(solution)/shard_map/all_to_all | solution.py:394
  201.9 9.4 %collective-permute-done.22.one_ref = bf16[4,128,1024]{2,1,0:T(8,128)(2,1)S(1)} collective-permute-done((bf16[4,128,1024]{2,1,0:T(8,128)(2,1)}, bf16[4,128,1024]{2,1,0:T(8,128)(2,1)S(1)}, u32[]{:S(2)}, u32[]{:S(2)}) %collective-permute-start.22) | collective-permute-done | bytes 1048608 | tf_op jit(solution)/shard_map/ppermute | solution.py:148
  211.4 16.4 %collective-permute-done.26.one_ref = bf16[4,128,1024]{2,1,0:T(8,128)(2,1)} collective-permute-done((bf16[4,128,1024]{2,1,0:T(8,128)(2,1)}, bf16[4,128,1024]{2,1,0:T(8,128)(2,1)}, u32[]{:S(2)}, u32[]{:S(2)}) %collective-permute-start.26) | collective-permute-done | bytes 1048608 | tf_op jit(solution)/shard_map/ppermute | solution.py:148
  232.3 4.7 %collective-permute-start.29 = (bf16[128,1024]{1,0:T(8,128)(2,1)S(1)}, bf16[128,1024]{1,0:T(8,128)(2,1)S(1)}, u32[]{:S(2)}, u32[]{:S(2)}) collective-permute-start(bf16[128,1024]{1,0:T(8,128)(2,1)S(1)} %get-tuple-element.67), channel_id=1, source_target_pairs={{0,8},{1,9},{2,10},{3,11},{4,12},{5,13},{6,14},{7,15},{8,0},{9,1},... | collective-permute-start | bytes 786440 | tf_op jit(solution)/shard_map/ppermute | solution.py:148
  243.7 6.2 %collective-permute-done.31.refs_5_ = bf16[128,1024]{1,0:T(8,128)(2,1)S(1)} collective-permute-done((bf16[128,1024]{1,0:T(8,128)(2,1)S(1)}, bf16[128,1024]{1,0:T(8,128)(2,1)S(1)}, u32[]{:S(2)}, u32[]{:S(2)}) %collective-permute-start.31) | collective-permute-done | bytes 262176 | tf_op jit(solution)/shard_map/ppermute | solution.py:148
  251.8 3.6 %shard_map.147 = (bf16[128,2048]{1,0:T(8,128)(2,1)}, bf16[128,2048]{1,0:T(8,128)(2,1)}, f32[4,128,128]{2,1,0:T(8,128)S(1)}) custom-call(s32[1,16]{1,0:T(1,128)S(1)} %copy-done.5, bf16[16,3,128,128]{3,2,1,0:T(8,128)(2,1)} %copy-done.8, bf16[128,2048]{1,0:T(8,128)(2,1)} %copy-done.7, bf16[128,2048]{1,0:T(8,128)(2,1)} %copy-done.9, ...), custom_call_target="tpu_custom_call" | custom-call | bytes 1048576 | tf_op jit(solution)/shard_map/pallas_call | solution.py:218
  255.4 9.7 %collective-permute-start.34 = (f32[4,128,128]{2,1,0:T(8,128)S(1)}, f32[4,128,128]{2,1,0:T(8,128)S(1)}, u32[]{:S(2)}, u32[]{:S(2)}) collective-permute-start(f32[4,128,128]{2,1,0:T(8,128)S(1)} %get-tuple-element.76), channel_id=1, source_target_pairs={{0,16},{16,0},{32,48},{48,32},{64,80},{80,64},{96,112},{112,96},{1... | collective-permute-start | bytes 786440 | tf_op jit(solution)/shard_map/ppermute | solution.py:208
  266.2 3.2 %collective-permute-start.35 = (bf16[4,128,128]{2,1,0:T(8,128)(2,1)S(1)}, bf16[4,128,128]{2,1,0:T(8,128)(2,1)S(1)}, u32[]{:S(2)}, u32[]{:S(2)}) collective-permute-start(bf16[4,128,128]{2,1,0:T(8,128)(2,1)S(1)} %add_convert_fusion.a), channel_id=1, source_target_pairs={{0,96},{16,112},{32,0},{48,16},{64,32},{80,48},{96,64},{112,80},{1... | collective-permute-start | bytes 393224 | tf_op jit(solution)/shard_map/ppermute | solution.py:210
  271.0 3.8 %collective-permute-done.35.b = bf16[4,128,128]{2,1,0:T(8,128)(2,1)S(1)} collective-permute-done((bf16[4,128,128]{2,1,0:T(8,128)(2,1)S(1)}, bf16[4,128,128]{2,1,0:T(8,128)(2,1)S(1)}, u32[]{:S(2)}, u32[]{:S(2)}) %collective-permute-start.35) | collective-permute-done | bytes 131104 | tf_op jit(solution)/shard_map/ppermute | solution.py:210
  275.5 3.2 %collective-permute-done.37.d = bf16[4,128,128]{2,1,0:T(8,128)(2,1)S(1)} collective-permute-done((bf16[4,128,128]{2,1,0:T(8,128)(2,1)S(1)}, bf16[4,128,128]{2,1,0:T(8,128)(2,1)S(1)}, u32[]{:S(2)}, u32[]{:S(2)}) %collective-permute-start.37) | collective-permute-done | bytes 131104 | tf_op jit(solution)/shard_map/ppermute | solution.py:210
  (143 shorter events, 62.4 us)
Async XLA Ops:
  7.2 188.0 %reduce-scatter.2.cloned.1.call-start = ((), (), s32[]{:S(2)}) async-start(), calls=%async_computation.3 | async-start | bytes 8912896 | tf_op jit(solution)/shard_map/reduce_scatter | solution.py:357
  9.2 11.9 %collective-permute-start = (bf16[128,1024]{1,0:T(8,128)(2,1)S(1)}, bf16[128,1024]{1,0:T(8,128)(2,1)S(1)}, u32[]{:S(2)}, u32[]{:S(2)}) collective-permute-start(bf16[128,1024]{1,0:T(8,128)(2,1)S(1)} %get-tuple-element.93), channel_id=1, source_target_pairs={{0,0},{1,1},{2,16},{3,17},{4,32},{5,33},{6,48},{7,49},{8,64},{9,65... | collective-permute-start | bytes 786440 | tf_op jit(solution)/shard_map/ppermute | solution.py:46
  23.7 24.3 %collective-permute-start.5 = (bf16[2,128,1024]{2,1,0:T(8,128)(2,1)S(1)}, bf16[2,128,1024]{2,1,0:T(8,128)(2,1)S(1)}, u32[]{:S(2)}, u32[]{:S(2)}) collective-permute-start(bf16[2,128,1024]{2,1,0:T(8,128)(2,1)S(1)} %pad_maximum_fusion.refs_0_), channel_id=1, source_target_pairs={{0,96},{16,112},{32,0},{48,16},{64,32},{80,48},{96,64},{112,80},{1... | collective-permute-start | bytes 1572872 | tf_op jit(solution)/shard_map/ppermute | solution.py:58
  39.1 12.4 %collective-permute-start.3 = (bf16[2,128,1024]{2,1,0:T(8,128)(2,1)S(1)}, bf16[2,128,1024]{2,1,0:T(8,128)(2,1)S(1)}, u32[]{:S(2)}, u32[]{:S(2)}) collective-permute-start(bf16[2,128,1024]{2,1,0:T(8,128)(2,1)S(1)} %pad_maximum_fusion.refs_0_), channel_id=1, source_target_pairs={{0,32},{16,48},{32,64},{48,80},{64,96},{80,112},{96,0},{112,16},{1... | collective-permute-start | bytes 1572872 | tf_op jit(solution)/shard_map/ppermute | solution.py:57
  48.0 11.0 %collective-permute-start.8 = (bf16[128,1024]{1,0:T(8,128)(2,1)S(1)}, bf16[128,1024]{1,0:T(8,128)(2,1)S(1)}, u32[]{:S(2)}, u32[]{:S(2)}) collective-permute-start(bf16[128,1024]{1,0:T(8,128)(2,1)S(1)} %slice_bitcast_fusion.2), channel_id=1, source_target_pairs={{0,96},{16,112},{32,0},{48,16},{64,32},{80,48},{96,64},{112,80},{1... | collective-permute-start | bytes 786440 | tf_op jit(solution)/shard_map/ppermute | solution.py:60
  51.6 14.7 %collective-permute-start.2 = (bf16[2,128,1024]{2,1,0:T(8,128)(2,1)S(1)}, bf16[2,128,1024]{2,1,0:T(8,128)(2,1)S(1)}, u32[]{:S(2)}, u32[]{:S(2)}) collective-permute-start(bf16[2,128,1024]{2,1,0:T(8,128)(2,1)S(1)} %pad_maximum_fusion.refs_0_), channel_id=1, source_target_pairs={{0,16},{16,0},{32,48},{48,32},{64,80},{80,64},{96,112},{112,96},{1... | collective-permute-start | bytes 1572872 | tf_op jit(solution)/shard_map/ppermute | solution.py:64
  59.2 8.6 %collective-permute-start.9 = (bf16[2,128,1024]{2,1,0:T(8,128)(2,1)S(1)}, bf16[2,128,1024]{2,1,0:T(8,128)(2,1)S(1)}, u32[]{:S(2)}, u32[]{:S(2)}) collective-permute-start(bf16[2,128,1024]{2,1,0:T(8,128)(2,1)S(1)} %pad_maximum_fusion.1.refs_6_), channel_id=1, source_target_pairs={{0,16},{16,0},{32,48},{48,32},{64,80},{80,64},{96,112},{112,96},{1... | collective-permute-start | bytes 1572872 | tf_op jit(solution)/shard_map/ppermute | solution.py:64
  84.7 11.8 %collective-permute-start.10 = (bf16[128,1024]{1,0:T(8,128)(2,1)S(1)}, bf16[128,1024]{1,0:T(8,128)(2,1)S(1)}, u32[]{:S(2)}, u32[]{:S(2)}) collective-permute-start(bf16[128,1024]{1,0:T(8,128)(2,1)S(1)} %get-tuple-element.90), channel_id=1, source_target_pairs={{0,0},{1,1},{2,16},{3,17},{4,32},{5,33},{6,48},{7,49},{8,64},{9,65... | collective-permute-start | bytes 786440 | tf_op jit(solution)/shard_map/ppermute | solution.py:46
  89.0 11.3 %collective-permute-start.11 = (bf16[128,1024]{1,0:T(8,128)(2,1)S(1)}, bf16[128,1024]{1,0:T(8,128)(2,1)S(1)}, u32[]{:S(2)}, u32[]{:S(2)}) collective-permute-start(bf16[128,1024]{1,0:T(8,128)(2,1)S(1)} %get-tuple-element.89), channel_id=1, source_target_pairs={{0,1},{1,0},{2,17},{3,16},{4,33},{5,32},{6,49},{7,48},{8,65},{9,64... | collective-permute-start | bytes 786440 | tf_op jit(solution)/shard_map/ppermute | solution.py:46
  101.9 19.1 %collective-permute-start.13 = (bf16[2,128,1024]{2,1,0:T(8,128)(2,1)S(1)}, bf16[2,128,1024]{2,1,0:T(8,128)(2,1)S(1)}, u32[]{:S(2)}, u32[]{:S(2)}) collective-permute-start(bf16[2,128,1024]{2,1,0:T(8,128)(2,1)S(1)} %pad_maximum_fusion.2), channel_id=1, source_target_pairs={{0,32},{16,48},{32,64},{48,80},{64,96},{80,112},{96,0},{112,16},{1... | collective-permute-start | bytes 1572872 | tf_op jit(solution)/shard_map/ppermute | solution.py:57
  111.7 18.8 %collective-permute-start.15 = (bf16[2,128,1024]{2,1,0:T(8,128)(2,1)S(1)}, bf16[2,128,1024]{2,1,0:T(8,128)(2,1)S(1)}, u32[]{:S(2)}, u32[]{:S(2)}) collective-permute-start(bf16[2,128,1024]{2,1,0:T(8,128)(2,1)S(1)} %pad_maximum_fusion.2), channel_id=1, source_target_pairs={{0,96},{16,112},{32,0},{48,16},{64,32},{80,48},{96,64},{112,80},{1... | collective-permute-start | bytes 1572872 | tf_op jit(solution)/shard_map/ppermute | solution.py:58
  111.9 23.3 %collective-permute-start.12 = (bf16[2,128,1024]{2,1,0:T(8,128)(2,1)S(1)}, bf16[2,128,1024]{2,1,0:T(8,128)(2,1)}, u32[]{:S(2)}, u32[]{:S(2)}) collective-permute-start(bf16[2,128,1024]{2,1,0:T(8,128)(2,1)S(1)} %pad_maximum_fusion.2), channel_id=1, source_target_pairs={{0,16},{16,0},{32,48},{48,32},{64,80},{80,64},{96,112},{112,96},{1... | collective-permute-start | bytes 1572872 | tf_op jit(solution)/shard_map/ppermute | solution.py:64
  121.1 16.9 %collective-permute-start.17 = (bf16[128,1024]{1,0:T(8,128)(2,1)S(1)}, bf16[128,1024]{1,0:T(8,128)(2,1)S(1)}, u32[]{:S(2)}, u32[]{:S(2)}) collective-permute-start(bf16[128,1024]{1,0:T(8,128)(2,1)S(1)} %slice_bitcast_fusion.1), channel_id=1, source_target_pairs={{0,32},{16,48},{32,64},{48,80},{64,96},{80,112},{96,0},{112,16},{1... | collective-permute-start | bytes 786440 | tf_op jit(solution)/shard_map/ppermute | solution.py:60
  126.4 14.7 %collective-permute-start.14 = (bf16[2,128,1024]{2,1,0:T(8,128)(2,1)S(1)}, bf16[2,128,1024]{2,1,0:T(8,128)(2,1)S(1)}, u32[]{:S(2)}, u32[]{:S(2)}) collective-permute-start(bf16[2,128,1024]{2,1,0:T(8,128)(2,1)S(1)} %collective-permute-done.13), channel_id=1, source_target_pairs={{0,16},{16,0},{32,48},{48,32},{64,80},{80,64},{96,112},{112,96},{1... | collective-permute-start | bytes 1572872 | tf_op jit(solution)/shard_map/ppermute | solution.py:64
  131.3 8.9 %collective-permute-start.18 = (bf16[128,1024]{1,0:T(8,128)(2,1)}, bf16[128,1024]{1,0:T(8,128)(2,1)S(1)}, u32[]{:S(2)}, u32[]{:S(2)}) collective-permute-start(bf16[128,1024]{1,0:T(8,128)(2,1)} %slice_bitcast_fusion), channel_id=1, source_target_pairs={{0,96},{16,112},{32,0},{48,16},{64,32},{80,48},{96,64},{112,80},{1... | collective-permute-start | bytes 786440 | tf_op jit(solution)/shard_map/ppermute | solution.py:60
  147.0 47.5 %all-to-all-start = ((bf16[16,144,128]{2,1,0:T(8,128)(2,1)}), bf16[16,144,128]{2,1,0:T(8,128)(2,1)S(1)}, u32[]{:S(2)}, u32[]{:S(2)}) async-start(bf16[16,144,128]{2,1,0:T(8,128)(2,1)} %fusion.1), calls=%async_computation | async-start | bytes 1179648 | tf_op jit(solution)/shard_map/all_to_all | solution.py:390
  156.6 24.9 %collective-permute-start.20 = (bf16[4,64,1024]{2,1,0:T(8,128)(2,1)S(1)}, bf16[4,64,1024]{2,1,0:T(8,128)(2,1)S(1)}, u32[]{:S(2)}, u32[]{:S(2)}) collective-permute-start(bf16[4,64,1024]{2,1,0:T(8,128)(2,1)S(1)} %bitcast.66), channel_id=1, source_target_pairs={{0,1},{1,2},{2,3},{3,0},{4,5},{5,6},{6,7},{7,4},{8,9},{9,10},{10,1... | collective-permute-start | bytes 1572872 | tf_op jit(solution)/shard_map/ppermute | solution.py:148
  157.9 23.5 %collective-permute-start.21 = (bf16[4,64,1024]{2,1,0:T(8,128)(2,1)S(1)}, bf16[4,64,1024]{2,1,0:T(8,128)(2,1)S(1)}, u32[]{:S(2)}, u32[]{:S(2)}) collective-permute-start(bf16[4,64,1024]{2,1,0:T(8,128)(2,1)S(1)} %bitcast.65), channel_id=1, source_target_pairs={{0,3},{1,0},{2,1},{3,2},{4,7},{5,4},{6,5},{7,6},{8,11},{9,8},{10,9... | collective-permute-start | bytes 1572872 | tf_op jit(solution)/shard_map/ppermute | solution.py:148
  163.0 25.0 %collective-permute-start.24 = (bf16[4,64,1024]{2,1,0:T(8,128)(2,1)S(1)}, bf16[4,64,1024]{2,1,0:T(8,128)(2,1)S(1)}, u32[]{:S(2)}, u32[]{:S(2)}) collective-permute-start(bf16[4,64,1024]{2,1,0:T(8,128)(2,1)S(1)} %bitcast.64), channel_id=1, source_target_pairs={{0,4},{1,5},{2,6},{3,7},{4,8},{5,9},{6,10},{7,11},{8,12},{9,13},{1... | collective-permute-start | bytes 1572872 | tf_op jit(solution)/shard_map/ppermute | solution.py:148
  164.6 23.4 %collective-permute-start.25 = (bf16[4,64,1024]{2,1,0:T(8,128)(2,1)S(1)}, bf16[4,64,1024]{2,1,0:T(8,128)(2,1)S(1)}, u32[]{:S(2)}, u32[]{:S(2)}) collective-permute-start(bf16[4,64,1024]{2,1,0:T(8,128)(2,1)S(1)} %bitcast.63), channel_id=1, source_target_pairs={{0,12},{1,13},{2,14},{3,15},{4,0},{5,1},{6,2},{7,3},{8,4},{9,5},{1... | collective-permute-start | bytes 1572872 | tf_op jit(solution)/shard_map/ppermute | solution.py:148
  185.3 26.0 %collective-permute-start.22 = (bf16[4,128,1024]{2,1,0:T(8,128)(2,1)}, bf16[4,128,1024]{2,1,0:T(8,128)(2,1)S(1)}, u32[]{:S(2)}, u32[]{:S(2)}) collective-permute-start(bf16[4,128,1024]{2,1,0:T(8,128)(2,1)} %get-tuple-element.56), channel_id=1, source_target_pairs={{0,1},{1,2},{2,3},{3,0},{4,5},{5,6},{6,7},{7,4},{8,9},{9,10},{10,1... | collective-permute-start | bytes 3145736 | tf_op jit(solution)/shard_map/ppermute | solution.py:148
  185.3 26.0 %collective-permute-start.23 = (bf16[4,128,1024]{2,1,0:T(8,128)(2,1)}, bf16[4,128,1024]{2,1,0:T(8,128)(2,1)}, u32[]{:S(2)}, u32[]{:S(2)}) collective-permute-start(bf16[4,128,1024]{2,1,0:T(8,128)(2,1)} %get-tuple-element.57), channel_id=1, source_target_pairs={{0,3},{1,0},{2,1},{3,2},{4,7},{5,4},{6,5},{7,6},{8,11},{9,8},{10,9... | collective-permute-start | bytes 3145736 | tf_op jit(solution)/shard_map/ppermute | solution.py:148
  191.8 36.0 %collective-permute-start.26 = (bf16[4,128,1024]{2,1,0:T(8,128)(2,1)}, bf16[4,128,1024]{2,1,0:T(8,128)(2,1)}, u32[]{:S(2)}, u32[]{:S(2)}) collective-permute-start(bf16[4,128,1024]{2,1,0:T(8,128)(2,1)} %get-tuple-element.61), channel_id=1, source_target_pairs={{0,4},{1,5},{2,6},{3,7},{4,8},{5,9},{6,10},{7,11},{8,12},{9,13},{1... | collective-permute-start | bytes 3145736 | tf_op jit(solution)/shard_map/ppermute | solution.py:148
  191.8 36.9 %collective-permute-start.27 = (bf16[4,128,1024]{2,1,0:T(8,128)(2,1)}, bf16[4,128,1024]{2,1,0:T(8,128)(2,1)}, u32[]{:S(2)}, u32[]{:S(2)}) collective-permute-start(bf16[4,128,1024]{2,1,0:T(8,128)(2,1)} %get-tuple-element.62), channel_id=1, source_target_pairs={{0,12},{1,13},{2,14},{3,15},{4,0},{5,1},{6,2},{7,3},{8,4},{9,5},{1... | collective-permute-start | bytes 3145736 | tf_op jit(solution)/shard_map/ppermute | solution.py:148
  198.2 52.4 %all-to-all-start.1 = ((bf16[16,3,128,128]{3,2,1,0:T(8,128)(2,1)}), bf16[16,3,128,128]{3,2,1,0:T(8,128)(2,1)S(1)}, u32[]{:S(2)}, u32[]{:S(2)}) async-start(bf16[16,3,128,128]{3,2,1,0:T(8,128)(2,1)} %shard_map.138), calls=%async_computation.2 | async-start | bytes 3145728 | tf_op jit(solution)/shard_map/all_to_all | solution.py:394
  232.3 11.4 %collective-permute-start.29 = (bf16[128,1024]{1,0:T(8,128)(2,1)S(1)}, bf16[128,1024]{1,0:T(8,128)(2,1)S(1)}, u32[]{:S(2)}, u32[]{:S(2)}) collective-permute-start(bf16[128,1024]{1,0:T(8,128)(2,1)S(1)} %get-tuple-element.67), channel_id=1, source_target_pairs={{0,8},{1,9},{2,10},{3,11},{4,12},{5,13},{6,14},{7,15},{8,0},{9,1},... | collective-permute-start | bytes 786440 | tf_op jit(solution)/shard_map/ppermute | solution.py:148
  240.7 9.2 %collective-permute-start.31 = (bf16[128,1024]{1,0:T(8,128)(2,1)S(1)}, bf16[128,1024]{1,0:T(8,128)(2,1)S(1)}, u32[]{:S(2)}, u32[]{:S(2)}) collective-permute-start(bf16[128,1024]{1,0:T(8,128)(2,1)S(1)} %get-tuple-element.72), channel_id=1, source_target_pairs={{0,1},{1,2},{2,3},{3,0},{4,5},{5,6},{6,7},{7,4},{8,9},{9,10},{10,1... | collective-permute-start | bytes 786440 | tf_op jit(solution)/shard_map/ppermute | solution.py:148
  240.7 9.2 %collective-permute-start.32 = (bf16[128,1024]{1,0:T(8,128)(2,1)S(1)}, bf16[128,1024]{1,0:T(8,128)(2,1)S(1)}, u32[]{:S(2)}, u32[]{:S(2)}) collective-permute-start(bf16[128,1024]{1,0:T(8,128)(2,1)S(1)} %get-tuple-element.73), channel_id=1, source_target_pairs={{0,2},{1,3},{2,0},{3,1},{4,6},{5,7},{6,4},{7,5},{8,10},{9,11},{10,... | collective-permute-start | bytes 786440 | tf_op jit(solution)/shard_map/ppermute | solution.py:148
  240.7 9.8 %collective-permute-start.33 = (bf16[128,1024]{1,0:T(8,128)(2,1)S(1)}, bf16[128,1024]{1,0:T(8,128)(2,1)S(1)}, u32[]{:S(2)}, u32[]{:S(2)}) collective-permute-start(bf16[128,1024]{1,0:T(8,128)(2,1)S(1)} %get-tuple-element.74), channel_id=1, source_target_pairs={{0,3},{1,0},{2,1},{3,2},{4,7},{5,4},{6,5},{7,6},{8,11},{9,8},{10,9... | collective-permute-start | bytes 786440 | tf_op jit(solution)/shard_map/ppermute | solution.py:148
  255.4 10.8 %collective-permute-start.34 = (f32[4,128,128]{2,1,0:T(8,128)S(1)}, f32[4,128,128]{2,1,0:T(8,128)S(1)}, u32[]{:S(2)}, u32[]{:S(2)}) collective-permute-start(f32[4,128,128]{2,1,0:T(8,128)S(1)} %get-tuple-element.76), channel_id=1, source_target_pairs={{0,16},{16,0},{32,48},{48,32},{64,80},{80,64},{96,112},{112,96},{1... | collective-permute-start | bytes 786440 | tf_op jit(solution)/shard_map/ppermute | solution.py:208
  266.2 8.6 %collective-permute-start.35 = (bf16[4,128,128]{2,1,0:T(8,128)(2,1)S(1)}, bf16[4,128,128]{2,1,0:T(8,128)(2,1)S(1)}, u32[]{:S(2)}, u32[]{:S(2)}) collective-permute-start(bf16[4,128,128]{2,1,0:T(8,128)(2,1)S(1)} %add_convert_fusion.a), channel_id=1, source_target_pairs={{0,96},{16,112},{32,0},{48,16},{64,32},{80,48},{96,64},{112,80},{1... | collective-permute-start | bytes 393224 | tf_op jit(solution)/shard_map/ppermute | solution.py:210
  269.5 9.1 %collective-permute-start.37 = (bf16[4,128,128]{2,1,0:T(8,128)(2,1)S(1)}, bf16[4,128,128]{2,1,0:T(8,128)(2,1)S(1)}, u32[]{:S(2)}, u32[]{:S(2)}) collective-permute-start(bf16[4,128,128]{2,1,0:T(8,128)(2,1)S(1)} %add_convert_fusion.a), channel_id=1, source_target_pairs={{0,32},{16,48},{32,64},{48,80},{64,96},{80,112},{96,0},{112,16},{1... | collective-permute-start | bytes 393224 | tf_op jit(solution)/shard_map/ppermute | solution.py:210
  (26 other events, 465.2 us)
Sparse Core Ops, SparseCore 0:
  83.4 105.0 reduce-scatter.1
